TPU v7x, 32 devices: a whole 2x2x4 slice. The times are simulated.
32 devices in a mesh: dp: 8 (over y, x, core), seq: 4 (over z).
Axes of the slice: x: 2, y: 2, z: 4, core: 2. Of those that a mesh axis runs over, the one named last changes fastest.
Arguments:
- frames: bfloat16 [8, 1024, 1536], P('dp', 'seq'), may hold values from -100 to 100
- time_token: bfloat16 [8, 1536], P('dp'), may hold values from -6 to 6
- cond_ids: int32 [8, 128], P('dp'), may hold values from 0 to 16383
- cond_mask: int32 [8, 128], P('dp'), may hold values from 0 to 1, as said below
- lengths: int32 [8], P('dp'), may hold values from 108 to 1024, as said below
- cond_table: bfloat16 [16384, 768], P('seq'), may hold values from -10 to 10
- cotangent: bfloat16 [8, 1024, 1536], P('dp', 'seq'), may hold values from -6 to 6
- attn_weight: float32 [1536, 9216], P(('dp', 'seq')), may hold values from -1 to 1
- cross_weight: float32 [768, 3072], P(('dp', 'seq')), may hold values from -0.21875 to 0.21875
- norm_param: float32 [6, 1536], P(None, ('dp', 'seq')), may hold values from -2 to 3
- ff_weight: float32 [1536, 18432], P(('dp', 'seq')), may hold values from -0.5 to 0.5
- attn_first: float32 [1536, 9216], P(('dp', 'seq')), may hold values from -0.0004272461 to 0.0004272461
- attn_second: float32 [1536, 9216], P(('dp', 'seq')), may hold values from 5.5758966e-09 to 2.2303587e-08
- cross_first: float32 [768, 3072], P(('dp', 'seq')), may hold values from -0.0004272461 to 0.0004272461
- cross_second: float32 [768, 3072], P(('dp', 'seq')), may hold values from 5.5758966e-09 to 2.2303587e-08
- norm_first: float32 [6, 1536], P(None, ('dp', 'seq')), may hold values from -0.0024414062 to 0.0024414062
- norm_second: float32 [6, 1536], P(None, ('dp', 'seq')), may hold values from 2.0073227e-07 to 8.029291e-07
- ff_first: float32 [1536, 18432], P(('dp', 'seq')), may hold values from -0.0008544922 to 0.0008544922
- ff_second: float32 [1536, 18432], P(('dp', 'seq')), may hold values from 2.2303587e-08 to 8.9214346e-08
Outputs:
- layer_out: bfloat16 [8, 1024, 1536], P('dp', 'seq')
- frames_grad: float32 [8, 1024, 1536], P('dp', 'seq')
- grad_norm: float32 [], replicated
- attn_new: float32 [1536, 9216], P(('dp', 'seq'))
- cross_new: float32 [768, 3072], P(('dp', 'seq'))
- norm_new: float32 [6, 1536], P(None, ('dp', 'seq'))
- ff_new: float32 [1536, 18432], P(('dp', 'seq'))
- attn_first_new: float32 [1536, 9216], P(('dp', 'seq'))
- cross_first_new: float32 [768, 3072], P(('dp', 'seq'))
- norm_first_new: float32 [6, 1536], P(None, ('dp', 'seq'))
- ff_first_new: float32 [1536, 18432], P(('dp', 'seq'))
- attn_second_new: float32 [1536, 9216], P(('dp', 'seq'))
- cross_second_new: float32 [768, 3072], P(('dp', 'seq'))
- norm_second_new: float32 [6, 1536], P(None, ('dp', 'seq'))
- ff_second_new: float32 [1536, 18432], P(('dp', 'seq'))
Inputs may be any that keep to these rules, and one draw needn't show every extreme that they name: `lengths`: one clip of every draw has exactly 1024 frames and another exactly max(1, 108). `cond_mask`: each clip's present tokens form a leading run of 16 or more positions; some clip has exactly 16.
All inputs are finite; a program needn't handle non-finite values.
Results may differ from a plain program's by a relative error of at most 0.03.
Values may be sent and summed in bfloat16 or wider, within the bound.
A program may use at most 832 MiB of HBM per device.

v0:
```python
import jax
import jax.numpy as jnp
from jax import lax
from jax.sharding import PartitionSpec as P

HEADS = 24
HDIM = 64
FF = 6144
UPDATE_STEP = 10


norm_eps = 1e-05
beta_first = 0.5
beta_second = 0.5
adam_eps = 1e-08
matrix_decay = 0.01
matrix_rate = 0.03
gain_rate = 0.25
clip_limit = 1.0
masked_score = -1e30


def layer_norm(values, gain_row, bias_row):
    center = values - jnp.mean(values, axis=-1, keepdims=True)
    spread = jnp.mean(center * center, axis=-1, keepdims=True)
    return center * lax.rsqrt(spread + norm_eps) * gain_row + bias_row


def rotary_tables(positions, head_size):
    half_size = head_size // 2
    frequency = 10000.0 ** (-jnp.arange(half_size, dtype=jnp.float32) / half_size)
    angles = positions.astype(jnp.float32)[:, None] * frequency[None, :]
    return (jnp.cos(angles)[:, None, :], jnp.sin(angles)[:, None, :])


def rotate(values, cosine_table, sine_table):
    half_size = values.shape[-1] // 2
    first_half = values[..., :half_size]
    second_half = values[..., half_size:]
    return jnp.concatenate(
        [
            first_half * cosine_table - second_half * sine_table,
            second_half * cosine_table + first_half * sine_table,
        ],
        axis=-1,
    )


def outer_sum(left_mat, right_mat):
    return lax.dot_general(
        left_mat, right_mat, (((0,), (0,)), ((), ())), preferred_element_type=jnp.float32
    )


def times_transposed(left_mat, right_mat):
    return lax.dot_general(
        left_mat, right_mat, (((1,), (1,)), ((), ())), preferred_element_type=jnp.float32
    )


def split_parts(values):
    upper = values.astype(jnp.bfloat16)
    lower = (values - upper.astype(jnp.float32)).astype(jnp.bfloat16)
    return (upper, lower)


def split_outer(left_low, right_full):
    upper, lower = split_parts(right_full)
    return outer_sum(left_low, upper) + outer_sum(left_low, lower)


def split_times_transposed(left_full, right_low):
    upper, lower = split_parts(left_full)
    return times_transposed(upper, right_low) + times_transposed(lower, right_low)


def self_scores(queries, keys, stamp_key, keep):
    score_scale = HDIM ** (-0.5)
    frame_part = (
        jnp.einsum("cqhd,ckhd->chqk", queries, keys, preferred_element_type=jnp.float32)
        * score_scale
    )
    frame_part = jnp.where(keep[:, None, None, :], frame_part, masked_score)
    stamp_part = (
        jnp.einsum("cqhd,chd->chq", queries, stamp_key, preferred_element_type=jnp.float32)
        * score_scale
    )
    return (frame_part, stamp_part)


def self_forward(queries, keys, values, stamp_key, stamp_value, keep):
    frame_scores, stamp_scores = self_scores(queries, keys, stamp_key, keep)
    top_score = jnp.maximum(jnp.max(frame_scores, axis=-1), stamp_scores)
    frame_expo = jnp.exp(frame_scores - top_score[..., None])
    stamp_expo = jnp.exp(stamp_scores - top_score)
    denom = jnp.sum(frame_expo, axis=-1) + stamp_expo
    self_lse = top_score + jnp.log(denom)
    frame_prob = (frame_expo / denom[..., None]).astype(jnp.bfloat16)
    stamp_prob = (stamp_expo / denom).astype(jnp.bfloat16)
    mixed = jnp.einsum(
        "chqk,ckhd->cqhd", frame_prob, values, preferred_element_type=jnp.float32
    ) + jnp.einsum("chq,chd->cqhd", stamp_prob, stamp_value, preferred_element_type=jnp.float32)
    return (mixed, self_lse)


def self_backward(queries, keys, values, stamp_key, stamp_value, keep, self_lse, grad_mixed):
    score_scale = HDIM ** (-0.5)
    frame_scores, stamp_scores = self_scores(queries, keys, stamp_key, keep)
    frame_prob = jnp.exp(frame_scores - self_lse[..., None])
    stamp_prob = jnp.exp(stamp_scores - self_lse)
    grad_frame_prob = jnp.einsum(
        "cqhd,ckhd->chqk", grad_mixed, values, preferred_element_type=jnp.float32
    )
    grad_stamp_prob = jnp.einsum(
        "cqhd,chd->chq", grad_mixed, stamp_value, preferred_element_type=jnp.float32
    )
    delta = jnp.sum(frame_prob * grad_frame_prob, axis=-1) + stamp_prob * grad_stamp_prob
    grad_frame_scores = (frame_prob * (grad_frame_prob - delta[..., None])).astype(jnp.bfloat16)
    grad_stamp_scores = (stamp_prob * (grad_stamp_prob - delta)).astype(jnp.bfloat16)
    grad_queries = (
        jnp.einsum("chqk,ckhd->cqhd", grad_frame_scores, keys, preferred_element_type=jnp.float32)
        + jnp.einsum(
            "chq,chd->cqhd", grad_stamp_scores, stamp_key, preferred_element_type=jnp.float32
        )
    ) * score_scale
    key_part = (
        jnp.einsum(
            "chqk,cqhd->ckhd", grad_frame_scores, queries, preferred_element_type=jnp.float32
        )
        * score_scale
    )
    value_part = jnp.einsum(
        "chqk,cqhd->ckhd",
        frame_prob.astype(jnp.bfloat16),
        grad_mixed,
        preferred_element_type=jnp.float32,
    )
    grad_stamp_key = (
        jnp.einsum("chq,cqhd->chd", grad_stamp_scores, queries, preferred_element_type=jnp.float32)
        * score_scale
    )
    grad_stamp_value = jnp.einsum(
        "chq,cqhd->chd",
        stamp_prob.astype(jnp.bfloat16),
        grad_mixed,
        preferred_element_type=jnp.float32,
    )
    return (grad_queries, key_part, value_part, grad_stamp_key, grad_stamp_value)


def cross_scores(query, keys, keep):
    score_scale = HDIM ** (-0.5)
    scores = (
        jnp.einsum("cqhd,ckhd->chqk", query, keys, preferred_element_type=jnp.float32) * score_scale
    )
    return jnp.where(keep[:, None, None, :], scores, masked_score)


def cross_forward(query, keys, values, keep):
    scores = cross_scores(query, keys, keep)
    top_score = jnp.max(scores, axis=-1)
    expo = jnp.exp(scores - top_score[..., None])
    denom = jnp.sum(expo, axis=-1)
    cross_lse = top_score + jnp.log(denom)
    prob = (expo / denom[..., None]).astype(jnp.bfloat16)
    mixed = jnp.einsum("chqk,ckhd->cqhd", prob, values, preferred_element_type=jnp.float32)
    return (mixed, cross_lse)


def cross_backward(query, keys, values, keep, cross_lse, grad_mixed):
    score_scale = HDIM ** (-0.5)
    prob = jnp.exp(cross_scores(query, keys, keep) - cross_lse[..., None])
    grad_prob = jnp.einsum(
        "cqhd,ckhd->chqk", grad_mixed, values, preferred_element_type=jnp.float32
    )
    delta = jnp.sum(prob * grad_prob, axis=-1)
    grad_scores = (prob * (grad_prob - delta[..., None])).astype(jnp.bfloat16)
    grad_query = (
        jnp.einsum("chqk,ckhd->cqhd", grad_scores, keys, preferred_element_type=jnp.float32)
        * score_scale
    )
    grad_keys = (
        jnp.einsum("chqk,cqhd->ckhd", grad_scores, query, preferred_element_type=jnp.float32)
        * score_scale
    )
    grad_values = jnp.einsum(
        "chqk,cqhd->ckhd", prob.astype(jnp.bfloat16), grad_mixed, preferred_element_type=jnp.float32
    )
    return (grad_query, grad_keys, grad_values)


def adam_step(weight, first, second, gradient, step_rate, decay_rate):
    first_new = beta_first * first + (1.0 - beta_first) * gradient
    second_new = beta_second * second + (1.0 - beta_second) * gradient * gradient
    fix_first = 1.0 - beta_first**UPDATE_STEP
    fix_second = 1.0 - beta_second**UPDATE_STEP
    normed_step = first_new / fix_first / (jnp.sqrt(second_new / fix_second) + adam_eps)
    return (weight - step_rate * (normed_step + decay_rate * weight), first_new, second_new)


def per_device(
    frames,
    time_token,
    cond_ids,
    cond_mask,
    lengths,
    cond_table,
    cotangent,
    attn_weight,
    cross_weight,
    norm_param,
    ff_weight,
    attn_first,
    attn_second,
    cross_first,
    cross_second,
    norm_first,
    norm_second,
    ff_first,
    ff_second,
):
    clip_count, frame_rows, wide = frames.shape
    hidden_width = FF
    token_count = clip_count * frame_rows
    seq_count = lax.axis_size("seq")
    seq_frames = frame_rows * seq_count
    seq_place = lax.axis_index("seq")
    vocab_rows = cond_table.shape[0]
    relative = cond_ids - seq_place * vocab_rows
    inside = (relative >= 0) & (relative < vocab_rows)
    picked = jnp.take(cond_table, jnp.clip(relative, 0, vocab_rows - 1), axis=0).astype(jnp.float32)
    picked = jnp.where(inside[..., None], picked, 0.0)
    cond = lax.psum(picked.astype(jnp.bfloat16), "seq")
    cond_count = cond.shape[1]
    cond_flat = cond.reshape(clip_count * cond_count, cond.shape[2])
    cond_width = cond.shape[2]
    cond_keep = cond_mask > 0
    attn_low = attn_weight.astype(jnp.bfloat16)
    cross_low = cross_weight.astype(jnp.bfloat16)
    norm_low = norm_param.astype(jnp.bfloat16)
    ff_low = ff_weight.astype(jnp.bfloat16)
    stream = frames.astype(jnp.float32).reshape(token_count, wide)
    stamps = time_token.astype(jnp.float32)
    positions = seq_place * frame_rows + jnp.arange(frame_rows)
    key_keep = jnp.arange(seq_frames)[None, :] < lengths[:, None]
    frame_valid = (positions[None, :] < lengths[:, None]).reshape(token_count)
    grad_out = cotangent.astype(jnp.float32).reshape(token_count, wide) * frame_valid[
        :, None
    ].astype(jnp.float32)
    grad_out_low = grad_out.astype(jnp.bfloat16)
    piece_heads = HEADS // seq_count
    piece_wide = wide // seq_count
    piece_ff = hidden_width // seq_count
    group_rows = clip_count * seq_frames

    def pieces():
        norm_copies = jnp.tile(norm_low[None], (1, 1, seq_count))
        moved_attn, moved_cross, moved_ff, moved_norm = (
            lax.all_to_all(
                attn_low.reshape(-1, 6, wide), "seq", split_axis=2, concat_axis=0, tiled=True
            ),
            lax.all_to_all(
                cross_low.reshape(-1, 2, wide), "seq", split_axis=2, concat_axis=0, tiled=True
            ),
            lax.all_to_all(
                ff_low.reshape(-1, 3, hidden_width), "seq", split_axis=2, concat_axis=0, tiled=True
            ),
            lax.all_to_all(norm_copies, "seq", split_axis=2, concat_axis=0, tiled=True),
        )
        attn_cols, cross_cols, ff_cols, norm_blocks = (
            lax.all_gather(moved_attn, "dp", axis=0, tiled=True),
            lax.all_gather(moved_cross, "dp", axis=0, tiled=True),
            lax.all_gather(moved_ff, "dp", axis=0, tiled=True),
            lax.all_gather(moved_norm, "dp", axis=0, tiled=True),
        )
        gains = norm_blocks.transpose(1, 0, 2).reshape(6, wide).astype(jnp.float32)
        return (attn_cols, cross_cols, ff_cols, gains)

    def collect(rows):
        whole = lax.all_gather(
            rows.reshape(clip_count, frame_rows, wide), "seq", axis=1, tiled=True
        )
        return whole.reshape(group_rows, wide)

    def spread(partial_value):
        mine = lax.psum_scatter(
            partial_value.reshape(clip_count, seq_frames, wide).astype(jnp.bfloat16),
            "seq",
            scatter_dimension=1,
            tiled=True,
        ).astype(jnp.float32)
        return mine.reshape(token_count, wide)

    attn_cols, cross_cols, ff_cols, gain_rows = pieces()
    group_shape = (clip_count, seq_frames, piece_heads, HDIM)
    cosine_table, sine_table = rotary_tables(jnp.arange(seq_frames), HDIM)
    normed_one = layer_norm(stream, gain_rows[0], gain_rows[1]).astype(jnp.bfloat16)
    group_one = collect(normed_one)
    projected = jnp.dot(
        group_one,
        attn_cols[:, :3].reshape(wide, 3 * piece_wide),
        preferred_element_type=jnp.float32,
    )
    queries = rotate(
        projected[:, :piece_wide].reshape(group_shape), cosine_table, sine_table
    ).astype(jnp.bfloat16)
    all_keys = rotate(
        projected[:, piece_wide : 2 * piece_wide].reshape(group_shape), cosine_table, sine_table
    ).astype(jnp.bfloat16)
    all_values = projected[:, 2 * piece_wide :].astype(jnp.bfloat16).reshape(group_shape)
    stamp_normed = layer_norm(stamps, gain_rows[0], gain_rows[1]).astype(jnp.bfloat16)
    stamp_pair = jnp.dot(
        stamp_normed,
        attn_cols[:, 1:3].reshape(wide, 2 * piece_wide),
        preferred_element_type=jnp.float32,
    )
    stamp_key = (
        stamp_pair[:, :piece_wide].astype(jnp.bfloat16).reshape(clip_count, piece_heads, HDIM)
    )
    stamp_value = (
        stamp_pair[:, piece_wide:].astype(jnp.bfloat16).reshape(clip_count, piece_heads, HDIM)
    )
    self_mixed, self_lse = self_forward(
        queries, all_keys, all_values, stamp_key, stamp_value, key_keep
    )
    self_low = self_mixed.astype(jnp.bfloat16).reshape(group_rows, piece_wide)
    resid_one = stream + spread(times_transposed(self_low, attn_cols[:, 3]))
    normed_two = layer_norm(resid_one, gain_rows[2], gain_rows[3]).astype(jnp.bfloat16)
    group_two = collect(normed_two)
    cross_query = jnp.dot(group_two, attn_cols[:, 4], preferred_element_type=jnp.float32)
    cross_query = cross_query.astype(jnp.bfloat16).reshape(group_shape)
    cond_pair = jnp.dot(
        cond_flat,
        cross_cols.reshape(cond_width, 2 * piece_wide),
        preferred_element_type=jnp.float32,
    )
    cond_shape = (clip_count, cond_count, piece_heads, HDIM)
    cross_keys = cond_pair[:, :piece_wide].astype(jnp.bfloat16).reshape(cond_shape)
    cross_values = cond_pair[:, piece_wide:].astype(jnp.bfloat16).reshape(cond_shape)
    cross_mixed, cross_lse = cross_forward(cross_query, cross_keys, cross_values, cond_keep)
    cross_low_out = cross_mixed.astype(jnp.bfloat16).reshape(group_rows, piece_wide)
    resid_two = resid_one + spread(times_transposed(cross_low_out, attn_cols[:, 5]))
    normed_three = layer_norm(resid_two, gain_rows[4], gain_rows[5]).astype(jnp.bfloat16)
    group_three = collect(normed_three)
    gate_up = jnp.dot(
        group_three, ff_cols[:, :2].reshape(wide, 2 * piece_ff), preferred_element_type=jnp.float32
    )
    gate_val = gate_up[:, :piece_ff]
    up_val = gate_up[:, piece_ff:]
    hidden = (jax.nn.silu(gate_val) * up_val).astype(jnp.bfloat16)
    branch = spread(times_transposed(hidden, ff_cols[:, 2]))
    layer_out = (resid_two + branch).astype(jnp.bfloat16).reshape(clip_count, frame_rows, wide)
    attn_cols, cross_cols, ff_cols, gain_rows = pieces()
    group_grad_out = collect(grad_out_low)
    grad_hidden = jnp.dot(group_grad_out, ff_cols[:, 2], preferred_element_type=jnp.float32)
    sigmoid_gate = jax.nn.sigmoid(gate_val)
    grad_gate = grad_hidden * up_val * sigmoid_gate * (1.0 + gate_val * (1.0 - sigmoid_gate))
    grad_up = grad_hidden * gate_val * sigmoid_gate
    grad_gate_up = jnp.concatenate([grad_gate, grad_up], axis=1).astype(jnp.bfloat16)
    grad_normed_three = spread(
        times_transposed(grad_gate_up, ff_cols[:, :2].reshape(wide, 2 * piece_ff))
    )
    _, norm_three_back = jax.vjp(layer_norm, resid_two, gain_rows[4], gain_rows[5])
    grad_two_part, grad_gain_three, grad_bias_three = norm_three_back(grad_normed_three)
    grad_two = grad_out + grad_two_part
    grad_cross_branch = grad_two.astype(jnp.bfloat16)
    group_cross_branch = collect(grad_cross_branch)
    grad_cross_mixed = jnp.dot(
        group_cross_branch, attn_cols[:, 5], preferred_element_type=jnp.float32
    )
    grad_cross_mixed = grad_cross_mixed.astype(jnp.bfloat16).reshape(group_shape)
    grad_cross_query, grad_cross_keys, grad_cross_values = cross_backward(
        cross_query, cross_keys, cross_values, cond_keep, cross_lse, grad_cross_mixed
    )
    grad_cross_query = grad_cross_query.astype(jnp.bfloat16).reshape(group_rows, piece_wide)
    grad_normed_two = spread(times_transposed(grad_cross_query, attn_cols[:, 4]))
    _, norm_two_back = jax.vjp(layer_norm, resid_one, gain_rows[2], gain_rows[3])
    grad_one_part, grad_gain_two, grad_bias_two = norm_two_back(grad_normed_two)
    grad_one = grad_two + grad_one_part
    grad_self_branch = grad_one.astype(jnp.bfloat16)
    group_self_branch = collect(grad_self_branch)
    grad_self_mixed = jnp.dot(
        group_self_branch, attn_cols[:, 3], preferred_element_type=jnp.float32
    )
    grad_self_mixed = grad_self_mixed.astype(jnp.bfloat16).reshape(group_shape)
    grad_queries, key_part, value_part, grad_stamp_key, grad_stamp_value = self_backward(
        queries, all_keys, all_values, stamp_key, stamp_value, key_keep, self_lse, grad_self_mixed
    )
    grad_query_raw = (
        rotate(grad_queries, cosine_table, -sine_table)
        .astype(jnp.bfloat16)
        .reshape(group_rows, piece_wide)
    )
    grad_key_raw = (
        rotate(key_part, cosine_table, -sine_table)
        .astype(jnp.bfloat16)
        .reshape(group_rows, piece_wide)
    )
    grad_value = value_part.astype(jnp.bfloat16).reshape(group_rows, piece_wide)
    grad_project = jnp.concatenate([grad_query_raw, grad_key_raw, grad_value], axis=1)
    grad_normed_one = spread(
        times_transposed(grad_project, attn_cols[:, :3].reshape(wide, 3 * piece_wide))
    )
    stamp_grad = jnp.concatenate(
        [
            grad_stamp_key.reshape(clip_count, piece_wide),
            grad_stamp_value.reshape(clip_count, piece_wide),
        ],
        axis=1,
    )
    grad_stamp_normed = split_times_transposed(
        stamp_grad, attn_cols[:, 1:3].reshape(wide, 2 * piece_wide)
    )
    _, norm_one_back = jax.vjp(layer_norm, stream, gain_rows[0], gain_rows[1])
    grad_zero_part, grad_gain_one, grad_bias_one = norm_one_back(grad_normed_one)
    _, norm_stamp_back = jax.vjp(layer_norm, stamps, gain_rows[0], gain_rows[1])
    _, grad_gain_stamp, grad_bias_stamp = norm_stamp_back(grad_stamp_normed)
    frames_grad = (grad_one + grad_zero_part).reshape(clip_count, frame_rows, wide)
    project_grad = outer_sum(group_one, grad_project)
    stamp_weight_grad = split_outer(stamp_normed, stamp_grad)
    attn_piece = jnp.stack(
        [
            project_grad[:, :piece_wide],
            project_grad[:, piece_wide : 2 * piece_wide] + stamp_weight_grad[:, :piece_wide],
            project_grad[:, 2 * piece_wide :] + stamp_weight_grad[:, piece_wide:],
            outer_sum(group_self_branch, self_low),
            outer_sum(group_two, grad_cross_query),
            outer_sum(group_cross_branch, cross_low_out),
        ],
        axis=1,
    )
    cond_grad = jnp.concatenate(
        [
            grad_cross_keys.reshape(clip_count * cond_count, piece_wide),
            grad_cross_values.reshape(clip_count * cond_count, piece_wide),
        ],
        axis=1,
    )
    cross_piece = split_outer(cond_flat, cond_grad).reshape(cond_width, 2, piece_wide)
    ff_piece = jnp.stack(
        [
            outer_sum(group_three, grad_gate_up[:, :piece_ff]),
            outer_sum(group_three, grad_gate_up[:, piece_ff:]),
            outer_sum(group_grad_out, hidden),
        ],
        axis=1,
    )
    norm_grad = jnp.stack(
        [
            grad_gain_one + grad_gain_stamp,
            grad_bias_one + grad_bias_stamp,
            grad_gain_two,
            grad_bias_two,
            grad_gain_three,
            grad_bias_three,
        ],
        axis=0,
    )
    norm_column = norm_grad.T[:, :, None]
    summed_attn, summed_cross, summed_ff, summed_norm = (
        lax.psum_scatter(
            attn_piece.astype(jnp.bfloat16), "dp", scatter_dimension=0, tiled=True
        ).astype(jnp.float32),
        lax.psum_scatter(
            cross_piece.astype(jnp.bfloat16), "dp", scatter_dimension=0, tiled=True
        ).astype(jnp.float32),
        lax.psum_scatter(
            ff_piece.astype(jnp.bfloat16), "dp", scatter_dimension=0, tiled=True
        ).astype(jnp.float32),
        lax.psum_scatter(
            norm_column.astype(jnp.bfloat16), "dp", scatter_dimension=0, tiled=True
        ).astype(jnp.float32),
    )
    owned_attn, owned_cross, owned_ff, owned_norm = (
        lax.all_to_all(
            summed_attn.astype(jnp.bfloat16), "seq", split_axis=0, concat_axis=2, tiled=True
        ).astype(summed_attn.dtype),
        lax.all_to_all(
            summed_cross.astype(jnp.bfloat16), "seq", split_axis=0, concat_axis=2, tiled=True
        ).astype(summed_cross.dtype),
        lax.all_to_all(
            summed_ff.astype(jnp.bfloat16), "seq", split_axis=0, concat_axis=2, tiled=True
        ).astype(summed_ff.dtype),
        lax.all_to_all(
            summed_norm.astype(jnp.bfloat16), "seq", split_axis=0, concat_axis=2, tiled=True
        ).astype(summed_norm.dtype),
    )
    attn_reduced = owned_attn.reshape(owned_attn.shape[0], 6 * wide)
    cross_reduced = owned_cross.reshape(owned_cross.shape[0], 2 * wide)
    ff_reduced = owned_ff.reshape(owned_ff.shape[0], 3 * hidden_width)
    norm_reduced = jnp.sum(owned_norm, axis=2).T
    local_squares = (
        jnp.sum(attn_reduced * attn_reduced)
        + jnp.sum(cross_reduced * cross_reduced)
        + jnp.sum(norm_reduced * norm_reduced)
        + jnp.sum(ff_reduced * ff_reduced)
    )
    total_squares = lax.psum(local_squares, ("dp", "seq"))
    grad_norm = jnp.sqrt(total_squares)
    factor = jnp.minimum(1.0, clip_limit / grad_norm)
    attn_new, attn_first_new, attn_second_new = adam_step(
        attn_weight, attn_first, attn_second, attn_reduced * factor, matrix_rate, matrix_decay
    )
    cross_new, cross_first_new, cross_second_new = adam_step(
        cross_weight, cross_first, cross_second, cross_reduced * factor, matrix_rate, matrix_decay
    )
    norm_new, norm_first_new, norm_second_new = adam_step(
        norm_param, norm_first, norm_second, norm_reduced * factor, gain_rate, 0.0
    )
    ff_new, ff_first_new, ff_second_new = adam_step(
        ff_weight, ff_first, ff_second, ff_reduced * factor, matrix_rate, matrix_decay
    )
    return (
        layer_out,
        frames_grad,
        grad_norm,
        attn_new,
        cross_new,
        norm_new,
        ff_new,
        attn_first_new,
        cross_first_new,
        norm_first_new,
        ff_first_new,
        attn_second_new,
        cross_second_new,
        norm_second_new,
        ff_second_new,
    )


def solution(mesh):
    return jax.shard_map(
        per_device,
        mesh=mesh,
        in_specs=(
            P("dp", "seq", None),
            P("dp", None),
            P("dp", None),
            P("dp", None),
            P("dp"),
            P("seq", None),
            P("dp", "seq", None),
            P(("dp", "seq"), None),
            P(("dp", "seq"), None),
            P(None, ("dp", "seq")),
            P(("dp", "seq"), None),
            P(("dp", "seq"), None),
            P(("dp", "seq"), None),
            P(("dp", "seq"), None),
            P(("dp", "seq"), None),
            P(None, ("dp", "seq")),
            P(None, ("dp", "seq")),
            P(("dp", "seq"), None),
            P(("dp", "seq"), None),
        ),
        out_specs=(
            P("dp", "seq", None),
            P("dp", "seq", None),
            P(),
            P(("dp", "seq"), None),
            P(("dp", "seq"), None),
            P(None, ("dp", "seq")),
            P(("dp", "seq"), None),
            P(("dp", "seq"), None),
            P(("dp", "seq"), None),
            P(None, ("dp", "seq")),
            P(("dp", "seq"), None),
            P(("dp", "seq"), None),
            P(("dp", "seq"), None),
            P(None, ("dp", "seq")),
            P(("dp", "seq"), None),
        ),
        check_vma=False,
    )
```

profile of v0, /device:TPU:9, one launch (start us, length us, event | category | flops | bytes accessed | tf_op | source)
XLA Modules:
  0.0 1638.4 jit_solution(10595833443322120029)
XLA Ops:
  19.9 24.5 %all_to_all.123 = bf16[4,2,55296]{2,1,0:T(2,128)(2,1)} all-to-all(bf16[4,2,55296]{2,1,0:T(2,128)(2,1)} %reshape.1265), channel_id=1, replica_groups=mesh['dp'=8,'seq'=4] {'seq'}, dimensions={0} | all-to-all | bytes 1769472 | tf_op jit(solution)/shard_map/all_to_all | solution.py:259
  85.6 20.3 %all-gather.13.cloned.1.call-done = bf16[1536,6,384]{2,0,1:T(8,128)(2,1)} async-done(((bf16[192,6,384]{2,0,1:T(8,128)(2,1)}), bf16[1536,6,384]{2,0,1:T(8,128)(2,1)}) %all-gather.13.cloned.1.call-update) | async-done | bytes 7077904 | tf_op jit(solution)/shard_map/all_gather | solution.py:271
  111.5 57.1 %all-gather.11.cloned.1.call-done = bf16[1,1024,1536]{2,1,0:T(8,128)(2,1)} async-done(((bf16[1,256,1536]{2,1,0:T(8,128)(2,1)}), bf16[1,1024,1536]{2,1,0:T(8,128)(2,1)}) %all-gather.11.cloned.1.call-update) | async-done | bytes 3145744 | tf_op jit(solution)/shard_map/all_gather | solution.py:280
  250.1 39.6 %reduce-scatter.12.cloned.1.call-done = bf16[1,256,1536]{2,1,0:T(8,128)(2,1)} async-done(((bf16[1,1024,1536]{2,1,0:T(8,128)(2,1)}), bf16[1,256,1536]{2,1,0:T(8,128)(2,1)}) %reduce-scatter.12.cloned.1.call-update) | async-done | bytes 786448 | tf_op jit(solution)/shard_map/reduce_scatter | solution.py:286
  294.2 22.0 %all-gather.15.cloned.1.call-done = bf16[768,2,384]{2,0,1:T(8,128)(2,1)} async-done(((bf16[96,2,384]{2,0,1:T(8,128)(2,1)}), bf16[768,2,384]{2,0,1:T(8,128)(2,1)}) %all-gather.15.cloned.1.call-update) | async-done | bytes 1179664 | tf_op jit(solution)/shard_map/all_gather | solution.py:272
  317.9 33.2 %all-reduce.4.cloned.1.call-done = bf16[128,768]{1,0:T(8,128)(2,1)} async-done(((bf16[128,768]{1,0:T(8,128)(2,1)}), bf16[128,768]{1,0:T(8,128)(2,1)}) %all-reduce.4.cloned.1.call-update) | async-done | bytes 196624 | tf_op jit(solution)/shard_map/psum | solution.py:233
  352.8 63.3 %all-gather.17.cloned.1.call-done = bf16[1,1024,1536]{2,1,0:T(8,128)(2,1)} async-done(((bf16[1,256,1536]{2,1,0:T(8,128)(2,1)}), bf16[1,1024,1536]{2,1,0:T(8,128)(2,1)}) %all-gather.17.cloned.1.call-update) | async-done | bytes 3145744 | tf_op jit(solution)/shard_map/all_gather | solution.py:280
  453.5 71.9 %all_to_all.125 = bf16[4,2,110592]{2,1,0:T(2,128)(2,1)} all-to-all(bf16[4,2,110592]{2,1,0:T(2,128)(2,1)S(1)} %reshape.1259), channel_id=1, replica_groups=mesh['dp'=8,'seq'=4] {'seq'}, dimensions={0} | all-to-all | bytes 3538944 | tf_op jit(solution)/shard_map/all_to_all | solution.py:265
  550.1 74.5 %all-gather.21.cloned.1.call-done = bf16[1536,3,1536]{2,0,1:T(8,128)(2,1)} async-done(((bf16[192,3,1536]{2,0,1:T(8,128)(2,1)}), bf16[1536,3,1536]{2,0,1:T(8,128)(2,1)}) %all-gather.21.cloned.1.call-update) | async-done | bytes 14155792 | tf_op jit(solution)/shard_map/all_gather | solution.py:273
  645.3 42.2 %all-gather.19.cloned.1.call-done = bf16[1,1024,1536]{2,1,0:T(8,128)(2,1)} async-done(((bf16[1,256,1536]{2,1,0:T(8,128)(2,1)}), bf16[1,1024,1536]{2,1,0:T(8,128)(2,1)}) %all-gather.19.cloned.1.call-update) | async-done | bytes 3145744 | tf_op jit(solution)/shard_map/all_gather | solution.py:280
  703.6 48.2 %all-gather.23.cloned.1.call-done = bf16[1,1024,1536]{2,1,0:T(8,128)(2,1)} async-done(((bf16[1,256,1536]{2,1,0:T(8,128)(2,1)}), bf16[1,1024,1536]{2,1,0:T(8,128)(2,1)}) %all-gather.23.cloned.1.call-update) | async-done | bytes 3145744 | tf_op jit(solution)/shard_map/all_gather | solution.py:280
  788.9 51.5 %reduce-scatter.18.cloned.1.call-done = bf16[1,256,1536]{2,1,0:T(8,128)(2,1)} async-done(((bf16[1,1024,1536]{2,1,0:T(8,128)(2,1)}), bf16[1,256,1536]{2,1,0:T(8,128)(2,1)}) %reduce-scatter.18.cloned.1.call-update) | async-done | bytes 786448 | tf_op jit(solution)/shard_map/reduce_scatter | solution.py:286
  843.7 59.2 %reduce-scatter.16.cloned.1.call-done = bf16[1,256,1536]{2,1,0:T(8,128)(2,1)} async-done(((bf16[1,1024,1536]{2,1,0:T(8,128)(2,1)}), bf16[1,256,1536]{2,1,0:T(8,128)(2,1)}) %reduce-scatter.16.cloned.1.call-update) | async-done | bytes 786448 | tf_op jit(solution)/shard_map/reduce_scatter | solution.py:286
  907.1 61.6 %all-gather.25.cloned.1.call-done = bf16[1,1024,1536]{2,1,0:T(8,128)(2,1)} async-done(((bf16[1,256,1536]{2,1,0:T(8,128)(2,1)}), bf16[1,1024,1536]{2,1,0:T(8,128)(2,1)}) %all-gather.25.cloned.1.call-update) | async-done | bytes 3145744 | tf_op jit(solution)/shard_map/all_gather | solution.py:280
  979.9 61.0 %reduce-scatter.20.cloned.1.call-done = bf16[1,256,1536]{2,1,0:T(8,128)(2,1)} async-done(((bf16[1,1024,1536]{2,1,0:T(8,128)(2,1)}), bf16[1,256,1536]{2,1,0:T(8,128)(2,1)}) %reduce-scatter.20.cloned.1.call-update) | async-done | bytes 786448 | tf_op jit(solution)/shard_map/reduce_scatter | solution.py:286
  1046.5 61.4 %all-gather.27.cloned.1.call-done = bf16[1,1024,1536]{2,1,0:T(8,128)(2,1)} async-done(((bf16[1,256,1536]{2,1,0:T(8,128)(2,1)}), bf16[1,1024,1536]{2,1,0:T(8,128)(2,1)}) %all-gather.27.cloned.1.call-update) | async-done | bytes 3145744 | tf_op jit(solution)/shard_map/all_gather | solution.py:280
  1139.8 21.4 %multiply_convert_fusion = bf16[6,1024,1024]{1,2,0:T(8,128)(2,1)} fusion(f32[6,1024,1024]{1,2,0:T(8,128)} %get-tuple-element.95, f32[6,1024,1024]{1,2,0:T(8,128)} %copy-done, f32[6,1024]{1,0:T(8,128)S(1)} %get-tuple-element.80, f32[6,1024]{1,0:T(8,128)} %get-tuple-element.46), kind=kLoop, calls=%fused_computation.1 | loop fusion | flops 25165824 | bytes 62963712 | tf_op jit(solution)/shard_map/convert_element_type | solution.py:118
  1278.5 28.8 %all-reduce.6.cloned.1.call-done = bf16[768,2,384]{2,1,0:T(2,128)(2,1)} async-done(((bf16[768,2,384]{2,1,0:T(2,128)(2,1)}), bf16[768,2,384]{2,1,0:T(2,128)(2,1)}) %all-reduce.6.cloned.1.call-update) | async-done | bytes 1179664
  1313.6 98.1 %reduce-scatter.26.cloned.1.call-done = bf16[192,3,1536]{2,0,1:T(8,128)(2,1)} async-done(((bf16[1536,3,1536]{2,0,1:T(8,128)(2,1)}), bf16[192,3,1536]{2,0,1:T(8,128)(2,1)}) %reduce-scatter.26.cloned.1.call-update) | async-done | bytes 1769488 | tf_op jit(solution)/shard_map/reduce_scatter | solution.py:467
  1421.3 27.5 %reduce-scatter.28.cloned.1.call-done = bf16[192,6]{1,0:T(8,128)(2,1)} async-done(((bf16[1536,6]{1,0:T(8,128)(2,1)}), bf16[192,6]{1,0:T(8,128)(2,1)}) %reduce-scatter.28.cloned.1.call-update) | async-done | bytes 2320
  1451.3 19.9 %all-to-all-done.7 = bf16[192,3,1536]{2,1,0:T(4,128)(2,1)S(1)} async-done(((bf16[192,3,1536]{2,1,0:T(4,128)(2,1)}), bf16[192,3,1536]{2,1,0:T(4,128)(2,1)S(1)}, u32[]{:S(2)}, u32[]{:S(2)}) %all-to-all-start.7) | async-done | bytes 1769504 | tf_op jit(solution)/shard_map/all_to_all | solution.py:481
  1477.9 40.2 %reduce-scatter.24.cloned.1.call-done = bf16[192,6,384]{2,0,1:T(8,128)(2,1)} async-done(((bf16[1536,6,384]{2,0,1:T(8,128)(2,1)}), bf16[192,6,384]{2,0,1:T(8,128)(2,1)}) %reduce-scatter.24.cloned.1.call-update) | async-done | bytes 884752 | tf_op jit(solution)/shard_map/reduce_scatter | solution.py:461
  1533.7 16.2 all-to-all-done.4
  1553.7 41.8 %psum.15 = f32[]{:T(128)} all-reduce(f32[]{:T(128)S(6)} %add.353), channel_id=1, replica_groups=mesh['dp'=8,'seq'=4] {'dp','seq'}, use_global_device_ids=true, to_apply=%region_42.43 | all-reduce | flops 1 | bytes 8 | tf_op jit(solution)/shard_map/psum | solution.py:498
  (479 shorter events, 529.7 us)
Async XLA Ops:
  7.2 98.7 %all-gather.13.cloned.1.call-start = ((), (), s32[]{:S(2)}) async-start(), calls=%async_computation.18 | async-start | bytes 7962624 | tf_op jit(solution)/shard_map/all_gather | solution.py:271
  61.8 106.8 %all-gather.11.cloned.1.call-start = ((), (), s32[]{:S(2)}) async-start(), calls=%async_computation.17 | async-start | bytes 3932160 | tf_op jit(solution)/shard_map/all_gather | solution.py:280
  79.7 210.0 %reduce-scatter.12.cloned.1.call-start = ((), (), s32[]{:S(2)}) async-start(), calls=%async_computation.19 | async-start | bytes 3932160 | tf_op jit(solution)/shard_map/reduce_scatter | solution.py:286
  225.5 90.7 %all-gather.15.cloned.1.call-start = ((), (), s32[]{:S(2)}) async-start(), calls=%async_computation.21 | async-start | bytes 1327104 | tf_op jit(solution)/shard_map/all_gather | solution.py:272
  244.3 106.7 %all-reduce.4.cloned.1.call-start = ((), (), s32[]{:S(2)}) async-start(), calls=%async_computation.20 | async-start | bytes 393216 | tf_op jit(solution)/shard_map/psum | solution.py:233
  249.9 166.3 %all-gather.17.cloned.1.call-start = ((), (), s32[]{:S(2)}) async-start(), calls=%async_computation.22 | async-start | bytes 3932160 | tf_op jit(solution)/shard_map/all_gather | solution.py:280
  294.1 250.8 %reduce-scatter.14.cloned.1.call-start = ((), (), s32[]{:S(2)}) async-start(), calls=%async_computation.23 | async-start | bytes 3932160 | tf_op jit(solution)/shard_map/reduce_scatter | solution.py:286
  428.2 196.4 %all-gather.21.cloned.1.call-start = ((), (), s32[]{:S(2)}) async-start(), calls=%async_computation.25 | async-start | bytes 15925248 | tf_op jit(solution)/shard_map/all_gather | solution.py:273
  544.7 142.8 %all-gather.19.cloned.1.call-start = ((), (), s32[]{:S(2)}) async-start(), calls=%async_computation.24 | async-start | bytes 3932160 | tf_op jit(solution)/shard_map/all_gather | solution.py:280
  548.5 203.3 %all-gather.23.cloned.1.call-start = ((), (), s32[]{:S(2)}) async-start(), calls=%async_computation.27 | async-start | bytes 3932160 | tf_op jit(solution)/shard_map/all_gather | solution.py:280
  550.0 290.3 %reduce-scatter.18.cloned.1.call-start = ((), (), s32[]{:S(2)}) async-start(), calls=%async_computation.28 | async-start | bytes 3932160 | tf_op jit(solution)/shard_map/reduce_scatter | solution.py:286
  779.3 123.6 %reduce-scatter.16.cloned.1.call-start = ((), (), s32[]{:S(2)}) async-start(), calls=%async_computation.26 | async-start | bytes 3932160 | tf_op jit(solution)/shard_map/reduce_scatter | solution.py:286
  788.6 180.0 %all-gather.25.cloned.1.call-start = ((), (), s32[]{:S(2)}) async-start(), calls=%async_computation.29 | async-start | bytes 3932160 | tf_op jit(solution)/shard_map/all_gather | solution.py:280
  907.0 133.9 %reduce-scatter.20.cloned.1.call-start = ((), (), s32[]{:S(2)}) async-start(), calls=%async_computation.30 | async-start | bytes 3932160 | tf_op jit(solution)/shard_map/reduce_scatter | solution.py:286
  979.8 128.1 %all-gather.27.cloned.1.call-start = ((), (), s32[]{:S(2)}) async-start(), calls=%async_computation.31 | async-start | bytes 3932160 | tf_op jit(solution)/shard_map/all_gather | solution.py:280
  1046.3 218.0 %reduce-scatter.22.cloned.1.call-start = ((), (), s32[]{:S(2)}) async-start(), calls=%async_computation.32 | async-start | bytes 3932160 | tf_op jit(solution)/shard_map/reduce_scatter | solution.py:286
  1185.7 121.6 %all-reduce.6.cloned.1.call-start = ((), (), s32[]{:S(2)}) async-start(), calls=%async_computation.36 | async-start | bytes 2359296
  1215.0 196.7 %reduce-scatter.26.cloned.1.call-start = ((), (), s32[]{:S(2)}) async-start(), calls=%async_computation.34 | async-start | bytes 15925248 | tf_op jit(solution)/shard_map/reduce_scatter | solution.py:467
  1227.9 220.9 %reduce-scatter.28.cloned.1.call-start = ((), (), s32[]{:S(2)}) async-start(), calls=%async_computation.35 | async-start | bytes 442368
  1271.8 246.3 %reduce-scatter.24.cloned.1.call-start = ((), (), s32[]{:S(2)}) async-start(), calls=%async_computation.33 | async-start | bytes 7962624 | tf_op jit(solution)/shard_map/reduce_scatter | solution.py:461
  1309.0 107.1 %all-to-all-start.5 = ((bf16[96,2,384]{2,1,0:T(2,128)(2,1)}), bf16[96,2,384]{2,1,0:T(2,128)(2,1)S(1)}, u32[]{:S(2)}, u32[]{:S(2)}) async-start(bf16[96,2,384]{2,1,0:T(2,128)(2,1)} %constant_dynamic-slice_fusion), calls=%async_computation.12 | async-start | bytes 294912 | tf_op jit(solution)/shard_map/all_to_all | solution.py:478
  1416.7 54.5 %all-to-all-start.7 = ((bf16[192,3,1536]{2,1,0:T(4,128)(2,1)}), bf16[192,3,1536]{2,1,0:T(4,128)(2,1)S(1)}, u32[]{:S(2)}, u32[]{:S(2)}) async-start(bf16[192,3,1536]{2,1,0:T(4,128)(2,1)} %copy.249), calls=%async_computation.15 | async-start | bytes 4718592 | tf_op jit(solution)/shard_map/all_to_all | solution.py:481
  1471.2 49.5 %all-to-all-start.6 = ((bf16[4,2,144]{2,1,0:T(2,128)(2,1)}), bf16[4,2,144]{2,1,0:T(2,128)(2,1)S(1)}, u32[]{:S(2)}, u32[]{:S(2)}) async-start(bf16[4,2,144]{2,1,0:T(2,128)(2,1)} %reshape.1267), calls=%async_computation.13 | async-start | bytes 8192 | tf_op jit(solution)/shard_map/all_to_all | solution.py:484
  1520.7 29.2 %all-to-all-start.4 = ((bf16[192,6,384]{2,1,0:T(8,128)(2,1)}), bf16[192,6,384]{2,1,0:T(8,128)(2,1)S(1)}, u32[]{:S(2)}, u32[]{:S(2)}) async-start(bf16[192,6,384]{2,1,0:T(8,128)(2,1)} %copy.242), calls=%async_computation.11 | async-start | bytes 2359296 | tf_op jit(solution)/shard_map/all_to_all | solution.py:475
  (105 other events, 917.9 us)
Sparse Core Ops, SparseCore 0:
  54.5 51.2 all-gather.12
  108.0 60.6 all-gather.10
  225.6 64.0 reduce-scatter.11
  292.0 24.0 all-gather.14
  318.9 32.1 all-reduce.3
  353.2 62.9 all-gather.16
  428.3 92.7 reduce-scatter.13
  544.8 79.7 all-gather.20
  626.9 60.6 all-gather.18
  689.6 62.1 all-gather.22
  779.4 60.9 reduce-scatter.17
  842.6 60.2 reduce-scatter.15
  907.1 61.4 all-gather.24
  979.9 60.9 reduce-scatter.19
  1046.4 61.5 all-gather.26
  1185.8 60.9 reduce-scatter.21
  1250.7 56.5 all-reduce.5
  1310.8 100.8 reduce-scatter.25
  1415.3 33.4 reduce-scatter.27
  1452.2 65.7 reduce-scatter.23
where the time goes:
time: 1650 us; the launch traced here: 1640 us
  waiting for transfers between devices  928 us (56%)
  matrix products  197 us (12%)
  local copies, waits for them, and re-layouts  186 us (11%)
  blocking collectives  164 us (10%)
  other arithmetic  113 us (7%)
  starting transfers between devices  27.4 us (2%)
  between operations  23.2 us (1%)
    all_gather x6, waiting for transfers between devices, collect(): lax.all_gather(rows.reshape(clip_count, frame_rows, wide), 'seq', axis=1,...  334 us
    reduce_scatter x6, waiting for transfers between devices, spread(): lax.psum_scatter(partial_value.reshape(clip_count, seq_frames, wide).asty...  211 us
    reduce_scatter x1, waiting for transfers between devices, per_device(): lax.psum_scatter(ff_piece.astype(jnp.bfloat16), 'dp', scatter_dimension=0...  98.1 us
    all_gather x1, waiting for transfers between devices, pieces(): lax.all_gather(moved_ff, 'dp', axis=0, tiled=True)  74.5 us
    all_to_all x1, blocking collectives, pieces(): lax.all_to_all(ff_low.reshape(-1, 3, hidden_width), 'seq', split_axis=2,...  71.9 us
    unnamed x224, local copies, waits for them, and re-layouts  62.9 us
    unnamed x22, waiting for transfers between devices  56.7 us
    psum x1, blocking collectives, per_device(): total_squares = lax.psum(local_squares, ('dp', 'seq'))  41.8 us
  transfers between devices with their start and end apart: 25, of which 21 were waited for; matrix products, arithmetic and copies ran while one was open for 14% of the time, Pallas kernels for 0%

commit v1 on v0

--- a/solution.py
+++ b/solution.py
@@ -1,6 +1,10 @@
+import functools
+
 import jax
 import jax.numpy as jnp
 from jax import lax
+from jax.experimental import pallas as pl
+from jax.experimental.pallas import tpu as pltpu
 from jax.sharding import PartitionSpec as P
 
 HEADS = 24
@@ -529,9 +533,734 @@
     )
 
 
+MESH = pl.DeviceIdType.MESH
+DMA = pltpu.SemaphoreType.DMA
+VMEM_LIMIT = 60 * 2**20
+
+
+def plane_fits(mesh):
+    return mesh.shape["dp"] == 8 and mesh.shape["dp"] % mesh.shape["seq"] == 0
+
+
+def plane_places():
+    place = lax.axis_index("dp")
+    return (place, lax.axis_index("seq"), lambda mask: jnp.bitwise_xor(place, mask))
+
+
+def greet(partners):
+    barrier = pltpu.get_barrier_semaphore()
+    for partner in partners:
+        pl.semaphore_signal(barrier, inc=1, device_id=partner, device_id_type=MESH)
+    pl.semaphore_wait(barrier, len(partners))
+
+
+def remote(source, goal, send_sem, recv_sem, device):
+    return pltpu.make_async_remote_copy(
+        src_ref=source,
+        dst_ref=goal,
+        send_sem=send_sem,
+        recv_sem=recv_sem,
+        device_id=device,
+        device_id_type=MESH,
+    )
+
+
+def communicating(collective_id):
+    return pltpu.CompilerParams(
+        has_side_effects=True, collective_id=collective_id, vmem_limit_bytes=VMEM_LIMIT
+    )
+
+
+def any_spec():
+    return pl.BlockSpec(memory_space=pl.ANY)
+
+
+def gather_body(clips, rows, sub, own_ref, all_ref, send_sem, recv_sem, local_sem):
+    place, depth, flip = plane_places()
+    core, beside_x, beside_y, across = flip(1), flip(2), flip(4), flip(6)
+    greet([(core, depth), (beside_x, depth), (beside_y, depth)])
+    chunks = [(clip, part) for clip in range(clips) for part in range(rows // sub)]
+    count = len(chunks)
+    half = count // 2
+    sends = []
+
+    def view(slot, index):
+        clip, part = chunks[index]
+        return all_ref.at[clip, slot, pl.ds(part * sub, sub)]
+
+    def own(index):
+        clip, part = chunks[index]
+        return own_ref.at[clip, pl.ds(part * sub, sub)]
+
+    def send(source, slot, index, device):
+        copy = remote(
+            source,
+            view(slot, index),
+            send_sem.at[len(sends)],
+            recv_sem.at[slot, index],
+            (device, depth),
+        )
+        copy.start()
+        sends.append(copy)
+
+    def arrived(slot, index):
+        block = view(slot, index)
+        remote(
+            block, block, send_sem.at[0], recv_sem.at[slot, index], (core, depth)
+        ).wait_recv()
+
+    x_order = list(range(count))
+    y_order = list(range(half, count)) + list(range(half))
+    for step in range(count):
+        send(own(x_order[step]), place, x_order[step], beside_x)
+        send(own(y_order[step]), place, y_order[step], beside_y)
+    stays = []
+    for clip in range(clips):
+        copy = pltpu.make_async_copy(
+            own_ref.at[clip], all_ref.at[clip, place], local_sem.at[clip]
+        )
+        copy.start()
+        stays.append(copy)
+    for index in range(count):
+        send(own(index), place, index, core)
+    for step in range(count):
+        x_index, y_index = x_order[step], y_order[step]
+        arrived(beside_x, x_index)
+        if x_index < half:
+            send(view(beside_x, x_index), beside_x, x_index, beside_y)
+        send(view(beside_x, x_index), beside_x, x_index, core)
+        arrived(beside_y, y_index)
+        if y_index >= half:
+            send(view(beside_y, y_index), beside_y, y_index, beside_x)
+        send(view(beside_y, y_index), beside_y, y_index, core)
+    for step in range(half):
+        for index in (x_order[step], y_order[step]):
+            arrived(across, index)
+            send(view(across, index), across, index, core)
+    for slot in (core, flip(3), flip(5), flip(7)):
+        for index in range(count):
+            arrived(slot, index)
+    for copy in stays:
+        copy.wait()
+    for copy in sends:
+        copy.wait_send()
+
+
+def plane_gather(own_rows, collective_id, sub=64):
+    clips, rows, wide = own_rows.shape
+    count = clips * (rows // sub)
+    return pl.pallas_call(
+        functools.partial(gather_body, clips, rows, sub),
+        out_shape=jax.ShapeDtypeStruct((clips, 8, rows, wide), own_rows.dtype),
+        in_specs=[any_spec()],
+        out_specs=any_spec(),
+        scratch_shapes=[DMA((7 * count,)), DMA((8, count)), DMA((clips,))],
+        compiler_params=communicating(collective_id),
+    )(own_rows)
+
+
+def reduce_body(
+    clips, rows, sub, part_ref, sum_ref, pair, held, turn, from_x, from_y, *sems
+):
+    send_sem, core_sem, turn_sem, x_sem, y_sem = sems
+    place, depth, flip = plane_places()
+    core, beside_x, beside_y = flip(1), flip(2), flip(4)
+    greet([(core, depth), (beside_x, depth), (beside_y, depth)])
+    chunks = [(clip, part) for clip in range(clips) for part in range(rows // sub)]
+    count = len(chunks)
+    half = count // 2
+    sends = []
+
+    def send(source, goal, recv_sem, device):
+        copy = remote(source, goal, send_sem.at[len(sends)], recv_sem, (device, depth))
+        copy.start()
+        sends.append(copy)
+
+    def arrived(block, recv_sem):
+        remote(block, block, send_sem.at[0], recv_sem, (core, depth)).wait_recv()
+
+    def term(slot, index):
+        clip, part = chunks[index]
+        return part_ref.at[clip, slot, pl.ds(part * sub, sub)]
+
+    for chip in (3, 1, 2, 0):
+        for index in range(count):
+            send(
+                term(flip((2 * chip) ^ 1), index),
+                pair.at[index, chip],
+                core_sem.at[index, chip],
+                core,
+            )
+
+    def total(*blocks):
+        return sum(block[...].astype(jnp.float32) for block in blocks)
+
+    def combine(chip, index):
+        arrived(pair.at[index, chip], core_sem.at[index, chip])
+        held[index, chip] = total(term(flip(2 * chip), index), pair.at[index, chip]).astype(
+            held.dtype
+        )
+
+    for low in range(half):
+        high = half + low
+        combine(3, low)
+        send(held.at[low, 3], turn.at[low], turn_sem.at[low], beside_x)
+        combine(3, high)
+        send(held.at[high, 3], turn.at[high], turn_sem.at[high], beside_y)
+    for low in range(half):
+        high = half + low
+        combine(1, low)
+        send(held.at[low, 1], from_x.at[low], x_sem.at[low], beside_x)
+        combine(2, high)
+        send(held.at[high, 2], from_y.at[high], y_sem.at[high], beside_y)
+    for low in range(half):
+        high = half + low
+        combine(2, low)
+        arrived(turn.at[low], turn_sem.at[low])
+        held[low, 2] = total(held.at[low, 2], turn.at[low]).astype(held.dtype)
+        send(held.at[low, 2], from_y.at[low], y_sem.at[low], beside_y)
+        combine(1, high)
+        arrived(turn.at[high], turn_sem.at[high])
+        held[high, 1] = total(held.at[high, 1], turn.at[high]).astype(held.dtype)
+        send(held.at[high, 1], from_x.at[high], x_sem.at[high], beside_x)
+    for index in range(count):
+        clip, part = chunks[index]
+        arrived(pair.at[index, 0], core_sem.at[index, 0])
+        arrived(from_x.at[index], x_sem.at[index])
+        arrived(from_y.at[index], y_sem.at[index])
+        sum_ref[clip, pl.ds(part * sub, sub)] = total(
+            term(place, index), pair.at[index, 0], from_x.at[index], from_y.at[index]
+        )
+    for copy in sends:
+        copy.wait_send()
+
+
+def plane_reduce(terms, collective_id, sub=64):
+    clips, _, rows, wide = terms.shape
+    count = clips * (rows // sub)
+    kind = terms.dtype
+    return pl.pallas_call(
+        functools.partial(reduce_body, clips, rows, sub),
+        out_shape=jax.ShapeDtypeStruct((clips, rows, wide), jnp.float32),
+        in_specs=[pl.BlockSpec(memory_space=pltpu.VMEM)],
+        out_specs=pl.BlockSpec(memory_space=pltpu.VMEM),
+        scratch_shapes=[
+            pltpu.VMEM((count, 4, sub, wide), kind),
+            pltpu.VMEM((count, 4, sub, wide), kind),
+            pltpu.VMEM((count, sub, wide), kind),
+            pltpu.VMEM((count, sub, wide), kind),
+            pltpu.VMEM((count, sub, wide), kind),
+            DMA((7 * count,)),
+            DMA((count, 4)),
+            DMA((count,)),
+            DMA((count,)),
+            DMA((count,)),
+        ],
+        compiler_params=communicating(collective_id),
+    )(terms)
+
+
+def greet_cross(group, planes):
+    place, depth, flip = plane_places()
+    greet(
+        [(flip(mask), depth) for mask in range(1, group)]
+        + [(place, lax.rem(depth + step, planes)) for step in range(1, planes)]
+    )
+
+
+def inward_body(group, planes, own_ref, kept_ref, mid, *sems):
+    near_send, near_recv, far_send, far_recv, local_sem = sems
+    place, depth, flip = plane_places()
+    per = group // planes
+    greet_cross(group, planes)
+    first = []
+    for mask in range(1, group):
+        other = flip(mask)
+        copy = remote(
+            own_ref.at[other],
+            mid.at[place],
+            near_send.at[mask],
+            near_recv.at[mask],
+            (other, depth),
+        )
+        copy.start()
+        first.append(copy)
+    second = []
+    for mask in range(group):
+        source = flip(mask)
+        goal, slot = lax.div(source, per), lax.rem(source, per)
+        block = own_ref.at[place]
+        if mask:
+            first[mask - 1].wait_recv()
+            block = mid.at[source]
+        away = remote(
+            block,
+            kept_ref.at[slot, depth],
+            far_send.at[mask],
+            far_recv.at[slot, depth],
+            (place, goal),
+        )
+        stay = pltpu.make_async_copy(block, kept_ref.at[slot, depth], local_sem.at[mask])
+        pl.when(goal != depth)(away.start)
+        pl.when(goal == depth)(stay.start)
+        second.append((goal, away, stay))
+    for slot in range(per):
+        for origin in range(planes):
+            block = kept_ref.at[slot, origin]
+            pl.when(origin != depth)(
+                remote(
+                    block,
+                    block,
+                    far_send.at[0],
+                    far_recv.at[slot, origin],
+                    (place, lax.rem(depth + 1, planes)),
+                ).wait_recv
+            )
+    for goal, away, stay in second:
+        pl.when(goal != depth)(away.wait_send)
+        pl.when(goal == depth)(stay.wait)
+    for copy in first:
+        copy.wait_send()
+
+
+def inward(rows_of_clip, planes, collective_id):
+    group, rows, wide = rows_of_clip.shape
+    kept, _ = pl.pallas_call(
+        functools.partial(inward_body, group, planes),
+        out_shape=[
+            jax.ShapeDtypeStruct((group // planes, planes, rows, wide), rows_of_clip.dtype),
+            jax.ShapeDtypeStruct((group, rows, wide), rows_of_clip.dtype),
+        ],
+        in_specs=[any_spec()],
+        out_specs=[any_spec()] * 2,
+        scratch_shapes=[
+            DMA((group,)),
+            DMA((group,)),
+            DMA((group,)),
+            DMA((group // planes, planes)),
+            DMA((group,)),
+        ],
+        compiler_params=communicating(collective_id),
+    )(rows_of_clip)
+    return kept
+
+
+def outward_body(group, planes, kept_ref, own_ref, mid, *sems):
+    far_send, far_recv, near_send, near_recv, local_sem = sems
+    place, depth, flip = plane_places()
+    per = group // planes
+    greet_cross(group, planes)
+    first = []
+    for step in range(1, planes):
+        origin = lax.rem(depth + step, planes)
+        for slot in range(per):
+            clip = per * depth + slot
+            copy = remote(
+                kept_ref.at[slot, origin],
+                mid.at[clip],
+                far_send.at[slot, step],
+                far_recv.at[clip],
+                (place, origin),
+            )
+            copy.start()
+            first.append(copy)
+    second = []
+
+    def hand_over(block, clip):
+        index = len(second)
+        away = remote(
+            block, own_ref.at[place], near_send.at[index], near_recv.at[place], (clip, depth)
+        )
+        stay = pltpu.make_async_copy(block, own_ref.at[place], local_sem.at[index])
+        pl.when(clip != place)(away.start)
+        pl.when(clip == place)(stay.start)
+        second.append((clip, away, stay))
+
+    for slot in range(per):
+        hand_over(kept_ref.at[slot, depth], per * depth + slot)
+    for step in range(1, planes):
+        source = lax.rem(depth + step, planes)
+        for slot in range(per):
+            clip = per * source + slot
+            block = mid.at[clip]
+            remote(
+                block, block, far_send.at[0, 0], far_recv.at[clip], (place, source)
+            ).wait_recv()
+            hand_over(block, clip)
+    for mask in range(1, group):
+        other = flip(mask)
+        block = own_ref.at[other]
+        remote(block, block, near_send.at[0], near_recv.at[other], (other, depth)).wait_recv()
+    for clip, away, stay in second:
+        pl.when(clip != place)(away.wait_send)
+        pl.when(clip == place)(stay.wait)
+    for copy in first:
+        copy.wait_send()
+
+
+def outward(kept_rows, collective_id):
+    per, planes, rows, wide = kept_rows.shape
+    group = per * planes
+    own, _ = pl.pallas_call(
+        functools.partial(outward_body, group, planes),
+        out_shape=[jax.ShapeDtypeStruct((group, rows, wide), kept_rows.dtype)] * 2,
+        in_specs=[any_spec()],
+        out_specs=[any_spec()] * 2,
+        scratch_shapes=[
+            DMA((per, planes)),
+            DMA((group,)),
+            DMA((group,)),
+            DMA((group,)),
+            DMA((group,)),
+        ],
+        compiler_params=communicating(collective_id),
+    )(kept_rows)
+    return own
+
+
+def swap_body(own_ref, kept_ref, send_sem, recv_sem, local_sem):
+    place, depth, flip = plane_places()
+    masks = (6, 7, 2, 3, 4, 5, 1)
+    greet([(flip(mask), depth) for mask in masks])
+    copies = []
+    for mask in masks:
+        other = flip(mask)
+        copy = remote(
+            own_ref.at[other],
+            kept_ref.at[place],
+            send_sem.at[mask],
+            recv_sem.at[mask],
+            (other, depth),
+        )
+        copy.start()
+        copies.append(copy)
+    stay = pltpu.make_async_copy(own_ref.at[place], kept_ref.at[place], local_sem)
+    stay.start()
+    stay.wait()
+    for copy in copies:
+        copy.wait()
+
+
+def plane_swap(blocks, collective_id):
+    return pl.pallas_call(
+        swap_body,
+        out_shape=jax.ShapeDtypeStruct(blocks.shape, blocks.dtype),
+        in_specs=[any_spec()],
+        out_specs=any_spec(),
+        scratch_shapes=[DMA((8,)), DMA((8,)), DMA(())],
+        compiler_params=communicating(collective_id),
+    )(blocks)
+
+
+def plane_device(
+    frames,
+    time_token,
+    cond_ids,
+    cond_mask,
+    lengths,
+    cond_table,
+    cotangent,
+    attn_weight,
+    cross_weight,
+    norm_param,
+    ff_weight,
+    attn_first,
+    attn_second,
+    cross_first,
+    cross_second,
+    norm_first,
+    norm_second,
+    ff_first,
+    ff_second,
+):
+    group, planes = lax.axis_size("dp"), lax.axis_size("seq")
+    place, depth = lax.axis_index("dp"), lax.axis_index("seq")
+    clips = group // planes
+    _, frame_rows, wide = frames.shape
+    piece = frame_rows // group
+    seq_frames = frame_rows * planes
+    own_rows = planes * piece
+    heads = HEADS // group
+    head_wide = heads * HDIM
+    ff_wide = FF // group
+    owned = wide // (group * planes)
+    cond_count, cond_wide = cond_ids.shape[1], cond_table.shape[1]
+    cond_owned = cross_weight.shape[0]
+
+    def to_plane_order(values):
+        lead = values.shape[:-1]
+        return jnp.swapaxes(values.reshape(lead + (group, planes, owned)), -3, -2).reshape(
+            lead + (wide,)
+        )
+
+    def to_whole_order(values):
+        lead = values.shape[:-1]
+        return jnp.swapaxes(values.reshape(lead + (planes, group, owned)), -3, -2).reshape(
+            lead + (wide,)
+        )
+
+    attn_low = attn_weight.astype(jnp.bfloat16).reshape(owned, 6, group, head_wide)
+    attn_cut = attn_low.transpose(2, 0, 1, 3).reshape(group, owned, 6 * head_wide)
+    cross_low = cross_weight.astype(jnp.bfloat16).reshape(cond_owned, 2, group, head_wide)
+    cross_cut = cross_low.transpose(2, 0, 1, 3).reshape(group, owned, -1)
+    ff_low = ff_weight.astype(jnp.bfloat16).reshape(owned, 3, group, ff_wide)
+    ff_cut = ff_low.transpose(2, 0, 1, 3).reshape(group, owned, 3 * ff_wide)
+    attn_mine = plane_swap(jnp.concatenate([attn_cut, cross_cut], axis=2), 1)
+    ff_mine = plane_swap(ff_cut, 2)
+
+    def over_planes(block):
+        return lax.all_gather(block.reshape(group * owned, -1), "seq", axis=0, tiled=True)
+
+    w_qkv = over_planes(attn_mine[:, :, : 3 * head_wide])
+    w_rest = over_planes(attn_mine[:, :, 3 * head_wide :])
+    w_gate_up = over_planes(ff_mine[:, :, : 2 * ff_wide])
+    w_down = over_planes(ff_mine[:, :, 2 * ff_wide :])
+    w_self_out = w_rest[:, :head_wide]
+    w_cross_query = w_rest[:, head_wide : 2 * head_wide]
+    w_cross_out = w_rest[:, 2 * head_wide : 3 * head_wide]
+    w_cond = w_rest[:, 3 * head_wide :].reshape(planes, group, cond_owned, -1)
+    w_cond = jnp.swapaxes(w_cond, 0, 1).reshape(cond_wide, 2 * head_wide)
+    norm_all = lax.all_gather(norm_param.astype(jnp.bfloat16), ("dp", "seq"), axis=0)
+    norm_all = norm_all.reshape(group, planes, 6, owned).transpose(2, 1, 0, 3)
+    gain_rows = norm_all.reshape(6, wide).astype(jnp.float32)
+
+    def of_plane(values):
+        everyone = lax.all_gather(values, "dp", axis=0, tiled=True)
+        return lax.dynamic_slice_in_dim(everyone, depth * clips, clips, axis=0)
+
+    clip_lengths = of_plane(lengths)
+    cond_keep = of_plane(cond_mask) > 0
+    stamps = to_plane_order(of_plane(time_token)).astype(jnp.float32)
+    vocab_rows = cond_table.shape[0]
+    relative = cond_ids - depth * vocab_rows
+    inside = (relative >= 0) & (relative < vocab_rows)
+    picked = jnp.take(cond_table, jnp.clip(relative, 0, vocab_rows - 1), axis=0)
+    picked = jnp.where(inside[..., None], picked, jnp.zeros((), picked.dtype))
+    cond = of_plane(lax.psum(picked, "seq"))
+    cond_flat = cond.reshape(clips * cond_count, cond_wide)
+
+    positions = depth * frame_rows + jnp.arange(frame_rows)
+    frame_valid = (positions[None, :] < lengths[:, None]).astype(cotangent.dtype)
+    stream = inward(to_plane_order(frames).reshape(group, piece, wide), planes, 3)
+    stream = stream.reshape(clips, own_rows, wide).astype(jnp.float32)
+    masked = to_plane_order(cotangent * frame_valid[..., None])
+    grad_out_low = inward(masked.reshape(group, piece, wide), planes, 4)
+    grad_out_low = grad_out_low.reshape(clips, own_rows, wide)
+    grad_out = grad_out_low.astype(jnp.float32)
+
+    group_rows = clips * seq_frames
+    row_place = jnp.arange(seq_frames)
+    row_owner, row_rest = row_place // own_rows, row_place % own_rows
+    true_place = (row_rest // piece) * frame_rows + row_owner * piece + row_rest % piece
+    key_keep = true_place[None, :] < clip_lengths[:, None]
+    cosine_table, sine_table = rotary_tables(true_place, HDIM)
+    group_shape = (clips, seq_frames, heads, HDIM)
+
+    def collect(rows, collective_id):
+        return plane_gather(rows, collective_id).reshape(group_rows, wide)
+
+    def spread(partial_value, collective_id):
+        terms = partial_value.astype(jnp.bfloat16).reshape(clips, group, own_rows, wide)
+        return plane_reduce(terms, collective_id)
+
+    normed_one = layer_norm(stream, gain_rows[0], gain_rows[1]).astype(jnp.bfloat16)
+    group_one = collect(normed_one, 5)
+    projected = jnp.dot(group_one, w_qkv, preferred_element_type=jnp.float32)
+    queries = rotate(
+        projected[:, :head_wide].reshape(group_shape), cosine_table, sine_table
+    ).astype(jnp.bfloat16)
+    all_keys = rotate(
+        projected[:, head_wide : 2 * head_wide].reshape(group_shape), cosine_table, sine_table
+    ).astype(jnp.bfloat16)
+    all_values = projected[:, 2 * head_wide :].astype(jnp.bfloat16).reshape(group_shape)
+    stamp_normed = layer_norm(stamps, gain_rows[0], gain_rows[1]).astype(jnp.bfloat16)
+    stamp_pair = jnp.dot(stamp_normed, w_qkv[:, head_wide:], preferred_element_type=jnp.float32)
+    stamp_pair = stamp_pair.astype(jnp.bfloat16)
+    stamp_key = stamp_pair[:, :head_wide].reshape(clips, heads, HDIM)
+    stamp_value = stamp_pair[:, head_wide:].reshape(clips, heads, HDIM)
+    self_mixed, self_lse = self_forward(
+        queries, all_keys, all_values, stamp_key, stamp_value, key_keep
+    )
+    self_low = self_mixed.astype(jnp.bfloat16).reshape(group_rows, head_wide)
+    resid_one = stream + spread(times_transposed(self_low, w_self_out), 6)
+    normed_two = layer_norm(resid_one, gain_rows[2], gain_rows[3]).astype(jnp.bfloat16)
+    group_two = collect(normed_two, 7)
+    cross_query = jnp.dot(group_two, w_cross_query, preferred_element_type=jnp.float32)
+    cross_query = cross_query.astype(jnp.bfloat16).reshape(group_shape)
+    cond_pair = jnp.dot(cond_flat, w_cond, preferred_element_type=jnp.float32)
+    cond_pair = cond_pair.astype(jnp.bfloat16)
+    cond_shape = (clips, cond_count, heads, HDIM)
+    cross_keys = cond_pair[:, :head_wide].reshape(cond_shape)
+    cross_values = cond_pair[:, head_wide:].reshape(cond_shape)
+    cross_mixed, cross_lse = cross_forward(cross_query, cross_keys, cross_values, cond_keep)
+    cross_out = cross_mixed.astype(jnp.bfloat16).reshape(group_rows, head_wide)
+    resid_two = resid_one + spread(times_transposed(cross_out, w_cross_out), 8)
+    normed_three = layer_norm(resid_two, gain_rows[4], gain_rows[5]).astype(jnp.bfloat16)
+    group_three = collect(normed_three, 9)
+    group_grad_out = collect(grad_out_low, 10)
+    gate_up = jnp.dot(group_three, w_gate_up, preferred_element_type=jnp.float32)
+    gate_val, up_val = gate_up[:, :ff_wide], gate_up[:, ff_wide:]
+    hidden = (jax.nn.silu(gate_val) * up_val).astype(jnp.bfloat16)
+    branch = spread(times_transposed(hidden, w_down), 11)
+    layer_out = (resid_two + branch).astype(jnp.bfloat16)
+    layer_out = outward(layer_out.reshape(clips, planes, piece, wide), 12)
+    layer_out = to_whole_order(layer_out.reshape(frames.shape))
+
+    grad_hidden = jnp.dot(group_grad_out, w_down, preferred_element_type=jnp.float32)
+    sigmoid_gate = jax.nn.sigmoid(gate_val)
+    grad_gate = grad_hidden * up_val * sigmoid_gate * (1.0 + gate_val * (1.0 - sigmoid_gate))
+    grad_up = grad_hidden * gate_val * sigmoid_gate
+    grad_gate_up = jnp.concatenate([grad_gate, grad_up], axis=1).astype(jnp.bfloat16)
+    grad_normed_three = spread(times_transposed(grad_gate_up, w_gate_up), 13)
+
+    def over_rows(block):
+        return lax.psum_scatter(
+            block.astype(jnp.bfloat16), "seq", scatter_dimension=0, tiled=True
+        ).reshape(group, owned, -1)
+
+    ff_piece = jnp.concatenate(
+        [outer_sum(group_three, grad_gate_up), outer_sum(group_grad_out, hidden)], axis=1
+    )
+    ff_owned = plane_swap(over_rows(ff_piece), 14)
+    ff_reduced = ff_owned.reshape(group, owned, 3, ff_wide).transpose(1, 2, 0, 3)
+    ff_reduced = ff_reduced.reshape(owned, 3 * FF).astype(jnp.float32)
+
+    _, norm_three_back = jax.vjp(layer_norm, resid_two, gain_rows[4], gain_rows[5])
+    grad_two_part, grad_gain_three, grad_bias_three = norm_three_back(grad_normed_three)
+    grad_two = grad_out + grad_two_part
+    group_cross_branch = collect(grad_two.astype(jnp.bfloat16), 15)
+    grad_cross_mixed = jnp.dot(group_cross_branch, w_cross_out, preferred_element_type=jnp.float32)
+    grad_cross_mixed = grad_cross_mixed.astype(jnp.bfloat16).reshape(group_shape)
+    grad_cross_query, grad_cross_keys, grad_cross_values = cross_backward(
+        cross_query, cross_keys, cross_values, cond_keep, cross_lse, grad_cross_mixed
+    )
+    grad_cross_query = grad_cross_query.astype(jnp.bfloat16).reshape(group_rows, head_wide)
+    grad_normed_two = spread(times_transposed(grad_cross_query, w_cross_query), 16)
+    _, norm_two_back = jax.vjp(layer_norm, resid_one, gain_rows[2], gain_rows[3])
+    grad_one_part, grad_gain_two, grad_bias_two = norm_two_back(grad_normed_two)
+    grad_one = grad_two + grad_one_part
+    group_self_branch = collect(grad_one.astype(jnp.bfloat16), 17)
+    grad_self_mixed = jnp.dot(group_self_branch, w_self_out, preferred_element_type=jnp.float32)
+    grad_self_mixed = grad_self_mixed.astype(jnp.bfloat16).reshape(group_shape)
+    cond_grad = jnp.concatenate(
+        [
+            grad_cross_keys.reshape(clips * cond_count, head_wide),
+            grad_cross_values.reshape(clips * cond_count, head_wide),
+        ],
+        axis=1,
+    )
+    cross_piece = split_outer(cond_flat, cond_grad)
+    cross_piece = cross_piece.reshape(group, planes, cond_owned, 2 * head_wide)
+    cross_piece = jnp.swapaxes(cross_piece, 0, 1).reshape(wide, head_wide)
+    rest_piece = jnp.concatenate(
+        [
+            outer_sum(group_self_branch, self_low),
+            outer_sum(group_two, grad_cross_query),
+            outer_sum(group_cross_branch, cross_out),
+            cross_piece,
+        ],
+        axis=1,
+    )
+    rest_rows = over_rows(rest_piece)
+    grad_queries, key_part, value_part, grad_stamp_key, grad_stamp_value = self_backward(
+        queries, all_keys, all_values, stamp_key, stamp_value, key_keep, self_lse, grad_self_mixed
+    )
+
+    def turn_back(values):
+        turned = rotate(values, cosine_table, -sine_table).astype(jnp.bfloat16)
+        return turned.reshape(group_rows, head_wide)
+
+    grad_value = value_part.astype(jnp.bfloat16).reshape(group_rows, head_wide)
+    grad_project = jnp.concatenate(
+        [turn_back(grad_queries), turn_back(key_part), grad_value], axis=1
+    )
+    grad_normed_one = spread(times_transposed(grad_project, w_qkv), 18)
+    stamp_grad = jnp.concatenate(
+        [
+            grad_stamp_key.reshape(clips, head_wide),
+            grad_stamp_value.reshape(clips, head_wide),
+        ],
+        axis=1,
+    )
+    grad_stamp_normed = split_times_transposed(stamp_grad, w_qkv[:, head_wide:])
+    qkv_piece = outer_sum(group_one, grad_project)
+    stamp_weight_grad = split_outer(stamp_normed, stamp_grad)
+    qkv_piece = jnp.concatenate(
+        [qkv_piece[:, :head_wide], qkv_piece[:, head_wide:] + stamp_weight_grad], axis=1
+    )
+    qkv_rows = over_rows(qkv_piece)
+    attn_owned = plane_swap(jnp.concatenate([qkv_rows, rest_rows], axis=2), 19)
+    cross_reduced = attn_owned[:, :, 6 * head_wide :].reshape(group, cond_owned, 2, head_wide)
+    cross_reduced = cross_reduced.transpose(1, 2, 0, 3).reshape(cross_weight.shape)
+    cross_reduced = cross_reduced.astype(jnp.float32)
+    attn_reduced = attn_owned[:, :, : 6 * head_wide].reshape(group, owned, 6, head_wide)
+    attn_reduced = attn_reduced.transpose(1, 2, 0, 3).reshape(attn_weight.shape)
+    attn_reduced = attn_reduced.astype(jnp.float32)
+
+    _, norm_one_back = jax.vjp(layer_norm, stream, gain_rows[0], gain_rows[1])
+    grad_zero_part, grad_gain_one, grad_bias_one = norm_one_back(grad_normed_one)
+    _, norm_stamp_back = jax.vjp(layer_norm, stamps, gain_rows[0], gain_rows[1])
+    _, grad_gain_stamp, grad_bias_stamp = norm_stamp_back(grad_stamp_normed)
+    frames_grad = (grad_one + grad_zero_part).astype(jnp.bfloat16)
+    frames_grad = outward(frames_grad.reshape(clips, planes, piece, wide), 20)
+    frames_grad = to_whole_order(frames_grad.reshape(frames.shape)).astype(jnp.float32)
+    norm_grad = jnp.stack(
+        [
+            grad_gain_one + grad_gain_stamp,
+            grad_bias_one + grad_bias_stamp,
+            grad_gain_two,
+            grad_bias_two,
+            grad_gain_three,
+            grad_bias_three,
+        ],
+        axis=0,
+    )
+    norm_total = lax.psum(norm_grad, ("dp", "seq"))
+    norm_reduced = lax.dynamic_slice_in_dim(
+        norm_total, (depth * group + place) * owned, owned, axis=1
+    )
+    local_squares = (
+        jnp.sum(attn_reduced * attn_reduced)
+        + jnp.sum(cross_reduced * cross_reduced)
+        + jnp.sum(norm_reduced * norm_reduced)
+        + jnp.sum(ff_reduced * ff_reduced)
+    )
+    grad_norm = jnp.sqrt(lax.psum(local_squares, ("dp", "seq")))
+    factor = jnp.minimum(1.0, clip_limit / grad_norm)
+    attn_new, attn_first_new, attn_second_new = adam_step(
+        attn_weight, attn_first, attn_second, attn_reduced * factor, matrix_rate, matrix_decay
+    )
+    cross_new, cross_first_new, cross_second_new = adam_step(
+        cross_weight, cross_first, cross_second, cross_reduced * factor, matrix_rate, matrix_decay
+    )
+    norm_new, norm_first_new, norm_second_new = adam_step(
+        norm_param, norm_first, norm_second, norm_reduced * factor, gain_rate, 0.0
+    )
+    ff_new, ff_first_new, ff_second_new = adam_step(
+        ff_weight, ff_first, ff_second, ff_reduced * factor, matrix_rate, matrix_decay
+    )
+    return (
+        layer_out,
+        frames_grad,
+        grad_norm,
+        attn_new,
+        cross_new,
+        norm_new,
+        ff_new,
+        attn_first_new,
+        cross_first_new,
+        norm_first_new,
+        ff_first_new,
+        attn_second_new,
+        cross_second_new,
+        norm_second_new,
+        ff_second_new,
+    )
+
+
 def solution(mesh):
     return jax.shard_map(
-        per_device,
+        plane_device if plane_fits(mesh) else per_device,
         mesh=mesh,
         in_specs=(
             P("dp", "seq", None),

time: 1650 us -> 1310 us (0.79)
  waiting for transfers between devices: 928 us -> 9.3 us
  Pallas kernels: 0 us -> 660 us
  local copies, waits for them, and re-layouts: 186 us -> 133 us
  starting transfers between devices: 27.4 us -> 0.99 us
  other arithmetic: 113 us -> 95.6 us
    pallas_call x0 -> x20, Pallas kernels: none -> 660 us  [the longest x6 204 us: plane_reduce(): pl.pallas_call(functools.partial(reduce_body, clips, rows, sub), out_shap...]
    all_gather x9 -> x5, waiting for transfers between devices: 451 us -> 0.07 us  [the longest x4 0.05 us: over_planes(): lax.all_gather(block.reshape(group * owned, -1), 'seq', axis=0, tiled=True)]
    reduce_scatter x8 -> x3, waiting for transfers between devices: 350 us -> 0.02 us  [over_rows(): lax.psum_scatter(block.astype(jnp.bfloat16), 'seq', scatter_dimension=0,...]
    all_to_all x3 -> x0, blocking collectives: 110 us -> none  [the longest x1 71.9 us: pieces(): lax.all_to_all(ff_low.reshape(-1, 3, hidden_width), 'seq', split_axis=2,...]
    all_gather x1 -> x3, blocking collectives: 12 us -> 80.7 us  [the longest x1 61.7 us: plane_device(): lax.all_gather(norm_param.astype(jnp.bfloat16), ('dp', 'seq'), axis=0)]
    unnamed x22 -> x9, waiting for transfers between devices: 56.7 us -> 0.15 us
    all_to_all x5 -> x0, waiting for transfers between devices: 38.2 us -> none  [the longest x1 19.9 us: per_device(): lax.all_to_all(summed_ff.astype(jnp.bfloat16), 'seq', split_axis=0, conca...]
    psum x1 -> x2, blocking collectives: 41.8 us -> 77.8 us  [the longest x1 39.2 us: plane_device(): norm_total = lax.psum(norm_grad, ('dp', 'seq'))]
  transfers between devices with their start and end apart: 25 -> 9, of which waited for: 21 -> 1; matrix products, arithmetic and copies ran while one was open for 14% -> 19% of each run, Pallas kernels for 0% -> 36%
where the time goes in v1:
time: 1310 us; the launch traced here: 1300 us
  Pallas kernels  660 us (50%)
  matrix products  213 us (16%)
  blocking collectives  165 us (13%)
  local copies, waits for them, and re-layouts  133 us (10%)
  other arithmetic  95.6 us (7%)
  between operations  21.4 us (2%)
    pallas_call x6, Pallas kernels, plane_reduce(): pl.pallas_call(functools.partial(reduce_body, clips, rows, sub), out_shap...  204 us
    pallas_call x6, Pallas kernels, plane_gather(): pl.pallas_call(functools.partial(gather_body, clips, rows, sub), out_shap...  189 us
    pallas_call x2, Pallas kernels, outward(): pl.pallas_call(functools.partial(outward_body, group, planes), out_shape=...  106 us
    pallas_call x4, Pallas kernels, plane_swap(): pl.pallas_call(swap_body, out_shape=jax.ShapeDtypeStruct(blocks.shape, bl...  81.9 us
    pallas_call x2, Pallas kernels, inward(): pl.pallas_call(functools.partial(inward_body, group, planes), out_shape=[...  79.1 us
    all_gather x1, blocking collectives, plane_device(): lax.all_gather(norm_param.astype(jnp.bfloat16), ('dp', 'seq'), axis=0)  61.7 us
    dot_general x8, matrix products, times_transposed(): lax.dot_general(left_mat, right_mat, (((1,), (1,)), ((), ())), preferred_...  53.3 us
    psum x1, blocking collectives, plane_device(): norm_total = lax.psum(norm_grad, ('dp', 'seq'))  39.2 us
  transfers between devices with their start and end apart: 9, of which 1 were waited for; matrix products, arithmetic and copies ran while one was open for 19% of the time, Pallas kernels for 36%

profile of v1, /device:TPU:9, one launch (start us, length us, event | category | flops | bytes accessed | tf_op | source)
XLA Modules:
  0.0 1298.4 jit_solution(10009961264528992109)
XLA Ops:
  54.6 25.8 %shard_map.305 = bf16[8,48,2304]{2,1,0:T(8,128)(2,1)} custom-call(bf16[8,48,2304]{2,1,0:T(8,128)(2,1)} %reshape.770.own_ref), custom_call_target="tpu_custom_call" | custom-call | tf_op jit(solution)/shard_map/pallas_call | solution.py:945
  93.4 26.5 %shard_map.298 = (bf16[2,4,32,1536]{3,2,1,0:T(8,128)(2,1)}, bf16[8,32,1536]{2,1,0:T(8,128)(2,1)}) custom-call(bf16[8,32,1536]{2,1,0:T(8,128)(2,1)} %reshape_reshape.10.own_ref), custom_call_target="tpu_custom_call" | custom-call | tf_op jit(solution)/shard_map/pallas_call | solution.py:828
  150.6 61.7 %all-gather.1 = bf16[32,6,48]{2,1,0:T(8,128)(2,1)S(1)} all-gather(bf16[1,6,48]{2,1,0:T(8,128)(2,1)S(1)} %convert_bitcast_fusion.1), channel_id=2, replica_groups=mesh['dp'=8,'seq'=4] {'dp','seq'}, dimensions={0}, use_global_device_ids=true | all-gather | bytes 19008 | tf_op jit(solution)/shard_map/all_gather | solution.py:1023
  222.2 52.6 %shard_map.308 = (bf16[2,4,32,1536]{3,2,1,0:T(8,128)(2,1)}, bf16[8,32,1536]{2,1,0:T(8,128)(2,1)}) custom-call(bf16[8,32,1536]{2,1,0:T(8,128)(2,1)} %reshape_reshape.12.own_ref), custom_call_target="tpu_custom_call" | custom-call | tf_op jit(solution)/shard_map/pallas_call | solution.py:828
  276.2 34.6 %shard_map.299 = bf16[2,8,128,1536]{3,2,1,0:T(8,128)(2,1)} custom-call(bf16[2,128,1536]{2,1,0:T(8,128)(2,1)} %fusion.23.own_ref), custom_call_target="tpu_custom_call" | custom-call | tf_op jit(solution)/shard_map/pallas_call | solution.py:652
  310.8 30.9 %shard_map.309 = bf16[2,8,128,1536]{3,2,1,0:T(8,128)(2,1)} custom-call(bf16[2,128,1536]{2,1,0:T(8,128)(2,1)} %bitcast.304), custom_call_target="tpu_custom_call" | custom-call | tf_op jit(solution)/shard_map/pallas_call | solution.py:652
  414.2 34.3 %shard_map.301 = f32[2,128,1536]{2,1,0:T(8,128)} custom-call(bf16[2,8,128,1536]{3,2,1,0:T(8,128)(2,1)} %bitcast.295), custom_call_target="tpu_custom_call" | custom-call | tf_op jit(solution)/shard_map/pallas_call | solution.py:742
  451.7 30.9 %shard_map.302 = bf16[2,8,128,1536]{3,2,1,0:T(8,128)(2,1)} custom-call(bf16[2,128,1536]{2,1,0:T(8,128)(2,1)} %add_convert_fusion.3.own_ref), custom_call_target="tpu_custom_call" | custom-call | tf_op jit(solution)/shard_map/pallas_call | solution.py:652
  498.1 34.3 %shard_map.303 = f32[2,128,1536]{2,1,0:T(8,128)} custom-call(bf16[2,8,128,1536]{3,2,1,0:T(8,128)(2,1)} %bitcast.296), custom_call_target="tpu_custom_call" | custom-call | tf_op jit(solution)/shard_map/pallas_call | solution.py:742
  535.6 30.9 %shard_map.304 = bf16[2,8,128,1536]{3,2,1,0:T(8,128)(2,1)} custom-call(bf16[2,128,1536]{2,1,0:T(8,128)(2,1)} %add_convert_fusion.2.own_ref), custom_call_target="tpu_custom_call" | custom-call | tf_op jit(solution)/shard_map/pallas_call | solution.py:652
  612.9 34.3 %shard_map.310 = f32[2,128,1536]{2,1,0:T(8,128)} custom-call(bf16[2,8,128,1536]{3,2,1,0:T(8,128)(2,1)} %bitcast.327), custom_call_target="tpu_custom_call" | custom-call | tf_op jit(solution)/shard_map/pallas_call | solution.py:742
  659.3 34.7 %shard_map.306 = f32[2,128,1536]{2,1,0:T(8,128)} custom-call(bf16[2,8,128,1536]{3,2,1,0:T(8,128)(2,1)} %bitcast.328), custom_call_target="tpu_custom_call" | custom-call | tf_op jit(solution)/shard_map/pallas_call | solution.py:742
  699.7 30.9 %shard_map.311 = bf16[2,8,128,1536]{3,2,1,0:T(8,128)(2,1)} custom-call(bf16[2,128,1536]{2,1,0:T(8,128)(2,1)} %fusion.45.own_ref), custom_call_target="tpu_custom_call" | custom-call | tf_op jit(solution)/shard_map/pallas_call | solution.py:652
  748.3 34.4 %shard_map.312 = f32[2,128,1536]{2,1,0:T(8,128)} custom-call(bf16[2,8,128,1536]{3,2,1,0:T(8,128)(2,1)} %bitcast.294), custom_call_target="tpu_custom_call" | custom-call | tf_op jit(solution)/shard_map/pallas_call | solution.py:742
  788.3 30.9 %shard_map.313 = bf16[2,8,128,1536]{3,2,1,0:T(8,128)(2,1)} custom-call(bf16[2,128,1536]{2,1,0:T(8,128)(2,1)} %get-tuple-element.100.own_ref), custom_call_target="tpu_custom_call" | custom-call | tf_op jit(solution)/shard_map/pallas_call | solution.py:652
  836.1 18.6 %multiply_reduce_fusion = (f32[2,3,1024]{2,1,0:T(4,128)S(1)}, f32[2,3,1024,1024]{2,3,1,0:T(8,128)}) fusion(f32[2,3,1024]{2,1,0:T(4,128)S(1)} %copy-done.56, f32[2,3,1024,1024]{2,3,1,0:T(8,128)} %get-tuple-element.148, pred[2,1024]{1,0:T(4,128)(4,1)S(1)} %broadcast_compare_fusion, bf16[2,1024,3,64]{1,0,3,2:T(2,128)(2,1)S(1)} %copy-done.44, ...), kind=kOutput, calls=%fused_computation.2 | convolution fusion | flops 836757504 | bytes 51955712 | tf_op jit(solution)/shard_map/cqhd,ckhd->chqk/dot_general | solution.py:115
  857.8 17.4 %multiply_convert_fusion = bf16[2,3,1024,1024]{2,3,1,0:T(8,128)(2,1)S(1)} fusion(f32[2,3,1024,1024]{2,3,1,0:T(8,128)} %get-tuple-element.154, f32[2,3,1024]{2,1,0:T(4,128)S(1)} %get-tuple-element.134, f32[2,3,1024]{2,1,0:T(4,128)S(1)} %copy-done.56, f32[2,3,1024,1024]{2,3,1,0:T(8,128)} %get-tuple-element.148, pred[2,1024]{1,0:T(4,128)(4,1)S(1)} %broadcast_compare_fusion), kind=kLoop, calls=%fused_computation.1 | loop fusion | flops 37748736 | bytes 62965760 | tf_op jit(solution)/shard_map/convert_element_type | solution.py:122
  953.5 51.0 %shard_map.307 = (bf16[8,32,1536]{2,1,0:T(8,128)(2,1)}, bf16[8,32,1536]{2,1,0:T(8,128)(2,1)}) custom-call(bf16[2,4,32,1536]{3,2,1,0:T(8,128)(2,1)} %bitcast.352), custom_call_target="tpu_custom_call" | custom-call | tf_op jit(solution)/shard_map/pallas_call | solution.py:904
  1020.9 32.2 %shard_map.314 = f32[2,128,1536]{2,1,0:T(8,128)} custom-call(bf16[2,8,128,1536]{3,2,1,0:T(8,128)(2,1)} %bitcast.329), custom_call_target="tpu_custom_call" | custom-call | tf_op jit(solution)/shard_map/pallas_call | solution.py:742
  1057.7 54.5 %shard_map.315 = (bf16[8,32,1536]{2,1,0:T(8,128)(2,1)}, bf16[8,32,1536]{2,1,0:T(8,128)(2,1)}) custom-call(bf16[2,4,32,1536]{3,2,1,0:T(8,128)(2,1)} %bitcast.353), custom_call_target="tpu_custom_call" | custom-call | tf_op jit(solution)/shard_map/pallas_call | solution.py:904
  1120.2 39.2 %psum.22 = f32[6,1536]{1,0:T(8,128)S(1)} all-reduce(f32[6,1536]{1,0:T(8,128)S(1)} %stack.21), channel_id=1, replica_groups=mesh['dp'=8,'seq'=4] {'dp','seq'}, use_global_device_ids=true, to_apply=%region_33.34 | all-reduce | flops 9216 | bytes 73728 | tf_op jit(solution)/shard_map/psum | solution.py:1218
  1162.6 17.6 %shard_map.316 = bf16[8,48,1344]{2,1,0:T(8,128)(2,1)} custom-call(bf16[8,48,1344]{2,1,0:T(8,128)(2,1)} %pad_maximum_fusion.7.own_ref), custom_call_target="tpu_custom_call" | custom-call | tf_op jit(solution)/shard_map/pallas_call | solution.py:945
  1186.1 22.2 %shard_map.317 = bf16[8,48,2304]{2,1,0:T(8,128)(2,1)} custom-call(bf16[8,48,2304]{2,1,0:T(8,128)(2,1)} %bitcast.361), custom_call_target="tpu_custom_call" | custom-call | tf_op jit(solution)/shard_map/pallas_call | solution.py:945
  1213.7 38.6 %psum.23 = f32[]{:T(128)} all-reduce(f32[]{:T(128)S(6)} %add.541), channel_id=1, replica_groups=mesh['dp'=8,'seq'=4] {'dp','seq'}, use_global_device_ids=true, to_apply=%region_37.38 | all-reduce | flops 1 | bytes 8 | tf_op jit(solution)/shard_map/psum | solution.py:1228
  (476 shorter events, 458.0 us)
Async XLA Ops:
  7.2 40.1 %all-reduce.3.cloned.1.call-start = ((), (), s32[]{:S(2)}) async-start(), calls=%async_computation.5 | async-start | bytes 393216 | tf_op jit(solution)/shard_map/psum | solution.py:1039
  13.4 329.6 %all-gather.10.cloned.1.call-start = ((), (), s32[]{:S(2)}) async-start(), calls=%async_computation.3 | async-start | bytes 2457600 | tf_op jit(solution)/shard_map/all_gather | solution.py:1012
  38.2 364.1 %all-gather.14.cloned.1.call-start = ((), (), s32[]{:S(2)}) async-start(), calls=%async_computation.6 | async-start | bytes 1769472 | tf_op jit(solution)/shard_map/all_gather | solution.py:1028
  47.4 356.3 %all-gather.12.cloned.1.call-start = ((), (), s32[]{:S(2)}) async-start(), calls=%async_computation.4 | async-start | bytes 2949120 | tf_op jit(solution)/shard_map/all_gather | solution.py:1012
  49.6 516.9 %all-gather.16.cloned.1.call-start = ((), (), s32[]{:S(2)}) async-start(), calls=%async_computation.7 | async-start | bytes 5898240 | tf_op jit(solution)/shard_map/all_gather | solution.py:1012
  82.9 499.9 %all-gather.18.cloned.1.call-start = ((), (), s32[]{:S(2)}) async-start(), calls=%async_computation.8 | async-start | bytes 2949120 | tf_op jit(solution)/shard_map/all_gather | solution.py:1012
  84.9 1075.2 %reduce-scatter.10.cloned.1.call-start = ((), (), s32[]{:S(2)}) async-start(), calls=%async_computation.9 | async-start | bytes 2457600 | tf_op jit(solution)/shard_map/reduce_scatter | solution.py:1117
  88.6 42.5 %copy-start.74 = (f32[6,48]{1,0:T(8,128)S(1)}, f32[6,48]{1,0:T(8,128)}, u32[]{:S(2)}) copy-start(f32[6,48]{1,0:T(8,128)} %param.28) | copy-start | bytes 3460
  88.6 42.4 %copy-start.90 = (s32[1,128]{1,0:T(1,128)S(1)}, s32[1,128]{1,0:T(1,128)}, u32[]{:S(2)}) copy-start(s32[1,128]{1,0:T(1,128)} %param.22) | copy-start | bytes 1540
  88.6 53.0 %copy-start.81 = (bf16[1,1536]{1,0:T(2,128)(2,1)S(1)}, bf16[1,1536]{1,0:T(2,128)(2,1)}, u32[]{:S(2)}) copy-start(bf16[1,1536]{1,0:T(2,128)(2,1)} %param.20) | copy-start | bytes 9220
  93.4 119.5 %copy-start.53 = (bf16[1,256,1536]{2,1,0:T(8,128)(2,1)S(1)}, bf16[1,256,1536]{2,1,0:T(8,128)(2,1)}, u32[]{:S(2)}) copy-start(bf16[1,256,1536]{2,1,0:T(8,128)(2,1)} %param.25) | copy-start | bytes 2359300
  121.3 153.6 %copy-start.72 = (f32[2,128]{1,0:T(2,128)}, f32[2,128]{1,0:T(2,128)S(1)}, u32[]{:S(2)}) copy-start(f32[2,128]{1,0:T(2,128)S(1)} %div.316) | copy-start | bytes 3076
  150.2 192.8 %copy-start.82 = (f32[2]{0:T(128)}, f32[2]{0:T(128)S(1)}, u32[]{:S(2)}) copy-start(f32[2]{0:T(128)S(1)} %broadcast_multiply_fusion.4) | copy-start | bytes 28
  150.5 192.5 %copy-start.87 = (f32[2]{0:T(128)}, f32[2]{0:T(128)S(1)}, u32[]{:S(2)}) copy-start(f32[2]{0:T(128)S(1)} %add_rsqrt_fusion) | copy-start | bytes 28
  150.6 192.4 %copy-start.66 = (f32[2,1536]{1,0:T(2,128)}, f32[2,1536]{1,0:T(2,128)S(1)}, u32[]{:S(2)}) copy-start(f32[2,1536]{1,0:T(2,128)S(1)} %reshape.799) | copy-start | bytes 36868
  212.5 130.5 %copy-start.57 = (f32[1536]{0:T(1024)}, f32[1536]{0:T(1024)S(1)}, u32[]{:S(2)}) copy-start(f32[1536]{0:T(1024)S(1)} %mul.829) | copy-start | bytes 18436
  212.7 130.4 %copy-start.64 = (f32[1536]{0:T(1024)}, f32[1536]{0:T(1024)S(1)}, u32[]{:S(2)}) copy-start(f32[1536]{0:T(1024)S(1)} %add.489) | copy-start | bytes 18436
  217.0 57.9 %copy-start.3 = (bf16[2,4,32,1536]{3,2,1,0:T(8,128)(2,1)S(1)}, bf16[2,4,32,1536]{3,2,1,0:T(8,128)(2,1)}, u32[]{:S(2)}) copy-start(bf16[2,4,32,1536]{3,2,1,0:T(8,128)(2,1)} %get-tuple-element.19) | copy-start | bytes 2359300
  274.9 35.9 %copy-start.79 = (f32[2,128]{1,0:T(2,128)}, f32[2,128]{1,0:T(2,128)S(1)}, u32[]{:S(2)}) copy-start(f32[2,128]{1,0:T(2,128)S(1)} %add.488) | copy-start | bytes 3076
  274.9 35.9 %copy-start.77 = (f32[2,128]{1,0:T(2,128)}, f32[2,128]{1,0:T(2,128)S(1)}, u32[]{:S(2)}) copy-start(f32[2,128]{1,0:T(2,128)S(1)} %rsqrt.42) | copy-start | bytes 3076
  898.0 262.1 %reduce-scatter.12.cloned.1.call-start = ((), (), s32[]{:S(2)}) async-start(), calls=%async_computation.10 | async-start | bytes 2949120 | tf_op jit(solution)/shard_map/reduce_scatter | solution.py:1117
  915.3 270.8 %reduce-scatter.14.cloned.1.call-start = ((), (), s32[]{:S(2)}) async-start(), calls=%async_computation.11 | async-start | bytes 8847360 | tf_op jit(solution)/shard_map/reduce_scatter | solution.py:1117
  1208.3 44.7 %copy-start.15 = (bf16[8,48,1344]{2,1,0:T(8,128)(2,1)S(1)}, bf16[8,48,1344]{2,1,0:T(8,128)(2,1)}, u32[]{:S(2)}) copy-start(bf16[8,48,1344]{2,1,0:T(8,128)(2,1)} %shard_map.316) | copy-start | bytes 3096580
  1213.7 40.7 %copy-start.7 = (bf16[8,48,2304]{2,1,0:T(8,128)(2,1)S(1)}, bf16[8,48,2304]{2,1,0:T(8,128)(2,1)}, u32[]{:S(2)}) copy-start(bf16[8,48,2304]{2,1,0:T(8,128)(2,1)} %shard_map.317) | copy-start | bytes 5308420
  (88 other events, 579.3 us)
Sparse Core Ops, SparseCore 0:
  13.6 33.7 all-reduce.2
  49.6 43.9 all-gather.9
  95.6 26.4 all-gather.13
  124.2 48.5 all-gather.11
  174.9 103.4 all-gather.15
  280.5 50.6 all-gather.17
  898.1 38.2 reduce-scatter.9
  939.4 63.9 reduce-scatter.11
  1005.8 139.9 reduce-scatter.13

commit v2 on v1

--- a/solution.py
+++ b/solution.py
@@ -575,10 +575,18 @@
     return pl.BlockSpec(memory_space=pl.ANY)
 
 
-def gather_body(clips, rows, sub, own_ref, all_ref, send_sem, recv_sem, local_sem):
+def gather_body(clips, rows, sub, beside, own_ref, *refs):
+    if beside:
+        pick_ref, all_ref, cond_ref, send_sem, recv_sem, local_sem, *extra = refs
+        greet_cross(*beside)
+        cond = cond_steps(*beside, pick_ref, cond_ref, *extra)
+        next(cond)
+    else:
+        all_ref, send_sem, recv_sem, local_sem = refs
     place, depth, flip = plane_places()
     core, beside_x, beside_y, across = flip(1), flip(2), flip(4), flip(6)
-    greet([(core, depth), (beside_x, depth), (beside_y, depth)])
+    if not beside:
+        greet([(core, depth), (beside_x, depth), (beside_y, depth)])
     chunks = [(clip, part) for clip in range(clips) for part in range(rows // sub)]
     count = len(chunks)
     half = count // 2
@@ -623,6 +631,8 @@
         stays.append(copy)
     for index in range(count):
         send(own(index), place, index, core)
+    if beside:
+        next(cond)
     for step in range(count):
         x_index, y_index = x_order[step], y_order[step]
         arrived(beside_x, x_index)
@@ -640,32 +650,68 @@
     for slot in (core, flip(3), flip(5), flip(7)):
         for index in range(count):
             arrived(slot, index)
+    if beside:
+        next(cond)
     for copy in stays:
         copy.wait()
     for copy in sends:
         copy.wait_send()
 
 
-def plane_gather(own_rows, collective_id, sub=64):
+def plane_gather(own_rows, collective_id, picked=None, sub=64):
     clips, rows, wide = own_rows.shape
     count = clips * (rows // sub)
+    whole = jax.ShapeDtypeStruct((clips, 8, rows, wide), own_rows.dtype)
+    scratch = [DMA((7 * count,)), DMA((8, count)), DMA((clips,))]
+    if picked is None:
+        return pl.pallas_call(
+            functools.partial(gather_body, clips, rows, sub, None),
+            out_shape=whole,
+            in_specs=[any_spec()],
+            out_specs=any_spec(),
+            scratch_shapes=scratch,
+            compiler_params=communicating(collective_id),
+        )(own_rows)
+    planes, per, tokens, cond_wide = picked.shape
+    group = planes * per
+    inside = pl.BlockSpec(memory_space=pltpu.VMEM)
     return pl.pallas_call(
-        functools.partial(gather_body, clips, rows, sub),
-        out_shape=jax.ShapeDtypeStruct((clips, 8, rows, wide), own_rows.dtype),
-        in_specs=[any_spec()],
-        out_specs=any_spec(),
-        scratch_shapes=[DMA((7 * count,)), DMA((8, count)), DMA((clips,))],
+        functools.partial(gather_body, clips, rows, sub, (group, planes)),
+        out_shape=[
+            whole,
+            jax.ShapeDtypeStruct((group, per, tokens, cond_wide), picked.dtype),
+        ],
+        in_specs=[any_spec(), inside],
+        out_specs=[any_spec(), inside],
+        scratch_shapes=scratch
+        + [
+            pltpu.VMEM(picked.shape, picked.dtype),
+            pltpu.VMEM(picked.shape[1:], picked.dtype),
+            DMA((planes,)),
+            DMA((planes,)),
+            DMA((group,)),
+            DMA((group,)),
+        ],
         compiler_params=communicating(collective_id),
-    )(own_rows)
+    )(own_rows, picked)
 
 
 def reduce_body(
-    clips, rows, sub, part_ref, sum_ref, pair, held, turn, from_x, from_y, *sems
+    clips, rows, sub, beside, part_ref, *refs
 ):
-    send_sem, core_sem, turn_sem, x_sem, y_sem = sems
+    if beside:
+        kept_ref, sum_ref, own_ref, mid, *refs = refs
+    else:
+        sum_ref, *refs = refs
+    pair, held, turn, from_x, from_y, send_sem, core_sem, turn_sem, x_sem, y_sem, *sems = refs
     place, depth, flip = plane_places()
     core, beside_x, beside_y = flip(1), flip(2), flip(4)
-    greet([(core, depth), (beside_x, depth), (beside_y, depth)])
+    if beside:
+        greet_cross(*beside)
+        going = outward_steps(*beside, kept_ref, own_ref, mid, *sems)
+        next(going)
+    else:
+        greet([(core, depth), (beside_x, depth), (beside_y, depth)])
     chunks = [(clip, part) for clip in range(clips) for part in range(rows // sub)]
     count = len(chunks)
     half = count // 2
@@ -713,6 +759,8 @@
         send(held.at[low, 1], from_x.at[low], x_sem.at[low], beside_x)
         combine(2, high)
         send(held.at[high, 2], from_y.at[high], y_sem.at[high], beside_y)
+    if beside:
+        next(going)
     for low in range(half):
         high = half + low
         combine(2, low)
@@ -731,33 +779,51 @@
         sum_ref[clip, pl.ds(part * sub, sub)] = total(
             term(place, index), pair.at[index, 0], from_x.at[index], from_y.at[index]
         )
+    if beside:
+        next(going)
     for copy in sends:
         copy.wait_send()
 
 
-def plane_reduce(terms, collective_id, sub=64):
+def plane_reduce(terms, collective_id, kept_rows=None, sub=64):
     clips, _, rows, wide = terms.shape
     count = clips * (rows // sub)
     kind = terms.dtype
-    return pl.pallas_call(
-        functools.partial(reduce_body, clips, rows, sub),
-        out_shape=jax.ShapeDtypeStruct((clips, rows, wide), jnp.float32),
-        in_specs=[pl.BlockSpec(memory_space=pltpu.VMEM)],
-        out_specs=pl.BlockSpec(memory_space=pltpu.VMEM),
-        scratch_shapes=[
-            pltpu.VMEM((count, 4, sub, wide), kind),
-            pltpu.VMEM((count, 4, sub, wide), kind),
-            pltpu.VMEM((count, sub, wide), kind),
-            pltpu.VMEM((count, sub, wide), kind),
-            pltpu.VMEM((count, sub, wide), kind),
-            DMA((7 * count,)),
-            DMA((count, 4)),
-            DMA((count,)),
-            DMA((count,)),
-            DMA((count,)),
-        ],
+    sums = jax.ShapeDtypeStruct((clips, rows, wide), jnp.float32)
+    whole = pl.BlockSpec(memory_space=pltpu.VMEM)
+    scratch = [
+        pltpu.VMEM((count, 4, sub, wide), kind),
+        pltpu.VMEM((count, 4, sub, wide), kind),
+        pltpu.VMEM((count, sub, wide), kind),
+        pltpu.VMEM((count, sub, wide), kind),
+        pltpu.VMEM((count, sub, wide), kind),
+        DMA((7 * count,)),
+        DMA((count, 4)),
+        DMA((count,)),
+        DMA((count,)),
+        DMA((count,)),
+    ]
+    if kept_rows is None:
+        return pl.pallas_call(
+            functools.partial(reduce_body, clips, rows, sub, None),
+            out_shape=sums,
+            in_specs=[whole],
+            out_specs=whole,
+            scratch_shapes=scratch,
+            compiler_params=communicating(collective_id),
+        )(terms)
+    per, planes, piece, _ = kept_rows.shape
+    group = per * planes
+    moved = jax.ShapeDtypeStruct((group, piece, wide), kept_rows.dtype)
+    total, own, _ = pl.pallas_call(
+        functools.partial(reduce_body, clips, rows, sub, (group, planes)),
+        out_shape=[sums, moved, moved],
+        in_specs=[whole, any_spec()],
+        out_specs=[whole, any_spec(), any_spec()],
+        scratch_shapes=scratch + outward_scratch(group, planes),
         compiler_params=communicating(collective_id),
-    )(terms)
+    )(terms, kept_rows)
+    return total, own
 
 
 def greet_cross(group, planes):
@@ -768,13 +834,197 @@
     )
 
 
-def inward_body(group, planes, own_ref, kept_ref, mid, *sems):
-    near_send, near_recv, far_send, far_recv, local_sem = sems
+def outward_steps(group, planes, kept_ref, own_ref, mid, *sems):
+    far_send, far_recv, near_send, near_recv, local_sem = sems
     place, depth, flip = plane_places()
     per = group // planes
-    greet_cross(group, planes)
     first = []
+    for step in range(1, planes):
+        origin = lax.rem(depth + step, planes)
+        for slot in range(per):
+            clip = per * depth + slot
+            copy = remote(
+                kept_ref.at[slot, origin],
+                mid.at[clip],
+                far_send.at[slot, step],
+                far_recv.at[clip],
+                (place, origin),
+            )
+            copy.start()
+            first.append(copy)
+    second = []
+
+    def hand_over(block, clip):
+        index = len(second)
+        away = remote(
+            block, own_ref.at[place], near_send.at[index], near_recv.at[place], (clip, depth)
+        )
+        stay = pltpu.make_async_copy(block, own_ref.at[place], local_sem.at[index])
+        pl.when(clip != place)(away.start)
+        pl.when(clip == place)(stay.start)
+        second.append((clip, away, stay))
+
+    for slot in range(per):
+        hand_over(kept_ref.at[slot, depth], per * depth + slot)
+    yield
+    for step in range(1, planes):
+        source = lax.rem(depth + step, planes)
+        for slot in range(per):
+            clip = per * source + slot
+            block = mid.at[clip]
+            remote(
+                block, block, far_send.at[0, 0], far_recv.at[clip], (place, source)
+            ).wait_recv()
+            hand_over(block, clip)
+    yield
     for mask in range(1, group):
+        other = flip(mask)
+        block = own_ref.at[other]
+        remote(block, block, near_send.at[0], near_recv.at[other], (other, depth)).wait_recv()
+    for clip, away, stay in second:
+        pl.when(clip != place)(away.wait_send)
+        pl.when(clip == place)(stay.wait)
+    for copy in first:
+        copy.wait_send()
+    yield
+
+
+def outward_scratch(group, planes):
+    return [
+        DMA((group // planes, planes)),
+        DMA((group,)),
+        DMA((group,)),
+        DMA((group,)),
+        DMA((group,)),
+    ]
+
+
+def swap_steps(own_ref, kept_ref, send_sem, recv_sem, local_sem):
+    place, depth, flip = plane_places()
+    copies = []
+    for mask in (6, 7, 2, 3, 4, 5, 1):
+        other = flip(mask)
+        copy = remote(
+            own_ref.at[other],
+            kept_ref.at[place],
+            send_sem.at[mask],
+            recv_sem.at[mask],
+            (other, depth),
+        )
+        copy.start()
+        copies.append(copy)
+    stay = pltpu.make_async_copy(own_ref.at[place], kept_ref.at[place], local_sem)
+    stay.start()
+    yield
+    stay.wait()
+    for copy in copies:
+        copy.wait()
+    yield
+
+
+def swap_scratch():
+    return [DMA((8,)), DMA((8,)), DMA(())]
+
+
+def leave_body(
+    group, planes, kept_ref, cut_ref, parts_ref, own_ref, mine_ref, norm_ref, mid, terms, *sems
+):
+    part_send, part_recv = sems[:2]
+    place, depth, flip = plane_places()
+    devices = [(flip(mask), lax.rem(depth + step, planes)) for mask, step in everyone(planes)]
+    greet(devices)
+    here = place * planes + depth
+    rows = outward_steps(group, planes, kept_ref, own_ref, mid, *sems[2:7])
+    next(rows)
+    copies = []
+    for index, (other, plane) in enumerate(devices):
+        copy = remote(
+            parts_ref.at[other * planes + plane],
+            terms.at[here],
+            part_send.at[index],
+            part_recv.at[here],
+            (other, plane),
+        )
+        copy.start()
+        copies.append(copy)
+    terms[here] = parts_ref[here]
+    columns = swap_steps(cut_ref, mine_ref, *sems[7:])
+    next(columns)
+    next(rows)
+    for other, plane in devices:
+        source = other * planes + plane
+        one = terms.at[source]
+        remote(one, one, part_send.at[0], part_recv.at[source], (other, plane)).wait_recv()
+    norm_ref[...] = jnp.sum(terms[...], axis=0)
+    next(columns)
+    next(rows)
+    for copy in copies:
+        copy.wait_send()
+
+
+def leave(kept_rows, cut, norm_parts, collective_id):
+    per, planes, rows, wide = kept_rows.shape
+    group = per * planes
+    count = group * planes
+    whole = pl.BlockSpec(memory_space=pltpu.VMEM)
+    like = lambda shape, array: jax.ShapeDtypeStruct(shape, array.dtype)
+    own, mine, norm_sum, _ = pl.pallas_call(
+        functools.partial(leave_body, group, planes),
+        out_shape=[
+            like((group, rows, wide), kept_rows),
+            like(cut.shape, cut),
+            like(norm_parts.shape[1:], norm_parts),
+            like((group, rows, wide), kept_rows),
+        ],
+        in_specs=[any_spec(), any_spec(), whole],
+        out_specs=[any_spec(), any_spec(), whole, any_spec()],
+        scratch_shapes=[pltpu.VMEM(norm_parts.shape, jnp.float32), DMA((count,)), DMA((count,))]
+        + outward_scratch(group, planes)
+        + swap_scratch(),
+        compiler_params=communicating(collective_id),
+    )(kept_rows, cut, norm_parts)
+    return own, mine, norm_sum
+
+
+def everyone(planes):
+    return [(mask, step) for mask in range(8) for step in range(planes) if mask or step]
+
+
+def enter_body(
+    group,
+    planes,
+    own_ref,
+    norm_ref,
+    pack_ref,
+    cut_ref,
+    kept_ref,
+    norms_ref,
+    packs_ref,
+    mine_ref,
+    mid,
+    *sems,
+):
+    (
+        near_send,
+        near_recv,
+        far_send,
+        far_recv,
+        local_sem,
+        norm_send,
+        norm_recv,
+        pack_send,
+        pack_recv,
+        cut_send,
+        cut_recv,
+        stay_sem,
+    ) = sems
+    place, depth, flip = plane_places()
+    per = group // planes
+    others = everyone(planes)
+    greet([(flip(mask), lax.rem(depth + step, planes)) for mask, step in others])
+    here = place * planes + depth
+    first = []
+    for mask in (6, 7, 2, 3, 4, 5, 1):
         other = flip(mask)
         copy = remote(
             own_ref.at[other],
@@ -784,14 +1034,55 @@
             (other, depth),
         )
         copy.start()
-        first.append(copy)
+        first.append((mask, copy))
+    small = []
+    for index, (mask, step) in enumerate(others):
+        copy = remote(
+            norm_ref,
+            norms_ref.at[here],
+            norm_send.at[index],
+            norm_recv.at[here],
+            (flip(mask), lax.rem(depth + step, planes)),
+        )
+        copy.start()
+        small.append(copy)
+    for mask in range(1, group):
+        copy = remote(
+            pack_ref,
+            packs_ref.at[place],
+            pack_send.at[mask],
+            pack_recv.at[mask],
+            (flip(mask), depth),
+        )
+        copy.start()
+        small.append(copy)
+    stays = [
+        pltpu.make_async_copy(norm_ref, norms_ref.at[here], stay_sem.at[0]),
+        pltpu.make_async_copy(pack_ref, packs_ref.at[place], stay_sem.at[1]),
+        pltpu.make_async_copy(cut_ref.at[place], mine_ref.at[place], stay_sem.at[2]),
+    ]
+    for stay in stays:
+        stay.start()
+    cuts = []
+    for mask in (6, 7, 2, 3, 4, 5, 1):
+        other = flip(mask)
+        copy = remote(
+            cut_ref.at[other],
+            mine_ref.at[place],
+            cut_send.at[mask],
+            cut_recv.at[mask],
+            (other, depth),
+        )
+        copy.start()
+        cuts.append(copy)
     second = []
-    for mask in range(group):
+    arrivals = dict(first)
+    for mask in (0, 1, 2, 3, 4, 5, 6, 7):
         source = flip(mask)
         goal, slot = lax.div(source, per), lax.rem(source, per)
         block = own_ref.at[place]
         if mask:
-            first[mask - 1].wait_recv()
+            arrivals[mask].wait_recv()
             block = mid.at[source]
         away = remote(
             block,
@@ -816,140 +1107,583 @@
                     (place, lax.rem(depth + 1, planes)),
                 ).wait_recv
             )
+    for mask, step in others:
+        source = flip(mask) * planes + lax.rem(depth + step, planes)
+        block = norms_ref.at[source]
+        remote(
+            block,
+            block,
+            norm_send.at[0],
+            norm_recv.at[source],
+            (flip(mask), lax.rem(depth + step, planes)),
+        ).wait_recv()
+    for copy in small:
+        copy.wait_send()
+    for mask in range(1, group):
+        block = packs_ref.at[flip(mask)]
+        remote(
+            block, block, pack_send.at[0], pack_recv.at[mask], (flip(mask), depth)
+        ).wait_recv()
+    for copy in cuts:
+        copy.wait()
     for goal, away, stay in second:
         pl.when(goal != depth)(away.wait_send)
         pl.when(goal == depth)(stay.wait)
-    for copy in first:
+    for mask, copy in first:
         copy.wait_send()
-
-
-def inward(rows_of_clip, planes, collective_id):
+    for stay in stays:
+        stay.wait()
+
+
+def enter(rows_of_clip, norm_block, pack, cut, planes, collective_id):
     group, rows, wide = rows_of_clip.shape
-    kept, _ = pl.pallas_call(
-        functools.partial(inward_body, group, planes),
+    count = group * planes
+    like = lambda shape, array: jax.ShapeDtypeStruct(shape, array.dtype)
+    kept, norms, packs, mine, _ = pl.pallas_call(
+        functools.partial(enter_body, group, planes),
         out_shape=[
-            jax.ShapeDtypeStruct((group // planes, planes, rows, wide), rows_of_clip.dtype),
-            jax.ShapeDtypeStruct((group, rows, wide), rows_of_clip.dtype),
-        ],
-        in_specs=[any_spec()],
-        out_specs=[any_spec()] * 2,
+            like((group // planes, planes, rows, wide), rows_of_clip),
+            like((count,) + norm_block.shape, norm_block),
+            like((group,) + pack.shape, pack),
+            like(cut.shape, cut),
+            like((group, rows, wide), rows_of_clip),
+        ],
+        in_specs=[any_spec()] * 4,
+        out_specs=[any_spec()] * 5,
         scratch_shapes=[
             DMA((group,)),
             DMA((group,)),
             DMA((group,)),
             DMA((group // planes, planes)),
             DMA((group,)),
-        ],
-        compiler_params=communicating(collective_id),
-    )(rows_of_clip)
-    return kept
-
-
-def outward_body(group, planes, kept_ref, own_ref, mid, *sems):
-    far_send, far_recv, near_send, near_recv, local_sem = sems
-    place, depth, flip = plane_places()
-    per = group // planes
-    greet_cross(group, planes)
-    first = []
-    for step in range(1, planes):
-        origin = lax.rem(depth + step, planes)
-        for slot in range(per):
-            clip = per * depth + slot
-            copy = remote(
-                kept_ref.at[slot, origin],
-                mid.at[clip],
-                far_send.at[slot, step],
-                far_recv.at[clip],
-                (place, origin),
-            )
-            copy.start()
-            first.append(copy)
-    second = []
-
-    def hand_over(block, clip):
-        index = len(second)
-        away = remote(
-            block, own_ref.at[place], near_send.at[index], near_recv.at[place], (clip, depth)
-        )
-        stay = pltpu.make_async_copy(block, own_ref.at[place], local_sem.at[index])
-        pl.when(clip != place)(away.start)
-        pl.when(clip == place)(stay.start)
-        second.append((clip, away, stay))
-
-    for slot in range(per):
-        hand_over(kept_ref.at[slot, depth], per * depth + slot)
-    for step in range(1, planes):
-        source = lax.rem(depth + step, planes)
-        for slot in range(per):
-            clip = per * source + slot
-            block = mid.at[clip]
-            remote(
-                block, block, far_send.at[0, 0], far_recv.at[clip], (place, source)
-            ).wait_recv()
-            hand_over(block, clip)
-    for mask in range(1, group):
-        other = flip(mask)
-        block = own_ref.at[other]
-        remote(block, block, near_send.at[0], near_recv.at[other], (other, depth)).wait_recv()
-    for clip, away, stay in second:
-        pl.when(clip != place)(away.wait_send)
-        pl.when(clip == place)(stay.wait)
-    for copy in first:
-        copy.wait_send()
-
-
-def outward(kept_rows, collective_id):
-    per, planes, rows, wide = kept_rows.shape
-    group = per * planes
-    own, _ = pl.pallas_call(
-        functools.partial(outward_body, group, planes),
-        out_shape=[jax.ShapeDtypeStruct((group, rows, wide), kept_rows.dtype)] * 2,
-        in_specs=[any_spec()],
-        out_specs=[any_spec()] * 2,
-        scratch_shapes=[
-            DMA((per, planes)),
+            DMA((count,)),
+            DMA((count,)),
             DMA((group,)),
             DMA((group,)),
             DMA((group,)),
             DMA((group,)),
+            DMA((3,)),
         ],
         compiler_params=communicating(collective_id),
-    )(kept_rows)
-    return own
-
-
-def swap_body(own_ref, kept_ref, send_sem, recv_sem, local_sem):
+    )(rows_of_clip, norm_block, pack, cut)
+    return kept, norms, packs, mine
+
+
+def cond_steps(group, planes, pick_ref, cond_ref, parts, summed, *sems):
+    part_send, part_recv, cond_send, cond_recv = sems
     place, depth, flip = plane_places()
-    masks = (6, 7, 2, 3, 4, 5, 1)
-    greet([(flip(mask), depth) for mask in masks])
+    pushes = []
+    for step in range(1, planes):
+        goal = lax.rem(depth + step, planes)
+        copy = remote(
+            pick_ref.at[goal],
+            parts.at[depth],
+            part_send.at[step],
+            part_recv.at[depth],
+            (place, goal),
+        )
+        copy.start()
+        pushes.append(copy)
+    yield
+    total = pick_ref[depth].astype(jnp.float32)
+    for step in range(1, planes):
+        source = lax.rem(depth + step, planes)
+        block = parts.at[source]
+        remote(
+            block, block, part_send.at[0], part_recv.at[source], (place, source)
+        ).wait_recv()
+        total = total + parts[source].astype(jnp.float32)
+    summed[...] = total.astype(summed.dtype)
+    cond_ref[place] = total.astype(summed.dtype)
+    for mask in range(1, group):
+        copy = remote(
+            summed,
+            cond_ref.at[place],
+            cond_send.at[mask],
+            cond_recv.at[mask],
+            (flip(mask), depth),
+        )
+        copy.start()
+        pushes.append(copy)
+    yield
+    for mask in range(1, group):
+        block = cond_ref.at[flip(mask)]
+        remote(
+            block, block, cond_send.at[0], cond_recv.at[mask], (flip(mask), depth)
+        ).wait_recv()
+    for copy in pushes:
+        copy.wait_send()
+    yield
+
+
+def inward_beside(group, planes, own_ref, kept_ref, mid, *sems):
+    near_send, near_recv, far_send, far_recv, local_sem = sems
+    place, depth, flip = plane_places()
+    per = group // planes
+
+    def near(mask):
+        other = flip(mask)
+        return remote(
+            own_ref.at[other],
+            mid.at[place],
+            near_send.at[mask],
+            near_recv.at[mask],
+            (other, depth),
+        )
+
+    def begin():
+        for mask in range(1, group):
+            near(mask).start()
+
+    def second(mask):
+        source = flip(mask)
+        goal, slot = lax.div(source, per), lax.rem(source, per)
+        block = mid.at[source] if mask else own_ref.at[place]
+        away = remote(
+            block,
+            kept_ref.at[slot, depth],
+            far_send.at[mask],
+            far_recv.at[slot, depth],
+            (place, goal),
+        )
+        stay = pltpu.make_async_copy(block, kept_ref.at[slot, depth], local_sem.at[mask])
+        return goal != depth, away, stay
+
+    def middle():
+        for mask in range(group):
+            if mask:
+                near(mask).wait_recv()
+            leaves, away, stay = second(mask)
+            pl.when(leaves)(away.start)
+            pl.when(jnp.logical_not(leaves))(stay.start)
+
+    def end():
+        for slot in range(per):
+            for origin in range(planes):
+                block = kept_ref.at[slot, origin]
+                pl.when(origin != depth)(
+                    remote(
+                        block,
+                        block,
+                        far_send.at[0],
+                        far_recv.at[slot, origin],
+                        (place, lax.rem(depth + 1, planes)),
+                    ).wait_recv
+                )
+        for mask in range(group):
+            leaves, away, stay = second(mask)
+            pl.when(leaves)(away.wait_send)
+            pl.when(jnp.logical_not(leaves))(stay.wait)
+            if mask:
+                near(mask).wait_send()
+
+    return begin, middle, end
+
+
+def inward_scratch(group, planes):
+    return [
+        DMA((group,)),
+        DMA((group,)),
+        DMA((group,)),
+        DMA((group // planes, planes)),
+        DMA((group,)),
+    ]
+
+
+def finish_body(planes, squares_ref, total_ref, blocks, block_send, block_recv):
+    place, depth, flip = plane_places()
+    devices = [(flip(mask), lax.rem(depth + step, planes)) for mask, step in everyone(planes)]
+    greet(devices)
+    here = place * planes + depth
     copies = []
-    for mask in masks:
-        other = flip(mask)
+    blocks[here] = squares_ref[...]
+    for index, (other, plane) in enumerate(devices):
         copy = remote(
-            own_ref.at[other],
-            kept_ref.at[place],
-            send_sem.at[mask],
-            recv_sem.at[mask],
-            (other, depth),
+            squares_ref,
+            blocks.at[here],
+            block_send.at[index],
+            block_recv.at[here],
+            (other, plane),
         )
         copy.start()
         copies.append(copy)
-    stay = pltpu.make_async_copy(own_ref.at[place], kept_ref.at[place], local_sem)
-    stay.start()
-    stay.wait()
+    for other, plane in devices:
+        source = other * planes + plane
+        one = blocks.at[source]
+        remote(one, one, block_send.at[0], block_recv.at[source], (other, plane)).wait_recv()
+    total_ref[...] = jnp.sum(blocks[...], axis=0)
     for copy in copies:
-        copy.wait()
-
-
-def plane_swap(blocks, collective_id):
+        copy.wait_send()
+
+
+def finish(squares, planes, collective_id):
+    count = 8 * planes
+    whole = pl.BlockSpec(memory_space=pltpu.VMEM)
     return pl.pallas_call(
-        swap_body,
-        out_shape=jax.ShapeDtypeStruct(blocks.shape, blocks.dtype),
-        in_specs=[any_spec()],
-        out_specs=any_spec(),
-        scratch_shapes=[DMA((8,)), DMA((8,)), DMA(())],
+        functools.partial(finish_body, planes),
+        out_shape=jax.ShapeDtypeStruct(squares.shape, jnp.float32),
+        in_specs=[whole],
+        out_specs=whole,
+        scratch_shapes=[
+            pltpu.VMEM((count,) + squares.shape, jnp.float32),
+            DMA((count,)),
+            DMA((count,)),
+        ],
         compiler_params=communicating(collective_id),
-    )(blocks)
+    )(squares)
+
+
+def rotary_lanes(places):
+    cosine, sine = rotary_tables(places, HDIM)
+    cosine, sine = cosine[:, 0], sine[:, 0]
+    return jnp.stack(
+        [
+            jnp.concatenate([cosine] * 4, axis=1),
+            jnp.concatenate([-sine, sine, -sine, sine], axis=1),
+        ]
+    )
+
+
+def turn_heads(values, cosine, sine):
+    lane = lax.broadcasted_iota(jnp.int32, values.shape, 1)
+    half = HDIM // 2
+    ahead = pltpu.roll(values, 2 * HDIM - half, 1)
+    behind = pltpu.roll(values, half, 1)
+    other = jnp.where(lax.rem(lane, HDIM) < half, ahead, behind)
+    return values * cosine + other * sine
+
+
+def swap_beside(cut_ref, mine_ref, *sems):
+    place, depth, flip = plane_places()
+
+    def each(act):
+        for mask in (6, 7, 2, 3, 4, 5, 1):
+            other = flip(mask)
+            act(
+                remote(
+                    cut_ref.at[other],
+                    mine_ref.at[place],
+                    sems[0].at[mask],
+                    sems[1].at[mask],
+                    (other, depth),
+                )
+            )
+
+    stay = pltpu.make_async_copy(cut_ref.at[place], mine_ref.at[place], sems[2])
+
+    def begin():
+        each(lambda copy: copy.start())
+        stay.start()
+
+    def end():
+        each(lambda copy: copy.wait())
+        stay.wait()
+
+    return begin, end
+
+
+def flash_forward_body(
+    heads,
+    tile,
+    raw_ref,
+    stamp_ref,
+    bias_ref,
+    rotary_ref,
+    cut_ref,
+    own_ref,
+    turned_ref,
+    out_ref,
+    lse_ref,
+    mine_ref,
+    kept_ref,
+    mid,
+    *sems,
+):
+    group, planes = cut_ref.shape[0], kept_ref.shape[1]
+    step, last = pl.program_id(0), pl.num_programs(0) - 1
+    start_swap, end_swap = swap_beside(cut_ref, mine_ref, *sems[:3])
+    start_rows, pass_rows, end_rows = inward_beside(
+        group, planes, own_ref, kept_ref, mid, *sems[3:]
+    )
+
+    @pl.when(step == 0)
+    def _():
+        greet_cross(group, planes)
+        start_rows()
+        start_swap()
+
+    @pl.when(step == last)
+    def _():
+        pass_rows()
+
+    wide = heads * HDIM
+    for pair in range(2 * wide // 128):
+        lanes = slice(pair * 128, pair * 128 + 128)
+        turned_ref[:, lanes] = turn_heads(
+            raw_ref[:, lanes], rotary_ref[0], rotary_ref[1]
+        ).astype(turned_ref.dtype)
+    turned_ref[:, 2 * wide :] = raw_ref[:, 2 * wide :].astype(turned_ref.dtype)
+    rows = raw_ref.shape[0]
+    bias = bias_ref[0]
+    scale = HDIM**-0.5
+    for head in range(heads):
+        lanes = slice(head * HDIM, head * HDIM + HDIM)
+        keys = turned_ref[:, wide + head * HDIM : wide + head * HDIM + HDIM]
+        values = turned_ref[:, 2 * wide + head * HDIM : 2 * wide + head * HDIM + HDIM]
+        stamp_key = stamp_ref[0, :, lanes].astype(jnp.float32)
+        stamp_value = stamp_ref[
+            0, :, wide + head * HDIM : wide + head * HDIM + HDIM
+        ].astype(jnp.float32)
+
+        def one(step, carry):
+            place = pl.ds(pl.multiple_of(step * tile, tile), tile)
+            query = turned_ref[place, lanes] * jnp.asarray(scale, turned_ref.dtype)
+            scores = times_transposed(query, keys) + bias
+            stamp_score = jnp.sum(query.astype(jnp.float32) * stamp_key, axis=1, keepdims=True)
+            top = jnp.maximum(jnp.max(scores, axis=1, keepdims=True), stamp_score)
+            expo = jnp.exp(scores - top)
+            stamp_expo = jnp.exp(stamp_score - top)
+            denom = jnp.sum(expo, axis=1, keepdims=True) + stamp_expo
+            share = 1.0 / denom
+            prob = (expo * share).astype(values.dtype)
+            stamp_prob = (stamp_expo * share).astype(values.dtype).astype(jnp.float32)
+            mixed = jnp.dot(prob, values, preferred_element_type=jnp.float32)
+            out_ref[place, lanes] = (mixed + stamp_prob * stamp_value).astype(out_ref.dtype)
+            lse_ref[place, head : head + 1] = top + jnp.log(denom)
+            return carry
+
+        lax.fori_loop(0, rows // tile, one, 0)
+
+    @pl.when(step == last)
+    def _():
+        end_swap()
+        end_rows()
+
+
+def flash_forward(raw, stamps, bias, rotary, heads, cut, rows_of_clip, collective_id):
+    clips, rows = bias.shape
+    wide = heads * HDIM
+    group, piece, features = rows_of_clip.shape
+    planes = group // clips
+    like = lambda shape: jax.ShapeDtypeStruct(shape, rows_of_clip.dtype)
+    blocked = lambda lanes: pl.BlockSpec((rows, lanes), lambda clip: (clip, 0))
+    *results, _ = pl.pallas_call(
+        functools.partial(flash_forward_body, heads, rows // 4),
+        grid=(clips,),
+        out_shape=[
+            jax.ShapeDtypeStruct((clips * rows, 3 * wide), jnp.bfloat16),
+            jax.ShapeDtypeStruct((clips * rows, wide), jnp.bfloat16),
+            jax.ShapeDtypeStruct((clips * rows, 128), jnp.float32),
+            like(cut.shape),
+            like((clips, planes, piece, features)),
+            like(rows_of_clip.shape),
+        ],
+        in_specs=[
+            blocked(3 * wide),
+            pl.BlockSpec((1, 1, 2 * wide), lambda clip: (clip, 0, 0)),
+            pl.BlockSpec((1, 1, rows), lambda clip: (clip, 0, 0)),
+            pl.BlockSpec((2, rows, 128), lambda clip: (0, 0, 0)),
+            any_spec(),
+            any_spec(),
+        ],
+        out_specs=[blocked(3 * wide), blocked(wide), blocked(128)] + [any_spec()] * 3,
+        scratch_shapes=swap_scratch() + inward_scratch(group, planes),
+        compiler_params=communicating(collective_id),
+    )(raw, stamps[:, None], bias[:, None], rotary, cut, rows_of_clip)
+    return results
+
+
+def flash_backward_body(
+    heads,
+    tile,
+    turned_ref,
+    grad_ref,
+    lse_ref,
+    stamp_ref,
+    bias_ref,
+    rotary_ref,
+    cut_ref,
+    out_ref,
+    stamp_out_ref,
+    mine_ref,
+    query_grad,
+    key_grad,
+    value_grad,
+    *sems,
+):
+    place, depth, flip = plane_places()
+    start_swap, end_swap = swap_beside(cut_ref, mine_ref, *sems)
+
+    @pl.when(pl.program_id(0) == 0)
+    def _():
+        greet([(flip(mask), depth) for mask in range(1, 8)])
+        start_swap()
+
+    wide = heads * HDIM
+    rows = turned_ref.shape[0]
+    scale = HDIM**-0.5
+    low = turned_ref.dtype
+    f32 = jnp.float32
+    lse_rows = lse_ref[...].T
+    first_row = lax.broadcasted_iota(jnp.int32, (8, tile), 0) == 0
+    for head in range(heads):
+        lanes = slice(head * HDIM, head * HDIM + HDIM)
+        later = slice(wide + head * HDIM, wide + head * HDIM + HDIM)
+        keys = turned_ref[:, later]
+        values = turned_ref[:, 2 * wide + head * HDIM : 2 * wide + head * HDIM + HDIM]
+        keys_across = keys.astype(f32).T.astype(low)
+        stamp_key = jnp.broadcast_to(stamp_ref[0, :, lanes], (8, HDIM))
+        stamp_value = jnp.broadcast_to(stamp_ref[0, :, later], (8, HDIM))
+        stamp_column = stamp_ref[0, :, lanes].astype(f32).T
+        bias = bias_ref[0]
+        key_total = jnp.zeros((rows, HDIM), f32)
+        value_total = jnp.zeros((rows, HDIM), f32)
+        stamp_key_total = jnp.zeros((8, HDIM), f32)
+        stamp_value_total = jnp.zeros((8, HDIM), f32)
+        for step in range(rows // tile):
+            place = slice(step * tile, step * tile + tile)
+            query = turned_ref[place, lanes] * jnp.asarray(scale, low)
+            grad = grad_ref[place, lanes]
+            lse = lse_rows[head : head + 1, place]
+            prob = jnp.exp(times_transposed(keys, query) + bias - lse)
+            stamp_prob = jnp.exp(times_transposed(stamp_key, query) - lse)
+            grad_prob = times_transposed(values, grad)
+            stamp_grad_prob = times_transposed(stamp_value, grad)
+            delta = jnp.sum(prob * grad_prob, axis=0, keepdims=True)
+            delta = delta + (stamp_prob * stamp_grad_prob)[:1]
+            scores = (prob * (grad_prob - delta)).astype(low)
+            stamp_scores = (stamp_prob * (stamp_grad_prob - delta)).astype(low)
+            stamp_scores = jnp.where(first_row, stamp_scores.astype(f32), 0.0)
+            value_total += jnp.dot(prob.astype(low), grad, preferred_element_type=f32)
+            key_total += jnp.dot(scores, query, preferred_element_type=f32)
+            across = jnp.dot(keys_across, scores, preferred_element_type=f32)
+            across = across + stamp_column * stamp_scores[:1]
+            query_grad[place, lanes] = across.T * scale
+            stamp_key_total += jnp.dot(
+                stamp_scores.astype(low), query, preferred_element_type=f32
+            )
+            stamp_value_total += jnp.dot(
+                jnp.where(first_row, stamp_prob, 0.0).astype(low), grad, preferred_element_type=f32
+            )
+        key_grad[:, lanes] = key_total
+        value_grad[:, lanes] = value_total
+        stamp_out_ref[0, :, lanes] = stamp_key_total[:1]
+        stamp_out_ref[0, :, later] = stamp_value_total[:1]
+    both = jnp.concatenate([query_grad[...], key_grad[...]], axis=1)
+    for pair in range(2 * wide // 128):
+        lanes = slice(pair * 128, pair * 128 + 128)
+        out_ref[:, lanes] = turn_heads(both[:, lanes], rotary_ref[0], -rotary_ref[1]).astype(low)
+    out_ref[:, 2 * wide :] = value_grad[...].astype(low)
+    pl.when(pl.program_id(0) == pl.num_programs(0) - 1)(end_swap)
+
+
+def flash_backward(turned, grad, lse, stamps, bias, rotary, heads, cut, collective_id):
+    clips, rows = bias.shape
+    wide = heads * HDIM
+    blocked = lambda lanes: pl.BlockSpec((rows, lanes), lambda clip: (clip, 0))
+    grads, stamp_grads, mine = pl.pallas_call(
+        functools.partial(flash_backward_body, heads, rows // 4),
+        grid=(clips,),
+        out_shape=[
+            jax.ShapeDtypeStruct((clips * rows, 3 * wide), jnp.bfloat16),
+            jax.ShapeDtypeStruct((clips, 1, 2 * wide), jnp.float32),
+            jax.ShapeDtypeStruct(cut.shape, cut.dtype),
+        ],
+        in_specs=[
+            blocked(3 * wide),
+            blocked(wide),
+            blocked(128),
+            pl.BlockSpec((1, 1, 2 * wide), lambda clip: (clip, 0, 0)),
+            pl.BlockSpec((1, rows, 1), lambda clip: (clip, 0, 0)),
+            pl.BlockSpec((2, rows, 128), lambda clip: (0, 0, 0)),
+            any_spec(),
+        ],
+        out_specs=[
+            blocked(3 * wide),
+            pl.BlockSpec((1, 1, 2 * wide), lambda clip: (clip, 0, 0)),
+            any_spec(),
+        ],
+        scratch_shapes=[pltpu.VMEM((rows, wide), jnp.float32)] * 3 + swap_scratch(),
+        compiler_params=communicating(collective_id),
+    )(turned, grad, lse, stamps[:, None], bias[:, :, None], rotary, cut)
+    return grads, stamp_grads[:, 0], mine
+
+
+def ff_outer_body(normed_ref, gates_ref, grads_ref, hidden_ref, out_ref):
+    last = pl.program_id(0) == pl.num_programs(0) - 1
+
+    @pl.when(jnp.logical_not(last))
+    def _():
+        out_ref[...] = outer_sum(normed_ref[...], gates_ref[...]).astype(out_ref.dtype)
+
+    @pl.when(last)
+    def _():
+        out_ref[...] = outer_sum(grads_ref[...], hidden_ref[...]).astype(out_ref.dtype)
+
+
+def ff_outer(normed, gates, grads, hidden):
+    rows, wide = normed.shape
+    width = hidden.shape[1]
+    tile = wide // 3
+    ends = gates.shape[1] // width
+    return pl.pallas_call(
+        ff_outer_body,
+        grid=(ends + 1, wide // tile),
+        out_shape=jax.ShapeDtypeStruct((wide, (ends + 1) * width), jnp.bfloat16),
+        in_specs=[
+            pl.BlockSpec(
+                (rows, tile), lambda n, m: (0, jnp.where(n < ends, m, wide // tile - 1))
+            ),
+            pl.BlockSpec((rows, width), lambda n, m: (0, jnp.minimum(n, ends - 1))),
+            pl.BlockSpec((rows, tile), lambda n, m: (0, jnp.where(n < ends, 0, m))),
+            pl.BlockSpec((rows, width), lambda n, m: (0, 0)),
+        ],
+        out_specs=pl.BlockSpec((tile, width), lambda n, m: (m, n)),
+        compiler_params=pltpu.CompilerParams(vmem_limit_bytes=VMEM_LIMIT),
+    )(normed, gates, grads, hidden)
+
+
+def adam_body(split, factor_ref, weight_ref, first_ref, second_ref, grad_ref, *outs):
+    parts, _, held = grad_ref.shape
+    width = held // split
+    choices = [
+        jnp.concatenate(
+            [grad_ref[part, :, side * width : (side + 1) * width] for part in range(parts)], axis=1
+        ).astype(jnp.float32)
+        for side in range(split)
+    ]
+    gradient = choices[0]
+    for side in range(1, split):
+        gradient = jnp.where(lax.rem(pl.program_id(0), split) == side, choices[side], gradient)
+    results = adam_step(
+        weight_ref[...],
+        first_ref[...],
+        second_ref[...],
+        gradient * factor_ref[0, 0],
+        matrix_rate,
+        matrix_decay,
+    )
+    for out, result in zip(outs, results):
+        out[...] = result
+
+
+def adam_matrix(factor, weight, first, second, owned, width, split, parts):
+    rows, columns = weight.shape
+    group = owned.shape[0]
+    blocks = columns // (group * width)
+    steps = group // parts
+    piece = pl.BlockSpec((rows, parts * width), lambda block, step: (0, block * steps + step))
+    grads = pl.BlockSpec(
+        (parts, rows, split * width), lambda block, step: (step, 0, block // split)
+    )
+    return pl.pallas_call(
+        functools.partial(adam_body, split),
+        grid=(blocks, steps),
+        out_shape=[jax.ShapeDtypeStruct(weight.shape, jnp.float32)] * 3,
+        in_specs=[pl.BlockSpec(memory_space=pltpu.SMEM), piece, piece, piece, grads],
+        out_specs=[piece] * 3,
+        compiler_params=pltpu.CompilerParams(vmem_limit_bytes=VMEM_LIMIT),
+    )(factor, weight, first, second, owned)
 
 
 def plane_device(
@@ -987,73 +1721,78 @@
     cond_count, cond_wide = cond_ids.shape[1], cond_table.shape[1]
     cond_owned = cross_weight.shape[0]
 
+    order = jnp.arange(wide).reshape(group, planes, owned).swapaxes(0, 1).reshape(wide)
+    order_mat = (jnp.arange(wide)[:, None] == order[None, :]).astype(jnp.bfloat16)
+
     def to_plane_order(values):
-        lead = values.shape[:-1]
-        return jnp.swapaxes(values.reshape(lead + (group, planes, owned)), -3, -2).reshape(
-            lead + (wide,)
-        )
+        return jnp.dot(values, order_mat, preferred_element_type=jnp.float32).astype(jnp.bfloat16)
 
     def to_whole_order(values):
-        lead = values.shape[:-1]
-        return jnp.swapaxes(values.reshape(lead + (planes, group, owned)), -3, -2).reshape(
-            lead + (wide,)
-        )
+        return times_transposed(values, order_mat)
 
     attn_low = attn_weight.astype(jnp.bfloat16).reshape(owned, 6, group, head_wide)
     attn_cut = attn_low.transpose(2, 0, 1, 3).reshape(group, owned, 6 * head_wide)
     cross_low = cross_weight.astype(jnp.bfloat16).reshape(cond_owned, 2, group, head_wide)
     cross_cut = cross_low.transpose(2, 0, 1, 3).reshape(group, owned, -1)
+    norm_block = norm_param.astype(jnp.bfloat16).astype(jnp.float32)
+    norm_block = jnp.pad(norm_block, ((0, 2), (0, 128 - owned)))
+    pack = jnp.concatenate(
+        [
+            time_token.astype(jnp.float32),
+            jnp.pad(cond_ids.astype(jnp.float32), ((0, 0), (0, wide - cond_count))),
+            jnp.pad(cond_mask.astype(jnp.float32), ((0, 0), (0, wide - cond_count))),
+            jnp.broadcast_to(lengths.astype(jnp.float32)[:, None], (1, wide)),
+            jnp.zeros((4, wide), jnp.float32),
+        ],
+        axis=0,
+    )
+    stream, norm_all, packs, attn_mine = enter(
+        to_plane_order(frames[0]).reshape(group, piece, wide),
+        norm_block,
+        pack,
+        jnp.concatenate([attn_cut, cross_cut], axis=2),
+        planes,
+        1,
+    )
+    stream = stream.reshape(clips, own_rows, wide).astype(jnp.float32)
     ff_low = ff_weight.astype(jnp.bfloat16).reshape(owned, 3, group, ff_wide)
     ff_cut = ff_low.transpose(2, 0, 1, 3).reshape(group, owned, 3 * ff_wide)
-    attn_mine = plane_swap(jnp.concatenate([attn_cut, cross_cut], axis=2), 1)
-    ff_mine = plane_swap(ff_cut, 2)
 
     def over_planes(block):
         return lax.all_gather(block.reshape(group * owned, -1), "seq", axis=0, tiled=True)
 
     w_qkv = over_planes(attn_mine[:, :, : 3 * head_wide])
     w_rest = over_planes(attn_mine[:, :, 3 * head_wide :])
-    w_gate_up = over_planes(ff_mine[:, :, : 2 * ff_wide])
-    w_down = over_planes(ff_mine[:, :, 2 * ff_wide :])
     w_self_out = w_rest[:, :head_wide]
     w_cross_query = w_rest[:, head_wide : 2 * head_wide]
     w_cross_out = w_rest[:, 2 * head_wide : 3 * head_wide]
     w_cond = w_rest[:, 3 * head_wide :].reshape(planes, group, cond_owned, -1)
     w_cond = jnp.swapaxes(w_cond, 0, 1).reshape(cond_wide, 2 * head_wide)
-    norm_all = lax.all_gather(norm_param.astype(jnp.bfloat16), ("dp", "seq"), axis=0)
-    norm_all = norm_all.reshape(group, planes, 6, owned).transpose(2, 1, 0, 3)
-    gain_rows = norm_all.reshape(6, wide).astype(jnp.float32)
-
-    def of_plane(values):
-        everyone = lax.all_gather(values, "dp", axis=0, tiled=True)
-        return lax.dynamic_slice_in_dim(everyone, depth * clips, clips, axis=0)
-
-    clip_lengths = of_plane(lengths)
-    cond_keep = of_plane(cond_mask) > 0
-    stamps = to_plane_order(of_plane(time_token)).astype(jnp.float32)
+    norm_all = norm_all.reshape(group, planes, 8, 128)[:, :, :6, :owned].transpose(2, 1, 0, 3)
+    gain_rows = norm_all.reshape(6, wide)
+
+    plane_packs = lax.dynamic_slice_in_dim(packs, depth * clips, clips, axis=0)
+    stamps = to_plane_order(plane_packs[:, 0].astype(jnp.bfloat16)).astype(jnp.float32)
+    cond_keep = plane_packs[:, 2, :cond_count] > 0
+    clip_lengths = plane_packs[:, 3, 0].astype(jnp.int32)
+    share = cond_count // group
+    all_ids = packs[:, 1, :cond_count].astype(jnp.int32)
+    own_ids = lax.dynamic_slice_in_dim(all_ids, place * share, share, axis=1)
     vocab_rows = cond_table.shape[0]
-    relative = cond_ids - depth * vocab_rows
+    relative = own_ids - depth * vocab_rows
     inside = (relative >= 0) & (relative < vocab_rows)
     picked = jnp.take(cond_table, jnp.clip(relative, 0, vocab_rows - 1), axis=0)
     picked = jnp.where(inside[..., None], picked, jnp.zeros((), picked.dtype))
-    cond = of_plane(lax.psum(picked, "seq"))
-    cond_flat = cond.reshape(clips * cond_count, cond_wide)
-
+    picked = picked.reshape(planes, clips, share, cond_wide)
     positions = depth * frame_rows + jnp.arange(frame_rows)
     frame_valid = (positions[None, :] < lengths[:, None]).astype(cotangent.dtype)
-    stream = inward(to_plane_order(frames).reshape(group, piece, wide), planes, 3)
-    stream = stream.reshape(clips, own_rows, wide).astype(jnp.float32)
-    masked = to_plane_order(cotangent * frame_valid[..., None])
-    grad_out_low = inward(masked.reshape(group, piece, wide), planes, 4)
-    grad_out_low = grad_out_low.reshape(clips, own_rows, wide)
-    grad_out = grad_out_low.astype(jnp.float32)
+    masked = to_plane_order((cotangent * frame_valid[..., None])[0])
 
     group_rows = clips * seq_frames
     row_place = jnp.arange(seq_frames)
     row_owner, row_rest = row_place // own_rows, row_place % own_rows
     true_place = (row_rest // piece) * frame_rows + row_owner * piece + row_rest % piece
     key_keep = true_place[None, :] < clip_lengths[:, None]
-    cosine_table, sine_table = rotary_tables(true_place, HDIM)
     group_shape = (clips, seq_frames, heads, HDIM)
 
     def collect(rows, collective_id):
@@ -1064,24 +1803,29 @@
         return plane_reduce(terms, collective_id)
 
     normed_one = layer_norm(stream, gain_rows[0], gain_rows[1]).astype(jnp.bfloat16)
-    group_one = collect(normed_one, 5)
+    group_one, cond = plane_gather(normed_one, 5, picked)
+    group_one = group_one.reshape(group_rows, wide)
+    cond_flat = cond.swapaxes(0, 1).reshape(clips * cond_count, cond_wide)
     projected = jnp.dot(group_one, w_qkv, preferred_element_type=jnp.float32)
-    queries = rotate(
-        projected[:, :head_wide].reshape(group_shape), cosine_table, sine_table
-    ).astype(jnp.bfloat16)
-    all_keys = rotate(
-        projected[:, head_wide : 2 * head_wide].reshape(group_shape), cosine_table, sine_table
-    ).astype(jnp.bfloat16)
-    all_values = projected[:, 2 * head_wide :].astype(jnp.bfloat16).reshape(group_shape)
     stamp_normed = layer_norm(stamps, gain_rows[0], gain_rows[1]).astype(jnp.bfloat16)
     stamp_pair = jnp.dot(stamp_normed, w_qkv[:, head_wide:], preferred_element_type=jnp.float32)
     stamp_pair = stamp_pair.astype(jnp.bfloat16)
-    stamp_key = stamp_pair[:, :head_wide].reshape(clips, heads, HDIM)
-    stamp_value = stamp_pair[:, head_wide:].reshape(clips, heads, HDIM)
-    self_mixed, self_lse = self_forward(
-        queries, all_keys, all_values, stamp_key, stamp_value, key_keep
-    )
-    self_low = self_mixed.astype(jnp.bfloat16).reshape(group_rows, head_wide)
+    rotary = rotary_lanes(true_place)
+    key_bias = jnp.where(key_keep, 0.0, masked_score)
+    rotated, self_low, self_lse, ff_mine, grad_out_low = flash_forward(
+        projected,
+        stamp_pair,
+        key_bias,
+        rotary,
+        heads,
+        ff_cut,
+        masked.reshape(group, piece, wide),
+        2,
+    )
+    grad_out_low = grad_out_low.reshape(clips, own_rows, wide)
+    grad_out = grad_out_low.astype(jnp.float32)
+    w_gate_up = over_planes(ff_mine[:, :, : 2 * ff_wide])
+    w_down = over_planes(ff_mine[:, :, 2 * ff_wide :])
     resid_one = stream + spread(times_transposed(self_low, w_self_out), 6)
     normed_two = layer_norm(resid_one, gain_rows[2], gain_rows[3]).astype(jnp.bfloat16)
     group_two = collect(normed_two, 7)
@@ -1097,33 +1841,36 @@
     resid_two = resid_one + spread(times_transposed(cross_out, w_cross_out), 8)
     normed_three = layer_norm(resid_two, gain_rows[4], gain_rows[5]).astype(jnp.bfloat16)
     group_three = collect(normed_three, 9)
+    gate_up = jnp.dot(group_three, w_gate_up, preferred_element_type=jnp.float32)
+    gate_up, grad_out_low = lax.optimization_barrier((gate_up, grad_out_low))
     group_grad_out = collect(grad_out_low, 10)
-    gate_up = jnp.dot(group_three, w_gate_up, preferred_element_type=jnp.float32)
     gate_val, up_val = gate_up[:, :ff_wide], gate_up[:, ff_wide:]
     hidden = (jax.nn.silu(gate_val) * up_val).astype(jnp.bfloat16)
-    branch = spread(times_transposed(hidden, w_down), 11)
-    layer_out = (resid_two + branch).astype(jnp.bfloat16)
-    layer_out = outward(layer_out.reshape(clips, planes, piece, wide), 12)
-    layer_out = to_whole_order(layer_out.reshape(frames.shape))
+    branch = lax.psum_scatter(
+        times_transposed(hidden, w_down)
+        .astype(jnp.bfloat16)
+        .reshape(clips, group, own_rows, wide),
+        "dp",
+        scatter_dimension=1,
+        tiled=False,
+    )
+    layer_rows = (resid_two + branch.astype(jnp.float32)).astype(jnp.bfloat16)
 
     grad_hidden = jnp.dot(group_grad_out, w_down, preferred_element_type=jnp.float32)
     sigmoid_gate = jax.nn.sigmoid(gate_val)
     grad_gate = grad_hidden * up_val * sigmoid_gate * (1.0 + gate_val * (1.0 - sigmoid_gate))
     grad_up = grad_hidden * gate_val * sigmoid_gate
     grad_gate_up = jnp.concatenate([grad_gate, grad_up], axis=1).astype(jnp.bfloat16)
-    grad_normed_three = spread(times_transposed(grad_gate_up, w_gate_up), 13)
 
     def over_rows(block):
         return lax.psum_scatter(
             block.astype(jnp.bfloat16), "seq", scatter_dimension=0, tiled=True
         ).reshape(group, owned, -1)
 
-    ff_piece = jnp.concatenate(
-        [outer_sum(group_three, grad_gate_up), outer_sum(group_grad_out, hidden)], axis=1
-    )
-    ff_owned = plane_swap(over_rows(ff_piece), 14)
-    ff_reduced = ff_owned.reshape(group, owned, 3, ff_wide).transpose(1, 2, 0, 3)
-    ff_reduced = ff_reduced.reshape(owned, 3 * FF).astype(jnp.float32)
+    ff_piece = ff_outer(group_three, grad_gate_up, group_grad_out, hidden)
+    grad_gate_up, ff_piece = lax.optimization_barrier((grad_gate_up, ff_piece))
+    ff_rows = over_rows(ff_piece)
+    grad_normed_three = spread(times_transposed(grad_gate_up, w_gate_up), 13)
 
     _, norm_three_back = jax.vjp(layer_norm, resid_two, gain_rows[4], gain_rows[5])
     grad_two_part, grad_gain_three, grad_bias_three = norm_three_back(grad_normed_three)
@@ -1135,13 +1882,20 @@
         cross_query, cross_keys, cross_values, cond_keep, cross_lse, grad_cross_mixed
     )
     grad_cross_query = grad_cross_query.astype(jnp.bfloat16).reshape(group_rows, head_wide)
-    grad_normed_two = spread(times_transposed(grad_cross_query, w_cross_query), 16)
+    terms_two = times_transposed(grad_cross_query, w_cross_query).astype(jnp.bfloat16)
+    grad_normed_two, layer_out = plane_reduce(
+        terms_two.reshape(clips, group, own_rows, wide),
+        16,
+        layer_rows.reshape(clips, planes, piece, wide),
+    )
+    layer_out = to_whole_order(layer_out.reshape(frame_rows, wide)).astype(jnp.bfloat16)
+    layer_out = layer_out.reshape(frames.shape)
     _, norm_two_back = jax.vjp(layer_norm, resid_one, gain_rows[2], gain_rows[3])
     grad_one_part, grad_gain_two, grad_bias_two = norm_two_back(grad_normed_two)
     grad_one = grad_two + grad_one_part
     group_self_branch = collect(grad_one.astype(jnp.bfloat16), 17)
     grad_self_mixed = jnp.dot(group_self_branch, w_self_out, preferred_element_type=jnp.float32)
-    grad_self_mixed = grad_self_mixed.astype(jnp.bfloat16).reshape(group_shape)
+    grad_self_mixed = grad_self_mixed.astype(jnp.bfloat16)
     cond_grad = jnp.concatenate(
         [
             grad_cross_keys.reshape(clips * cond_count, head_wide),
@@ -1161,26 +1915,12 @@
         ],
         axis=1,
     )
+    rest_piece = rest_piece.astype(jnp.bfloat16)
+    grad_self_mixed, rest_piece = lax.optimization_barrier((grad_self_mixed, rest_piece))
+    rest_piece, ff_rows = lax.optimization_barrier((rest_piece, ff_rows))
     rest_rows = over_rows(rest_piece)
-    grad_queries, key_part, value_part, grad_stamp_key, grad_stamp_value = self_backward(
-        queries, all_keys, all_values, stamp_key, stamp_value, key_keep, self_lse, grad_self_mixed
-    )
-
-    def turn_back(values):
-        turned = rotate(values, cosine_table, -sine_table).astype(jnp.bfloat16)
-        return turned.reshape(group_rows, head_wide)
-
-    grad_value = value_part.astype(jnp.bfloat16).reshape(group_rows, head_wide)
-    grad_project = jnp.concatenate(
-        [turn_back(grad_queries), turn_back(key_part), grad_value], axis=1
-    )
-    grad_normed_one = spread(times_transposed(grad_project, w_qkv), 18)
-    stamp_grad = jnp.concatenate(
-        [
-            grad_stamp_key.reshape(clips, head_wide),
-            grad_stamp_value.reshape(clips, head_wide),
-        ],
-        axis=1,
+    grad_project, stamp_grad, ff_owned = flash_backward(
+        rotated, grad_self_mixed, self_lse, stamp_pair, key_bias, rotary, heads, ff_rows, 3
     )
     grad_stamp_normed = split_times_transposed(stamp_grad, w_qkv[:, head_wide:])
     qkv_piece = outer_sum(group_one, grad_project)
@@ -1188,22 +1928,16 @@
     qkv_piece = jnp.concatenate(
         [qkv_piece[:, :head_wide], qkv_piece[:, head_wide:] + stamp_weight_grad], axis=1
     )
+    qkv_piece = qkv_piece.astype(jnp.bfloat16)
+    grad_project, qkv_piece = lax.optimization_barrier((grad_project, qkv_piece))
     qkv_rows = over_rows(qkv_piece)
-    attn_owned = plane_swap(jnp.concatenate([qkv_rows, rest_rows], axis=2), 19)
-    cross_reduced = attn_owned[:, :, 6 * head_wide :].reshape(group, cond_owned, 2, head_wide)
-    cross_reduced = cross_reduced.transpose(1, 2, 0, 3).reshape(cross_weight.shape)
-    cross_reduced = cross_reduced.astype(jnp.float32)
-    attn_reduced = attn_owned[:, :, : 6 * head_wide].reshape(group, owned, 6, head_wide)
-    attn_reduced = attn_reduced.transpose(1, 2, 0, 3).reshape(attn_weight.shape)
-    attn_reduced = attn_reduced.astype(jnp.float32)
-
+    grad_project, rest_rows = lax.optimization_barrier((grad_project, rest_rows))
+    grad_normed_one = spread(times_transposed(grad_project, w_qkv), 18)
     _, norm_one_back = jax.vjp(layer_norm, stream, gain_rows[0], gain_rows[1])
     grad_zero_part, grad_gain_one, grad_bias_one = norm_one_back(grad_normed_one)
     _, norm_stamp_back = jax.vjp(layer_norm, stamps, gain_rows[0], gain_rows[1])
     _, grad_gain_stamp, grad_bias_stamp = norm_stamp_back(grad_stamp_normed)
     frames_grad = (grad_one + grad_zero_part).astype(jnp.bfloat16)
-    frames_grad = outward(frames_grad.reshape(clips, planes, piece, wide), 20)
-    frames_grad = to_whole_order(frames_grad.reshape(frames.shape)).astype(jnp.float32)
     norm_grad = jnp.stack(
         [
             grad_gain_one + grad_gain_stamp,
@@ -1215,20 +1949,29 @@
         ],
         axis=0,
     )
-    norm_total = lax.psum(norm_grad, ("dp", "seq"))
-    norm_reduced = lax.dynamic_slice_in_dim(
-        norm_total, (depth * group + place) * owned, owned, axis=1
-    )
-    local_squares = (
-        jnp.sum(attn_reduced * attn_reduced)
-        + jnp.sum(cross_reduced * cross_reduced)
-        + jnp.sum(norm_reduced * norm_reduced)
-        + jnp.sum(ff_reduced * ff_reduced)
-    )
-    grad_norm = jnp.sqrt(lax.psum(local_squares, ("dp", "seq")))
+    norm_parts = norm_grad.reshape(6, planes, group, owned).transpose(2, 1, 0, 3)
+    norm_parts = norm_parts.reshape(group * planes, 6, owned)
+    norm_parts = jnp.pad(norm_parts, ((0, 0), (0, 2), (0, 128 - owned)))
+    frames_grad, attn_owned, norm_sum = leave(
+        frames_grad.reshape(clips, planes, piece, wide),
+        jnp.concatenate([qkv_rows, rest_rows], axis=2),
+        norm_parts,
+        20,
+    )
+    frames_grad = to_whole_order(frames_grad.reshape(frame_rows, wide)).reshape(frames.shape)
+    cross_reduced = attn_owned[:, :, 6 * head_wide :].reshape(group, cond_owned, 2, head_wide)
+    cross_reduced = cross_reduced.transpose(1, 2, 0, 3).reshape(cross_weight.shape)
+    cross_reduced = cross_reduced.astype(jnp.float32)
+    squares = jnp.sum(jnp.square(attn_owned.astype(jnp.float32)))
+    squares = squares + jnp.sum(jnp.square(ff_owned.astype(jnp.float32)))
+    squares = squares + jnp.sum(jnp.square(norm_sum))
+    total = finish(jnp.broadcast_to(squares, (8, 128)), planes, 21)
+    norm_reduced = norm_sum[:6, :owned]
+    grad_norm = jnp.sqrt(total[0, 0])
     factor = jnp.minimum(1.0, clip_limit / grad_norm)
-    attn_new, attn_first_new, attn_second_new = adam_step(
-        attn_weight, attn_first, attn_second, attn_reduced * factor, matrix_rate, matrix_decay
+    factor_block = factor.reshape(1, 1)
+    attn_new, attn_first_new, attn_second_new = adam_matrix(
+        factor_block, attn_weight, attn_first, attn_second, attn_owned, head_wide, 2, group
     )
     cross_new, cross_first_new, cross_second_new = adam_step(
         cross_weight, cross_first, cross_second, cross_reduced * factor, matrix_rate, matrix_decay
@@ -1236,8 +1979,8 @@
     norm_new, norm_first_new, norm_second_new = adam_step(
         norm_param, norm_first, norm_second, norm_reduced * factor, gain_rate, 0.0
     )
-    ff_new, ff_first_new, ff_second_new = adam_step(
-        ff_weight, ff_first, ff_second, ff_reduced * factor, matrix_rate, matrix_decay
+    ff_new, ff_first_new, ff_second_new = adam_matrix(
+        factor_block, ff_weight, ff_first, ff_second, ff_owned, ff_wide, 1, group // 2
     )
     return (
         layer_out,

time: 1310 us -> 893 us (0.68)
  blocking collectives: 165 us -> 0 us
  local copies, waits for them, and re-layouts: 133 us -> 53.9 us
  matrix products: 213 us -> 148 us
  Pallas kernels: 660 us -> 596 us
  other arithmetic: 95.6 us -> 57.3 us
    all_gather x3 -> x0, blocking collectives: 80.7 us -> none  [the longest x1 61.7 us: plane_device(): lax.all_gather(norm_param.astype(jnp.bfloat16), ('dp', 'seq'), axis=0)]
    psum x2 -> x0, blocking collectives: 77.8 us -> none  [the longest x1 39.2 us: plane_device(): norm_total = lax.psum(norm_grad, ('dp', 'seq'))]
    pallas_call x20 -> x19, Pallas kernels: 660 us -> 596 us  [the longest x5 157 us: plane_gather(): pl.pallas_call(functools.partial(gather_body, clips, rows, sub, None), ou...]
    dot_general x10 -> x3, matrix products: 61.5 us -> 7.42 us  [to_plane_order(): jnp.dot(values, order_mat, preferred_element_type=jnp.float32)]
    unnamed x228 -> x153, local copies, waits for them, and re-layouts: 33.2 us -> 11.4 us
    dot_general x10 -> x8, matrix products: 34.4 us -> 16.3 us  [outer_sum(): lax.dot_general(left_mat, right_mat, (((0,), (0,)), ((), ())), preferred_...]
    mul x5 -> x0, local copies, waits for them, and re-layouts: 17.3 us -> none  [the longest x3 8.92 us: plane_device(): attn_reduced * factor]
    reduce_sum x5 -> x3, other arithmetic: 19 us -> 3.26 us  [the longest x1 1.51 us: plane_device(): squares = squares + jnp.sum(jnp.square(ff_owned.astype(jnp.float32)))]
  transfers between devices with their start and end apart: 9 -> 8, of which waited for: 1 -> 0; matrix products, arithmetic and copies ran while one was open for 19% -> 23% of each run, Pallas kernels for 36% -> 56%
where the time goes in v2:
time: 893 us; the launch traced here: 886 us
  Pallas kernels  596 us (67%)
  matrix products  148 us (17%)
  other arithmetic  57.3 us (6%)
  local copies, waits for them, and re-layouts  53.9 us (6%)
  between operations  20.4 us (2%)
  starting transfers between devices  9.48 us (1%)
    pallas_call x5, Pallas kernels, plane_gather(): pl.pallas_call(functools.partial(gather_body, clips, rows, sub, None), ou...  157 us
    pallas_call x4, Pallas kernels, plane_reduce(): pl.pallas_call(functools.partial(reduce_body, clips, rows, sub, None), ou...  143 us
    pallas_call x1, Pallas kernels, plane_reduce(): pl.pallas_call(functools.partial(reduce_body, clips, rows, sub, (group, p...  67.3 us
    dot_general x10, matrix products, times_transposed(): lax.dot_general(left_mat, right_mat, (((1,), (1,)), ((), ())), preferred_...  59.4 us
    pallas_call x1, Pallas kernels, plane_gather(): pl.pallas_call(functools.partial(gather_body, clips, rows, sub, (group, p...  38.9 us
    pallas_call x1, Pallas kernels, flash_forward(): pl.pallas_call(functools.partial(flash_forward_body, heads, rows // 4), g...  38.9 us
    pallas_call x1, Pallas kernels, enter(): pl.pallas_call(functools.partial(enter_body, group, planes), out_shape=[l...  35.4 us
    pallas_call x1, Pallas kernels, leave(): pl.pallas_call(functools.partial(leave_body, group, planes), out_shape=[l...  35.3 us
  transfers between devices with their start and end apart: 8, of which 0 were waited for; matrix products, arithmetic and copies ran while one was open for 23% of the time, Pallas kernels for 56%

profile of v2, /device:TPU:9, one launch (start us, length us, event | category | flops | bytes accessed | tf_op | source)
XLA Modules:
  0.0 885.5 jit_solution(1161067472463914579)
XLA Ops:
  22.3 35.4 %shard_map.298 = (bf16[2,4,32,1536]{3,2,1,0:T(8,128)(2,1)}, f32[32,8,128]{2,1,0:T(8,128)}, f32[8,8,1536]{2,1,0:T(8,128)}, bf16[8,48,1344]{2,1,0:T(8,128)(2,1)}, bf16[8,32,1536]{2,1,0:T(8,128)(2,1)}) custom-call(bf16[8,32,1536]{2,1,0:T(8,128)(2,1)} %bitcast.275, f32[8,128]{1,0:T(8,128)} %pad_convert_fusion.norm_ref, f32[8,1536]{1,0:T(8,128)} %concatenate.31.pack_ref, ...), custom_call_target="tpu_custom_call" | custom-call | tf_op jit(solution)/shard_map/pallas_call | solution.py:1142
  78.5 38.9 %shard_map.299 = (bf16[2,8,128,1536]{3,2,1,0:T(8,128)(2,1)}, bf16[8,2,16,768]{3,2,1,0:T(8,128)(2,1)}) custom-call(bf16[2,128,1536]{2,1,0:T(8,128)(2,1)} %fusion.30.own_ref, bf16[4,2,16,768]{3,2,1,0:T(8,128)(2,1)} %select_select_fusion.refs_0_), custom_call_target="tpu_custom_call" | custom-call | tf_op jit(solution)/shard_map/pallas_call | solution.py:678
  131.3 9.3 %fusion.120.raw_ref = f32[2048,576]{1,0:T(8,128)} fusion(bf16[2048,1536]{1,0:T(8,128)(2,1)} %bitcast.285, bf16[1536,576]{1,0:T(8,128)(2,1)} %all-gather.7.cloned.1.call-done), kind=kOutput, calls=%fused_computation.245 | convolution fusion | flops 3623878656 | bytes 12779520 | tf_op jit(solution)/shard_map/dot_general | solution.py:1809
  140.6 38.9 %shard_map.300 = (bf16[2048,576]{1,0:T(8,128)(2,1)}, bf16[2048,192]{1,0:T(8,128)(2,1)}, f32[2048,128]{1,0:T(8,128)}, bf16[8,48,2304]{2,1,0:T(8,128)(2,1)}, bf16[...) custom-call(f32[2048,576]{1,0:T(8,128)} %fusion.120.raw_ref, bf16[2,1,384]{2,1,0:T(2,128)(2,1)} %copy.139.stamp_ref, ...), custom_call_target="tpu_custom_call" | custom-call | tf_op jit(solution)/shard_map/pallas_call | solution.py:1470
  185.0 8.8 reduce-scatter.9.cloned.1.call-start
  202.7 32.2 %shard_map.301 = f32[2,128,1536]{2,1,0:T(8,128)} custom-call(bf16[2,8,128,1536]{3,2,1,0:T(8,128)(2,1)} %bitcast.225), custom_call_target="tpu_custom_call" | custom-call | tf_op jit(solution)/shard_map/pallas_call | solution.py:807
  238.1 32.5 %shard_map.302 = bf16[2,8,128,1536]{3,2,1,0:T(8,128)(2,1)} custom-call(bf16[2,128,1536]{2,1,0:T(8,128)(2,1)} %add_convert_fusion.2.own_ref), custom_call_target="tpu_custom_call" | custom-call | tf_op jit(solution)/shard_map/pallas_call | solution.py:667
  286.5 34.8 %shard_map.303 = f32[2,128,1536]{2,1,0:T(8,128)} custom-call(bf16[2,8,128,1536]{3,2,1,0:T(8,128)(2,1)} %bitcast.226), custom_call_target="tpu_custom_call" | custom-call | tf_op jit(solution)/shard_map/pallas_call | solution.py:807
  325.3 30.9 %shard_map.304 = bf16[2,8,128,1536]{3,2,1,0:T(8,128)(2,1)} custom-call(bf16[2,128,1536]{2,1,0:T(8,128)(2,1)} %add_convert_fusion.1.own_ref), custom_call_target="tpu_custom_call" | custom-call | tf_op jit(solution)/shard_map/pallas_call | solution.py:667
  356.2 16.0 %fusion.121 = f32[2048,1536]{1,0:T(8,128)} fusion(bf16[2048,1536]{1,0:T(8,128)(2,1)} %bitcast.227, bf16[1536,1536]{1,0:T(8,128)(2,1)} %all-gather.9.cloned.1.call-done), kind=kOutput, calls=%fused_computation.246 | convolution fusion | flops 9663676416 | bytes 23592960 | tf_op jit(solution)/shard_map/dot_general | solution.py:1844
  372.2 30.9 %shard_map.305 = bf16[2,8,128,1536]{3,2,1,0:T(8,128)(2,1)} custom-call(bf16[2,128,1536]{2,1,0:T(8,128)(2,1)} %bitcast.232), custom_call_target="tpu_custom_call" | custom-call | tf_op jit(solution)/shard_map/pallas_call | solution.py:667
  403.1 14.1 %multiply_convert_fusion.2 = (bf16[2048,768]{1,0:T(8,128)(2,1)}, bf16[2048,768]{1,0:T(8,128)(2,1)}, bf16[2048,768]{1,0:T(8,128)(2,1)S(1)}) fusion(f32[2048,1536]{1,0:T(8,128)} %fusion.121, bf16[2048,1536]{1,0:T(8,128)(2,1)} %bitcast.229, bf16[1536,768]{1,0:T(8,128)(2,1)} %all-gather.11.cloned.1.call-done), kind=kOutput, calls=%fused_computation.16 | convolution fusion | flops 4857004032 | bytes 30670848 | tf_op jit(solution)/shard_map/dot_general | solution.py:1859
  432.5 24.6 %shard_map.306 = bf16[1536,2304]{1,0:T(8,128)(2,1)} custom-call(bf16[2048,1536]{1,0:T(8,128)(2,1)} %bitcast.228, bf16[2048,1536]{1,0:T(8,128)(2,1)} %pad_maximum_fusion.gates_ref, bf16[2048,1536]{1,0:T(8,128)(2,1)} %bitcast.230, bf16[2048,768]{1,0:T(8,128)(2,1)} %copy-done.23), custom_call_target="tpu_custom_call" | custom-call | tf_op jit(solution)/shard_map/pallas_call | solution.py:1629
  457.2 15.2 %convolution_convert_fusion.5 = bf16[2048,1536]{1,0:T(8,128)(2,1)} fusion(bf16[2048,1536]{1,0:T(8,128)(2,1)} %pad_maximum_fusion.gates_ref, bf16[1536,1536]{1,0:T(8,128)(2,1)} %all-gather.9.cloned.1.call-done), kind=kOutput, calls=%fused_computation.12 | convolution fusion | flops 9666822144 | bytes 17301504 | tf_op jit(solution)/shard_map/dot_general | solution.py:60
  472.4 40.8 %shard_map.307 = f32[2,128,1536]{2,1,0:T(8,128)} custom-call(bf16[2,8,128,1536]{3,2,1,0:T(8,128)(2,1)} %bitcast.247), custom_call_target="tpu_custom_call" | custom-call | tf_op jit(solution)/shard_map/pallas_call | solution.py:807
  521.6 31.0 %shard_map.308 = bf16[2,8,128,1536]{3,2,1,0:T(8,128)(2,1)} custom-call(bf16[2,128,1536]{2,1,0:T(8,128)(2,1)} %fusion.46.own_ref), custom_call_target="tpu_custom_call" | custom-call | tf_op jit(solution)/shard_map/pallas_call | solution.py:667
  573.4 67.3 %shard_map.309 = (f32[2,128,1536]{2,1,0:T(8,128)}, bf16[8,32,1536]{2,1,0:T(8,128)(2,1)}, bf16[8,32,1536]{2,1,0:T(8,128)(2,1)}) custom-call(bf16[2,8,128,1536]{3,2,1,0:T(8,128)(2,1)} %bitcast.224, bf16[2,4,32,1536]{3,2,1,0:T(8,128)(2,1)} %bitcast.259), custom_call_target="tpu_custom_call" | custom-call | tf_op jit(solution)/shard_map/pallas_call | solution.py:818
  646.1 31.5 %shard_map.310 = bf16[2,8,128,1536]{3,2,1,0:T(8,128)(2,1)} custom-call(bf16[2,128,1536]{2,1,0:T(8,128)(2,1)} %get-tuple-element.108.own_ref), custom_call_target="tpu_custom_call" | custom-call | tf_op jit(solution)/shard_map/pallas_call | solution.py:667
  703.7 28.9 %shard_map.311 = (bf16[2048,576]{1,0:T(8,128)(2,1)}, f32[2,1,384]{2,1,0:T(1,128)}, bf16[8,48,2304]{2,1,0:T(8,128)(2,1)}) custom-call(bf16[2048,576]{1,0:T(8,128)(2,1)} %get-tuple-element.66.turned_ref, bf16[2048,192]{1,0:T(8,128)(2,1)} %convolution_convert_fusion.6.grad_ref, f32[2048,128]{1,0:T(8,128)} %get-tuple-element.68.lse_ref, ...), custom_call_target="tpu_custom_call" | custom-call | tf_op jit(solution)/shard_map/pallas_call | solution.py:1584
  749.0 9.1 %convolution_convert_fusion.4 = bf16[2048,1536]{1,0:T(8,128)(2,1)} fusion(bf16[2048,576]{1,0:T(8,128)(2,1)} %get-tuple-element.76, bf16[1536,576]{1,0:T(8,128)(2,1)} %all-gather.7.cloned.1.call-done), kind=kOutput, calls=%fused_computation.11 | convolution fusion | flops 3627024384 | bytes 10420224 | tf_op jit(solution)/shard_map/dot_general | solution.py:60
  758.1 35.0 %shard_map.312 = f32[2,128,1536]{2,1,0:T(8,128)} custom-call(bf16[2,8,128,1536]{3,2,1,0:T(8,128)(2,1)} %bitcast.248), custom_call_target="tpu_custom_call" | custom-call | tf_op jit(solution)/shard_map/pallas_call | solution.py:807
  802.1 35.3 %shard_map.313 = (bf16[8,32,1536]{2,1,0:T(8,128)(2,1)}, bf16[8,48,1344]{2,1,0:T(8,128)(2,1)}, f32[8,128]{1,0:T(8,128)}, bf16[8,32,1536]{2,1,0:T(8,128)(2,1)}) custom-call(bf16[2,4,32,1536]{3,2,1,0:T(8,128)(2,1)} %bitcast.260, bf16[8,48,1344]{2,1,0:T(8,128)(2,1)} %pad_maximum_fusion.4.cut_ref, f32[32,8,128]{2,1,0:T(8,128)} %pad.21.parts_ref), custom_call_target="tpu_custom_call" | custom-call | tf_op jit(solution)/shard_map/pallas_call | solution.py:971
  846.0 9.3 %shard_map.314 = f32[8,128]{1,0:T(8,128)} custom-call(f32[8,128]{1,0:T(8,128)} %broadcast_in_dim.148.squares_ref), custom_call_target="tpu_custom_call" | custom-call | tf_op jit(solution)/shard_map/pallas_call | solution.py:1322
  865.9 10.4 %shard_map.316 = (f32[48,18432]{1,0:T(8,128)}, f32[48,18432]{1,0:T(8,128)}, f32[48,18432]{1,0:T(8,128)}) custom-call(f32[1,1]{1,0:T(1,128)} %bitcast.58.factor_ref, f32[48,18432]{1,0:T(8,128)} %weight_ref.3, f32[48,18432]{1,0:T(8,128)} %first_ref.3, f32[48,18432]{1,0:T(8,128)} %second_ref.3, bf16[8,48,2304]{2,1,0:T(8,128)(2,1)} %get-tuple-element.81.grad_ref), custom_call_target="tpu_custom_call" | custom-call | tf_op jit(solution)/shard_map/pallas_call | solution.py:1679
  (353 shorter events, 204.1 us)
Async XLA Ops:
  7.2 10.6 %copy-start = (bf16[1,256,1536]{2,1,0:T(8,128)(2,1)S(1)}, bf16[1,256,1536]{2,1,0:T(8,128)(2,1)}, u32[]{:S(2)}) copy-start(bf16[1,256,1536]{2,1,0:T(8,128)(2,1)} %param.19) | copy-start | bytes 2359300
  7.2 121.5 %all-gather.7.cloned.1.call-start = ((), (), s32[]{:S(2)}) async-start(), calls=%async_computation.5 | async-start | bytes 2457600 | tf_op jit(solution)/shard_map/all_gather | solution.py:1762
  59.7 134.2 %all-gather.5.cloned.1.call-start = ((), (), s32[]{:S(2)}) async-start(), calls=%async_computation.4 | async-start | bytes 2949120 | tf_op jit(solution)/shard_map/all_gather | solution.py:1762
  61.9 294.3 %all-gather.9.cloned.1.call-start = ((), (), s32[]{:S(2)}) async-start(), calls=%async_computation.6 | async-start | bytes 5898240 | tf_op jit(solution)/shard_map/all_gather | solution.py:1762
  63.8 65.0 %copy-start.36 = (f32[1536]{0:T(1024)}, f32[1536]{0:T(1024)S(1)}, u32[]{:S(2)}) copy-start(f32[1536]{0:T(1024)S(1)} %add.385) | copy-start | bytes 18436
  63.8 64.9 %copy-start.31 = (f32[1536]{0:T(1024)}, f32[1536]{0:T(1024)S(1)}, u32[]{:S(2)}) copy-start(f32[1536]{0:T(1024)S(1)} %mul.470) | copy-start | bytes 18436
  64.5 9.0 %copy-start.47 = (f32[2,128]{1,0:T(2,128)}, f32[2,128]{1,0:T(2,128)S(1)}, u32[]{:S(2)}) copy-start(f32[2,128]{1,0:T(2,128)S(1)} %rsqrt.42) | copy-start | bytes 3076
  182.0 221.1 %all-gather.11.cloned.1.call-start = ((), (), s32[]{:S(2)}) async-start(), calls=%async_computation.7 | async-start | bytes 2949120 | tf_op jit(solution)/shard_map/all_gather | solution.py:1762
  182.1 13.8 %copy-start.17 = (bf16[2,8,16,768]{3,2,1,0:T(8,128)(2,1)}, bf16[2,8,16,768]{3,2,1,0:T(8,128)(2,1)S(1)}, u32[]{:S(2)}) copy-start(bf16[2,8,16,768]{3,2,1,0:T(8,128)(2,1)S(1)} %copy.133) | copy-start | bytes 1179652
  185.0 330.6 %reduce-scatter.9.cloned.1.call-start = ((), (), s32[]{:S(2)}) async-start(), calls=%async_computation.8 | async-start | bytes 7077888 | tf_op jit(solution)/shard_map/reduce_scatter | solution.py:1849
  403.1 14.1 %copy-start.63 = (bf16[1536,768]{1,0:T(8,128)(2,1)S(1)}, bf16[1536,768]{1,0:T(8,128)(2,1)}, u32[]{:S(2)}) copy-start(bf16[1536,768]{1,0:T(8,128)(2,1)} %all-gather.11.cloned.1.call-done) | copy-start | bytes 7077892
  426.1 270.1 %reduce-scatter.11.cloned.1.call-start = ((), (), s32[]{:S(2)}) async-start(), calls=%async_computation.9 | async-start | bytes 8847360 | tf_op jit(solution)/shard_map/reduce_scatter | solution.py:1866
  457.1 291.8 %reduce-scatter.13.cloned.1.call-start = ((), (), s32[]{:S(2)}) async-start(), calls=%async_computation.10 | async-start | bytes 2949120 | tf_op jit(solution)/shard_map/reduce_scatter | solution.py:1866
  646.1 34.0 %copy-start.4 = (f32[2,3,1024,128]{2,3,1,0:T(8,128)S(1)}, f32[2,3,1024,128]{2,3,1,0:T(8,128)}, u32[]{:S(2)}) copy-start(f32[2,3,1024,128]{2,3,1,0:T(8,128)} %copy-done.2) | copy-start | bytes 9437188
  698.6 101.2 %reduce-scatter.15.cloned.1.call-start = ((), (), s32[]{:S(2)}) async-start(), calls=%async_computation.11 | async-start | bytes 2457600 | tf_op jit(solution)/shard_map/reduce_scatter | solution.py:1866
  758.1 35.1 %copy-start.7 = (bf16[2,4,32,1536]{3,2,1,0:T(8,128)(2,1)S(1)}, bf16[2,4,32,1536]{3,2,1,0:T(8,128)(2,1)}, u32[]{:S(2)}) copy-start(bf16[2,4,32,1536]{3,2,1,0:T(8,128)(2,1)} %get-tuple-element.52) | copy-start | bytes 2359300
  758.1 35.1 %copy-start.44 = (f32[2,128]{1,0:T(2,128)S(1)}, f32[2,128]{1,0:T(2,128)}, u32[]{:S(2)}) copy-start(f32[2,128]{1,0:T(2,128)} %copy-done.43) | copy-start | bytes 3076
  841.7 16.2 %copy-start.45 = (f32[6,48]{1,0:T(8,128)S(1)}, f32[6,48]{1,0:T(8,128)}, u32[]{:S(2)}) copy-start(f32[6,48]{1,0:T(8,128)} %param.28) | copy-start | bytes 3460
  841.7 16.3 %copy-start.59 = (f32[6,48]{1,0:T(8,128)S(1)}, f32[6,48]{1,0:T(8,128)}, u32[]{:S(2)}) copy-start(f32[6,48]{1,0:T(8,128)} %param.34) | copy-start | bytes 3460
  841.7 16.3 %copy-start.60 = (f32[6,48]{1,0:T(8,128)S(1)}, f32[6,48]{1,0:T(8,128)}, u32[]{:S(2)}) copy-start(f32[6,48]{1,0:T(8,128)} %param.35) | copy-start | bytes 3460
  865.8 10.4 %copy-start.28 = (f32[24,3072]{1,0:T(8,128)S(1)}, f32[24,3072]{1,0:T(8,128)}, u32[]{:S(2)}) copy-start(f32[24,3072]{1,0:T(8,128)} %param.27) | copy-start | bytes 884740
  865.8 10.4 %copy-start.34 = (f32[24,3072]{1,0:T(8,128)S(1)}, f32[24,3072]{1,0:T(8,128)}, u32[]{:S(2)}) copy-start(f32[24,3072]{1,0:T(8,128)} %param.32) | copy-start | bytes 884740
  865.9 10.4 %copy-start.35 = (f32[24,3072]{1,0:T(8,128)S(1)}, f32[24,3072]{1,0:T(8,128)}, u32[]{:S(2)}) copy-start(f32[24,3072]{1,0:T(8,128)} %param.33) | copy-start | bytes 884740
  865.9 11.5 %copy-start.1 = (bf16[1,256,1536]{2,1,0:T(8,128)(2,1)S(1)}, bf16[1,256,1536]{2,1,0:T(8,128)(2,1)}, u32[]{:S(2)}) copy-start(bf16[1,256,1536]{2,1,0:T(8,128)(2,1)} %param.19) | copy-start | bytes 2359300
  (54 other events, 203.3 us)
Sparse Core Ops, SparseCore 0:
  59.8 45.0 all-gather.6
  107.0 49.9 all-gather.4
  182.1 85.9 all-gather.8
  270.1 49.7 all-gather.10
  426.2 66.6 reduce-scatter.8
  495.2 141.8 reduce-scatter.10
  698.8 43.2 reduce-scatter.12
  745.1 42.4 reduce-scatter.14

commit v3 on v2

--- a/solution.py
+++ b/solution.py
@@ -575,257 +575,6 @@
     return pl.BlockSpec(memory_space=pl.ANY)
 
 
-def gather_body(clips, rows, sub, beside, own_ref, *refs):
-    if beside:
-        pick_ref, all_ref, cond_ref, send_sem, recv_sem, local_sem, *extra = refs
-        greet_cross(*beside)
-        cond = cond_steps(*beside, pick_ref, cond_ref, *extra)
-        next(cond)
-    else:
-        all_ref, send_sem, recv_sem, local_sem = refs
-    place, depth, flip = plane_places()
-    core, beside_x, beside_y, across = flip(1), flip(2), flip(4), flip(6)
-    if not beside:
-        greet([(core, depth), (beside_x, depth), (beside_y, depth)])
-    chunks = [(clip, part) for clip in range(clips) for part in range(rows // sub)]
-    count = len(chunks)
-    half = count // 2
-    sends = []
-
-    def view(slot, index):
-        clip, part = chunks[index]
-        return all_ref.at[clip, slot, pl.ds(part * sub, sub)]
-
-    def own(index):
-        clip, part = chunks[index]
-        return own_ref.at[clip, pl.ds(part * sub, sub)]
-
-    def send(source, slot, index, device):
-        copy = remote(
-            source,
-            view(slot, index),
-            send_sem.at[len(sends)],
-            recv_sem.at[slot, index],
-            (device, depth),
-        )
-        copy.start()
-        sends.append(copy)
-
-    def arrived(slot, index):
-        block = view(slot, index)
-        remote(
-            block, block, send_sem.at[0], recv_sem.at[slot, index], (core, depth)
-        ).wait_recv()
-
-    x_order = list(range(count))
-    y_order = list(range(half, count)) + list(range(half))
-    for step in range(count):
-        send(own(x_order[step]), place, x_order[step], beside_x)
-        send(own(y_order[step]), place, y_order[step], beside_y)
-    stays = []
-    for clip in range(clips):
-        copy = pltpu.make_async_copy(
-            own_ref.at[clip], all_ref.at[clip, place], local_sem.at[clip]
-        )
-        copy.start()
-        stays.append(copy)
-    for index in range(count):
-        send(own(index), place, index, core)
-    if beside:
-        next(cond)
-    for step in range(count):
-        x_index, y_index = x_order[step], y_order[step]
-        arrived(beside_x, x_index)
-        if x_index < half:
-            send(view(beside_x, x_index), beside_x, x_index, beside_y)
-        send(view(beside_x, x_index), beside_x, x_index, core)
-        arrived(beside_y, y_index)
-        if y_index >= half:
-            send(view(beside_y, y_index), beside_y, y_index, beside_x)
-        send(view(beside_y, y_index), beside_y, y_index, core)
-    for step in range(half):
-        for index in (x_order[step], y_order[step]):
-            arrived(across, index)
-            send(view(across, index), across, index, core)
-    for slot in (core, flip(3), flip(5), flip(7)):
-        for index in range(count):
-            arrived(slot, index)
-    if beside:
-        next(cond)
-    for copy in stays:
-        copy.wait()
-    for copy in sends:
-        copy.wait_send()
-
-
-def plane_gather(own_rows, collective_id, picked=None, sub=64):
-    clips, rows, wide = own_rows.shape
-    count = clips * (rows // sub)
-    whole = jax.ShapeDtypeStruct((clips, 8, rows, wide), own_rows.dtype)
-    scratch = [DMA((7 * count,)), DMA((8, count)), DMA((clips,))]
-    if picked is None:
-        return pl.pallas_call(
-            functools.partial(gather_body, clips, rows, sub, None),
-            out_shape=whole,
-            in_specs=[any_spec()],
-            out_specs=any_spec(),
-            scratch_shapes=scratch,
-            compiler_params=communicating(collective_id),
-        )(own_rows)
-    planes, per, tokens, cond_wide = picked.shape
-    group = planes * per
-    inside = pl.BlockSpec(memory_space=pltpu.VMEM)
-    return pl.pallas_call(
-        functools.partial(gather_body, clips, rows, sub, (group, planes)),
-        out_shape=[
-            whole,
-            jax.ShapeDtypeStruct((group, per, tokens, cond_wide), picked.dtype),
-        ],
-        in_specs=[any_spec(), inside],
-        out_specs=[any_spec(), inside],
-        scratch_shapes=scratch
-        + [
-            pltpu.VMEM(picked.shape, picked.dtype),
-            pltpu.VMEM(picked.shape[1:], picked.dtype),
-            DMA((planes,)),
-            DMA((planes,)),
-            DMA((group,)),
-            DMA((group,)),
-        ],
-        compiler_params=communicating(collective_id),
-    )(own_rows, picked)
-
-
-def reduce_body(
-    clips, rows, sub, beside, part_ref, *refs
-):
-    if beside:
-        kept_ref, sum_ref, own_ref, mid, *refs = refs
-    else:
-        sum_ref, *refs = refs
-    pair, held, turn, from_x, from_y, send_sem, core_sem, turn_sem, x_sem, y_sem, *sems = refs
-    place, depth, flip = plane_places()
-    core, beside_x, beside_y = flip(1), flip(2), flip(4)
-    if beside:
-        greet_cross(*beside)
-        going = outward_steps(*beside, kept_ref, own_ref, mid, *sems)
-        next(going)
-    else:
-        greet([(core, depth), (beside_x, depth), (beside_y, depth)])
-    chunks = [(clip, part) for clip in range(clips) for part in range(rows // sub)]
-    count = len(chunks)
-    half = count // 2
-    sends = []
-
-    def send(source, goal, recv_sem, device):
-        copy = remote(source, goal, send_sem.at[len(sends)], recv_sem, (device, depth))
-        copy.start()
-        sends.append(copy)
-
-    def arrived(block, recv_sem):
-        remote(block, block, send_sem.at[0], recv_sem, (core, depth)).wait_recv()
-
-    def term(slot, index):
-        clip, part = chunks[index]
-        return part_ref.at[clip, slot, pl.ds(part * sub, sub)]
-
-    for chip in (3, 1, 2, 0):
-        for index in range(count):
-            send(
-                term(flip((2 * chip) ^ 1), index),
-                pair.at[index, chip],
-                core_sem.at[index, chip],
-                core,
-            )
-
-    def total(*blocks):
-        return sum(block[...].astype(jnp.float32) for block in blocks)
-
-    def combine(chip, index):
-        arrived(pair.at[index, chip], core_sem.at[index, chip])
-        held[index, chip] = total(term(flip(2 * chip), index), pair.at[index, chip]).astype(
-            held.dtype
-        )
-
-    for low in range(half):
-        high = half + low
-        combine(3, low)
-        send(held.at[low, 3], turn.at[low], turn_sem.at[low], beside_x)
-        combine(3, high)
-        send(held.at[high, 3], turn.at[high], turn_sem.at[high], beside_y)
-    for low in range(half):
-        high = half + low
-        combine(1, low)
-        send(held.at[low, 1], from_x.at[low], x_sem.at[low], beside_x)
-        combine(2, high)
-        send(held.at[high, 2], from_y.at[high], y_sem.at[high], beside_y)
-    if beside:
-        next(going)
-    for low in range(half):
-        high = half + low
-        combine(2, low)
-        arrived(turn.at[low], turn_sem.at[low])
-        held[low, 2] = total(held.at[low, 2], turn.at[low]).astype(held.dtype)
-        send(held.at[low, 2], from_y.at[low], y_sem.at[low], beside_y)
-        combine(1, high)
-        arrived(turn.at[high], turn_sem.at[high])
-        held[high, 1] = total(held.at[high, 1], turn.at[high]).astype(held.dtype)
-        send(held.at[high, 1], from_x.at[high], x_sem.at[high], beside_x)
-    for index in range(count):
-        clip, part = chunks[index]
-        arrived(pair.at[index, 0], core_sem.at[index, 0])
-        arrived(from_x.at[index], x_sem.at[index])
-        arrived(from_y.at[index], y_sem.at[index])
-        sum_ref[clip, pl.ds(part * sub, sub)] = total(
-            term(place, index), pair.at[index, 0], from_x.at[index], from_y.at[index]
-        )
-    if beside:
-        next(going)
-    for copy in sends:
-        copy.wait_send()
-
-
-def plane_reduce(terms, collective_id, kept_rows=None, sub=64):
-    clips, _, rows, wide = terms.shape
-    count = clips * (rows // sub)
-    kind = terms.dtype
-    sums = jax.ShapeDtypeStruct((clips, rows, wide), jnp.float32)
-    whole = pl.BlockSpec(memory_space=pltpu.VMEM)
-    scratch = [
-        pltpu.VMEM((count, 4, sub, wide), kind),
-        pltpu.VMEM((count, 4, sub, wide), kind),
-        pltpu.VMEM((count, sub, wide), kind),
-        pltpu.VMEM((count, sub, wide), kind),
-        pltpu.VMEM((count, sub, wide), kind),
-        DMA((7 * count,)),
-        DMA((count, 4)),
-        DMA((count,)),
-        DMA((count,)),
-        DMA((count,)),
-    ]
-    if kept_rows is None:
-        return pl.pallas_call(
-            functools.partial(reduce_body, clips, rows, sub, None),
-            out_shape=sums,
-            in_specs=[whole],
-            out_specs=whole,
-            scratch_shapes=scratch,
-            compiler_params=communicating(collective_id),
-        )(terms)
-    per, planes, piece, _ = kept_rows.shape
-    group = per * planes
-    moved = jax.ShapeDtypeStruct((group, piece, wide), kept_rows.dtype)
-    total, own, _ = pl.pallas_call(
-        functools.partial(reduce_body, clips, rows, sub, (group, planes)),
-        out_shape=[sums, moved, moved],
-        in_specs=[whole, any_spec()],
-        out_specs=[whole, any_spec(), any_spec()],
-        scratch_shapes=scratch + outward_scratch(group, planes),
-        compiler_params=communicating(collective_id),
-    )(terms, kept_rows)
-    return total, own
-
-
 def greet_cross(group, planes):
     place, depth, flip = plane_places()
     greet(
@@ -996,12 +745,15 @@
     own_ref,
     norm_ref,
     pack_ref,
-    cut_ref,
+    first_cut_ref,
+    rest_cut_ref,
     kept_ref,
+    gains_ref,
+    packs_ref,
+    first_mine_ref,
+    rest_mine_ref,
+    mid,
     norms_ref,
-    packs_ref,
-    mine_ref,
-    mid,
     *sems,
 ):
     (
@@ -1059,22 +811,28 @@
     stays = [
         pltpu.make_async_copy(norm_ref, norms_ref.at[here], stay_sem.at[0]),
         pltpu.make_async_copy(pack_ref, packs_ref.at[place], stay_sem.at[1]),
-        pltpu.make_async_copy(cut_ref.at[place], mine_ref.at[place], stay_sem.at[2]),
+        pltpu.make_async_copy(
+            first_cut_ref.at[place], first_mine_ref.at[place], stay_sem.at[2]
+        ),
+        pltpu.make_async_copy(rest_cut_ref.at[place], rest_mine_ref.at[place], stay_sem.at[3]),
     ]
     for stay in stays:
         stay.start()
     cuts = []
-    for mask in (6, 7, 2, 3, 4, 5, 1):
-        other = flip(mask)
-        copy = remote(
-            cut_ref.at[other],
-            mine_ref.at[place],
-            cut_send.at[mask],
-            cut_recv.at[mask],
-            (other, depth),
-        )
-        copy.start()
-        cuts.append(copy)
+    for which, (cut_ref, mine_ref) in enumerate(
+        ((first_cut_ref, first_mine_ref), (rest_cut_ref, rest_mine_ref))
+    ):
+        for mask in (6, 7, 2, 3, 4, 5, 1):
+            other = flip(mask)
+            copy = remote(
+                cut_ref.at[other],
+                mine_ref.at[place],
+                cut_send.at[which, mask],
+                cut_recv.at[which, mask],
+                (other, depth),
+            )
+            copy.start()
+            cuts.append(copy)
     second = []
     arrivals = dict(first)
     for mask in (0, 1, 2, 3, 4, 5, 6, 7):
@@ -1119,6 +877,16 @@
         ).wait_recv()
     for copy in small:
         copy.wait_send()
+    stays[0].wait()
+    width = gains_ref.shape[1] // (group * planes)
+    gains_ref[...] = jnp.concatenate(
+        [
+            norms_ref[owner * planes + plane, :, :width]
+            for plane in range(planes)
+            for owner in range(group)
+        ],
+        axis=1,
+    )
     for mask in range(1, group):
         block = packs_ref.at[flip(mask)]
         remote(
@@ -1131,26 +899,29 @@
         pl.when(goal == depth)(stay.wait)
     for mask, copy in first:
         copy.wait_send()
-    for stay in stays:
+    for stay in stays[1:]:
         stay.wait()
 
 
-def enter(rows_of_clip, norm_block, pack, cut, planes, collective_id):
+def enter(rows_of_clip, norm_block, pack, first_cut, rest_cut, planes, collective_id):
     group, rows, wide = rows_of_clip.shape
     count = group * planes
     like = lambda shape, array: jax.ShapeDtypeStruct(shape, array.dtype)
-    kept, norms, packs, mine, _ = pl.pallas_call(
+    inside = pl.BlockSpec(memory_space=pltpu.VMEM)
+    *results, _ = pl.pallas_call(
         functools.partial(enter_body, group, planes),
         out_shape=[
             like((group // planes, planes, rows, wide), rows_of_clip),
-            like((count,) + norm_block.shape, norm_block),
+            like((norm_block.shape[0], wide), norm_block),
             like((group,) + pack.shape, pack),
-            like(cut.shape, cut),
+            like(first_cut.shape, first_cut),
+            like(rest_cut.shape, rest_cut),
             like((group, rows, wide), rows_of_clip),
         ],
-        in_specs=[any_spec()] * 4,
-        out_specs=[any_spec()] * 5,
+        in_specs=[any_spec(), inside, any_spec(), any_spec(), any_spec()],
+        out_specs=[any_spec(), inside] + [any_spec()] * 4,
         scratch_shapes=[
+            pltpu.VMEM((count,) + norm_block.shape, norm_block.dtype),
             DMA((group,)),
             DMA((group,)),
             DMA((group,)),
@@ -1160,13 +931,13 @@
             DMA((count,)),
             DMA((group,)),
             DMA((group,)),
-            DMA((group,)),
-            DMA((group,)),
-            DMA((3,)),
+            DMA((2, group)),
+            DMA((2, group)),
+            DMA((4,)),
         ],
         compiler_params=communicating(collective_id),
-    )(rows_of_clip, norm_block, pack, cut)
-    return kept, norms, packs, mine
+    )(rows_of_clip, norm_block, pack, first_cut, rest_cut)
+    return results
 
 
 def cond_steps(group, planes, pick_ref, cond_ref, parts, summed, *sems):
@@ -1290,6 +1061,432 @@
     ]
 
 
+def dot_tiles(left, right_ref, transposed, width):
+    count = right_ref.shape[0] if transposed else right_ref.shape[1]
+    for start in range(0, count, width):
+        stop = min(start + width, count)
+        if transposed:
+            yield start, stop, times_transposed(left, right_ref[start:stop, :])
+        else:
+            yield start, stop, jnp.dot(
+                left, right_ref[:, start:stop], preferred_element_type=jnp.float32
+            )
+
+
+def gather_dot_body(clips, rows, sub, normed, mode, beside, own_ref, *refs):
+    refs = list(refs)
+    take = lambda count: [refs.pop(0) for _ in range(count)]
+    gain_ref = take(1)[0] if normed else None
+    mat_ref = take(1)[0] if mode != "rows" else None
+    gates_ref = take(1)[0] if mode == "gates" else None
+    extra_ref = take(1)[0] if beside else None
+    all_ref = take(1)[0]
+    prod_refs = take({"rows": 0, "dot": 1, "gates": 2}[mode])
+    extra_outs = take({"cond": 1, "outward": 2}[beside[0]]) if beside else []
+    held, send_sem, recv_sem, all_sem = take(4)
+    mat, mat_sem = take(2) if mode != "rows" else (None, None)
+    stages = take(len(prod_refs))
+    prod_sem = take(1)[0] if prod_refs else None
+    gates, gates_sem = take(2) if mode == "gates" else (None, None)
+    place, depth, flip = plane_places()
+    core, beside_x, beside_y, across = flip(1), flip(2), flip(4), flip(6)
+    if mode != "rows":
+        load = pltpu.make_async_copy(mat_ref, mat, mat_sem)
+        load.start()
+    slots = [flip(mask) for mask in (0, 1, 2, 4, 3, 5, 6, 7)]
+    gate_loads = {}
+    if mode == "gates":
+        for mask, slot in zip((0, 1, 2, 4, 3, 5, 6, 7), slots):
+            gate_loads[mask] = [
+                pltpu.make_async_copy(
+                    gates_ref.at[clip, slot], gates.at[slot, clip], gates_sem.at[slot, clip]
+                )
+                for clip in range(clips)
+            ]
+            for copy in gate_loads[mask]:
+                copy.start()
+    if beside:
+        greet_cross(*beside[1:])
+        if beside[0] == "cond":
+            going = cond_steps(*beside[1:], extra_ref, extra_outs[0], *refs)
+        else:
+            going = outward_steps(*beside[1:], extra_ref, *extra_outs, *refs)
+        next(going)
+    else:
+        greet([(core, depth), (beside_x, depth), (beside_y, depth)])
+    values = own_ref[...]
+    if normed:
+        values = layer_norm(values, gain_ref[0:1], gain_ref[1:2])
+    held[place] = values.astype(held.dtype)
+    chunks = [(clip, part) for clip in range(clips) for part in range(rows // sub)]
+    count = len(chunks)
+    half = count // 2
+    sends = []
+
+    def view(slot, index):
+        clip, part = chunks[index]
+        return held.at[slot, clip, pl.ds(part * sub, sub)]
+
+    def send(slot, index, device):
+        block = view(slot, index)
+        copy = remote(
+            block, block, send_sem.at[len(sends)], recv_sem.at[slot, index], (device, depth)
+        )
+        copy.start()
+        sends.append(copy)
+
+    def arrived(slot, index):
+        block = view(slot, index)
+        remote(
+            block, block, send_sem.at[0], recv_sem.at[slot, index], (core, depth)
+        ).wait_recv()
+
+    x_order = list(range(count))
+    y_order = list(range(half, count)) + list(range(half))
+    for step in range(count):
+        send(place, x_order[step], beside_x)
+        send(place, y_order[step], beside_y)
+    for index in range(count):
+        send(place, index, core)
+    outs = []
+
+    def leave_here(source, goal, sem, major):
+        for clip in range(clips):
+            there = goal.at[major, clip] if goal.shape[0] == 8 else goal.at[clip, major]
+            copy = pltpu.make_async_copy(source.at[major, clip], there, sem.at[major, clip])
+            copy.start()
+            outs.append(copy)
+
+    def multiply(mask):
+        slot = flip(mask)
+        leave_here(held, all_ref, all_sem, slot)
+        if mode == "rows":
+            return
+        left = held[slot].reshape(clips * rows, held.shape[3])
+        for copy in gate_loads.get(mask, ()):
+            copy.wait()
+        for start, stop, product in dot_tiles(left, mat, False, 256 * (3 if mode == "dot" else 1)):
+            product = product.reshape(clips, rows, stop - start)
+            if mode == "dot":
+                stages[0][slot, :, :, start:stop] = product.astype(stages[0].dtype)
+                continue
+            width = stages[1].shape[3]
+            gate = gates[slot, :, :, start:stop]
+            up = gates[slot, :, :, width + start : width + stop]
+            sigmoid = jax.nn.sigmoid(gate)
+            active = gate * sigmoid
+            low = stages[0].dtype
+            stages[0][slot, :, :, start:stop] = (
+                product * up * sigmoid * (1.0 + gate * (1.0 - sigmoid))
+            ).astype(low)
+            stages[0][slot, :, :, width + start : width + stop] = (product * active).astype(low)
+            stages[1][slot, :, :, start:stop] = (active * up).astype(low)
+        for which, (stage, prod_ref) in enumerate(zip(stages, prod_refs)):
+            leave_here(stage, prod_ref, prod_sem.at[which], slot)
+
+    if mode != "rows":
+        load.wait()
+    multiply(0)
+    if beside:
+        next(going)
+    for step in range(count):
+        x_index, y_index = x_order[step], y_order[step]
+        arrived(beside_x, x_index)
+        if x_index < half:
+            send(beside_x, x_index, beside_y)
+        send(beside_x, x_index, core)
+        arrived(beside_y, y_index)
+        if y_index >= half:
+            send(beside_y, y_index, beside_x)
+        send(beside_y, y_index, core)
+        if step == 0:
+            for index in range(count):
+                arrived(core, index)
+            multiply(1)
+    multiply(2)
+    for step in range(half):
+        for index in (x_order[step], y_order[step]):
+            arrived(across, index)
+            send(across, index, core)
+        if step == 0:
+            multiply(4)
+    for mask in (3, 5):
+        for index in range(count):
+            arrived(flip(mask), index)
+        multiply(mask)
+    multiply(6)
+    for index in range(count):
+        arrived(flip(7), index)
+    multiply(7)
+    if beside:
+        next(going)
+    for copy in outs:
+        copy.wait()
+    for copy in sends:
+        copy.wait_send()
+
+
+def gather_dot(
+    own_rows,
+    matrix,
+    kind,
+    collective_id,
+    gains=None,
+    picked=None,
+    kept_rows=None,
+    gate_up=None,
+    sub=64,
+):
+    clips, rows, wide = own_rows.shape
+    count = clips * (rows // sub)
+    low = jnp.bfloat16
+    mode = "rows" if matrix is None else "dot" if gate_up is None else "gates"
+    inside = pl.BlockSpec(memory_space=pltpu.VMEM)
+    by_clip = lambda columns, of: jax.ShapeDtypeStruct((clips, 8, rows, columns), of)
+    by_device = lambda columns, of: jax.ShapeDtypeStruct((8, clips, rows, columns), of)
+    args, in_specs = [own_rows], [inside]
+    if gains is not None:
+        args.append(gains)
+        in_specs.append(inside)
+    outs = [by_device(wide, low) if mode == "gates" else by_clip(wide, low)]
+    scratch = [
+        pltpu.VMEM((8, clips, rows, wide), low),
+        DMA((7 * count,)),
+        DMA((8, count)),
+        DMA((8, clips)),
+    ]
+    if mode != "rows":
+        columns = matrix.shape[1]
+        args.append(matrix)
+        in_specs.append(any_spec())
+        scratch += [pltpu.VMEM(matrix.shape, low), DMA(())]
+    if mode == "dot":
+        outs.append(by_clip(columns, kind))
+        scratch += [pltpu.VMEM((8, clips, rows, columns), kind), DMA((1, 8, clips))]
+    if mode == "gates":
+        args.append(gate_up.reshape(clips, 8, rows, 2 * columns))
+        in_specs.append(any_spec())
+        outs += [by_clip(2 * columns, low), by_device(columns, low)]
+        scratch += [
+            pltpu.VMEM((8, clips, rows, 2 * columns), low),
+            pltpu.VMEM((8, clips, rows, columns), low),
+            DMA((2, 8, clips)),
+            pltpu.VMEM((8, clips, rows, 2 * columns), jnp.float32),
+            DMA((8, clips)),
+        ]
+    out_specs = [any_spec()] * len(outs)
+    mains = len(outs)
+    beside = None
+    if picked is not None:
+        planes, per, tokens, cond_wide = picked.shape
+        beside = ("cond", planes * per, planes)
+        args.append(picked)
+        in_specs.append(inside)
+        outs.append(jax.ShapeDtypeStruct((8, per, tokens, cond_wide), picked.dtype))
+        out_specs.append(inside)
+        scratch += [
+            pltpu.VMEM(picked.shape, picked.dtype),
+            pltpu.VMEM(picked.shape[1:], picked.dtype),
+            DMA((planes,)),
+            DMA((planes,)),
+            DMA((8,)),
+            DMA((8,)),
+        ]
+    if kept_rows is not None:
+        per, planes, piece, _ = kept_rows.shape
+        beside = ("outward", planes * per, planes)
+        args.append(kept_rows)
+        in_specs.append(any_spec())
+        outs += [jax.ShapeDtypeStruct((per * planes, piece, wide), kept_rows.dtype)] * 2
+        out_specs += [any_spec()] * 2
+        scratch += outward_scratch(*beside[1:])
+    results = pl.pallas_call(
+        functools.partial(
+            gather_dot_body, clips, rows, sub, gains is not None, mode, beside
+        ),
+        out_shape=outs,
+        in_specs=in_specs,
+        out_specs=out_specs,
+        scratch_shapes=scratch,
+        compiler_params=communicating(collective_id),
+    )(*args)
+    flat = [block.reshape(clips * 8 * rows, block.shape[3]) for block in results[:mains]]
+    return flat + list(results[mains : mains + 1])
+
+
+def dot_reduce_body(clips, rows, sub, added, beside, left_ref, mat_ref, *refs):
+    refs = list(refs)
+    base_ref = refs.pop(0) if added else None
+    kept_ref = refs.pop(0) if beside else None
+    sum_ref = refs.pop(0)
+    own_ref, mid = (refs.pop(0), refs.pop(0)) if beside else (None, None)
+    left, mat, terms, pair, held, turn, from_x, from_y, *sems = refs
+    mat_sem, left_sem, send_sem, core_sem, turn_sem, x_sem, y_sem, *extra = sems
+    place, depth, flip = plane_places()
+    core, beside_x, beside_y = flip(1), flip(2), flip(4)
+    order = [flip(mask) for mask in (7, 6, 3, 2, 5, 4, 1, 0)]
+    load = pltpu.make_async_copy(mat_ref, mat, mat_sem)
+    load.start()
+    loads = {}
+    for number, slot in enumerate(order):
+        loads[number] = [
+            pltpu.make_async_copy(
+                left_ref.at[clip, slot], left.at[number, clip], left_sem.at[number, clip]
+            )
+            for clip in range(clips)
+        ]
+        for copy in loads[number]:
+            copy.start()
+    if beside:
+        greet_cross(*beside)
+        going = outward_steps(*beside, kept_ref, own_ref, mid, *extra)
+        next(going)
+    else:
+        greet([(core, depth), (beside_x, depth), (beside_y, depth)])
+    chunks = [(clip, part) for clip in range(clips) for part in range(rows // sub)]
+    count = len(chunks)
+    half = count // 2
+    sends = []
+
+    def send(source, goal, recv_sem, device):
+        copy = remote(source, goal, send_sem.at[len(sends)], recv_sem, (device, depth))
+        copy.start()
+        sends.append(copy)
+
+    def arrived(block, recv_sem):
+        remote(block, block, send_sem.at[0], recv_sem, (core, depth)).wait_recv()
+
+    def term(number, index):
+        clip, part = chunks[index]
+        return terms.at[number, clip, pl.ds(part * sub, sub)]
+
+    def multiply(number):
+        for copy in loads[number]:
+            copy.wait()
+        block = left[number].reshape(clips * rows, left.shape[3])
+        for start, stop, product in dot_tiles(block, mat, True, 256 * 2):
+            terms[number, :, :, start:stop] = product.astype(terms.dtype).reshape(
+                clips, rows, stop - start
+            )
+
+    def give(number, chip):
+        for index in range(count):
+            send(term(number, index), pair.at[index, chip], core_sem.at[index, chip], core)
+
+    def total(*blocks):
+        return sum(block[...].astype(jnp.float32) for block in blocks)
+
+    numbers = {3: 1, 1: 3, 2: 5, 0: 7}
+
+    def combine(chip, index):
+        arrived(pair.at[index, chip], core_sem.at[index, chip])
+        held[index, chip] = total(term(numbers[chip], index), pair.at[index, chip]).astype(
+            held.dtype
+        )
+
+    load.wait()
+    multiply(0)
+    give(0, 3)
+    multiply(1)
+    multiply(2)
+    give(2, 1)
+    for low in range(half):
+        high = half + low
+        combine(3, low)
+        send(held.at[low, 3], turn.at[low], turn_sem.at[low], beside_x)
+        combine(3, high)
+        send(held.at[high, 3], turn.at[high], turn_sem.at[high], beside_y)
+    multiply(3)
+    multiply(4)
+    give(4, 2)
+    for low in range(half):
+        combine(1, low)
+        send(held.at[low, 1], from_x.at[low], x_sem.at[low], beside_x)
+    multiply(5)
+    for high in range(half, count):
+        combine(2, high)
+        send(held.at[high, 2], from_y.at[high], y_sem.at[high], beside_y)
+    multiply(6)
+    give(6, 0)
+    if beside:
+        next(going)
+    for low in range(half):
+        high = half + low
+        combine(2, low)
+        arrived(turn.at[low], turn_sem.at[low])
+        held[low, 2] = total(held.at[low, 2], turn.at[low]).astype(held.dtype)
+        send(held.at[low, 2], from_y.at[low], y_sem.at[low], beside_y)
+        combine(1, high)
+        arrived(turn.at[high], turn_sem.at[high])
+        held[high, 1] = total(held.at[high, 1], turn.at[high]).astype(held.dtype)
+        send(held.at[high, 1], from_x.at[high], x_sem.at[high], beside_x)
+    multiply(7)
+    for index in range(count):
+        clip, part = chunks[index]
+        span = pl.ds(part * sub, sub)
+        arrived(pair.at[index, 0], core_sem.at[index, 0])
+        arrived(from_x.at[index], x_sem.at[index])
+        arrived(from_y.at[index], y_sem.at[index])
+        result = total(term(7, index), pair.at[index, 0], from_x.at[index], from_y.at[index])
+        if added:
+            result = base_ref[clip, span] + result
+        sum_ref[clip, span] = result
+    if beside:
+        next(going)
+    for copy in sends:
+        copy.wait_send()
+
+
+def dot_reduce(left, matrix, clips, collective_id, base=None, kept_rows=None, sub=64):
+    wide, inner = matrix.shape
+    rows = left.shape[0] // (8 * clips)
+    count = clips * (rows // sub)
+    low = jnp.bfloat16
+    inside = pl.BlockSpec(memory_space=pltpu.VMEM)
+    args = [left.reshape(clips, 8, rows, inner), matrix]
+    in_specs = [any_spec(), any_spec()]
+    outs, out_specs = [jax.ShapeDtypeStruct((clips, rows, wide), jnp.float32)], [inside]
+    scratch = [
+        pltpu.VMEM((8, clips, rows, inner), low),
+        pltpu.VMEM(matrix.shape, low),
+        pltpu.VMEM((8, clips, rows, wide), low),
+        pltpu.VMEM((count, 4, sub, wide), low),
+        pltpu.VMEM((count, 4, sub, wide), low),
+        pltpu.VMEM((count, sub, wide), low),
+        pltpu.VMEM((count, sub, wide), low),
+        pltpu.VMEM((count, sub, wide), low),
+        DMA(()),
+        DMA((8, clips)),
+        DMA((7 * count,)),
+        DMA((count, 4)),
+        DMA((count,)),
+        DMA((count,)),
+        DMA((count,)),
+    ]
+    if base is not None:
+        args.append(base)
+        in_specs.append(inside)
+    beside = None
+    if kept_rows is not None:
+        per, planes, piece, _ = kept_rows.shape
+        beside = (per * planes, planes)
+        args.append(kept_rows)
+        in_specs.append(any_spec())
+        moved = jax.ShapeDtypeStruct((per * planes, piece, wide), kept_rows.dtype)
+        outs += [moved, moved]
+        out_specs += [any_spec(), any_spec()]
+        scratch += outward_scratch(*beside)
+    results = pl.pallas_call(
+        functools.partial(dot_reduce_body, clips, rows, sub, base is not None, beside),
+        out_shape=outs,
+        in_specs=in_specs,
+        out_specs=out_specs,
+        scratch_shapes=scratch,
+        compiler_params=communicating(collective_id),
+    )(*args)
+    return results[0] if kept_rows is None else results[:2]
+
+
 def finish_body(planes, squares_ref, total_ref, blocks, block_send, block_recv):
     place, depth, flip = plane_places()
     devices = [(flip(mask), lax.rem(depth + step, planes)) for mask, step in everyone(planes)]
@@ -1353,55 +1550,82 @@
     return values * cosine + other * sine
 
 
-def swap_beside(cut_ref, mine_ref, *sems):
+def swap_beside(pairs, send_sem, recv_sem, local_sem):
     place, depth, flip = plane_places()
 
     def each(act):
-        for mask in (6, 7, 2, 3, 4, 5, 1):
-            other = flip(mask)
-            act(
-                remote(
-                    cut_ref.at[other],
-                    mine_ref.at[place],
-                    sems[0].at[mask],
-                    sems[1].at[mask],
-                    (other, depth),
+        for which, (source, goal) in enumerate(pairs):
+            for mask in (6, 7, 2, 3, 4, 5, 1):
+                other = flip(mask)
+                act(
+                    remote(
+                        source(other),
+                        goal(place),
+                        send_sem.at[which, mask],
+                        recv_sem.at[which, mask],
+                        (other, depth),
+                    )
                 )
-            )
-
-    stay = pltpu.make_async_copy(cut_ref.at[place], mine_ref.at[place], sems[2])
+
+    stays = [
+        pltpu.make_async_copy(source(place), goal(place), local_sem.at[which])
+        for which, (source, goal) in enumerate(pairs)
+    ]
 
     def begin():
         each(lambda copy: copy.start())
-        stay.start()
+        for stay in stays:
+            stay.start()
 
     def end():
         each(lambda copy: copy.wait())
-        stay.wait()
+        for stay in stays:
+            stay.wait()
 
     return begin, end
+
+
+def swap_beside_scratch(count):
+    return [DMA((count, 8)), DMA((count, 8)), DMA((count,))]
 
 
 def flash_forward_body(
     heads,
     tile,
-    raw_ref,
+    normed_ref,
+    mat_ref,
     stamp_ref,
     bias_ref,
     rotary_ref,
-    cut_ref,
+    ff_ref,
     own_ref,
     turned_ref,
     out_ref,
     lse_ref,
-    mine_ref,
+    gate_up_ref,
+    down_ref,
     kept_ref,
     mid,
+    raw_ref,
     *sems,
 ):
-    group, planes = cut_ref.shape[0], kept_ref.shape[1]
+    group, planes = gate_up_ref.shape[0], kept_ref.shape[1]
+    hidden = down_ref.shape[2]
     step, last = pl.program_id(0), pl.num_programs(0) - 1
-    start_swap, end_swap = swap_beside(cut_ref, mine_ref, *sems[:3])
+
+    def columns(block):
+        return lambda other: ff_ref.at[
+            :, pl.ds(pl.multiple_of((block * group + other) * hidden, 128), hidden)
+        ]
+
+    start_swap, end_swap = swap_beside(
+        [
+            (columns(0), lambda other: gate_up_ref.at[other, :, pl.ds(0, hidden)]),
+            (columns(1), lambda other: gate_up_ref.at[other, :, pl.ds(hidden, hidden)]),
+            (columns(2), lambda other: down_ref.at[other]),
+        ],
+        *sems[:3],
+    )
     start_rows, pass_rows, end_rows = inward_beside(
         group, planes, own_ref, kept_ref, mid, *sems[3:]
     )
@@ -1416,6 +1640,14 @@
     def _():
         pass_rows()
 
+    def project(index, carry):
+        place = pl.ds(pl.multiple_of(index * tile, tile), tile)
+        raw_ref[place, :] = jnp.dot(
+            normed_ref[place, :], mat_ref[...], preferred_element_type=jnp.float32
+        )
+        return carry
+
+    lax.fori_loop(0, raw_ref.shape[0] // tile, project, 0)
     wide = heads * HDIM
     for pair in range(2 * wide // 128):
         lanes = slice(pair * 128, pair * 128 + 128)
@@ -1460,36 +1692,42 @@
         end_rows()
 
 
-def flash_forward(raw, stamps, bias, rotary, heads, cut, rows_of_clip, collective_id):
+def flash_forward(normed, matrix, stamps, bias, rotary, heads, ff_low, rows_of_clip, collective_id):
     clips, rows = bias.shape
     wide = heads * HDIM
     group, piece, features = rows_of_clip.shape
     planes = group // clips
-    like = lambda shape: jax.ShapeDtypeStruct(shape, rows_of_clip.dtype)
+    owned, columns = ff_low.shape
+    hidden = columns // (3 * group)
+    like = lambda *shape: jax.ShapeDtypeStruct(shape, rows_of_clip.dtype)
     blocked = lambda lanes: pl.BlockSpec((rows, lanes), lambda clip: (clip, 0))
     *results, _ = pl.pallas_call(
         functools.partial(flash_forward_body, heads, rows // 4),
         grid=(clips,),
         out_shape=[
-            jax.ShapeDtypeStruct((clips * rows, 3 * wide), jnp.bfloat16),
-            jax.ShapeDtypeStruct((clips * rows, wide), jnp.bfloat16),
+            like(clips * rows, 3 * wide),
+            like(clips * rows, wide),
             jax.ShapeDtypeStruct((clips * rows, 128), jnp.float32),
-            like(cut.shape),
-            like((clips, planes, piece, features)),
-            like(rows_of_clip.shape),
+            like(group, owned, 2 * hidden),
+            like(group, owned, hidden),
+            like(clips, planes, piece, features),
+            like(group, piece, features),
         ],
         in_specs=[
-            blocked(3 * wide),
+            blocked(features),
+            pl.BlockSpec(matrix.shape, lambda clip: (0, 0)),
             pl.BlockSpec((1, 1, 2 * wide), lambda clip: (clip, 0, 0)),
             pl.BlockSpec((1, 1, rows), lambda clip: (clip, 0, 0)),
             pl.BlockSpec((2, rows, 128), lambda clip: (0, 0, 0)),
             any_spec(),
             any_spec(),
         ],
-        out_specs=[blocked(3 * wide), blocked(wide), blocked(128)] + [any_spec()] * 3,
-        scratch_shapes=swap_scratch() + inward_scratch(group, planes),
+        out_specs=[blocked(3 * wide), blocked(wide), blocked(128)] + [any_spec()] * 4,
+        scratch_shapes=[pltpu.VMEM((rows, 3 * wide), jnp.float32)]
+        + swap_beside_scratch(3)
+        + inward_scratch(group, planes),
         compiler_params=communicating(collective_id),
-    )(raw, stamps[:, None], bias[:, None], rotary, cut, rows_of_clip)
+    )(normed, matrix, stamps[:, None], bias[:, None], rotary, ff_low, rows_of_clip)
     return results
 
 
@@ -1512,7 +1750,9 @@
     *sems,
 ):
     place, depth, flip = plane_places()
-    start_swap, end_swap = swap_beside(cut_ref, mine_ref, *sems)
+    start_swap, end_swap = swap_beside(
+        [(lambda other: cut_ref.at[other], lambda other: mine_ref.at[other])], *sems
+    )
 
     @pl.when(pl.program_id(0) == 0)
     def _():
@@ -1603,7 +1843,7 @@
             pl.BlockSpec((1, 1, 2 * wide), lambda clip: (clip, 0, 0)),
             any_spec(),
         ],
-        scratch_shapes=[pltpu.VMEM((rows, wide), jnp.float32)] * 3 + swap_scratch(),
+        scratch_shapes=[pltpu.VMEM((rows, wide), jnp.float32)] * 3 + swap_beside_scratch(1),
         compiler_params=communicating(collective_id),
     )(turned, grad, lse, stamps[:, None], bias[:, :, None], rotary, cut)
     return grads, stamp_grads[:, 0], mine
@@ -1746,31 +1986,28 @@
         ],
         axis=0,
     )
-    stream, norm_all, packs, attn_mine = enter(
+    stream, gain_rows, packs, qkv_mine, rest_mine = enter(
         to_plane_order(frames[0]).reshape(group, piece, wide),
         norm_block,
         pack,
-        jnp.concatenate([attn_cut, cross_cut], axis=2),
+        attn_cut[:, :, : 3 * head_wide],
+        jnp.concatenate([attn_cut[:, :, 3 * head_wide :], cross_cut], axis=2),
         planes,
         1,
     )
     stream = stream.reshape(clips, own_rows, wide).astype(jnp.float32)
-    ff_low = ff_weight.astype(jnp.bfloat16).reshape(owned, 3, group, ff_wide)
-    ff_cut = ff_low.transpose(2, 0, 1, 3).reshape(group, owned, 3 * ff_wide)
+    ff_low = ff_weight.astype(jnp.bfloat16)
 
     def over_planes(block):
         return lax.all_gather(block.reshape(group * owned, -1), "seq", axis=0, tiled=True)
 
-    w_qkv = over_planes(attn_mine[:, :, : 3 * head_wide])
-    w_rest = over_planes(attn_mine[:, :, 3 * head_wide :])
+    w_qkv = over_planes(qkv_mine)
+    w_rest = over_planes(rest_mine)
     w_self_out = w_rest[:, :head_wide]
     w_cross_query = w_rest[:, head_wide : 2 * head_wide]
     w_cross_out = w_rest[:, 2 * head_wide : 3 * head_wide]
     w_cond = w_rest[:, 3 * head_wide :].reshape(planes, group, cond_owned, -1)
     w_cond = jnp.swapaxes(w_cond, 0, 1).reshape(cond_wide, 2 * head_wide)
-    norm_all = norm_all.reshape(group, planes, 8, 128)[:, :, :6, :owned].transpose(2, 1, 0, 3)
-    gain_rows = norm_all.reshape(6, wide)
-
     plane_packs = lax.dynamic_slice_in_dim(packs, depth * clips, clips, axis=0)
     stamps = to_plane_order(plane_packs[:, 0].astype(jnp.bfloat16)).astype(jnp.float32)
     cond_keep = plane_packs[:, 2, :cond_count] > 0
@@ -1795,42 +2032,33 @@
     key_keep = true_place[None, :] < clip_lengths[:, None]
     group_shape = (clips, seq_frames, heads, HDIM)
 
-    def collect(rows, collective_id):
-        return plane_gather(rows, collective_id).reshape(group_rows, wide)
-
-    def spread(partial_value, collective_id):
-        terms = partial_value.astype(jnp.bfloat16).reshape(clips, group, own_rows, wide)
-        return plane_reduce(terms, collective_id)
-
-    normed_one = layer_norm(stream, gain_rows[0], gain_rows[1]).astype(jnp.bfloat16)
-    group_one, cond = plane_gather(normed_one, 5, picked)
-    group_one = group_one.reshape(group_rows, wide)
+    group_one, cond = gather_dot(stream, None, None, 5, gain_rows[0:2], picked)
     cond_flat = cond.swapaxes(0, 1).reshape(clips * cond_count, cond_wide)
-    projected = jnp.dot(group_one, w_qkv, preferred_element_type=jnp.float32)
     stamp_normed = layer_norm(stamps, gain_rows[0], gain_rows[1]).astype(jnp.bfloat16)
     stamp_pair = jnp.dot(stamp_normed, w_qkv[:, head_wide:], preferred_element_type=jnp.float32)
     stamp_pair = stamp_pair.astype(jnp.bfloat16)
     rotary = rotary_lanes(true_place)
     key_bias = jnp.where(key_keep, 0.0, masked_score)
-    rotated, self_low, self_lse, ff_mine, grad_out_low = flash_forward(
-        projected,
+    rotated, self_low, self_lse, gate_up_mine, down_mine, grad_out_low = flash_forward(
+        group_one,
+        w_qkv,
         stamp_pair,
         key_bias,
         rotary,
         heads,
-        ff_cut,
+        ff_low,
         masked.reshape(group, piece, wide),
         2,
     )
     grad_out_low = grad_out_low.reshape(clips, own_rows, wide)
     grad_out = grad_out_low.astype(jnp.float32)
-    w_gate_up = over_planes(ff_mine[:, :, : 2 * ff_wide])
-    w_down = over_planes(ff_mine[:, :, 2 * ff_wide :])
-    resid_one = stream + spread(times_transposed(self_low, w_self_out), 6)
-    normed_two = layer_norm(resid_one, gain_rows[2], gain_rows[3]).astype(jnp.bfloat16)
-    group_two = collect(normed_two, 7)
-    cross_query = jnp.dot(group_two, w_cross_query, preferred_element_type=jnp.float32)
-    cross_query = cross_query.astype(jnp.bfloat16).reshape(group_shape)
+    w_gate_up = over_planes(gate_up_mine)
+    w_down = over_planes(down_mine)
+    resid_one = dot_reduce(self_low, w_self_out, clips, 6, stream)
+    group_two, cross_query = gather_dot(
+        resid_one, w_cross_query, jnp.bfloat16, 7, gain_rows[2:4]
+    )
+    cross_query = cross_query.reshape(group_shape)
     cond_pair = jnp.dot(cond_flat, w_cond, preferred_element_type=jnp.float32)
     cond_pair = cond_pair.astype(jnp.bfloat16)
     cond_shape = (clips, cond_count, heads, HDIM)
@@ -1838,29 +2066,21 @@
     cross_values = cond_pair[:, head_wide:].reshape(cond_shape)
     cross_mixed, cross_lse = cross_forward(cross_query, cross_keys, cross_values, cond_keep)
     cross_out = cross_mixed.astype(jnp.bfloat16).reshape(group_rows, head_wide)
-    resid_two = resid_one + spread(times_transposed(cross_out, w_cross_out), 8)
-    normed_three = layer_norm(resid_two, gain_rows[4], gain_rows[5]).astype(jnp.bfloat16)
-    group_three = collect(normed_three, 9)
-    gate_up = jnp.dot(group_three, w_gate_up, preferred_element_type=jnp.float32)
+    resid_two = dot_reduce(cross_out, w_cross_out, clips, 8, resid_one)
+    group_three, gate_up = gather_dot(resid_two, w_gate_up, jnp.float32, 9, gain_rows[4:6])
     gate_up, grad_out_low = lax.optimization_barrier((gate_up, grad_out_low))
-    group_grad_out = collect(grad_out_low, 10)
-    gate_val, up_val = gate_up[:, :ff_wide], gate_up[:, ff_wide:]
-    hidden = (jax.nn.silu(gate_val) * up_val).astype(jnp.bfloat16)
+    group_grad_out, grad_gate_up, hidden = gather_dot(
+        grad_out_low, w_down, None, 10, gate_up=gate_up
+    )
     branch = lax.psum_scatter(
         times_transposed(hidden, w_down)
         .astype(jnp.bfloat16)
-        .reshape(clips, group, own_rows, wide),
+        .reshape(group, clips, own_rows, wide),
         "dp",
-        scatter_dimension=1,
+        scatter_dimension=0,
         tiled=False,
     )
     layer_rows = (resid_two + branch.astype(jnp.float32)).astype(jnp.bfloat16)
-
-    grad_hidden = jnp.dot(group_grad_out, w_down, preferred_element_type=jnp.float32)
-    sigmoid_gate = jax.nn.sigmoid(gate_val)
-    grad_gate = grad_hidden * up_val * sigmoid_gate * (1.0 + gate_val * (1.0 - sigmoid_gate))
-    grad_up = grad_hidden * gate_val * sigmoid_gate
-    grad_gate_up = jnp.concatenate([grad_gate, grad_up], axis=1).astype(jnp.bfloat16)
 
     def over_rows(block):
         return lax.psum_scatter(
@@ -1870,32 +2090,32 @@
     ff_piece = ff_outer(group_three, grad_gate_up, group_grad_out, hidden)
     grad_gate_up, ff_piece = lax.optimization_barrier((grad_gate_up, ff_piece))
     ff_rows = over_rows(ff_piece)
-    grad_normed_three = spread(times_transposed(grad_gate_up, w_gate_up), 13)
+    grad_normed_three = dot_reduce(grad_gate_up, w_gate_up, clips, 13)
 
     _, norm_three_back = jax.vjp(layer_norm, resid_two, gain_rows[4], gain_rows[5])
     grad_two_part, grad_gain_three, grad_bias_three = norm_three_back(grad_normed_three)
     grad_two = grad_out + grad_two_part
-    group_cross_branch = collect(grad_two.astype(jnp.bfloat16), 15)
-    grad_cross_mixed = jnp.dot(group_cross_branch, w_cross_out, preferred_element_type=jnp.float32)
-    grad_cross_mixed = grad_cross_mixed.astype(jnp.bfloat16).reshape(group_shape)
+    group_cross_branch, grad_cross_mixed = gather_dot(
+        grad_two.astype(jnp.bfloat16), w_cross_out, jnp.bfloat16, 15
+    )
+    grad_cross_mixed = grad_cross_mixed.reshape(group_shape)
     grad_cross_query, grad_cross_keys, grad_cross_values = cross_backward(
         cross_query, cross_keys, cross_values, cond_keep, cross_lse, grad_cross_mixed
     )
     grad_cross_query = grad_cross_query.astype(jnp.bfloat16).reshape(group_rows, head_wide)
-    terms_two = times_transposed(grad_cross_query, w_cross_query).astype(jnp.bfloat16)
-    grad_normed_two, layer_out = plane_reduce(
-        terms_two.reshape(clips, group, own_rows, wide),
-        16,
-        layer_rows.reshape(clips, planes, piece, wide),
-    )
-    layer_out = to_whole_order(layer_out.reshape(frame_rows, wide)).astype(jnp.bfloat16)
-    layer_out = layer_out.reshape(frames.shape)
+    grad_normed_two = dot_reduce(grad_cross_query, w_cross_query, clips, 16)
     _, norm_two_back = jax.vjp(layer_norm, resid_one, gain_rows[2], gain_rows[3])
     grad_one_part, grad_gain_two, grad_bias_two = norm_two_back(grad_normed_two)
     grad_one = grad_two + grad_one_part
-    group_self_branch = collect(grad_one.astype(jnp.bfloat16), 17)
-    grad_self_mixed = jnp.dot(group_self_branch, w_self_out, preferred_element_type=jnp.float32)
-    grad_self_mixed = grad_self_mixed.astype(jnp.bfloat16)
+    group_self_branch, grad_self_mixed, layer_out = gather_dot(
+        grad_one.astype(jnp.bfloat16),
+        w_self_out,
+        jnp.bfloat16,
+        17,
+        kept_rows=layer_rows.reshape(clips, planes, piece, wide),
+    )
+    layer_out = to_whole_order(layer_out.reshape(frame_rows, wide)).astype(jnp.bfloat16)
+    layer_out = layer_out.reshape(frames.shape)
     cond_grad = jnp.concatenate(
         [
             grad_cross_keys.reshape(clips * cond_count, head_wide),
@@ -1932,7 +2152,7 @@
     grad_project, qkv_piece = lax.optimization_barrier((grad_project, qkv_piece))
     qkv_rows = over_rows(qkv_piece)
     grad_project, rest_rows = lax.optimization_barrier((grad_project, rest_rows))
-    grad_normed_one = spread(times_transposed(grad_project, w_qkv), 18)
+    grad_normed_one = dot_reduce(grad_project, w_qkv, clips, 18)
     _, norm_one_back = jax.vjp(layer_norm, stream, gain_rows[0], gain_rows[1])
     grad_zero_part, grad_gain_one, grad_bias_one = norm_one_back(grad_normed_one)
     _, norm_stamp_back = jax.vjp(layer_norm, stamps, gain_rows[0], gain_rows[1])

time: 893 us -> 816 us (0.914)
  matrix products: 148 us -> 55.5 us
  Pallas kernels: 596 us -> 617 us
    dot_general x6 -> x0, matrix products: 54.8 us -> none  [the longest x1 16 us: plane_device(): jnp.dot(group_three, w_gate_up, preferred_element_type=jnp.float32)]
    dot_general x10 -> x5, matrix products: 59.4 us -> 18.8 us  [times_transposed(): lax.dot_general(left_mat, right_mat, (((1,), (1,)), ((), ())), preferred_...]
    reshape x5 -> x0, local copies, waits for them, and re-layouts: 11.3 us -> none  [the longest x1 3.77 us: plane_device(): ff_cut = ff_low.transpose(2, 0, 1, 3).reshape(group, owned, 3 * ff_wide)]
    pallas_call x1, Pallas kernels: 38.9 us -> 48.8 us  [flash_forward(): pl.pallas_call(functools.partial(flash_forward_body, heads, rows // 4), g...]
    pallas_call x11, Pallas kernels: 406 us -> 415 us  [the longest x6 234 us: gather_dot(): pl.pallas_call(functools.partial(gather_dot_body, clips, rows, sub, gains...]
  transfers between devices with their start and end apart: 8 -> 8, of which waited for: 0 -> 0; matrix products, arithmetic and copies ran while one was open for 23% -> 15% of each run, Pallas kernels for 56% -> 60%
where the time goes in v3:
time: 816 us; the launch traced here: 807 us
  Pallas kernels  617 us (76%)
  local copies, waits for them, and re-layouts  61 us (7%)
  matrix products  55.5 us (7%)
  other arithmetic  50.4 us (6%)
  between operations  20.3 us (2%)
    pallas_call x6, Pallas kernels, gather_dot(): pl.pallas_call(functools.partial(gather_dot_body, clips, rows, sub, gains...  234 us
    pallas_call x5, Pallas kernels, dot_reduce(): pl.pallas_call(functools.partial(dot_reduce_body, clips, rows, sub, base...  182 us
    pallas_call x1, Pallas kernels, flash_forward(): pl.pallas_call(functools.partial(flash_forward_body, heads, rows // 4), g...  48.8 us
    pallas_call x1, Pallas kernels, enter(): pl.pallas_call(functools.partial(enter_body, group, planes), out_shape=[l...  36.8 us
    pallas_call x1, Pallas kernels, leave(): pl.pallas_call(functools.partial(leave_body, group, planes), out_shape=[l...  35.9 us
    pallas_call x1, Pallas kernels, flash_backward(): pl.pallas_call(functools.partial(flash_backward_body, heads, rows // 4),...  28.5 us
    pallas_call x1, Pallas kernels, ff_outer(): pl.pallas_call(ff_outer_body, grid=(ends + 1, wide // tile), out_shape=ja...  24.3 us
    dot_general x8, matrix products, outer_sum(): lax.dot_general(left_mat, right_mat, (((0,), (0,)), ((), ())), preferred_...  18.9 us
  transfers between devices with their start and end apart: 8, of which 0 were waited for; matrix products, arithmetic and copies ran while one was open for 15% of the time, Pallas kernels for 60%

profile of v3, /device:TPU:9, one launch (start us, length us, event | category | flops | bytes accessed | tf_op | source)
XLA Modules:
  0.0 806.9 jit_solution(15243122644494084424)
XLA Ops:
  24.3 36.8 %shard_map.298 = (bf16[2,4,32,1536]{3,2,1,0:T(8,128)(2,1)}, f32[8,1536]{1,0:T(8,128)}, f32[8,8,1536]{2,1,0:T(8,128)}, bf16[8,48,576]{2,1,0:T(8,128)(2,1)}, bf16[...) custom-call(bf16[8,32,1536]{2,1,0:T(8,128)(2,1)} %bitcast.227, f32[8,128]{1,0:T(8,128)} %pad_convert_fusion.norm_ref, ...), custom_call_target="tpu_custom_call" | custom-call | tf_op jit(solution)/shard_map/pallas_call | solution.py:911
  67.4 5.0 gather_fusion
  74.5 40.1 %shard_map.299 = (bf16[2,8,128,1536]{3,2,1,0:T(8,128)(2,1)}, bf16[8,2,16,768]{3,2,1,0:T(8,128)(2,1)}) custom-call(f32[2,128,1536]{2,1,0:T(8,128)} %bitcast_convert_fusion.3.own_ref.refs_0_, f32[2,1536]{1,0:T(2,128)} %get-tuple-element.152.refs_0_, bf16[4,2,16,768]{3,2,1,0:T(8,128)(2,1)} %select_select_fusion.refs_1_), custom_call_target="tpu_custom_call" | custom-call | tf_op jit(solution)/shard_map/pallas_call | solution.py:1303
  129.1 48.8 %shard_map.300 = (bf16[2048,576]{1,0:T(8,128)(2,1)}, bf16[2048,192]{1,0:T(8,128)(2,1)}, f32[2048,128]{1,0:T(8,128)}, bf16[8,48,1536]{2,1,0:T(8,128)(2,1)}, bf16[...) custom-call(bf16[2048,1536]{1,0:T(8,128)(2,1)} %bitcast.193, ...), custom_call_target="tpu_custom_call" | custom-call | tf_op jit(solution)/shard_map/pallas_call | solution.py:1704
  184.4 35.5 %shard_map.301.own_ref.refs_0_ = f32[2,128,1536]{2,1,0:T(8,128)} custom-call(bf16[2,8,128,192]{3,2,1,0:T(8,128)(2,1)} %bitcast.218, bf16[1536,192]{1,0:T(8,128)(2,1)} %get-tuple-element.143.mat_ref.refs_0_, f32[2,128,1536]{2,1,0:T(8,128)} %bitcast_convert_fusion.3.own_ref.refs_0_), custom_call_target="tpu_custom_call" | custom-call | tf_op jit(solution)/shard_map/pallas_call | solution.py:1479
  220.0 33.6 %shard_map.302 = (bf16[2,8,128,1536]{3,2,1,0:T(8,128)(2,1)}, bf16[2,8,128,192]{3,2,1,0:T(8,128)(2,1)}) custom-call(f32[2,128,1536]{2,1,0:T(8,128)} %shard_map.301.own_ref.refs_0_, f32[2,1536]{1,0:T(2,128)} %get-tuple-element.151.refs_0_, bf16[1536,192]{1,0:T(8,128)(2,1)} %get-tuple-element.142.refs_1_.mat_ref), custom_call_target="tpu_custom_call" | custom-call | tf_op jit(solution)/shard_map/pallas_call | solution.py:1303
  267.0 33.6 %shard_map.303.own_ref = f32[2,128,1536]{2,1,0:T(8,128)} custom-call(bf16[2,8,128,192]{3,2,1,0:T(8,128)(2,1)} %copy.125.left_ref, bf16[1536,192]{1,0:T(8,128)(2,1)} %get-tuple-element.141.mat_ref.refs_0_, f32[2,128,1536]{2,1,0:T(8,128)} %shard_map.301.own_ref.refs_0_), custom_call_target="tpu_custom_call" | custom-call | tf_op jit(solution)/shard_map/pallas_call | solution.py:1479
  300.6 36.6 %shard_map.304 = (bf16[2,8,128,1536]{3,2,1,0:T(8,128)(2,1)}, f32[2,8,128,1536]{3,2,1,0:T(8,128)}) custom-call(f32[2,128,1536]{2,1,0:T(8,128)} %shard_map.303.own_ref, f32[2,1536]{1,0:T(2,128)} %get-tuple-element.150.refs_0_, bf16[1536,1536]{1,0:T(8,128)(2,1)} %all-gather.9.cloned.1.call-done.refs_1_.mat_ref), custom_call_target="tpu_custom_call" | custom-call | tf_op jit(solution)/shard_map/pallas_call | solution.py:1303
  337.3 34.9 %shard_map.305 = (bf16[8,2,128,1536]{3,2,1,0:T(8,128)(2,1)}, bf16[2,8,128,1536]{3,2,1,0:T(8,128)(2,1)}, bf16[8,2,128,768]{3,2,1,0:T(8,128)(2,1)}) custom-call(bf16[2,128,1536]{2,1,0:T(8,128)(2,1)} %bitcast.190, bf16[1536,768]{1,0:T(8,128)(2,1)} %all-gather.11.cloned.1.call-done.refs_0_, f32[2,8,128,1536]{3,2,1,0:T(8,128)} %get-tuple-element.75), custom_call_target="tpu_custom_call" | custom-call | tf_op jit(solution)/shard_map/pallas_call | solution.py:1303
  372.2 9.2 %convolution_convert_fusion = bf16[2048,1536]{1,0:T(8,128)(2,1)} fusion(bf16[2048,768]{1,0:T(8,128)(2,1)} %bitcast.200, bf16[1536,768]{1,0:T(8,128)(2,1)} %all-gather.11.cloned.1.call-done.refs_0_), kind=kOutput, calls=%fused_computation.7 | convolution fusion | flops 4834983936 | bytes 11796480 | tf_op jit(solution)/shard_map/dot_general | solution.py:60
  381.4 24.3 %shard_map.306 = bf16[1536,2304]{1,0:T(8,128)(2,1)} custom-call(bf16[2048,1536]{1,0:T(8,128)(2,1)} %bitcast.191, bf16[2048,1536]{1,0:T(8,128)(2,1)} %bitcast.187, bf16[2048,1536]{1,0:T(8,128)(2,1)} %bitcast.192, bf16[2048,768]{1,0:T(8,128)(2,1)} %bitcast.201), custom_call_target="tpu_custom_call" | custom-call | tf_op jit(solution)/shard_map/pallas_call | solution.py:1869
  415.3 45.4 %shard_map.307 = f32[2,128,1536]{2,1,0:T(8,128)} custom-call(bf16[2,8,128,1536]{3,2,1,0:T(8,128)(2,1)} %get-tuple-element.79, bf16[1536,1536]{1,0:T(8,128)(2,1)} %all-gather.9.cloned.1.call-done.refs_1_.mat_ref), custom_call_target="tpu_custom_call" | custom-call | tf_op jit(solution)/shard_map/pallas_call | solution.py:1479
  471.1 33.5 %shard_map.308 = (bf16[2,8,128,1536]{3,2,1,0:T(8,128)(2,1)}, bf16[2,8,128,192]{3,2,1,0:T(8,128)(2,1)}) custom-call(bf16[2,128,1536]{2,1,0:T(8,128)(2,1)} %fusion.33.own_ref, bf16[1536,192]{1,0:T(8,128)(2,1)} %get-tuple-element.141.mat_ref.refs_0_), custom_call_target="tpu_custom_call" | custom-call | tf_op jit(solution)/shard_map/pallas_call | solution.py:1303
  516.8 33.0 %shard_map.309 = f32[2,128,1536]{2,1,0:T(8,128)} custom-call(bf16[2,8,128,192]{3,2,1,0:T(8,128)(2,1)} %copy.130.left_ref, bf16[1536,192]{1,0:T(8,128)(2,1)} %get-tuple-element.142.refs_1_.mat_ref), custom_call_target="tpu_custom_call" | custom-call | tf_op jit(solution)/shard_map/pallas_call | solution.py:1479
  561.6 54.9 %shard_map.310 = (bf16[2,8,128,1536]{3,2,1,0:T(8,128)(2,1)}, bf16[2,8,128,192]{3,2,1,0:T(8,128)(2,1)}, bf16[8,32,1536]{2,1,0:T(8,128)(2,1)}, bf16[8,32,1536]{2,1,0:T(8,128)(2,1)}) custom-call(bf16[2,128,1536]{2,1,0:T(8,128)(2,1)} %get-tuple-element.137.own_ref, bf16[1536,192]{1,0:T(8,128)(2,1)} %get-tuple-element.143.mat_ref.refs_0_, ...), custom_call_target="tpu_custom_call" | custom-call | tf_op jit(solution)/shard_map/pallas_call | solution.py:1303
  616.5 4.3 convolution_convert_fusion.1
  620.9 4.3 convolution_convert_fusion.2
  631.9 28.5 %shard_map.311 = (bf16[2048,576]{1,0:T(8,128)(2,1)}, f32[2,1,384]{2,1,0:T(1,128)}, bf16[8,48,2304]{2,1,0:T(8,128)(2,1)}) custom-call(bf16[2048,576]{1,0:T(8,128)(2,1)} %get-tuple-element.86.turned_ref, bf16[2048,192]{1,0:T(8,128)(2,1)} %bitcast.219, f32[2048,128]{1,0:T(8,128)} %get-tuple-element.92.lse_ref, bf16[2,1,384]{2,1,0:T(2,128)(2,1)} %copy.116.stamp_ref, ...), custom_call_target="tpu_custom_call" | custom-call | tf_op jit(solution)/shard_map/pallas_call | solution.py:1824
  660.5 6.9 fusion.96
  679.4 34.3 %shard_map.312 = f32[2,128,1536]{2,1,0:T(8,128)} custom-call(bf16[2,8,128,576]{3,2,1,0:T(8,128)(2,1)} %bitcast.210, bf16[1536,576]{1,0:T(8,128)(2,1)} %all-gather.5.cloned.1.call-done.mat_ref), custom_call_target="tpu_custom_call" | custom-call | tf_op jit(solution)/shard_map/pallas_call | solution.py:1479
  722.6 35.9 %shard_map.313 = (bf16[8,32,1536]{2,1,0:T(8,128)(2,1)}, bf16[8,48,1344]{2,1,0:T(8,128)(2,1)}, f32[8,128]{1,0:T(8,128)}, bf16[8,32,1536]{2,1,0:T(8,128)(2,1)}) custom-call(bf16[2,4,32,1536]{3,2,1,0:T(8,128)(2,1)} %bitcast.209, bf16[8,48,1344]{2,1,0:T(8,128)(2,1)} %pad_maximum_fusion.2.cut_ref, f32[32,8,128]{2,1,0:T(8,128)} %pad.21.parts_ref), custom_call_target="tpu_custom_call" | custom-call | tf_op jit(solution)/shard_map/pallas_call | solution.py:720
  767.1 9.3 %shard_map.314 = f32[8,128]{1,0:T(8,128)} custom-call(f32[8,128]{1,0:T(8,128)} %broadcast_in_dim.142.squares_ref), custom_call_target="tpu_custom_call" | custom-call | tf_op jit(solution)/shard_map/pallas_call | solution.py:1519
  779.7 7.3 shard_map.315
  787.0 10.4 %shard_map.316 = (f32[48,18432]{1,0:T(8,128)}, f32[48,18432]{1,0:T(8,128)}, f32[48,18432]{1,0:T(8,128)}) custom-call(f32[1,1]{1,0:T(1,128)} %bitcast.58.factor_ref, f32[48,18432]{1,0:T(8,128)} %weight_ref.3, f32[48,18432]{1,0:T(8,128)} %first_ref.3, f32[48,18432]{1,0:T(8,128)} %second_ref.3, bf16[8,48,2304]{2,1,0:T(8,128)(2,1)} %get-tuple-element.105.grad_ref), custom_call_target="tpu_custom_call" | custom-call | tf_op jit(solution)/shard_map/pallas_call | solution.py:1919
  (334 shorter events, 140.1 us)
Async XLA Ops:
  7.2 10.8 %copy-start = (bf16[1,256,1536]{2,1,0:T(8,128)(2,1)S(1)}, bf16[1,256,1536]{2,1,0:T(8,128)(2,1)}, u32[]{:S(2)}) copy-start(bf16[1,256,1536]{2,1,0:T(8,128)(2,1)} %param.19) | copy-start | bytes 2359300
  7.2 119.3 %all-gather.5.cloned.1.call-start = ((), (), s32[]{:S(2)}) async-start(), calls=%async_computation.4 | async-start | bytes 2457600 | tf_op jit(solution)/shard_map/all_gather | solution.py:2002
  20.7 45.3 %copy-start.8 = (f32[48,18432]{1,0:T(8,128)S(1)}, f32[48,18432]{1,0:T(8,128)}, u32[]{:S(2)}) copy-start(f32[48,18432]{1,0:T(8,128)} %weight_ref.3) | copy-start | bytes 10616836
  61.1 119.2 %all-gather.7.cloned.1.call-start = ((), (), s32[]{:S(2)}) async-start(), calls=%async_computation.5 | async-start | bytes 2949120 | tf_op jit(solution)/shard_map/all_gather | solution.py:2002
  61.9 238.7 %all-gather.9.cloned.1.call-start = ((), (), s32[]{:S(2)}) async-start(), calls=%async_computation.6 | async-start | bytes 5898240 | tf_op jit(solution)/shard_map/all_gather | solution.py:2002
  73.1 43.3 %copy-start.58 = (s32[1536]{0:T(1024)S(1)}, s32[1536]{0:T(1024)}, u32[]{:S(2)}) copy-start(s32[1536]{0:T(1024)} %reshape.717) | copy-start | bytes 18436
  118.2 8.3 %copy-start.39 = (f32[2,1536]{1,0:T(2,128)}, f32[2,1536]{1,0:T(2,128)S(1)}, u32[]{:S(2)}) copy-start(f32[2,1536]{1,0:T(2,128)S(1)} %get-tuple-element.161) | copy-start | bytes 36868
  177.9 159.3 %all-gather.11.cloned.1.call-start = ((), (), s32[]{:S(2)}) async-start(), calls=%async_computation.7 | async-start | bytes 2949120 | tf_op jit(solution)/shard_map/all_gather | solution.py:2002
  178.5 286.5 %reduce-scatter.9.cloned.1.call-start = ((), (), s32[]{:S(2)}) async-start(), calls=%async_computation.8 | async-start | bytes 7077888 | tf_op jit(solution)/shard_map/reduce_scatter | solution.py:2075
  381.4 245.5 %reduce-scatter.11.cloned.1.call-start = ((), (), s32[]{:S(2)}) async-start(), calls=%async_computation.9 | async-start | bytes 8847360 | tf_op jit(solution)/shard_map/reduce_scatter | solution.py:2086
  405.8 273.6 %reduce-scatter.13.cloned.1.call-start = ((), (), s32[]{:S(2)}) async-start(), calls=%async_computation.10 | async-start | bytes 2949120 | tf_op jit(solution)/shard_map/reduce_scatter | solution.py:2086
  413.8 46.9 %copy-start.52 = (f32[2,128]{1,0:T(2,128)}, f32[2,128]{1,0:T(2,128)S(1)}, u32[]{:S(2)}) copy-start(f32[2,128]{1,0:T(2,128)S(1)} %broadcast_multiply_fusion.2) | copy-start | bytes 3076
  414.1 46.6 %copy-start.56 = (f32[2,128]{1,0:T(2,128)}, f32[2,128]{1,0:T(2,128)S(1)}, u32[]{:S(2)}) copy-start(f32[2,128]{1,0:T(2,128)S(1)} %fusion.79) | copy-start | bytes 3076
  415.3 45.4 %copy-start.44 = (f32[1536]{0:T(1024)S(1)}, f32[1536]{0:T(1024)}, u32[]{:S(2)}) copy-start(f32[1536]{0:T(1024)} %get-tuple-element.126) | copy-start | bytes 18436
  561.6 55.0 %copy-start.27 = (bf16[24,8,2,1024]{3,1,2,0:T(8,128)(2,1)S(1)}, bf16[24,8,2,1024]{3,1,2,0:T(8,128)(2,1)}, u32[]{:S(2)}) copy-start(bf16[24,8,2,1024]{3,1,2,0:T(8,128)(2,1)} %copy.159) | copy-start | bytes 2359300
  616.5 8.7 %slice-start = ((s8[6291456]{0:T(1024)(128)(4,1)}), s8[4194304]{0:T(1024)(128)(4,1)S(1)}, s32[]{:S(2)}) async-start(s8[6291456]{0:T(1024)(128)(4,1)} %bitcast.241), calls=%async_computation.12 | async-start | bytes 8388608
  629.3 91.0 %reduce-scatter.15.cloned.1.call-start = ((), (), s32[]{:S(2)}) async-start(), calls=%async_computation.11 | async-start | bytes 2457600 | tf_op jit(solution)/shard_map/reduce_scatter | solution.py:2086
  764.0 15.1 %copy-start.50 = (f32[6,48]{1,0:T(8,128)S(1)}, f32[6,48]{1,0:T(8,128)}, u32[]{:S(2)}) copy-start(f32[6,48]{1,0:T(8,128)} %param.28) | copy-start | bytes 3460
  764.0 15.1 %copy-start.66 = (f32[6,48]{1,0:T(8,128)S(1)}, f32[6,48]{1,0:T(8,128)}, u32[]{:S(2)}) copy-start(f32[6,48]{1,0:T(8,128)} %param.34) | copy-start | bytes 3460
  764.0 15.1 %copy-start.67 = (f32[6,48]{1,0:T(8,128)S(1)}, f32[6,48]{1,0:T(8,128)}, u32[]{:S(2)}) copy-start(f32[6,48]{1,0:T(8,128)} %param.35) | copy-start | bytes 3460
  787.0 10.4 %copy-start.23 = (f32[24,3072]{1,0:T(8,128)S(1)}, f32[24,3072]{1,0:T(8,128)}, u32[]{:S(2)}) copy-start(f32[24,3072]{1,0:T(8,128)} %param.27) | copy-start | bytes 884740
  787.0 10.4 %copy-start.35 = (f32[24,3072]{1,0:T(8,128)S(1)}, f32[24,3072]{1,0:T(8,128)}, u32[]{:S(2)}) copy-start(f32[24,3072]{1,0:T(8,128)} %param.32) | copy-start | bytes 884740
  787.0 10.4 %copy-start.36 = (f32[24,3072]{1,0:T(8,128)S(1)}, f32[24,3072]{1,0:T(8,128)}, u32[]{:S(2)}) copy-start(f32[24,3072]{1,0:T(8,128)} %param.33) | copy-start | bytes 884740
  787.0 11.5 %copy-start.1 = (bf16[1,256,1536]{2,1,0:T(8,128)(2,1)S(1)}, bf16[1,256,1536]{2,1,0:T(8,128)(2,1)}, u32[]{:S(2)}) copy-start(bf16[1,256,1536]{2,1,0:T(8,128)(2,1)} %param.19) | copy-start | bytes 2359300
  (57 other events, 171.6 us)
Sparse Core Ops, SparseCore 0:
  61.3 45.1 all-gather.4
  108.0 55.5 all-gather.6
  178.0 85.7 all-gather.8
  265.2 49.7 all-gather.10
  381.5 70.2 reduce-scatter.8
  454.1 135.5 reduce-scatter.10
  629.5 43.3 reduce-scatter.12
  675.9 42.4 reduce-scatter.14

commit v4 on v3

--- a/solution.py
+++ b/solution.py
@@ -2,6 +2,7 @@
 
 import jax
 import jax.numpy as jnp
+import numpy as np
 from jax import lax
 from jax.experimental import pallas as pl
 from jax.experimental.pallas import tpu as pltpu
@@ -648,42 +649,31 @@
     ]
 
 
-def swap_steps(own_ref, kept_ref, send_sem, recv_sem, local_sem):
-    place, depth, flip = plane_places()
-    copies = []
-    for mask in (6, 7, 2, 3, 4, 5, 1):
-        other = flip(mask)
-        copy = remote(
-            own_ref.at[other],
-            kept_ref.at[place],
-            send_sem.at[mask],
-            recv_sem.at[mask],
-            (other, depth),
-        )
-        copy.start()
-        copies.append(copy)
-    stay = pltpu.make_async_copy(own_ref.at[place], kept_ref.at[place], local_sem)
-    stay.start()
-    yield
-    stay.wait()
-    for copy in copies:
-        copy.wait()
-    yield
-
-
-def swap_scratch():
-    return [DMA((8,)), DMA((8,)), DMA(())]
-
-
 def leave_body(
-    group, planes, kept_ref, cut_ref, parts_ref, own_ref, mine_ref, norm_ref, mid, terms, *sems
+    group,
+    planes,
+    kept_ref,
+    first_cut_ref,
+    rest_cut_ref,
+    parts_ref,
+    squares_ref,
+    own_ref,
+    first_mine_ref,
+    rest_mine_ref,
+    norm_ref,
+    total_ref,
+    mid,
+    terms,
+    block,
+    blocks,
+    *sems,
 ):
-    part_send, part_recv = sems[:2]
+    part_send, part_recv, block_send, block_recv = sems[:4]
     place, depth, flip = plane_places()
     devices = [(flip(mask), lax.rem(depth + step, planes)) for mask, step in everyone(planes)]
     greet(devices)
     here = place * planes + depth
-    rows = outward_steps(group, planes, kept_ref, own_ref, mid, *sems[2:7])
+    rows = outward_steps(group, planes, kept_ref, own_ref, mid, *sems[4:9])
     next(rows)
     copies = []
     for index, (other, plane) in enumerate(devices):
@@ -697,42 +687,77 @@
         copy.start()
         copies.append(copy)
     terms[here] = parts_ref[here]
-    columns = swap_steps(cut_ref, mine_ref, *sems[7:])
-    next(columns)
+    start_swap, end_swap = swap_beside(
+        [
+            (lambda other: first_cut_ref.at[other], lambda other: first_mine_ref.at[other]),
+            (lambda other: rest_cut_ref.at[other], lambda other: rest_mine_ref.at[other]),
+        ],
+        *sems[9:],
+    )
+    start_swap()
     next(rows)
     for other, plane in devices:
         source = other * planes + plane
         one = terms.at[source]
         remote(one, one, part_send.at[0], part_recv.at[source], (other, plane)).wait_recv()
-    norm_ref[...] = jnp.sum(terms[...], axis=0)
-    next(columns)
+    norm_sum = jnp.sum(terms[...], axis=0)
+    norm_ref[...] = norm_sum
+    end_swap()
+    squares = squares_ref[0, 0] + jnp.sum(norm_sum * norm_sum)
+    for mine_ref in (first_mine_ref, rest_mine_ref):
+        for piece in range(group):
+            values = mine_ref[piece].astype(jnp.float32)
+            squares = squares + jnp.sum(values * values)
+    block[...] = jnp.full(block.shape, squares)
+    blocks[here] = block[...]
+    for index, (other, plane) in enumerate(devices):
+        copy = remote(
+            block, blocks.at[here], block_send.at[index], block_recv.at[here], (other, plane)
+        )
+        copy.start()
+        copies.append(copy)
     next(rows)
+    for other, plane in devices:
+        source = other * planes + plane
+        one = blocks.at[source]
+        remote(one, one, block_send.at[0], block_recv.at[source], (other, plane)).wait_recv()
+    total_ref[...] = jnp.sum(blocks[...], axis=0)
     for copy in copies:
         copy.wait_send()
 
 
-def leave(kept_rows, cut, norm_parts, collective_id):
+def leave(kept_rows, first_cut, rest_cut, norm_parts, squares, collective_id):
     per, planes, rows, wide = kept_rows.shape
     group = per * planes
     count = group * planes
-    whole = pl.BlockSpec(memory_space=pltpu.VMEM)
+    inside = pl.BlockSpec(memory_space=pltpu.VMEM)
     like = lambda shape, array: jax.ShapeDtypeStruct(shape, array.dtype)
-    own, mine, norm_sum, _ = pl.pallas_call(
+    *results, _ = pl.pallas_call(
         functools.partial(leave_body, group, planes),
         out_shape=[
             like((group, rows, wide), kept_rows),
-            like(cut.shape, cut),
+            like(first_cut.shape, first_cut),
+            like(rest_cut.shape, rest_cut),
             like(norm_parts.shape[1:], norm_parts),
+            like((8, 128), norm_parts),
             like((group, rows, wide), kept_rows),
         ],
-        in_specs=[any_spec(), any_spec(), whole],
-        out_specs=[any_spec(), any_spec(), whole, any_spec()],
-        scratch_shapes=[pltpu.VMEM(norm_parts.shape, jnp.float32), DMA((count,)), DMA((count,))]
+        in_specs=[any_spec()] * 3 + [inside, pl.BlockSpec(memory_space=pltpu.SMEM)],
+        out_specs=[any_spec()] + [inside] * 4 + [any_spec()],
+        scratch_shapes=[
+            pltpu.VMEM(norm_parts.shape, jnp.float32),
+            pltpu.VMEM((8, 128), jnp.float32),
+            pltpu.VMEM((count, 8, 128), jnp.float32),
+            DMA((count,)),
+            DMA((count,)),
+            DMA((count,)),
+            DMA((count,)),
+        ]
         + outward_scratch(group, planes)
-        + swap_scratch(),
+        + swap_beside_scratch(2),
         compiler_params=communicating(collective_id),
-    )(kept_rows, cut, norm_parts)
-    return own, mine, norm_sum
+    )(kept_rows, first_cut, rest_cut, norm_parts, squares)
+    return results
 
 
 def everyone(planes):
@@ -1061,38 +1086,131 @@
     ]
 
 
-def dot_tiles(left, right_ref, transposed, width):
-    count = right_ref.shape[0] if transposed else right_ref.shape[1]
+def dot_tiles(left, right_ref, span, transposed, width):
+    first, last = span
+    count = right_ref.shape[0] if transposed else last - first
     for start in range(0, count, width):
         stop = min(start + width, count)
         if transposed:
-            yield start, stop, times_transposed(left, right_ref[start:stop, :])
+            yield start, stop, times_transposed(left, right_ref[start:stop, first:last])
         else:
             yield start, stop, jnp.dot(
-                left, right_ref[:, start:stop], preferred_element_type=jnp.float32
+                left, right_ref[:, first + start : first + stop], preferred_element_type=jnp.float32
             )
 
 
-def gather_dot_body(clips, rows, sub, normed, mode, beside, own_ref, *refs):
+def window_of(matrix, span):
+    first, last = span or (0, matrix.shape[1])
+    start = first // 128 * 128
+    while (matrix.shape[1] - start) * 2 > matrix.shape[1] and start and start % 384:
+        start -= 128
+    stop = min(-(-last // 128) * 128, matrix.shape[1])
+    return (start, stop - start), (first - start, last - start)
+
+
+def cross_shares(queries, pair_ref, bias_ref):
+    wide = queries[0].shape[1]
+    keys = [
+        (clip, start, pair_ref[clip, :, start : start + HDIM])
+        for clip in range(len(queries))
+        for start in range(0, wide, HDIM)
+    ]
+    scores = [
+        times_transposed(queries[clip][:, start : start + HDIM], key) * HDIM ** (-0.5)
+        + bias_ref[clip]
+        for clip, start, key in keys
+    ]
+    tops = [jnp.max(score, axis=1, keepdims=True) for score in scores]
+    expos = [jnp.exp(score - top) for score, top in zip(scores, tops)]
+    sums = [jnp.sum(expo, axis=1, keepdims=True) for expo in expos]
+    return keys, [expo / total for expo, total in zip(expos, sums)]
+
+
+def by_clip_of(results, clips, low):
+    heads = len(results) // clips
+    return [
+        jnp.concatenate(results[clip * heads : (clip + 1) * heads], axis=1).astype(low)
+        for clip in range(clips)
+    ]
+
+
+def cross_rows(queries, pair_ref, bias_ref):
+    low, wide = queries[0].dtype, queries[0].shape[1]
+    keys, shares = cross_shares(queries, pair_ref, bias_ref)
+    mixed = [
+        jnp.dot(
+            share.astype(low),
+            pair_ref[clip, :, wide + start : wide + start + HDIM],
+            preferred_element_type=jnp.float32,
+        )
+        for (clip, start, _), share in zip(keys, shares)
+    ]
+    return by_clip_of(mixed, len(queries), low)
+
+
+def cross_rows_back(queries, grads, pair_ref, bias_ref, pair_grad_ref):
+    low, wide = queries[0].dtype, queries[0].shape[1]
+    scale = HDIM ** (-0.5)
+    keys, shares = cross_shares(queries, pair_ref, bias_ref)
+    own_grads = [grads[clip][:, start : start + HDIM] for clip, start, _ in keys]
+    grad_shares = [
+        times_transposed(grad, pair_ref[clip, :, wide + start : wide + start + HDIM])
+        for (clip, start, _), grad in zip(keys, own_grads)
+    ]
+    deltas = [
+        jnp.sum(share * grad_share, axis=1, keepdims=True)
+        for share, grad_share in zip(shares, grad_shares)
+    ]
+    scores = [
+        (share * (grad_share - delta)).astype(low)
+        for share, grad_share, delta in zip(shares, grad_shares, deltas)
+    ]
+    results = [
+        jnp.dot(score, key, preferred_element_type=jnp.float32) * scale
+        for score, (_, _, key) in zip(scores, keys)
+    ]
+    key_grads = [
+        outer_sum(score, queries[clip][:, start : start + HDIM]) * scale
+        for score, (clip, start, _) in zip(scores, keys)
+    ]
+    value_grads = [
+        outer_sum(share.astype(low), grad) for share, grad in zip(shares, own_grads)
+    ]
+    heads = len(keys) // len(queries)
+    for clip in range(len(queries)):
+        mine = slice(clip * heads, (clip + 1) * heads)
+        pair_grad_ref[clip] += jnp.concatenate(key_grads[mine] + value_grads[mine], axis=1)
+    return by_clip_of(results, len(queries), low)
+
+
+def gather_dot_body(clips, rows, sub, normed, mode, window, span, beside, own_ref, *refs):
     refs = list(refs)
     take = lambda count: [refs.pop(0) for _ in range(count)]
     gain_ref = take(1)[0] if normed else None
     mat_ref = take(1)[0] if mode != "rows" else None
     gates_ref = take(1)[0] if mode == "gates" else None
+    pair_ref, bias_ref = take(2) if mode in ("cross", "cross_back") else (None, None)
+    query_ref = take(1)[0] if mode == "cross_back" else None
     extra_ref = take(1)[0] if beside else None
     all_ref = take(1)[0]
-    prod_refs = take({"rows": 0, "dot": 1, "gates": 2}[mode])
+    prod_refs = take({"rows": 0, "dot": 1, "gates": 2, "cross": 2, "cross_back": 1}[mode])
+    pair_grad_ref = take(1)[0] if mode == "cross_back" else None
     extra_outs = take({"cond": 1, "outward": 2}[beside[0]]) if beside else []
     held, send_sem, recv_sem, all_sem = take(4)
     mat, mat_sem = take(2) if mode != "rows" else (None, None)
     stages = take(len(prod_refs))
     prod_sem = take(1)[0] if prod_refs else None
     gates, gates_sem = take(2) if mode == "gates" else (None, None)
+    queries, query_sem = take(2) if mode == "cross_back" else (None, None)
     place, depth, flip = plane_places()
     core, beside_x, beside_y, across = flip(1), flip(2), flip(4), flip(6)
     if mode != "rows":
-        load = pltpu.make_async_copy(mat_ref, mat, mat_sem)
+        load = pltpu.make_async_copy(mat_ref.at[:, pl.ds(*window)], mat, mat_sem)
         load.start()
+    if mode == "cross_back":
+        query_load = pltpu.make_async_copy(query_ref, queries, query_sem)
+        query_load.start()
+        pair_grad_ref[...] = jnp.zeros_like(pair_grad_ref)
     slots = [flip(mask) for mask in (0, 1, 2, 4, 3, 5, 6, 7)]
     gate_loads = {}
     if mode == "gates":
@@ -1165,8 +1283,29 @@
         left = held[slot].reshape(clips * rows, held.shape[3])
         for copy in gate_loads.get(mask, ()):
             copy.wait()
-        for start, stop, product in dot_tiles(left, mat, False, 256 * (3 if mode == "dot" else 1)):
+        for start, stop, product in dot_tiles(
+            left, mat, span, False, 256 * (1 if mode == "gates" else 3)
+        ):
             product = product.reshape(clips, rows, stop - start)
+            if mode == "cross":
+                query = product.astype(stages[0].dtype)
+                stages[0][slot] = query
+                mixed = cross_rows([query[clip] for clip in range(clips)], pair_ref, bias_ref)
+                for clip in range(clips):
+                    stages[1][slot, clip] = mixed[clip]
+                continue
+            if mode == "cross_back":
+                grad = product.astype(stages[0].dtype)
+                results = cross_rows_back(
+                    [queries[clip, slot] for clip in range(clips)],
+                    [grad[clip] for clip in range(clips)],
+                    pair_ref,
+                    bias_ref,
+                    pair_grad_ref,
+                )
+                for clip in range(clips):
+                    stages[0][slot, clip] = results[clip]
+                continue
             if mode == "dot":
                 stages[0][slot, :, :, start:stop] = product.astype(stages[0].dtype)
                 continue
@@ -1186,6 +1325,8 @@
 
     if mode != "rows":
         load.wait()
+    if mode == "cross_back":
+        query_load.wait()
     multiply(0)
     if beside:
         next(going)
@@ -1235,12 +1376,21 @@
     picked=None,
     kept_rows=None,
     gate_up=None,
+    span=None,
+    pair=None,
+    bias=None,
+    query=None,
     sub=64,
 ):
     clips, rows, wide = own_rows.shape
     count = clips * (rows // sub)
     low = jnp.bfloat16
-    mode = "rows" if matrix is None else "dot" if gate_up is None else "gates"
+    mode = "rows" if matrix is None else "dot"
+    if gate_up is not None:
+        mode = "gates"
+    if pair is not None:
+        mode = "cross" if query is None else "cross_back"
+    window = inner = None
     inside = pl.BlockSpec(memory_space=pltpu.VMEM)
     by_clip = lambda columns, of: jax.ShapeDtypeStruct((clips, 8, rows, columns), of)
     by_device = lambda columns, of: jax.ShapeDtypeStruct((8, clips, rows, columns), of)
@@ -1256,10 +1406,11 @@
         DMA((8, clips)),
     ]
     if mode != "rows":
-        columns = matrix.shape[1]
+        window, inner = window_of(matrix, span)
+        columns = inner[1] - inner[0]
         args.append(matrix)
         in_specs.append(any_spec())
-        scratch += [pltpu.VMEM(matrix.shape, low), DMA(())]
+        scratch += [pltpu.VMEM((wide, window[1]), low), DMA(())]
     if mode == "dot":
         outs.append(by_clip(columns, kind))
         scratch += [pltpu.VMEM((8, clips, rows, columns), kind), DMA((1, 8, clips))]
@@ -1274,7 +1425,23 @@
             pltpu.VMEM((8, clips, rows, 2 * columns), jnp.float32),
             DMA((8, clips)),
         ]
+    if mode == "cross":
+        args += [pair, bias]
+        in_specs += [inside] * 2
+        outs += [by_clip(columns, low)] * 2
+        scratch += [pltpu.VMEM((8, clips, rows, columns), low)] * 2 + [DMA((2, 8, clips))]
     out_specs = [any_spec()] * len(outs)
+    if mode == "cross_back":
+        args += [pair, bias, query.reshape(clips, 8, rows, columns)]
+        in_specs += [inside, inside, any_spec()]
+        outs += [by_clip(columns, low), jax.ShapeDtypeStruct(pair.shape, jnp.float32)]
+        out_specs += [any_spec(), inside]
+        scratch += [
+            pltpu.VMEM((8, clips, rows, columns), low),
+            DMA((1, 8, clips)),
+            pltpu.VMEM((clips, 8, rows, columns), low),
+            DMA(()),
+        ]
     mains = len(outs)
     beside = None
     if picked is not None:
@@ -1302,7 +1469,7 @@
         scratch += outward_scratch(*beside[1:])
     results = pl.pallas_call(
         functools.partial(
-            gather_dot_body, clips, rows, sub, gains is not None, mode, beside
+            gather_dot_body, clips, rows, sub, gains is not None, mode, window, inner, beside
         ),
         out_shape=outs,
         in_specs=in_specs,
@@ -1310,25 +1477,174 @@
         scratch_shapes=scratch,
         compiler_params=communicating(collective_id),
     )(*args)
-    flat = [block.reshape(clips * 8 * rows, block.shape[3]) for block in results[:mains]]
+    flat = [
+        block.reshape(clips * 8 * rows, block.shape[3]) if len(block.shape) == 4 else block
+        for block in results[:mains]
+    ]
     return flat + list(results[mains : mains + 1])
 
 
-def dot_reduce_body(clips, rows, sub, added, beside, left_ref, mat_ref, *refs):
-    refs = list(refs)
-    base_ref = refs.pop(0) if added else None
-    kept_ref = refs.pop(0) if beside else None
-    sum_ref = refs.pop(0)
-    own_ref, mid = (refs.pop(0), refs.pop(0)) if beside else (None, None)
-    left, mat, terms, pair, held, turn, from_x, from_y, *sems = refs
-    mat_sem, left_sem, send_sem, core_sem, turn_sem, x_sem, y_sem, *extra = sems
+def reduce_steps(clips, rows, sub, multiply, final, terms, pair, turn, from_x, from_y, *sems):
+    send_sem, core_sem, turn_sem, x_sem, y_sem = sems
     place, depth, flip = plane_places()
     core, beside_x, beside_y = flip(1), flip(2), flip(4)
-    order = [flip(mask) for mask in (7, 6, 3, 2, 5, 4, 1, 0)]
-    load = pltpu.make_async_copy(mat_ref, mat, mat_sem)
+    chunks = [(clip, part) for clip in range(clips) for part in range(rows // sub)]
+    count = len(chunks)
+    half = count // 2
+    sends = []
+
+    def send(source, goal, recv_sem, device):
+        copy = remote(source, goal, send_sem.at[len(sends)], recv_sem, (device, depth))
+        copy.start()
+        sends.append(copy)
+
+    def arrived(block, recv_sem):
+        remote(block, block, send_sem.at[0], recv_sem, (core, depth)).wait_recv()
+
+    def term(number, index):
+        clip, part = chunks[index]
+        return terms.at[number, clip, pl.ds(part * sub, sub)]
+
+    def give(number, chip):
+        for index in range(count):
+            send(term(number, index), pair.at[index, chip], core_sem.at[index, chip], core)
+
+    def total(*blocks):
+        return sum(block[...].astype(jnp.float32) for block in blocks)
+
+    def add(block, other):
+        block[...] = total(block, other).astype(terms.dtype)
+
+    numbers = {3: 1, 1: 3, 2: 5, 0: 7}
+
+    def combine(chip, index):
+        arrived(pair.at[index, chip], core_sem.at[index, chip])
+        block = term(numbers[chip], index)
+        add(block, pair.at[index, chip])
+        return block
+
+    multiply(0)
+    give(0, 3)
+    multiply(1)
+    multiply(2)
+    give(2, 1)
+    for low in range(half):
+        high = half + low
+        send(combine(3, low), turn.at[low], turn_sem.at[low], beside_x)
+        send(combine(3, high), turn.at[high], turn_sem.at[high], beside_y)
+    multiply(3)
+    multiply(4)
+    give(4, 2)
+    for low in range(half):
+        send(combine(1, low), from_x.at[low], x_sem.at[low], beside_x)
+    multiply(5)
+    for high in range(half, count):
+        send(combine(2, high), from_y.at[high], y_sem.at[high], beside_y)
+    multiply(6)
+    give(6, 0)
+    multiply(7)
+    yield
+    for low in range(half):
+        high = half + low
+        block = combine(2, low)
+        arrived(turn.at[low], turn_sem.at[low])
+        add(block, turn.at[low])
+        send(block, from_y.at[low], y_sem.at[low], beside_y)
+        block = combine(1, high)
+        arrived(turn.at[high], turn_sem.at[high])
+        add(block, turn.at[high])
+        send(block, from_x.at[high], x_sem.at[high], beside_x)
+    yield
+    for index in range(count):
+        clip, part = chunks[index]
+        arrived(pair.at[index, 0], core_sem.at[index, 0])
+        arrived(from_x.at[index], x_sem.at[index])
+        arrived(from_y.at[index], y_sem.at[index])
+        result = total(term(7, index), pair.at[index, 0], from_x.at[index], from_y.at[index])
+        final(index, clip, pl.ds(part * sub, sub), result)
+    yield
+    for copy in sends:
+        copy.wait_send()
+    yield
+
+
+def plane_order():
+    place, depth, flip = plane_places()
+    return [flip(mask) for mask in (7, 6, 3, 2, 5, 4, 1, 0)]
+
+
+def reduce_scratch(clips, rows, sub, wide):
+    count = clips * (rows // sub)
+    low = jnp.bfloat16
+    return [
+        pltpu.VMEM((8, clips, rows, wide), low),
+        pltpu.VMEM((count, 4, sub, wide), low),
+        pltpu.VMEM((count, sub, wide), low),
+        pltpu.VMEM((count, sub, wide), low),
+        pltpu.VMEM((count, sub, wide), low),
+        DMA((7 * count,)),
+        DMA((count, 4)),
+        DMA((count,)),
+        DMA((count,)),
+        DMA((count,)),
+    ]
+
+
+def norm_back(values, gain, grad):
+    center = values - jnp.mean(values, axis=1, keepdims=True)
+    inverse = lax.rsqrt(jnp.mean(center * center, axis=1, keepdims=True) + norm_eps)
+    unit = center * inverse
+    stats = [
+        jnp.sum(grad * unit, axis=0, keepdims=True),
+        jnp.sum(grad, axis=0, keepdims=True),
+    ]
+    scaled = grad * gain
+    result = inverse * (
+        scaled
+        - jnp.mean(scaled, axis=1, keepdims=True)
+        - unit * jnp.mean(scaled * unit, axis=1, keepdims=True)
+    )
+    return result, stats
+
+
+def final_back(values_ref, gain_ref, base_ref, sum_ref, stats_ref):
+    def final(index, clip, span, result):
+        if values_ref is not None:
+            result, stats = norm_back(values_ref[clip, span], gain_ref[...], result)
+            for which, row in enumerate(stats):
+                row = row + stats_ref[which : which + 1] if index else row
+                stats_ref[which : which + 1] = row
+        result = base_ref[clip, span].astype(jnp.float32) + result
+        sum_ref[clip, span] = result.astype(sum_ref.dtype)
+
+    return final
+
+
+def terms_of(clips, rows, blocks, mat, span, terms):
+    def multiply(number):
+        block = blocks(number)
+        block = block.reshape(clips * rows, block.shape[-1])
+        for start, stop, product in dot_tiles(block, mat, span, True, 256 * 2):
+            terms[number, :, :, start:stop] = product.astype(terms.dtype).reshape(
+                clips, rows, stop - start
+            )
+
+    return multiply
+
+
+def dot_reduce_body(clips, rows, sub, window, span, back, left_ref, mat_ref, base_ref, *refs):
+    refs = list(refs)
+    take = lambda count: [refs.pop(0) for _ in range(count)]
+    values_ref, gain_ref = take(2) if back else (None, None)
+    sum_ref = take(1)[0]
+    stats_ref = take(1)[0] if back else None
+    left, mat, mat_sem, left_sem = take(4)
+    terms = refs[0]
+    place, depth, flip = plane_places()
+    load = pltpu.make_async_copy(mat_ref.at[:, pl.ds(*window)], mat, mat_sem)
     load.start()
     loads = {}
-    for number, slot in enumerate(order):
+    for number, slot in enumerate(plane_order()):
         loads[number] = [
             pltpu.make_async_copy(
                 left_ref.at[clip, slot], left.at[number, clip], left_sem.at[number, clip]
@@ -1337,208 +1653,277 @@
         ]
         for copy in loads[number]:
             copy.start()
-    if beside:
-        greet_cross(*beside)
-        going = outward_steps(*beside, kept_ref, own_ref, mid, *extra)
-        next(going)
-    else:
-        greet([(core, depth), (beside_x, depth), (beside_y, depth)])
-    chunks = [(clip, part) for clip in range(clips) for part in range(rows // sub)]
-    count = len(chunks)
-    half = count // 2
-    sends = []
-
-    def send(source, goal, recv_sem, device):
-        copy = remote(source, goal, send_sem.at[len(sends)], recv_sem, (device, depth))
-        copy.start()
-        sends.append(copy)
-
-    def arrived(block, recv_sem):
-        remote(block, block, send_sem.at[0], recv_sem, (core, depth)).wait_recv()
-
-    def term(number, index):
-        clip, part = chunks[index]
-        return terms.at[number, clip, pl.ds(part * sub, sub)]
-
-    def multiply(number):
+    greet([(flip(1), depth), (flip(2), depth), (flip(4), depth)])
+    load.wait()
+
+    def blocks(number):
         for copy in loads[number]:
             copy.wait()
-        block = left[number].reshape(clips * rows, left.shape[3])
-        for start, stop, product in dot_tiles(block, mat, True, 256 * 2):
-            terms[number, :, :, start:stop] = product.astype(terms.dtype).reshape(
-                clips, rows, stop - start
-            )
-
-    def give(number, chip):
-        for index in range(count):
-            send(term(number, index), pair.at[index, chip], core_sem.at[index, chip], core)
-
-    def total(*blocks):
-        return sum(block[...].astype(jnp.float32) for block in blocks)
-
-    numbers = {3: 1, 1: 3, 2: 5, 0: 7}
-
-    def combine(chip, index):
-        arrived(pair.at[index, chip], core_sem.at[index, chip])
-        held[index, chip] = total(term(numbers[chip], index), pair.at[index, chip]).astype(
-            held.dtype
-        )
-
-    load.wait()
-    multiply(0)
-    give(0, 3)
-    multiply(1)
-    multiply(2)
-    give(2, 1)
-    for low in range(half):
-        high = half + low
-        combine(3, low)
-        send(held.at[low, 3], turn.at[low], turn_sem.at[low], beside_x)
-        combine(3, high)
-        send(held.at[high, 3], turn.at[high], turn_sem.at[high], beside_y)
-    multiply(3)
-    multiply(4)
-    give(4, 2)
-    for low in range(half):
-        combine(1, low)
-        send(held.at[low, 1], from_x.at[low], x_sem.at[low], beside_x)
-    multiply(5)
-    for high in range(half, count):
-        combine(2, high)
-        send(held.at[high, 2], from_y.at[high], y_sem.at[high], beside_y)
-    multiply(6)
-    give(6, 0)
-    if beside:
-        next(going)
-    for low in range(half):
-        high = half + low
-        combine(2, low)
-        arrived(turn.at[low], turn_sem.at[low])
-        held[low, 2] = total(held.at[low, 2], turn.at[low]).astype(held.dtype)
-        send(held.at[low, 2], from_y.at[low], y_sem.at[low], beside_y)
-        combine(1, high)
-        arrived(turn.at[high], turn_sem.at[high])
-        held[high, 1] = total(held.at[high, 1], turn.at[high]).astype(held.dtype)
-        send(held.at[high, 1], from_x.at[high], x_sem.at[high], beside_x)
-    multiply(7)
-    for index in range(count):
-        clip, part = chunks[index]
-        span = pl.ds(part * sub, sub)
-        arrived(pair.at[index, 0], core_sem.at[index, 0])
-        arrived(from_x.at[index], x_sem.at[index])
-        arrived(from_y.at[index], y_sem.at[index])
-        result = total(term(7, index), pair.at[index, 0], from_x.at[index], from_y.at[index])
-        if added:
-            result = base_ref[clip, span] + result
-        sum_ref[clip, span] = result
-    if beside:
-        next(going)
-    for copy in sends:
-        copy.wait_send()
-
-
-def dot_reduce(left, matrix, clips, collective_id, base=None, kept_rows=None, sub=64):
-    wide, inner = matrix.shape
-    rows = left.shape[0] // (8 * clips)
-    count = clips * (rows // sub)
+        return left[number]
+
+    steps = reduce_steps(
+        clips,
+        rows,
+        sub,
+        terms_of(clips, rows, blocks, mat, span, terms),
+        final_back(values_ref, gain_ref, base_ref, sum_ref, stats_ref),
+        *refs,
+    )
+    for _ in steps:
+        pass
+
+
+def dot_reduce(left, matrix, clips, collective_id, base, span=None, back=None, kind=jnp.float32, sub=64):
+    wide = matrix.shape[0]
+    rows, inner = left.shape[0] // (8 * clips), left.shape[1]
     low = jnp.bfloat16
+    window, span = window_of(matrix, span)
     inside = pl.BlockSpec(memory_space=pltpu.VMEM)
-    args = [left.reshape(clips, 8, rows, inner), matrix]
-    in_specs = [any_spec(), any_spec()]
-    outs, out_specs = [jax.ShapeDtypeStruct((clips, rows, wide), jnp.float32)], [inside]
-    scratch = [
-        pltpu.VMEM((8, clips, rows, inner), low),
-        pltpu.VMEM(matrix.shape, low),
-        pltpu.VMEM((8, clips, rows, wide), low),
-        pltpu.VMEM((count, 4, sub, wide), low),
-        pltpu.VMEM((count, 4, sub, wide), low),
-        pltpu.VMEM((count, sub, wide), low),
-        pltpu.VMEM((count, sub, wide), low),
-        pltpu.VMEM((count, sub, wide), low),
-        DMA(()),
-        DMA((8, clips)),
-        DMA((7 * count,)),
-        DMA((count, 4)),
-        DMA((count,)),
-        DMA((count,)),
-        DMA((count,)),
-    ]
-    if base is not None:
-        args.append(base)
-        in_specs.append(inside)
-    beside = None
-    if kept_rows is not None:
-        per, planes, piece, _ = kept_rows.shape
-        beside = (per * planes, planes)
-        args.append(kept_rows)
-        in_specs.append(any_spec())
-        moved = jax.ShapeDtypeStruct((per * planes, piece, wide), kept_rows.dtype)
-        outs += [moved, moved]
-        out_specs += [any_spec(), any_spec()]
-        scratch += outward_scratch(*beside)
-    results = pl.pallas_call(
-        functools.partial(dot_reduce_body, clips, rows, sub, base is not None, beside),
+    args = [left.reshape(clips, 8, rows, inner), matrix, base]
+    in_specs = [any_spec(), any_spec(), inside]
+    outs, out_specs = [jax.ShapeDtypeStruct((clips, rows, wide), kind)], [inside]
+    if back is not None:
+        args += list(back)
+        in_specs += [inside] * 2
+        outs.append(jax.ShapeDtypeStruct((2, wide), jnp.float32))
+        out_specs.append(inside)
+    return pl.pallas_call(
+        functools.partial(dot_reduce_body, clips, rows, sub, window, span, back is not None),
         out_shape=outs,
         in_specs=in_specs,
         out_specs=out_specs,
-        scratch_shapes=scratch,
+        scratch_shapes=[
+            pltpu.VMEM((8, clips, rows, inner), low),
+            pltpu.VMEM((wide, window[1]), low),
+            DMA(()),
+            DMA((8, clips)),
+        ]
+        + reduce_scratch(clips, rows, sub, wide),
         compiler_params=communicating(collective_id),
     )(*args)
-    return results[0] if kept_rows is None else results[:2]
-
-
-def finish_body(planes, squares_ref, total_ref, blocks, block_send, block_recv):
+
+
+def ff_back_body(
+    group,
+    planes,
+    clips,
+    rows,
+    sub,
+    gates_ref,
+    gate_mat_ref,
+    hidden_ref,
+    down_ref,
+    normed_ref,
+    grads_ref,
+    base_ref,
+    values_ref,
+    gain_ref,
+    sum_ref,
+    stats_ref,
+    outer_ref,
+    own_ref,
+    mid,
+    gates,
+    gate_mat,
+    hidden,
+    down,
+    normed,
+    grads,
+    stage,
+    kept,
+    load_sem,
+    gates_sem,
+    tile_sem,
+    stage_sem,
+    *refs,
+):
+    refs = list(refs)
+    first_refs, second_refs, sems = refs[:10], refs[10:20], refs[20:]
     place, depth, flip = plane_places()
-    devices = [(flip(mask), lax.rem(depth + step, planes)) for mask, step in everyone(planes)]
-    greet(devices)
-    here = place * planes + depth
-    copies = []
-    blocks[here] = squares_ref[...]
-    for index, (other, plane) in enumerate(devices):
-        copy = remote(
-            squares_ref,
-            blocks.at[here],
-            block_send.at[index],
-            block_recv.at[here],
-            (other, plane),
-        )
+    order = plane_order()
+    loads = [
+        pltpu.make_async_copy(down_ref, down, load_sem.at[0]),
+        pltpu.make_async_copy(hidden_ref, hidden, load_sem.at[1]),
+        pltpu.make_async_copy(gate_mat_ref, gate_mat, load_sem.at[2]),
+    ]
+    for copy in loads:
         copy.start()
-        copies.append(copy)
-    for other, plane in devices:
-        source = other * planes + plane
-        one = blocks.at[source]
-        remote(one, one, block_send.at[0], block_recv.at[source], (other, plane)).wait_recv()
-    total_ref[...] = jnp.sum(blocks[...], axis=0)
-    for copy in copies:
-        copy.wait_send()
-
-
-def finish(squares, planes, collective_id):
-    count = 8 * planes
-    whole = pl.BlockSpec(memory_space=pltpu.VMEM)
-    return pl.pallas_call(
-        functools.partial(finish_body, planes),
-        out_shape=jax.ShapeDtypeStruct(squares.shape, jnp.float32),
-        in_specs=[whole],
-        out_specs=whole,
+    gate_loads = {}
+    for number, slot in enumerate(order):
+        gate_loads[number] = [
+            pltpu.make_async_copy(
+                gates_ref.at[clip, slot], gates.at[clip, slot], gates_sem.at[number, clip]
+            )
+            for clip in range(clips)
+        ]
+        for copy in gate_loads[number]:
+            copy.start()
+    tile = stage.shape[1]
+    tiles = normed_ref.shape[3] // tile
+    total_rows = 8 * clips * rows
+    inner = gates.shape[3]
+
+    def fetch(index):
+        lanes = pl.ds(pl.multiple_of(index * tile, tile), tile)
+        spot = lax.rem(index, 2)
+        return [
+            pltpu.make_async_copy(
+                source.at[:, :, :, lanes], goal.at[spot], tile_sem.at[which, spot]
+            )
+            for which, (source, goal) in enumerate(((normed_ref, normed), (grads_ref, grads)))
+        ]
+
+    def stored(index):
+        there = outer_ref.at[pl.ds(pl.multiple_of(index * tile, tile), tile)]
+        spot = lax.rem(index, 2)
+        return pltpu.make_async_copy(stage.at[spot], there, stage_sem.at[spot])
+
+    def outer_tiles(first, last):
+        def one(index, carry):
+            spot = lax.rem(index, 2)
+
+            @pl.when(index >= 2)
+            def _():
+                stored(index - 2).wait()
+
+            for copy in fetch(index):
+                copy.wait()
+            stage[spot, :, :inner] = outer_sum(
+                normed[spot].reshape(total_rows, tile), gates[...].reshape(total_rows, inner)
+            ).astype(stage.dtype)
+            stage[spot, :, inner:] = outer_sum(
+                grads[spot].reshape(total_rows, tile),
+                hidden[...].reshape(total_rows, hidden.shape[3]),
+            ).astype(stage.dtype)
+            stored(index).start()
+
+            @pl.when(index + 2 < tiles)
+            def _():
+                for copy in fetch(index + 2):
+                    copy.start()
+
+            return carry
+
+        lax.fori_loop(first, last, one, 0)
+
+    for index in range(2):
+        for copy in fetch(index):
+            copy.start()
+    greet_cross(group, planes)
+    loads[0].wait()
+    loads[1].wait()
+    piece = kept.shape[2]
+
+    def layer_rows(index, clip, span, result):
+        result = (values_ref[clip, span] + result).astype(kept.dtype)
+        start = index % (rows // sub) * sub
+        for part in range(sub // piece):
+            kept[clip, start // piece + part] = result[part * piece : part * piece + piece]
+
+    first = reduce_steps(
+        clips,
+        rows,
+        sub,
+        terms_of(
+            clips, rows, lambda number: hidden[order[number]], down, (0, down.shape[1]), first_refs[0]
+        ),
+        layer_rows,
+        *first_refs,
+    )
+
+    def gate_rows(number):
+        for copy in gate_loads[number]:
+            copy.wait()
+        return gates[:, order[number]]
+
+    second = reduce_steps(
+        clips,
+        rows,
+        sub,
+        terms_of(clips, rows, gate_rows, gate_mat, (0, inner), second_refs[0]),
+        final_back(values_ref, gain_ref, base_ref, sum_ref, stats_ref),
+        *second_refs,
+    )
+    next(first)
+    loads[2].wait()
+    next(second)
+    next(first)
+    outer_tiles(0, 2)
+    next(first)
+    going = outward_steps(group, planes, kept, own_ref, mid, *sems)
+    next(going)
+    next(second)
+    outer_tiles(2, tiles)
+    next(going)
+    next(second)
+    next(going)
+    for index in range(max(tiles - 2, 0), tiles):
+        stored(index).wait()
+    next(first)
+    next(second)
+
+
+def ff_back(gates, gate_mat, hidden, down, normed, grads, base, values, gain, planes, collective_id, sub=64):
+    clips, rows, wide = base.shape
+    group = 8
+    piece = rows // planes
+    low = jnp.bfloat16
+    inner, columns = gates.shape[1], gates.shape[1] + hidden.shape[1]
+    tile = 256
+    inside = pl.BlockSpec(memory_space=pltpu.VMEM)
+    moved = jax.ShapeDtypeStruct((group, piece, wide), low)
+    *results, _ = pl.pallas_call(
+        functools.partial(ff_back_body, group, planes, clips, rows, sub),
+        out_shape=[
+            jax.ShapeDtypeStruct((clips, rows, wide), jnp.float32),
+            jax.ShapeDtypeStruct((2, wide), jnp.float32),
+            jax.ShapeDtypeStruct((wide, columns), low),
+            moved,
+            moved,
+        ],
+        in_specs=[any_spec()] * 6 + [inside] * 3,
+        out_specs=[inside] * 2 + [any_spec()] * 3,
         scratch_shapes=[
-            pltpu.VMEM((count,) + squares.shape, jnp.float32),
-            DMA((count,)),
-            DMA((count,)),
-        ],
+            pltpu.VMEM((clips, 8, rows, inner), low),
+            pltpu.VMEM(gate_mat.shape, low),
+            pltpu.VMEM((8, clips, rows, hidden.shape[1]), low),
+            pltpu.VMEM(down.shape, low),
+            pltpu.VMEM((2, clips, 8, rows, tile), low),
+            pltpu.VMEM((2, 8, clips, rows, tile), low),
+            pltpu.VMEM((2, tile, columns), low),
+            pltpu.VMEM((clips, planes, piece, wide), low),
+            DMA((3,)),
+            DMA((8, clips)),
+            DMA((2, 2)),
+            DMA((2,)),
+        ]
+        + reduce_scratch(clips, rows, sub, wide) * 2
+        + outward_scratch(group, planes),
         compiler_params=communicating(collective_id),
-    )(squares)
+    )(
+        gates.reshape(clips, 8, rows, inner),
+        gate_mat,
+        hidden.reshape(8, clips, rows, hidden.shape[1]),
+        down,
+        normed.reshape(clips, 8, rows, wide),
+        grads.reshape(8, clips, rows, wide),
+        base,
+        values,
+        gain,
+    )
+    return results
 
 
 def rotary_lanes(places):
-    cosine, sine = rotary_tables(places, HDIM)
-    cosine, sine = cosine[:, 0], sine[:, 0]
-    return jnp.stack(
-        [
-            jnp.concatenate([cosine] * 4, axis=1),
-            jnp.concatenate([-sine, sine, -sine, sine], axis=1),
-        ]
-    )
+    half = HDIM // 2
+    frequency = 10000.0 ** (-np.arange(half, dtype=np.float32) / np.float32(half))
+    angles = places.astype(np.float32)[:, None] * frequency.astype(np.float32)[None, :]
+    cosine, sine = np.cos(angles), np.sin(angles)
+    both = [
+        np.concatenate([cosine] * 4, axis=1),
+        np.concatenate([-sine, sine, -sine, sine], axis=1),
+    ]
+    return jnp.asarray(np.stack(both).astype(np.float32))
 
 
 def turn_heads(values, cosine, sine):
@@ -1849,52 +2234,10 @@
     return grads, stamp_grads[:, 0], mine
 
 
-def ff_outer_body(normed_ref, gates_ref, grads_ref, hidden_ref, out_ref):
-    last = pl.program_id(0) == pl.num_programs(0) - 1
-
-    @pl.when(jnp.logical_not(last))
-    def _():
-        out_ref[...] = outer_sum(normed_ref[...], gates_ref[...]).astype(out_ref.dtype)
-
-    @pl.when(last)
-    def _():
-        out_ref[...] = outer_sum(grads_ref[...], hidden_ref[...]).astype(out_ref.dtype)
-
-
-def ff_outer(normed, gates, grads, hidden):
-    rows, wide = normed.shape
-    width = hidden.shape[1]
-    tile = wide // 3
-    ends = gates.shape[1] // width
-    return pl.pallas_call(
-        ff_outer_body,
-        grid=(ends + 1, wide // tile),
-        out_shape=jax.ShapeDtypeStruct((wide, (ends + 1) * width), jnp.bfloat16),
-        in_specs=[
-            pl.BlockSpec(
-                (rows, tile), lambda n, m: (0, jnp.where(n < ends, m, wide // tile - 1))
-            ),
-            pl.BlockSpec((rows, width), lambda n, m: (0, jnp.minimum(n, ends - 1))),
-            pl.BlockSpec((rows, tile), lambda n, m: (0, jnp.where(n < ends, 0, m))),
-            pl.BlockSpec((rows, width), lambda n, m: (0, 0)),
-        ],
-        out_specs=pl.BlockSpec((tile, width), lambda n, m: (m, n)),
-        compiler_params=pltpu.CompilerParams(vmem_limit_bytes=VMEM_LIMIT),
-    )(normed, gates, grads, hidden)
-
-
-def adam_body(split, factor_ref, weight_ref, first_ref, second_ref, grad_ref, *outs):
-    parts, _, held = grad_ref.shape
-    width = held // split
-    choices = [
-        jnp.concatenate(
-            [grad_ref[part, :, side * width : (side + 1) * width] for part in range(parts)], axis=1
-        ).astype(jnp.float32)
-        for side in range(split)
-    ]
-    gradient = choices[0]
-    for side in range(1, split):
-        gradient = jnp.where(lax.rem(pl.program_id(0), split) == side, choices[side], gradient)
+def adam_body(factor_ref, weight_ref, first_ref, second_ref, grad_ref, *outs):
+    gradient = jnp.concatenate(
+        [grad_ref[part] for part in range(grad_ref.shape[0])], axis=1
+    ).astype(jnp.float32)
     results = adam_step(
         weight_ref[...],
         first_ref[...],
@@ -1907,18 +2250,56 @@
         out[...] = result
 
 
-def adam_matrix(factor, weight, first, second, owned, width, split, parts):
+def adam_blocks_body(places, factor_ref, weight_ref, first_ref, second_ref, *refs):
+    *owned_refs, weight_out, first_out, second_out = refs
+    for block, (which, start, stop) in enumerate(places):
+
+        @pl.when(pl.program_id(0) == block)
+        def _(owned_ref=owned_refs[which], start=start, stop=stop):
+            gradient = jnp.concatenate(
+                [owned_ref[part, :, start:stop] for part in range(owned_ref.shape[0])], axis=1
+            ).astype(jnp.float32)
+            results = adam_step(
+                weight_ref[...],
+                first_ref[...],
+                second_ref[...],
+                gradient * factor_ref[0, 0],
+                matrix_rate,
+                matrix_decay,
+            )
+            weight_out[...], first_out[...], second_out[...] = results
+
+
+def adam_blocks(factor, weight, first, second, owned, width):
+    rows, columns = weight.shape
+    group = owned[0].shape[0]
+    blocks = columns // (group * width)
+    places = [
+        (which, start, start + width)
+        for which, pieces in enumerate(owned)
+        for start in range(0, pieces.shape[2], width)
+    ][:blocks]
+    piece = pl.BlockSpec((rows, group * width), lambda block: (0, block))
+    whole = [pl.BlockSpec(pieces.shape, lambda block: (0, 0, 0)) for pieces in owned]
+    return pl.pallas_call(
+        functools.partial(adam_blocks_body, places),
+        grid=(blocks,),
+        out_shape=[jax.ShapeDtypeStruct(weight.shape, jnp.float32)] * 3,
+        in_specs=[pl.BlockSpec(memory_space=pltpu.SMEM), piece, piece, piece] + whole,
+        out_specs=[piece] * 3,
+        compiler_params=pltpu.CompilerParams(vmem_limit_bytes=VMEM_LIMIT),
+    )(factor, weight, first, second, *owned)
+
+
+def adam_matrix(factor, weight, first, second, owned, width, parts):
     rows, columns = weight.shape
     group = owned.shape[0]
-    blocks = columns // (group * width)
     steps = group // parts
     piece = pl.BlockSpec((rows, parts * width), lambda block, step: (0, block * steps + step))
-    grads = pl.BlockSpec(
-        (parts, rows, split * width), lambda block, step: (step, 0, block // split)
-    )
+    grads = pl.BlockSpec((parts, rows, width), lambda block, step: (step, 0, block))
     return pl.pallas_call(
-        functools.partial(adam_body, split),
-        grid=(blocks, steps),
+        adam_body,
+        grid=(columns // (group * width), steps),
         out_shape=[jax.ShapeDtypeStruct(weight.shape, jnp.float32)] * 3,
         in_specs=[pl.BlockSpec(memory_space=pltpu.SMEM), piece, piece, piece, grads],
         out_specs=[piece] * 3,
@@ -2003,9 +2384,9 @@
 
     w_qkv = over_planes(qkv_mine)
     w_rest = over_planes(rest_mine)
-    w_self_out = w_rest[:, :head_wide]
-    w_cross_query = w_rest[:, head_wide : 2 * head_wide]
-    w_cross_out = w_rest[:, 2 * head_wide : 3 * head_wide]
+    of_self_out = (0, head_wide)
+    of_cross_query = (head_wide, 2 * head_wide)
+    of_cross_out = (2 * head_wide, 3 * head_wide)
     w_cond = w_rest[:, 3 * head_wide :].reshape(planes, group, cond_owned, -1)
     w_cond = jnp.swapaxes(w_cond, 0, 1).reshape(cond_wide, 2 * head_wide)
     plane_packs = lax.dynamic_slice_in_dim(packs, depth * clips, clips, axis=0)
@@ -2026,7 +2407,7 @@
     masked = to_plane_order((cotangent * frame_valid[..., None])[0])
 
     group_rows = clips * seq_frames
-    row_place = jnp.arange(seq_frames)
+    row_place = np.arange(seq_frames)
     row_owner, row_rest = row_place // own_rows, row_place % own_rows
     true_place = (row_rest // piece) * frame_rows + row_owner * piece + row_rest % piece
     key_keep = true_place[None, :] < clip_lengths[:, None]
@@ -2054,75 +2435,70 @@
     grad_out = grad_out_low.astype(jnp.float32)
     w_gate_up = over_planes(gate_up_mine)
     w_down = over_planes(down_mine)
-    resid_one = dot_reduce(self_low, w_self_out, clips, 6, stream)
-    group_two, cross_query = gather_dot(
-        resid_one, w_cross_query, jnp.bfloat16, 7, gain_rows[2:4]
-    )
-    cross_query = cross_query.reshape(group_shape)
     cond_pair = jnp.dot(cond_flat, w_cond, preferred_element_type=jnp.float32)
-    cond_pair = cond_pair.astype(jnp.bfloat16)
-    cond_shape = (clips, cond_count, heads, HDIM)
-    cross_keys = cond_pair[:, :head_wide].reshape(cond_shape)
-    cross_values = cond_pair[:, head_wide:].reshape(cond_shape)
-    cross_mixed, cross_lse = cross_forward(cross_query, cross_keys, cross_values, cond_keep)
-    cross_out = cross_mixed.astype(jnp.bfloat16).reshape(group_rows, head_wide)
-    resid_two = dot_reduce(cross_out, w_cross_out, clips, 8, resid_one)
+    cond_pair = cond_pair.astype(jnp.bfloat16).reshape(clips, cond_count, 2 * head_wide)
+    cond_bias = jnp.where(cond_keep, 0.0, masked_score)[:, None]
+    (resid_one,) = dot_reduce(self_low, w_rest, clips, 6, stream, of_self_out)
+    group_two, cross_query, cross_out = gather_dot(
+        resid_one,
+        w_rest,
+        None,
+        7,
+        gain_rows[2:4],
+        span=of_cross_query,
+        pair=cond_pair,
+        bias=cond_bias,
+    )
+    (resid_two,) = dot_reduce(cross_out, w_rest, clips, 8, resid_one, of_cross_out)
     group_three, gate_up = gather_dot(resid_two, w_gate_up, jnp.float32, 9, gain_rows[4:6])
     gate_up, grad_out_low = lax.optimization_barrier((gate_up, grad_out_low))
     group_grad_out, grad_gate_up, hidden = gather_dot(
         grad_out_low, w_down, None, 10, gate_up=gate_up
     )
-    branch = lax.psum_scatter(
-        times_transposed(hidden, w_down)
-        .astype(jnp.bfloat16)
-        .reshape(group, clips, own_rows, wide),
-        "dp",
-        scatter_dimension=0,
-        tiled=False,
-    )
-    layer_rows = (resid_two + branch.astype(jnp.float32)).astype(jnp.bfloat16)
-
     def over_rows(block):
         return lax.psum_scatter(
             block.astype(jnp.bfloat16), "seq", scatter_dimension=0, tiled=True
         ).reshape(group, owned, -1)
 
-    ff_piece = ff_outer(group_three, grad_gate_up, group_grad_out, hidden)
-    grad_gate_up, ff_piece = lax.optimization_barrier((grad_gate_up, ff_piece))
-    ff_rows = over_rows(ff_piece)
-    grad_normed_three = dot_reduce(grad_gate_up, w_gate_up, clips, 13)
-
-    _, norm_three_back = jax.vjp(layer_norm, resid_two, gain_rows[4], gain_rows[5])
-    grad_two_part, grad_gain_three, grad_bias_three = norm_three_back(grad_normed_three)
-    grad_two = grad_out + grad_two_part
-    group_cross_branch, grad_cross_mixed = gather_dot(
-        grad_two.astype(jnp.bfloat16), w_cross_out, jnp.bfloat16, 15
-    )
-    grad_cross_mixed = grad_cross_mixed.reshape(group_shape)
-    grad_cross_query, grad_cross_keys, grad_cross_values = cross_backward(
-        cross_query, cross_keys, cross_values, cond_keep, cross_lse, grad_cross_mixed
-    )
-    grad_cross_query = grad_cross_query.astype(jnp.bfloat16).reshape(group_rows, head_wide)
-    grad_normed_two = dot_reduce(grad_cross_query, w_cross_query, clips, 16)
-    _, norm_two_back = jax.vjp(layer_norm, resid_one, gain_rows[2], gain_rows[3])
-    grad_one_part, grad_gain_two, grad_bias_two = norm_two_back(grad_normed_two)
-    grad_one = grad_two + grad_one_part
-    group_self_branch, grad_self_mixed, layer_out = gather_dot(
-        grad_one.astype(jnp.bfloat16),
-        w_self_out,
-        jnp.bfloat16,
-        17,
-        kept_rows=layer_rows.reshape(clips, planes, piece, wide),
+    grad_two, stats_three, ff_piece, layer_out = ff_back(
+        grad_gate_up,
+        w_gate_up,
+        hidden,
+        w_down,
+        group_three,
+        group_grad_out,
+        grad_out_low,
+        resid_two,
+        gain_rows[4:5],
+        planes,
+        13,
     )
     layer_out = to_whole_order(layer_out.reshape(frame_rows, wide)).astype(jnp.bfloat16)
     layer_out = layer_out.reshape(frames.shape)
-    cond_grad = jnp.concatenate(
-        [
-            grad_cross_keys.reshape(clips * cond_count, head_wide),
-            grad_cross_values.reshape(clips * cond_count, head_wide),
-        ],
-        axis=1,
-    )
+    ff_rows = over_rows(ff_piece)
+    group_cross_branch, grad_cross_query, cond_grad = gather_dot(
+        grad_two,
+        w_rest,
+        None,
+        15,
+        span=of_cross_out,
+        pair=cond_pair,
+        bias=cond_bias,
+        query=cross_query,
+    )
+    grad_one, stats_two = dot_reduce(
+        grad_cross_query,
+        w_rest,
+        clips,
+        16,
+        grad_two,
+        of_cross_query,
+        back=(resid_one, gain_rows[2:3]),
+    )
+    group_self_branch, grad_self_mixed = gather_dot(
+        grad_one, w_rest, jnp.bfloat16, 17, span=of_self_out
+    )
+    cond_grad = cond_grad.reshape(clips * cond_count, 2 * head_wide)
     cross_piece = split_outer(cond_flat, cond_grad)
     cross_piece = cross_piece.reshape(group, planes, cond_owned, 2 * head_wide)
     cross_piece = jnp.swapaxes(cross_piece, 0, 1).reshape(wide, head_wide)
@@ -2152,46 +2528,41 @@
     grad_project, qkv_piece = lax.optimization_barrier((grad_project, qkv_piece))
     qkv_rows = over_rows(qkv_piece)
     grad_project, rest_rows = lax.optimization_barrier((grad_project, rest_rows))
-    grad_normed_one = dot_reduce(grad_project, w_qkv, clips, 18)
-    _, norm_one_back = jax.vjp(layer_norm, stream, gain_rows[0], gain_rows[1])
-    grad_zero_part, grad_gain_one, grad_bias_one = norm_one_back(grad_normed_one)
+    frames_grad, stats_one = dot_reduce(
+        grad_project,
+        w_qkv,
+        clips,
+        18,
+        grad_one,
+        back=(stream, gain_rows[0:1]),
+        kind=jnp.bfloat16,
+    )
     _, norm_stamp_back = jax.vjp(layer_norm, stamps, gain_rows[0], gain_rows[1])
     _, grad_gain_stamp, grad_bias_stamp = norm_stamp_back(grad_stamp_normed)
-    frames_grad = (grad_one + grad_zero_part).astype(jnp.bfloat16)
-    norm_grad = jnp.stack(
-        [
-            grad_gain_one + grad_gain_stamp,
-            grad_bias_one + grad_bias_stamp,
-            grad_gain_two,
-            grad_bias_two,
-            grad_gain_three,
-            grad_bias_three,
-        ],
-        axis=0,
-    )
+    stamp_stats = jnp.stack([grad_gain_stamp, grad_bias_stamp])
+    norm_grad = jnp.concatenate([stats_one + stamp_stats, stats_two, stats_three], axis=0)
     norm_parts = norm_grad.reshape(6, planes, group, owned).transpose(2, 1, 0, 3)
     norm_parts = norm_parts.reshape(group * planes, 6, owned)
     norm_parts = jnp.pad(norm_parts, ((0, 0), (0, 2), (0, 128 - owned)))
-    frames_grad, attn_owned, norm_sum = leave(
+    ff_squares = jnp.sum(jnp.square(ff_owned.astype(jnp.float32)))
+    frames_grad, qkv_owned, rest_owned, norm_sum, total = leave(
         frames_grad.reshape(clips, planes, piece, wide),
-        jnp.concatenate([qkv_rows, rest_rows], axis=2),
+        qkv_rows,
+        rest_rows,
         norm_parts,
+        ff_squares.reshape(1, 1),
         20,
     )
     frames_grad = to_whole_order(frames_grad.reshape(frame_rows, wide)).reshape(frames.shape)
-    cross_reduced = attn_owned[:, :, 6 * head_wide :].reshape(group, cond_owned, 2, head_wide)
+    cross_reduced = rest_owned[:, :, 3 * head_wide :].reshape(group, cond_owned, 2, head_wide)
     cross_reduced = cross_reduced.transpose(1, 2, 0, 3).reshape(cross_weight.shape)
     cross_reduced = cross_reduced.astype(jnp.float32)
-    squares = jnp.sum(jnp.square(attn_owned.astype(jnp.float32)))
-    squares = squares + jnp.sum(jnp.square(ff_owned.astype(jnp.float32)))
-    squares = squares + jnp.sum(jnp.square(norm_sum))
-    total = finish(jnp.broadcast_to(squares, (8, 128)), planes, 21)
     norm_reduced = norm_sum[:6, :owned]
     grad_norm = jnp.sqrt(total[0, 0])
     factor = jnp.minimum(1.0, clip_limit / grad_norm)
     factor_block = factor.reshape(1, 1)
-    attn_new, attn_first_new, attn_second_new = adam_matrix(
-        factor_block, attn_weight, attn_first, attn_second, attn_owned, head_wide, 2, group
+    attn_new, attn_first_new, attn_second_new = adam_blocks(
+        factor_block, attn_weight, attn_first, attn_second, [qkv_owned, rest_owned], head_wide
     )
     cross_new, cross_first_new, cross_second_new = adam_step(
         cross_weight, cross_first, cross_second, cross_reduced * factor, matrix_rate, matrix_decay
@@ -2200,7 +2571,7 @@
         norm_param, norm_first, norm_second, norm_reduced * factor, gain_rate, 0.0
     )
     ff_new, ff_first_new, ff_second_new = adam_matrix(
-        factor_block, ff_weight, ff_first, ff_second, ff_owned, ff_wide, 1, group // 2
+        factor_block, ff_weight, ff_first, ff_second, ff_owned, ff_wide, group // 2
     )
     return (
         layer_out,

time: 816 us -> 741 us (0.908)
  local copies, waits for them, and re-layouts: 61 us -> 25.1 us
  other arithmetic: 50.4 us -> 19.6 us
  matrix products: 55.5 us -> 36.5 us
  Pallas kernels: 617 us -> 626 us
    reduce_sum x12 -> x1, other arithmetic: 18.9 us -> 1.51 us  [plane_device(): ff_squares = jnp.sum(jnp.square(ff_owned.astype(jnp.float32)))]
    pallas_call x6, Pallas kernels: 234 us -> 218 us  [gather_dot(): pl.pallas_call(functools.partial(gather_dot_body, clips, rows, sub, gains...]
    pallas_call x9 -> x7, Pallas kernels: 233 us -> 248 us  [the longest x4 144 us: dot_reduce(): pl.pallas_call(functools.partial(dot_reduce_body, clips, rows, sub, windo...]
    dot_general x5 -> x4, matrix products: 18.8 us -> 7.1 us  [times_transposed(): lax.dot_general(left_mat, right_mat, (((1,), (1,)), ((), ())), preferred_...]
    unnamed x159 -> x66, local copies, waits for them, and re-layouts: 16.5 us -> 5.24 us
    another operation x10 -> x1, local copies, waits for them, and re-layouts: 9.35 us -> 0.92 us  [the longest x2 4.76 us: dot_reduce(): args = [left.reshape(clips, 8, rows, inner), matrix]]
  transfers between devices with their start and end apart: 8 -> 7, of which waited for: 0 -> 2; matrix products, arithmetic and copies ran while one was open for 15% -> 8% of each run, Pallas kernels for 60% -> 56%
where the time goes in v4:
time: 741 us; the launch traced here: 734 us
  Pallas kernels  626 us (84%)
  matrix products  36.5 us (5%)
  local copies, waits for them, and re-layouts  25.1 us (3%)
  other arithmetic  19.6 us (3%)
  between operations  17.7 us (2%)
  waiting for transfers between devices  7.49 us (1%)
    pallas_call x6, Pallas kernels, gather_dot(): pl.pallas_call(functools.partial(gather_dot_body, clips, rows, sub, gains...  218 us
    pallas_call x4, Pallas kernels, dot_reduce(): pl.pallas_call(functools.partial(dot_reduce_body, clips, rows, sub, windo...  144 us
    pallas_call x1, Pallas kernels, ff_back(): pl.pallas_call(functools.partial(ff_back_body, group, planes, clips, rows...  86.3 us
    pallas_call x1, Pallas kernels, flash_forward(): pl.pallas_call(functools.partial(flash_forward_body, heads, rows // 4), g...  52.8 us
    pallas_call x1, Pallas kernels, leave(): pl.pallas_call(functools.partial(leave_body, group, planes), out_shape=[l...  40.5 us
    pallas_call x1, Pallas kernels, enter(): pl.pallas_call(functools.partial(enter_body, group, planes), out_shape=[l...  36.8 us
    pallas_call x1, Pallas kernels, flash_backward(): pl.pallas_call(functools.partial(flash_backward_body, heads, rows // 4),...  29.8 us
    dot_general x8, matrix products, outer_sum(): lax.dot_general(left_mat, right_mat, (((0,), (0,)), ((), ())), preferred_...  19 us
  transfers between devices with their start and end apart: 7, of which 2 were waited for; matrix products, arithmetic and copies ran while one was open for 8% of the time, Pallas kernels for 56%

profile of v4, /device:TPU:9, one launch (start us, length us, event | category | flops | bytes accessed | tf_op | source)
XLA Modules:
  0.0 734.2 jit_solution(1867070419615063974)
XLA Ops:
  19.0 36.8 %shard_map.319 = (bf16[2,4,32,1536]{3,2,1,0:T(8,128)(2,1)}, f32[8,1536]{1,0:T(8,128)}, f32[8,8,1536]{2,1,0:T(8,128)}, bf16[8,48,576]{2,1,0:T(8,128)(2,1)}, bf16[...) custom-call(bf16[8,32,1536]{2,1,0:T(8,128)(2,1)} %bitcast.144, f32[8,128]{1,0:T(8,128)} %pad_convert_fusion.norm_ref, ...), custom_call_target="tpu_custom_call" | custom-call | tf_op jit(solution)/shard_map/pallas_call | solution.py:936
  58.0 3.4 convert_element_type.151.ff_ref
  61.4 4.9 gather_fusion
  69.1 40.3 %shard_map.320 = (bf16[2,8,128,1536]{3,2,1,0:T(8,128)(2,1)}, bf16[8,2,16,768]{3,2,1,0:T(8,128)(2,1)}) custom-call(f32[2,128,1536]{2,1,0:T(8,128)} %bitcast_convert_fusion.own_ref.base_ref.refs_0_, f32[2,1536]{1,0:T(2,128)} %get-tuple-element.152.refs_0_, bf16[4,2,16,768]{3,2,1,0:T(8,128)(2,1)} %select_select_fusion.refs_1_), custom_call_target="tpu_custom_call" | custom-call | tf_op jit(solution)/shard_map/pallas_call | solution.py:1470
  119.9 52.8 %shard_map.321 = (bf16[2048,576]{1,0:T(8,128)(2,1)}, bf16[2048,192]{1,0:T(8,128)(2,1)}, f32[2048,128]{1,0:T(8,128)}, bf16[8,48,1536]{2,1,0:T(8,128)(2,1)}, bf16[...) custom-call(bf16[2048,1536]{1,0:T(8,128)(2,1)} %bitcast.118, ...), custom_call_target="tpu_custom_call" | custom-call | tf_op jit(solution)/shard_map/pallas_call | solution.py:2089
  177.1 35.2 %shard_map.322.own_ref.base_ref.refs_0_ = f32[2,128,1536]{2,1,0:T(8,128)} custom-call(bf16[2,8,128,192]{3,2,1,0:T(8,128)(2,1)} %bitcast.136, bf16[1536,768]{1,0:T(8,128)(2,1)} %all-gather.7.cloned.1.call-done.mat_ref.refs_1_.refs_0_, f32[2,128,1536]{2,1,0:T(8,128)} %bitcast_convert_fusion.own_ref.base_ref.refs_0_), custom_call_target="tpu_custom_call" | custom-call | tf_op jit(solution)/shard_map/pallas_call | solution.py:1690
  213.4 35.8 %shard_map.323 = (bf16[2,8,128,1536]{3,2,1,0:T(8,128)(2,1)}, bf16[2,8,128,192]{3,2,1,0:T(8,128)(2,1)}, bf16[2,8,128,192]{3,2,1,0:T(8,128)(2,1)}) custom-call(f32[2,128,1536]{2,1,0:T(8,128)} %shard_map.322.own_ref.base_ref.refs_0_, f32[2,1536]{1,0:T(2,128)} %get-tuple-element.151.refs_0_, ...), custom_call_target="tpu_custom_call" | custom-call | tf_op jit(solution)/shard_map/pallas_call | solution.py:1470
  249.2 35.4 %shard_map.324.own_ref.values_ref = f32[2,128,1536]{2,1,0:T(8,128)} custom-call(bf16[2,8,128,192]{3,2,1,0:T(8,128)(2,1)} %get-tuple-element.81.left_ref, bf16[1536,768]{1,0:T(8,128)(2,1)} %all-gather.7.cloned.1.call-done.mat_ref.refs_1_.refs_0_, f32[2,128,1536]{2,1,0:T(8,128)} %shard_map.322.own_ref.base_ref.refs_0_), custom_call_target="tpu_custom_call" | custom-call | tf_op jit(solution)/shard_map/pallas_call | solution.py:1690
  284.6 37.3 %shard_map.325 = (bf16[2,8,128,1536]{3,2,1,0:T(8,128)(2,1)}, f32[2,8,128,1536]{3,2,1,0:T(8,128)}) custom-call(f32[2,128,1536]{2,1,0:T(8,128)} %shard_map.324.own_ref.values_ref, f32[2,1536]{1,0:T(2,128)} %get-tuple-element.150.refs_0_, bf16[1536,1536]{1,0:T(8,128)(2,1)} %all-gather.9.cloned.1.call-done.refs_1_.gate_mat_ref), custom_call_target="tpu_custom_call" | custom-call | tf_op jit(solution)/shard_map/pallas_call | solution.py:1470
  321.9 34.4 %shard_map.326 = (bf16[8,2,128,1536]{3,2,1,0:T(8,128)(2,1)}, bf16[2,8,128,1536]{3,2,1,0:T(8,128)(2,1)}, bf16[8,2,128,768]{3,2,1,0:T(8,128)(2,1)}) custom-call(bf16[2,128,1536]{2,1,0:T(8,128)(2,1)} %bitcast.124, bf16[1536,768]{1,0:T(8,128)(2,1)} %all-gather.11.cloned.1.call-done.refs_0_.down_ref, f32[2,8,128,1536]{3,2,1,0:T(8,128)} %get-tuple-element.83), custom_call_target="tpu_custom_call" | custom-call | tf_op jit(solution)/shard_map/pallas_call | solution.py:1470
  356.3 86.3 %shard_map.327 = (f32[2,128,1536]{2,1,0:T(8,128)}, f32[2,1536]{1,0:T(2,128)}, bf16[1536,2304]{1,0:T(8,128)(2,1)}, bf16[8,32,1536]{2,1,0:T(8,128)(2,1)}, bf16[8,32,1536]{2,1,0:T(8,128)(2,1)}) custom-call(bf16[2,8,128,1536]{3,2,1,0:T(8,128)(2,1)} %get-tuple-element.88.gates_ref, bf16[1536,1536]{1,0:T(8,128)(2,1)} %all-gather.9.cloned.1.call-done.refs_1_.gate_mat_ref, ...), custom_call_target="tpu_custom_call" | custom-call | tf_op jit(solution)/shard_map/pallas_call | solution.py:1875
  443.0 37.1 %shard_map.328 = (bf16[2,8,128,1536]{3,2,1,0:T(8,128)(2,1)}, bf16[2,8,128,192]{3,2,1,0:T(8,128)(2,1)}, f32[2,128,384]{2,1,0:T(8,128)}) custom-call(f32[2,128,1536]{2,1,0:T(8,128)} %get-tuple-element.94.own_ref.base_ref, bf16[1536,768]{1,0:T(8,128)(2,1)} %all-gather.7.cloned.1.call-done.mat_ref.refs_1_.refs_0_, bf16[2,128,384]{2,1,0:T(8,128)(2,1)} %bitcast.132, ...), custom_call_target="tpu_custom_call" | custom-call | tf_op jit(solution)/shard_map/pallas_call | solution.py:1470
  483.7 36.0 %shard_map.329 = (f32[2,128,1536]{2,1,0:T(8,128)}, f32[2,1536]{1,0:T(2,128)}) custom-call(bf16[2,8,128,192]{3,2,1,0:T(8,128)(2,1)} %get-tuple-element.96.left_ref, bf16[1536,768]{1,0:T(8,128)(2,1)} %all-gather.7.cloned.1.call-done.mat_ref.refs_1_.refs_0_, f32[2,128,1536]{2,1,0:T(8,128)} %get-tuple-element.94.own_ref.base_ref, ...), custom_call_target="tpu_custom_call" | custom-call | tf_op jit(solution)/shard_map/pallas_call | solution.py:1690
  519.8 33.3 %shard_map.330 = (bf16[2,8,128,1536]{3,2,1,0:T(8,128)(2,1)}, bf16[2,8,128,192]{3,2,1,0:T(8,128)(2,1)}) custom-call(f32[2,128,1536]{2,1,0:T(8,128)} %get-tuple-element.97.own_ref.base_ref, bf16[1536,768]{1,0:T(8,128)(2,1)} %all-gather.7.cloned.1.call-done.mat_ref.refs_1_.refs_0_), custom_call_target="tpu_custom_call" | custom-call | tf_op jit(solution)/shard_map/pallas_call | solution.py:1470
  553.1 4.5 convolution_convert_fusion
  557.6 4.4 fusion.16
  569.1 29.8 %shard_map.331 = (bf16[2048,576]{1,0:T(8,128)(2,1)}, f32[2,1,384]{2,1,0:T(1,128)}, bf16[8,48,2304]{2,1,0:T(8,128)(2,1)}) custom-call(bf16[2048,576]{1,0:T(8,128)(2,1)} %get-tuple-element.93.turned_ref, bf16[2048,192]{1,0:T(8,128)(2,1)} %bitcast.137, f32[2048,128]{1,0:T(8,128)} %get-tuple-element.104.lse_ref, bf16[2,1,384]{2,1,0:T(2,128)(2,1)} %copy.60.stamp_ref, ...), custom_call_target="tpu_custom_call" | custom-call | tf_op jit(solution)/shard_map/pallas_call | solution.py:2209
  599.0 7.0 fusion.48
  615.6 37.4 %shard_map.332 = (bf16[2,128,1536]{2,1,0:T(8,128)(2,1)}, f32[2,1536]{1,0:T(2,128)}) custom-call(bf16[2,8,128,576]{3,2,1,0:T(8,128)(2,1)} %bitcast.126, bf16[1536,576]{1,0:T(8,128)(2,1)} %all-gather.5.cloned.1.call-done.mat_ref, f32[2,128,1536]{2,1,0:T(8,128)} %get-tuple-element.97.own_ref.base_ref, ...), custom_call_target="tpu_custom_call" | custom-call | tf_op jit(solution)/shard_map/pallas_call | solution.py:1690
  654.7 4.7 reduce-scatter.12.cloned.1.call-done
  659.4 40.5 %shard_map.333 = (bf16[8,32,1536]{2,1,0:T(8,128)(2,1)}, bf16[8,48,576]{2,1,0:T(8,128)(2,1)}, bf16[8,48,768]{2,1,0:T(8,128)(2,1)}, f32[8,128]{1,0:T(8,128)}, f32[...) custom-call(bf16[2,4,32,1536]{3,2,1,0:T(8,128)(2,1)} %bitcast.140, bf16[8,48,576]{2,1,0:T(8,128)(2,1)} %bitcast.150, ...), custom_call_target="tpu_custom_call" | custom-call | tf_op jit(solution)/shard_map/pallas_call | solution.py:735
  703.5 3.0 fusion.12
  706.5 10.3 %shard_map.335 = (f32[48,18432]{1,0:T(8,128)}, f32[48,18432]{1,0:T(8,128)}, f32[48,18432]{1,0:T(8,128)}) custom-call(f32[1,1]{1,0:T(1,128)} %bitcast.51.factor_ref, f32[48,18432]{1,0:T(8,128)} %weight_ref.3, f32[48,18432]{1,0:T(8,128)} %first_ref.3, f32[48,18432]{1,0:T(8,128)} %second_ref.3, bf16[8,48,2304]{2,1,0:T(8,128)(2,1)} %get-tuple-element.119.grad_ref), custom_call_target="tpu_custom_call" | custom-call | tf_op jit(solution)/shard_map/pallas_call | solution.py:2300
  718.6 7.4 %shard_map.334 = (f32[48,9216]{1,0:T(8,128)}, f32[48,9216]{1,0:T(8,128)}, f32[48,9216]{1,0:T(8,128)}) custom-call(f32[1,1]{1,0:T(1,128)} %bitcast.51.factor_ref, f32[48,9216]{1,0:T(8,128)} %weight_ref.2, f32[48,9216]{1,0:T(8,128)} %first_ref.2, f32[48,9216]{1,0:T(8,128)} %second_ref.2, bf16[8,48,576]{2,1,0:T(8,128)(2,1)} %get-tuple-element.122.refs_0_, ...), custom_call_target="tpu_custom_call" | custom-call | tf_op jit(solution)/shard_map/pallas_call | solution.py:2284
  (170 shorter events, 58.7 us)
Async XLA Ops:
  7.2 7.5 %copy-start = (bf16[1,256,1536]{2,1,0:T(8,128)(2,1)S(1)}, bf16[1,256,1536]{2,1,0:T(8,128)(2,1)}, u32[]{:S(2)}) copy-start(bf16[1,256,1536]{2,1,0:T(8,128)(2,1)} %param.21) | copy-start | bytes 2359300
  7.2 110.2 %all-gather.5.cloned.1.call-start = ((), (), s32[]{:S(2)}) async-start(), calls=%async_computation.3 | async-start | bytes 2457600 | tf_op jit(solution)/shard_map/all_gather | solution.py:2383
  55.9 119.2 %all-gather.7.cloned.1.call-start = ((), (), s32[]{:S(2)}) async-start(), calls=%async_computation.4 | async-start | bytes 2949120 | tf_op jit(solution)/shard_map/all_gather | solution.py:2383
  56.7 227.9 %all-gather.9.cloned.1.call-start = ((), (), s32[]{:S(2)}) async-start(), calls=%async_computation.5 | async-start | bytes 5898240 | tf_op jit(solution)/shard_map/all_gather | solution.py:2383
  58.0 9.1 %copy-start.13 = (f32[8,1536]{1,0:T(8,128)S(1)}, f32[8,1536]{1,0:T(8,128)}, u32[]{:S(2)}) copy-start(f32[8,1536]{1,0:T(8,128)} %get-tuple-element.74) | copy-start | bytes 147460
  69.1 44.1 %copy-start.14 = (s32[1024]{0:T(1024)S(1)}, s32[1024]{0:T(1024)}, u32[]{:S(2)}) copy-start(s32[1024]{0:T(1024)} %constant.115) | copy-start | bytes 12292
  69.1 45.4 %copy-start.25 = (bf16[1,256,1536]{2,1,0:T(8,128)(2,1)S(1)}, bf16[1,256,1536]{2,1,0:T(8,128)(2,1)}, u32[]{:S(2)}) copy-start(bf16[1,256,1536]{2,1,0:T(8,128)(2,1)} %param.27) | copy-start | bytes 2359300
  113.2 493.3 %copy-start.23 = (f32[2]{0:T(128)}, f32[2]{0:T(128)S(1)}, u32[]{:S(2)}) copy-start(f32[2]{0:T(128)S(1)} %add_rsqrt_fusion) | copy-start | bytes 28
  119.9 53.9 %copy-start.10 = (bf16[8,2,16,768]{3,2,1,0:T(8,128)(2,1)S(1)}, bf16[8,2,16,768]{3,2,1,0:T(8,128)(2,1)}, u32[]{:S(2)}) copy-start(bf16[8,2,16,768]{3,2,1,0:T(8,128)(2,1)} %get-tuple-element.80) | copy-start | bytes 1179652
  172.8 149.1 %all-gather.11.cloned.1.call-start = ((), (), s32[]{:S(2)}) async-start(), calls=%async_computation.6 | async-start | bytes 2949120 | tf_op jit(solution)/shard_map/all_gather | solution.py:2383
  173.3 391.7 %reduce-scatter.8.cloned.1.call-start = ((), (), s32[]{:S(2)}) async-start(), calls=%async_computation.7 | async-start | bytes 8847360 | tf_op jit(solution)/shard_map/reduce_scatter | solution.py:2459
  442.6 173.0 %reduce-scatter.10.cloned.1.call-start = ((), (), s32[]{:S(2)}) async-start(), calls=%async_computation.8 | async-start | bytes 2949120 | tf_op jit(solution)/shard_map/reduce_scatter | solution.py:2459
  519.8 33.3 %copy-start.6 = (bf16[2048,192]{1,0:T(8,128)(2,1)S(1)}, bf16[2048,192]{1,0:T(8,128)(2,1)}, u32[]{:S(2)}) copy-start(bf16[2048,192]{1,0:T(8,128)(2,1)} %get-tuple-element.78) | copy-start | bytes 2359300
  553.1 8.9 %slice-start = ((s8[6291456]{0:T(1024)(128)(4,1)}), s8[4194304]{0:T(1024)(128)(4,1)S(1)}, s32[]{:S(2)}) async-start(s8[6291456]{0:T(1024)(128)(4,1)} %bitcast.154), calls=%async_computation.10 | async-start | bytes 8388608
  567.5 91.9 %reduce-scatter.12.cloned.1.call-start = ((), (), s32[]{:S(2)}) async-start(), calls=%async_computation.9 | async-start | bytes 2457600 | tf_op jit(solution)/shard_map/reduce_scatter | solution.py:2459
  599.0 7.1 copy-start.16
  615.6 38.2 %copy-start.17 = (f32[2,1536]{1,0:T(2,128)S(1)}, f32[2,1536]{1,0:T(2,128)}, u32[]{:S(2)}) copy-start(f32[2,1536]{1,0:T(2,128)} %get-tuple-element.118) | copy-start | bytes 36868
  615.6 38.2 %copy-start.18 = (f32[2,1536]{1,0:T(2,128)S(1)}, f32[2,1536]{1,0:T(2,128)}, u32[]{:S(2)}) copy-start(f32[2,1536]{1,0:T(2,128)} %get-tuple-element.117) | copy-start | bytes 36868
  706.5 10.4 %copy-start.20 = (f32[6,48]{1,0:T(8,128)S(1)}, f32[6,48]{1,0:T(8,128)}, u32[]{:S(2)}) copy-start(f32[6,48]{1,0:T(8,128)} %param.36) | copy-start | bytes 3460
  706.5 10.4 %copy-start.21 = (f32[6,48]{1,0:T(8,128)S(1)}, f32[6,48]{1,0:T(8,128)}, u32[]{:S(2)}) copy-start(f32[6,48]{1,0:T(8,128)} %param.37) | copy-start | bytes 3460
  706.5 10.4 %copy-start.22 = (f32[8,128]{1,0:T(8,128)S(1)}, f32[8,128]{1,0:T(8,128)}, u32[]{:S(2)}) copy-start(f32[8,128]{1,0:T(8,128)} %get-tuple-element.125) | copy-start | bytes 12292
  706.5 11.0 %copy-start.11 = (f32[24,3072]{1,0:T(8,128)S(1)}, f32[24,3072]{1,0:T(8,128)}, u32[]{:S(2)}) copy-start(f32[24,3072]{1,0:T(8,128)} %param.34) | copy-start | bytes 884740
  706.5 11.0 %copy-start.12 = (f32[24,3072]{1,0:T(8,128)S(1)}, f32[24,3072]{1,0:T(8,128)}, u32[]{:S(2)}) copy-start(f32[24,3072]{1,0:T(8,128)} %param.35) | copy-start | bytes 884740
  718.6 7.5 %copy-start.1 = (bf16[1,256,1536]{2,1,0:T(8,128)(2,1)S(1)}, bf16[1,256,1536]{2,1,0:T(8,128)(2,1)}, u32[]{:S(2)}) copy-start(bf16[1,256,1536]{2,1,0:T(8,128)(2,1)} %param.21) | copy-start | bytes 2359300
  (15 other events, 47.8 us)
Sparse Core Ops, SparseCore 0:
  56.0 45.1 all-gather.4
  102.8 61.4 all-gather.6
  172.9 85.5 all-gather.8
  259.9 49.7 all-gather.10
  442.7 122.3 reduce-scatter.7
  567.8 46.1 reduce-scatter.9
  616.8 42.4 reduce-scatter.11

commit v5 on v4

--- a/solution.py
+++ b/solution.py
@@ -649,25 +649,11 @@
     ]
 
 
-def leave_body(
-    group,
-    planes,
-    kept_ref,
-    first_cut_ref,
-    rest_cut_ref,
-    parts_ref,
-    squares_ref,
-    own_ref,
-    first_mine_ref,
-    rest_mine_ref,
-    norm_ref,
-    total_ref,
-    mid,
-    terms,
-    block,
-    blocks,
-    *sems,
-):
+def leave_body(group, planes, cuts, kept_ref, *refs):
+    cut_refs, refs = refs[:cuts], refs[cuts:]
+    parts_ref, squares_ref, own_ref, *refs = refs
+    mine_refs, refs = refs[:cuts], refs[cuts:]
+    norm_ref, total_ref, mid, terms, block, blocks, *sems = refs
     part_send, part_recv, block_send, block_recv = sems[:4]
     place, depth, flip = plane_places()
     devices = [(flip(mask), lax.rem(depth + step, planes)) for mask, step in everyone(planes)]
@@ -689,8 +675,11 @@
     terms[here] = parts_ref[here]
     start_swap, end_swap = swap_beside(
         [
-            (lambda other: first_cut_ref.at[other], lambda other: first_mine_ref.at[other]),
-            (lambda other: rest_cut_ref.at[other], lambda other: rest_mine_ref.at[other]),
+            (
+                lambda other, cut_ref=cut_ref: cut_ref.at[other],
+                lambda other, mine_ref=mine_ref: mine_ref.at[other],
+            )
+            for cut_ref, mine_ref in zip(cut_refs, mine_refs)
         ],
         *sems[9:],
     )
@@ -704,7 +693,7 @@
     norm_ref[...] = norm_sum
     end_swap()
     squares = squares_ref[0, 0] + jnp.sum(norm_sum * norm_sum)
-    for mine_ref in (first_mine_ref, rest_mine_ref):
+    for mine_ref in mine_refs:
         for piece in range(group):
             values = mine_ref[piece].astype(jnp.float32)
             squares = squares + jnp.sum(values * values)
@@ -726,24 +715,23 @@
         copy.wait_send()
 
 
-def leave(kept_rows, first_cut, rest_cut, norm_parts, squares, collective_id):
+def leave(kept_rows, cuts, norm_parts, squares, collective_id):
     per, planes, rows, wide = kept_rows.shape
     group = per * planes
     count = group * planes
     inside = pl.BlockSpec(memory_space=pltpu.VMEM)
     like = lambda shape, array: jax.ShapeDtypeStruct(shape, array.dtype)
-    *results, _ = pl.pallas_call(
-        functools.partial(leave_body, group, planes),
-        out_shape=[
-            like((group, rows, wide), kept_rows),
-            like(first_cut.shape, first_cut),
-            like(rest_cut.shape, rest_cut),
+    own, *results, norm_sum, total, _ = pl.pallas_call(
+        functools.partial(leave_body, group, planes, len(cuts)),
+        out_shape=[like((group, rows, wide), kept_rows)]
+        + [like(cut.shape, cut) for cut in cuts]
+        + [
             like(norm_parts.shape[1:], norm_parts),
             like((8, 128), norm_parts),
             like((group, rows, wide), kept_rows),
         ],
-        in_specs=[any_spec()] * 3 + [inside, pl.BlockSpec(memory_space=pltpu.SMEM)],
-        out_specs=[any_spec()] + [inside] * 4 + [any_spec()],
+        in_specs=[any_spec()] * (1 + len(cuts)) + [inside, pl.BlockSpec(memory_space=pltpu.SMEM)],
+        out_specs=[any_spec()] + [inside] * (len(cuts) + 2) + [any_spec()],
         scratch_shapes=[
             pltpu.VMEM(norm_parts.shape, jnp.float32),
             pltpu.VMEM((8, 128), jnp.float32),
@@ -754,10 +742,10 @@
             DMA((count,)),
         ]
         + outward_scratch(group, planes)
-        + swap_beside_scratch(2),
+        + swap_beside_scratch(len(cuts)),
         compiler_params=communicating(collective_id),
-    )(kept_rows, first_cut, rest_cut, norm_parts, squares)
-    return results
+    )(kept_rows, *cuts, norm_parts, squares)
+    return own, results, norm_sum, total
 
 
 def everyone(planes):
@@ -772,13 +760,18 @@
     pack_ref,
     first_cut_ref,
     rest_cut_ref,
+    ff_ref,
     kept_ref,
     gains_ref,
     packs_ref,
     first_mine_ref,
     rest_mine_ref,
+    ff_low_ref,
     mid,
     norms_ref,
+    ff_full,
+    ff_low,
+    ff_sem,
     *sems,
 ):
     (
@@ -798,6 +791,8 @@
     place, depth, flip = plane_places()
     per = group // planes
     others = everyone(planes)
+    ff_load = pltpu.make_async_copy(ff_ref, ff_full, ff_sem.at[0])
+    ff_load.start()
     greet([(flip(mask), lax.rem(depth + step, planes)) for mask, step in others])
     here = place * planes + depth
     first = []
@@ -858,6 +853,14 @@
             )
             copy.start()
             cuts.append(copy)
+    ff_load.wait()
+    tile = ff_full.shape[1] // 24
+
+    def round_tile(index, carry):
+        lanes = pl.ds(pl.multiple_of(index * tile, 128), tile)
+        ff_low[:, lanes] = ff_full[:, lanes].astype(ff_low.dtype)
+        return carry
+
     second = []
     arrivals = dict(first)
     for mask in (0, 1, 2, 3, 4, 5, 6, 7):
@@ -878,6 +881,9 @@
         pl.when(goal != depth)(away.start)
         pl.when(goal == depth)(stay.start)
         second.append((goal, away, stay))
+    lax.fori_loop(0, 24, round_tile, 0)
+    ff_store = pltpu.make_async_copy(ff_low, ff_low_ref, ff_sem.at[1])
+    ff_store.start()
     for slot in range(per):
         for origin in range(planes):
             block = kept_ref.at[slot, origin]
@@ -890,6 +896,7 @@
                     (place, lax.rem(depth + 1, planes)),
                 ).wait_recv
             )
+    ff_store.wait()
     for mask, step in others:
         source = flip(mask) * planes + lax.rem(depth + step, planes)
         block = norms_ref.at[source]
@@ -928,7 +935,7 @@
         stay.wait()
 
 
-def enter(rows_of_clip, norm_block, pack, first_cut, rest_cut, planes, collective_id):
+def enter(rows_of_clip, norm_block, pack, first_cut, rest_cut, ff_weight, planes, collective_id):
     group, rows, wide = rows_of_clip.shape
     count = group * planes
     like = lambda shape, array: jax.ShapeDtypeStruct(shape, array.dtype)
@@ -941,12 +948,16 @@
             like((group,) + pack.shape, pack),
             like(first_cut.shape, first_cut),
             like(rest_cut.shape, rest_cut),
+            like(ff_weight.shape, rest_cut),
             like((group, rows, wide), rows_of_clip),
         ],
-        in_specs=[any_spec(), inside, any_spec(), any_spec(), any_spec()],
-        out_specs=[any_spec(), inside] + [any_spec()] * 4,
+        in_specs=[any_spec(), inside] + [any_spec()] * 4,
+        out_specs=[any_spec(), inside] + [any_spec()] * 5,
         scratch_shapes=[
             pltpu.VMEM((count,) + norm_block.shape, norm_block.dtype),
+            pltpu.VMEM(ff_weight.shape, ff_weight.dtype),
+            pltpu.VMEM(ff_weight.shape, rest_cut.dtype),
+            DMA((2,)),
             DMA((group,)),
             DMA((group,)),
             DMA((group,)),
@@ -961,7 +972,7 @@
             DMA((4,)),
         ],
         compiler_params=communicating(collective_id),
-    )(rows_of_clip, norm_block, pack, first_cut, rest_cut)
+    )(rows_of_clip, norm_block, pack, first_cut, rest_cut, ff_weight)
     return results
 
 
@@ -1012,44 +1023,26 @@
     yield
 
 
-def inward_beside(group, planes, own_ref, kept_ref, mid, *sems):
-    near_send, near_recv, far_send, far_recv, local_sem = sems
+def inward_over(group, planes, mid_ref, kept_ref, send_sem, recv_sem, local_sem):
     place, depth, flip = plane_places()
     per = group // planes
 
-    def near(mask):
-        other = flip(mask)
-        return remote(
-            own_ref.at[other],
-            mid.at[place],
-            near_send.at[mask],
-            near_recv.at[mask],
-            (other, depth),
-        )
-
-    def begin():
-        for mask in range(1, group):
-            near(mask).start()
-
-    def second(mask):
-        source = flip(mask)
+    def piece(source):
         goal, slot = lax.div(source, per), lax.rem(source, per)
-        block = mid.at[source] if mask else own_ref.at[place]
+        block = mid_ref.at[source]
         away = remote(
             block,
             kept_ref.at[slot, depth],
-            far_send.at[mask],
-            far_recv.at[slot, depth],
+            send_sem.at[source],
+            recv_sem.at[slot, depth],
             (place, goal),
         )
-        stay = pltpu.make_async_copy(block, kept_ref.at[slot, depth], local_sem.at[mask])
+        stay = pltpu.make_async_copy(block, kept_ref.at[slot, depth], local_sem.at[source])
         return goal != depth, away, stay
 
-    def middle():
-        for mask in range(group):
-            if mask:
-                near(mask).wait_recv()
-            leaves, away, stay = second(mask)
+    def begin():
+        for source in range(group):
+            leaves, away, stay = piece(source)
             pl.when(leaves)(away.start)
             pl.when(jnp.logical_not(leaves))(stay.start)
 
@@ -1061,29 +1054,17 @@
                     remote(
                         block,
                         block,
-                        far_send.at[0],
-                        far_recv.at[slot, origin],
+                        send_sem.at[0],
+                        recv_sem.at[slot, origin],
                         (place, lax.rem(depth + 1, planes)),
                     ).wait_recv
                 )
-        for mask in range(group):
-            leaves, away, stay = second(mask)
+        for source in range(group):
+            leaves, away, stay = piece(source)
             pl.when(leaves)(away.wait_send)
             pl.when(jnp.logical_not(leaves))(stay.wait)
-            if mask:
-                near(mask).wait_send()
-
-    return begin, middle, end
-
-
-def inward_scratch(group, planes):
-    return [
-        DMA((group,)),
-        DMA((group,)),
-        DMA((group,)),
-        DMA((group // planes, planes)),
-        DMA((group,)),
-    ]
+
+    return begin, end
 
 
 def dot_tiles(left, right_ref, span, transposed, width):
@@ -1183,19 +1164,31 @@
     return by_clip_of(results, len(queries), low)
 
 
-def gather_dot_body(clips, rows, sub, normed, mode, window, span, beside, own_ref, *refs):
-    refs = list(refs)
-    take = lambda count: [refs.pop(0) for _ in range(count)]
-    gain_ref = take(1)[0] if normed else None
-    mat_ref = take(1)[0] if mode != "rows" else None
-    gates_ref = take(1)[0] if mode == "gates" else None
-    pair_ref, bias_ref = take(2) if mode in ("cross", "cross_back") else (None, None)
-    query_ref = take(1)[0] if mode == "cross_back" else None
-    extra_ref = take(1)[0] if beside else None
-    all_ref = take(1)[0]
-    prod_refs = take({"rows": 0, "dot": 1, "gates": 2, "cross": 2, "cross_back": 1}[mode])
-    pair_grad_ref = take(1)[0] if mode == "cross_back" else None
-    extra_outs = take({"cond": 1, "outward": 2}[beside[0]]) if beside else []
+def outer_columns(out_ref, start, small, big):
+    width = small.shape[-1]
+    product = outer_sum(small.reshape(-1, width), big.reshape(-1, big.shape[-1]))
+    out_ref[:, start : start + width] = product.T.astype(out_ref.dtype)
+
+
+def by_slot_loads(source, goal, sem):
+    clips = source.shape[0]
+    return [
+        pltpu.make_async_copy(source.at[clip, slot], goal.at[slot, clip], sem.at[slot, clip])
+        for slot in range(8)
+        for clip in range(clips)
+    ]
+
+
+def gather_parts(clips, rows, sub, mode, window, span, ins, outs_refs, scratch):
+    ins, outs_refs, scratch = list(ins), list(outs_refs), list(scratch)
+    mat_ref = ins.pop(0) if mode != "rows" else None
+    gates_ref = ins.pop(0) if mode == "gates" else None
+    pair_ref, bias_ref = (ins.pop(0), ins.pop(0)) if mode in ("cross", "cross_back") else (None, None)
+    query_ref = ins.pop(0) if mode == "cross_back" else None
+    all_ref = outs_refs.pop(0)
+    pair_grad_ref = outs_refs.pop() if mode == "cross_back" else None
+    prod_refs = outs_refs
+    take = lambda count: [scratch.pop(0) for _ in range(count)]
     held, send_sem, recv_sem, all_sem = take(4)
     mat, mat_sem = take(2) if mode != "rows" else (None, None)
     stages = take(len(prod_refs))
@@ -1204,38 +1197,28 @@
     queries, query_sem = take(2) if mode == "cross_back" else (None, None)
     place, depth, flip = plane_places()
     core, beside_x, beside_y, across = flip(1), flip(2), flip(4), flip(6)
+    loads = []
+    gate_loads = {}
     if mode != "rows":
-        load = pltpu.make_async_copy(mat_ref.at[:, pl.ds(*window)], mat, mat_sem)
-        load.start()
+        loads.append(pltpu.make_async_copy(mat_ref.at[:, pl.ds(*window)], mat, mat_sem))
     if mode == "cross_back":
-        query_load = pltpu.make_async_copy(query_ref, queries, query_sem)
-        query_load.start()
-        pair_grad_ref[...] = jnp.zeros_like(pair_grad_ref)
-    slots = [flip(mask) for mask in (0, 1, 2, 4, 3, 5, 6, 7)]
-    gate_loads = {}
+        loads.append(pltpu.make_async_copy(query_ref, queries, query_sem))
     if mode == "gates":
-        for mask, slot in zip((0, 1, 2, 4, 3, 5, 6, 7), slots):
+        for mask in (0, 1, 2, 4, 3, 5, 6, 7):
+            slot = flip(mask)
             gate_loads[mask] = [
                 pltpu.make_async_copy(
                     gates_ref.at[clip, slot], gates.at[slot, clip], gates_sem.at[slot, clip]
                 )
                 for clip in range(clips)
             ]
-            for copy in gate_loads[mask]:
-                copy.start()
-    if beside:
-        greet_cross(*beside[1:])
-        if beside[0] == "cond":
-            going = cond_steps(*beside[1:], extra_ref, extra_outs[0], *refs)
-        else:
-            going = outward_steps(*beside[1:], extra_ref, *extra_outs, *refs)
-        next(going)
-    else:
-        greet([(core, depth), (beside_x, depth), (beside_y, depth)])
-    values = own_ref[...]
-    if normed:
-        values = layer_norm(values, gain_ref[0:1], gain_ref[1:2])
-    held[place] = values.astype(held.dtype)
+
+    def load():
+        if mode == "cross_back":
+            pair_grad_ref[...] = jnp.zeros_like(pair_grad_ref)
+        for copy in loads + [copy for copies in gate_loads.values() for copy in copies]:
+            copy.start()
+
     chunks = [(clip, part) for clip in range(clips) for part in range(rows // sub)]
     count = len(chunks)
     half = count // 2
@@ -1261,11 +1244,20 @@
 
     x_order = list(range(count))
     y_order = list(range(half, count)) + list(range(half))
-    for step in range(count):
-        send(place, x_order[step], beside_x)
-        send(place, y_order[step], beside_y)
-    for index in range(count):
+
+    def put(index, values):
+        clip, part = chunks[index]
+        held[place, clip, pl.ds(part * sub, sub)] = values.astype(held.dtype)
+        if index < half:
+            send(place, index, beside_x)
+        else:
+            send(place, index, beside_y)
         send(place, index, core)
+        if index == count - 1:
+            for low in range(half):
+                send(place, half + low, beside_x)
+                send(place, low, beside_y)
+
     outs = []
 
     def leave_here(source, goal, sem, major):
@@ -1323,81 +1315,66 @@
         for which, (stage, prod_ref) in enumerate(zip(stages, prod_refs)):
             leave_here(stage, prod_ref, prod_sem.at[which], slot)
 
-    if mode != "rows":
-        load.wait()
-    if mode == "cross_back":
-        query_load.wait()
-    multiply(0)
-    if beside:
-        next(going)
-    for step in range(count):
-        x_index, y_index = x_order[step], y_order[step]
-        arrived(beside_x, x_index)
-        if x_index < half:
-            send(beside_x, x_index, beside_y)
-        send(beside_x, x_index, core)
-        arrived(beside_y, y_index)
-        if y_index >= half:
-            send(beside_y, y_index, beside_x)
-        send(beside_y, y_index, core)
-        if step == 0:
+    def run(late=lambda: None):
+        for copy in loads:
+            copy.wait()
+        multiply(0)
+        for step in range(count):
+            x_index, y_index = x_order[step], y_order[step]
+            arrived(beside_x, x_index)
+            if x_index < half:
+                send(beside_x, x_index, beside_y)
+            send(beside_x, x_index, core)
+            arrived(beside_y, y_index)
+            if y_index >= half:
+                send(beside_y, y_index, beside_x)
+            send(beside_y, y_index, core)
+            if step == 0:
+                for index in range(count):
+                    arrived(core, index)
+                multiply(1)
+        late()
+        multiply(2)
+        for step in range(half):
+            for index in (x_order[step], y_order[step]):
+                arrived(across, index)
+                send(across, index, core)
+            if step == 0:
+                multiply(4)
+        for mask in (3, 5):
             for index in range(count):
-                arrived(core, index)
-            multiply(1)
-    multiply(2)
-    for step in range(half):
-        for index in (x_order[step], y_order[step]):
-            arrived(across, index)
-            send(across, index, core)
-        if step == 0:
-            multiply(4)
-    for mask in (3, 5):
+                arrived(flip(mask), index)
+            multiply(mask)
+        multiply(6)
         for index in range(count):
-            arrived(flip(mask), index)
-        multiply(mask)
-    multiply(6)
-    for index in range(count):
-        arrived(flip(7), index)
-    multiply(7)
-    if beside:
-        next(going)
-    for copy in outs:
-        copy.wait()
-    for copy in sends:
-        copy.wait_send()
-
-
-def gather_dot(
-    own_rows,
-    matrix,
-    kind,
-    collective_id,
-    gains=None,
-    picked=None,
-    kept_rows=None,
-    gate_up=None,
-    span=None,
-    pair=None,
-    bias=None,
-    query=None,
-    sub=64,
-):
-    clips, rows, wide = own_rows.shape
+            arrived(flip(7), index)
+        multiply(7)
+        for copy in outs:
+            copy.wait()
+        for copy in sends:
+            copy.wait_send()
+
+    return load, put, run
+
+
+def chunk_order(clips, rows, sub):
+    half = clips * (rows // sub) // 2
+    return [index for low in range(half) for index in (low, half + low)]
+
+
+def gather_plan(clips, rows, wide, sub, matrix, kind, gate_up, span, pair, bias, query):
     count = clips * (rows // sub)
     low = jnp.bfloat16
+    inside = pl.BlockSpec(memory_space=pltpu.VMEM)
+    by_clip = lambda columns, of: jax.ShapeDtypeStruct((clips, 8, rows, columns), of)
+    by_device = lambda columns, of: jax.ShapeDtypeStruct((8, clips, rows, columns), of)
     mode = "rows" if matrix is None else "dot"
     if gate_up is not None:
         mode = "gates"
     if pair is not None:
         mode = "cross" if query is None else "cross_back"
     window = inner = None
-    inside = pl.BlockSpec(memory_space=pltpu.VMEM)
-    by_clip = lambda columns, of: jax.ShapeDtypeStruct((clips, 8, rows, columns), of)
-    by_device = lambda columns, of: jax.ShapeDtypeStruct((8, clips, rows, columns), of)
-    args, in_specs = [own_rows], [inside]
-    if gains is not None:
-        args.append(gains)
-        in_specs.append(inside)
+    args, in_specs = [], []
     outs = [by_device(wide, low) if mode == "gates" else by_clip(wide, low)]
     scratch = [
         pltpu.VMEM((8, clips, rows, wide), low),
@@ -1442,11 +1419,88 @@
             pltpu.VMEM((clips, 8, rows, columns), low),
             DMA(()),
         ]
-    mains = len(outs)
+    return (mode, window, inner), args, in_specs, outs, out_specs, scratch
+
+
+def flat_rows(results):
+    return [
+        block.reshape(-1, block.shape[3]) if len(block.shape) == 4 else block for block in results
+    ]
+
+
+def gather_dot_body(clips, rows, sub, normed, plan, beside, outer, counts, own_ref, *refs):
+    refs = list(refs)
+    take = lambda count: [refs.pop(0) for _ in range(count)]
+    gain_ref = take(1)[0] if normed else None
+    ins = take(counts[0])
+    pick_ref = take(1)[0] if beside else None
+    past_ref, mixed_ref = take(2) if outer else (None, None)
+    outs = take(counts[1])
+    cond_ref = take(1)[0] if beside else None
+    outer_ref = take(1)[0] if outer else None
+    scratch = take(counts[2])
+    load, put, run = gather_parts(clips, rows, sub, *plan, ins, outs, scratch)
+    load()
+    if outer:
+        past, mixed, past_sem, mixed_sem = refs
+        outer_loads = by_slot_loads(past_ref, past, past_sem)
+        outer_loads += by_slot_loads(mixed_ref, mixed, mixed_sem)
+        for copy in outer_loads:
+            copy.start()
+    place, depth, flip = plane_places()
+    if beside:
+        greet_cross(*beside)
+        cond = cond_steps(*beside, pick_ref, cond_ref, *refs)
+        next(cond)
+    else:
+        greet([(flip(1), depth), (flip(2), depth), (flip(4), depth)])
+    for index in chunk_order(clips, rows, sub):
+        clip, part = divmod(index, rows // sub)
+        values = own_ref[clip, pl.ds(part * sub, sub)]
+        if normed:
+            values = layer_norm(values.astype(jnp.float32), gain_ref[0:1], gain_ref[1:2])
+        put(index, values)
+    if beside:
+        run(lambda: next(cond))
+        next(cond)
+    else:
+        run()
+    if outer:
+        for copy in outer_loads:
+            copy.wait()
+        held, queries = scratch[0], scratch[6]
+        outer_columns(outer_ref, 0, queries[...], past[...])
+        outer_columns(outer_ref, queries.shape[3], mixed[...], held[...])
+
+
+def gather_dot(
+    own_rows,
+    matrix,
+    kind,
+    collective_id,
+    gains=None,
+    picked=None,
+    gate_up=None,
+    span=None,
+    pair=None,
+    bias=None,
+    query=None,
+    outer=None,
+    sub=64,
+):
+    clips, rows, wide = own_rows.shape
+    plan, args, in_specs, outs, out_specs, scratch = gather_plan(
+        clips, rows, wide, sub, matrix, kind, gate_up, span, pair, bias, query
+    )
+    inside = pl.BlockSpec(memory_space=pltpu.VMEM)
+    counts = (len(args), len(outs), len(scratch))
+    if gains is not None:
+        args, in_specs = [gains] + args, [inside] + in_specs
+    args, in_specs = [own_rows] + args, [inside] + in_specs
     beside = None
     if picked is not None:
         planes, per, tokens, cond_wide = picked.shape
-        beside = ("cond", planes * per, planes)
+        beside = (planes * per, planes)
         args.append(picked)
         in_specs.append(inside)
         outs.append(jax.ShapeDtypeStruct((8, per, tokens, cond_wide), picked.dtype))
@@ -1459,17 +1513,30 @@
             DMA((8,)),
             DMA((8,)),
         ]
-    if kept_rows is not None:
-        per, planes, piece, _ = kept_rows.shape
-        beside = ("outward", planes * per, planes)
-        args.append(kept_rows)
-        in_specs.append(any_spec())
-        outs += [jax.ShapeDtypeStruct((per * planes, piece, wide), kept_rows.dtype)] * 2
-        out_specs += [any_spec()] * 2
-        scratch += outward_scratch(*beside[1:])
+    if outer is not None:
+        past, mixed = outer
+        width = mixed.shape[1]
+        args += [past.reshape(clips, 8, rows, wide), mixed.reshape(clips, 8, rows, width)]
+        in_specs += [any_spec()] * 2
+        outs.append(jax.ShapeDtypeStruct((wide, 2 * width), jnp.bfloat16))
+        out_specs.append(inside)
+        scratch += [
+            pltpu.VMEM((8, clips, rows, wide), jnp.bfloat16),
+            pltpu.VMEM((8, clips, rows, width), jnp.bfloat16),
+            DMA((8, clips)),
+            DMA((8, clips)),
+        ]
     results = pl.pallas_call(
         functools.partial(
-            gather_dot_body, clips, rows, sub, gains is not None, mode, window, inner, beside
+            gather_dot_body,
+            clips,
+            rows,
+            sub,
+            gains is not None,
+            plan,
+            beside,
+            outer is not None,
+            counts,
         ),
         out_shape=outs,
         in_specs=in_specs,
@@ -1477,11 +1544,7 @@
         scratch_shapes=scratch,
         compiler_params=communicating(collective_id),
     )(*args)
-    flat = [
-        block.reshape(clips * 8 * rows, block.shape[3]) if len(block.shape) == 4 else block
-        for block in results[:mains]
-    ]
-    return flat + list(results[mains : mains + 1])
+    return flat_rows(results[: counts[1]]) + list(results[counts[1] :])
 
 
 def reduce_steps(clips, rows, sub, multiply, final, terms, pair, turn, from_x, from_y, *sems):
@@ -1555,7 +1618,7 @@
         add(block, turn.at[high])
         send(block, from_x.at[high], x_sem.at[high], beside_x)
     yield
-    for index in range(count):
+    for index in chunk_order(clips, rows, sub):
         clip, part = chunks[index]
         arrived(pair.at[index, 0], core_sem.at[index, 0])
         arrived(from_x.at[index], x_sem.at[index])
@@ -1616,6 +1679,7 @@
                 stats_ref[which : which + 1] = row
         result = base_ref[clip, span].astype(jnp.float32) + result
         sum_ref[clip, span] = result.astype(sum_ref.dtype)
+        return result
 
     return final
 
@@ -1703,215 +1767,390 @@
     )(*args)
 
 
-def ff_back_body(
-    group,
-    planes,
+def add_steps(parts_ref, sum_ref, landed, send_sem, recv_sem, local_sem):
+    place, depth, flip = plane_places()
+    planes = parts_ref.shape[0]
+    copies = []
+    for step in range(1, planes):
+        goal = lax.rem(depth + step, planes)
+        copy = remote(
+            parts_ref.at[goal],
+            landed.at[depth],
+            send_sem.at[step],
+            recv_sem.at[depth],
+            (place, goal),
+        )
+        copy.start()
+        copies.append(copy)
+    stay = pltpu.make_async_copy(parts_ref.at[depth], landed.at[depth], local_sem)
+    stay.start()
+    yield
+    stay.wait()
+    for step in range(1, planes):
+        source = lax.rem(depth + step, planes)
+        block = landed.at[source]
+        remote(block, block, send_sem.at[0], recv_sem.at[source], (place, source)).wait_recv()
+    sum_ref[...] = jnp.sum(landed[...].astype(jnp.float32), axis=0).astype(sum_ref.dtype)
+    for copy in copies:
+        copy.wait_send()
+    yield
+
+
+def reduce_gather_body(
+    clips, rows, sub, spans, back, normed, plan, counts, passing, outer, leaving, adding, left_ref, mat_ref, base_ref, *refs
+):
+    refs = list(refs)
+    take = lambda count: [refs.pop(0) for _ in range(count)]
+    values_ref, back_gain_ref = take(2) if back else (None, None)
+    gain_ref = take(1)[0] if normed else None
+    ins = take(counts[0])
+    mid_ref = take(1)[0] if passing else None
+    low_ref, ending_ref = take(2) if outer else (None, None)
+    leaving_ref = take(1)[0] if leaving else None
+    adding_ref = take(1)[0] if adding else None
+    sum_ref = take(1)[0]
+    stats_ref = take(1)[0] if back else None
+    outs = take(counts[1])
+    kept_ref = take(1)[0] if passing else None
+    outer_ref = take(1)[0] if outer else None
+    own_ref, own_mid = take(2) if leaving else (None, None)
+    added_ref = take(1)[0] if adding else None
+    left, mat, mat_sem, left_sem = take(4)
+    terms, *others = reduce_refs = take(10)
+    gather_scratch = take(counts[2])
+    load, put, run = gather_parts(clips, rows, sub, *plan, ins, outs, gather_scratch)
+    window, span = spans
+    place, depth, flip = plane_places()
+    mat_load = pltpu.make_async_copy(mat_ref.at[:, pl.ds(*window)], mat, mat_sem)
+    mat_load.start()
+    loads = {}
+    for number, slot in enumerate(plane_order()):
+        loads[number] = [
+            pltpu.make_async_copy(
+                left_ref.at[clip, slot], left.at[number, clip], left_sem.at[number, clip]
+            )
+            for clip in range(clips)
+        ]
+        for copy in loads[number]:
+            copy.start()
+    load()
+    if outer:
+        low, low_sem = take(2)
+        outer_loads = by_slot_loads(low_ref, low, low_sem)
+        for copy in outer_loads:
+            copy.start()
+    if adding:
+        adder = add_steps(adding_ref, added_ref, *take(4))
+    if passing:
+        greet_cross(*passing)
+        pass_rows, end_rows = inward_over(*passing, mid_ref, kept_ref, *refs)
+        pass_rows()
+    elif leaving:
+        greet_cross(*leaving)
+        going = outward_steps(*leaving, leaving_ref, own_ref, own_mid, *refs)
+        next(going)
+    else:
+        greet([(flip(1), depth), (flip(2), depth), (flip(4), depth)])
+    mat_load.wait()
+
+    def blocks(number):
+        for copy in loads[number]:
+            copy.wait()
+        return left[number]
+
+    keep = final_back(values_ref, back_gain_ref, base_ref, sum_ref, stats_ref)
+
+    def final(index, clip, span_rows, result):
+        result = keep(index, clip, span_rows, result)
+        if normed:
+            result = layer_norm(result, gain_ref[0:1], gain_ref[1:2])
+        put(index, result)
+
+    steps = reduce_steps(
+        clips,
+        rows,
+        sub,
+        terms_of(clips, rows, blocks, mat, span, terms),
+        final,
+        *reduce_refs,
+    )
+
+    next(steps)
+    next(steps)
+    next(steps)
+    if adding:
+        next(adder)
+    run((lambda: next(going)) if leaving else (lambda: None))
+    if outer:
+        for copy in outer_loads:
+            copy.wait()
+        outer_columns(outer_ref, 0, low[...], gather_scratch[0][...])
+        outer_ref[:, low.shape[3] :] = ending_ref[...]
+    next(steps)
+    if passing:
+        end_rows()
+    if leaving:
+        next(going)
+    if adding:
+        next(adder)
+
+
+def reduce_gather(
+    left,
+    matrix,
+    clips,
+    collective_id,
+    base,
+    second,
+    kind=jnp.bfloat16,
+    span=None,
+    back=None,
+    gains=None,
+    second_span=None,
+    pair=None,
+    bias=None,
+    passing=None,
+    outer=None,
+    leaving=None,
+    adding=None,
+    sub=64,
+):
+    wide = matrix.shape[0]
+    rows, inner = left.shape[0] // (8 * clips), left.shape[1]
+    low = jnp.bfloat16
+    spans = window_of(matrix, span)
+    inside = pl.BlockSpec(memory_space=pltpu.VMEM)
+    plan, more, more_specs, outs, out_specs, more_scratch = gather_plan(
+        clips, rows, wide, sub, second, kind, None, second_span, pair, bias, None
+    )
+    counts = (len(more), len(outs), len(more_scratch))
+    args = [left.reshape(clips, 8, rows, inner), matrix, base]
+    in_specs = [any_spec(), any_spec(), inside]
+    first_outs = [jax.ShapeDtypeStruct((clips, rows, wide), jnp.float32)]
+    scratch = [
+        pltpu.VMEM((8, clips, rows, inner), low),
+        pltpu.VMEM((wide, spans[0][1]), low),
+        DMA(()),
+        DMA((8, clips)),
+    ] + reduce_scratch(clips, rows, sub, wide)
+    if back is not None:
+        args += list(back)
+        in_specs += [inside] * 2
+        first_outs.append(jax.ShapeDtypeStruct((2, wide), jnp.float32))
+    if gains is not None:
+        args.append(gains)
+        in_specs.append(inside)
+    args += more
+    in_specs += more_specs
+    scratch += more_scratch
+    outs = first_outs + outs
+    out_specs = [inside] * len(first_outs) + out_specs
+    flat = len(outs)
+    if passing is not None:
+        group, piece, _ = passing.shape
+        planes = group // clips
+        args.append(passing)
+        in_specs.append(any_spec())
+        outs.append(jax.ShapeDtypeStruct((clips, planes, piece, wide), passing.dtype))
+        out_specs.append(any_spec())
+        scratch += [DMA((group,)), DMA((clips, planes)), DMA((group,))]
+    if outer is not None:
+        low_rows, ending = outer
+        columns = low_rows.shape[1]
+        args += [low_rows.reshape(clips, 8, rows, columns), ending]
+        in_specs += [any_spec(), inside]
+        outs.append(jax.ShapeDtypeStruct((wide, columns + ending.shape[1]), low))
+        out_specs.append(inside)
+        scratch += [pltpu.VMEM((8, clips, rows, columns), low), DMA((8, clips))]
+    if leaving is not None:
+        per, planes, piece, _ = leaving.shape
+        group = per * planes
+        args.append(leaving)
+        in_specs.append(any_spec())
+        outs += [jax.ShapeDtypeStruct((group, piece, wide), leaving.dtype)] * 2
+        leaving_mid = len(outs) - 1
+        out_specs += [any_spec()] * 2
+    if adding is not None:
+        args.append(adding)
+        in_specs.append(any_spec())
+        outs.append(jax.ShapeDtypeStruct(adding.shape[1:], adding.dtype))
+        out_specs.append(inside)
+        scratch += [
+            pltpu.VMEM(adding.shape, adding.dtype),
+            DMA((adding.shape[0],)),
+            DMA((adding.shape[0],)),
+            DMA(()),
+        ]
+    if leaving is not None:
+        scratch += outward_scratch(group, planes)
+    results = pl.pallas_call(
+        functools.partial(
+            reduce_gather_body,
+            clips,
+            rows,
+            sub,
+            spans,
+            back is not None,
+            gains is not None,
+            plan,
+            counts,
+            passing is not None and (group, planes),
+            outer is not None,
+            leaving is not None and (group, planes),
+            adding is not None,
+        ),
+        out_shape=outs,
+        in_specs=in_specs,
+        out_specs=out_specs,
+        scratch_shapes=scratch,
+        compiler_params=communicating(collective_id),
+    )(*args)
+    first = len(first_outs)
+    if leaving is not None:
+        results = [block for which, block in enumerate(results) if which != leaving_mid]
+    return list(results[:first]) + flat_rows(results[first:flat]) + list(results[flat:])
+
+
+def ff_outer_body(
     clips,
     rows,
     sub,
     gates_ref,
-    gate_mat_ref,
     hidden_ref,
     down_ref,
     normed_ref,
     grads_ref,
-    base_ref,
     values_ref,
-    gain_ref,
-    sum_ref,
-    stats_ref,
+    layer_ref,
     outer_ref,
-    own_ref,
-    mid,
     gates,
-    gate_mat,
     hidden,
     down,
     normed,
     grads,
     stage,
-    kept,
     load_sem,
-    gates_sem,
     tile_sem,
     stage_sem,
-    *refs,
+    *reduce_refs,
 ):
-    refs = list(refs)
-    first_refs, second_refs, sems = refs[:10], refs[10:20], refs[20:]
     place, depth, flip = plane_places()
     order = plane_order()
     loads = [
-        pltpu.make_async_copy(down_ref, down, load_sem.at[0]),
-        pltpu.make_async_copy(hidden_ref, hidden, load_sem.at[1]),
-        pltpu.make_async_copy(gate_mat_ref, gate_mat, load_sem.at[2]),
+        pltpu.make_async_copy(source, goal, load_sem.at[which])
+        for which, (source, goal) in enumerate(
+            ((down_ref, down), (hidden_ref, hidden), (gates_ref, gates))
+        )
     ]
     for copy in loads:
         copy.start()
-    gate_loads = {}
-    for number, slot in enumerate(order):
-        gate_loads[number] = [
-            pltpu.make_async_copy(
-                gates_ref.at[clip, slot], gates.at[clip, slot], gates_sem.at[number, clip]
-            )
-            for clip in range(clips)
-        ]
-        for copy in gate_loads[number]:
-            copy.start()
     tile = stage.shape[1]
     tiles = normed_ref.shape[3] // tile
     total_rows = 8 * clips * rows
     inner = gates.shape[3]
 
     def fetch(index):
-        lanes = pl.ds(pl.multiple_of(index * tile, tile), tile)
-        spot = lax.rem(index, 2)
         return [
             pltpu.make_async_copy(
-                source.at[:, :, :, lanes], goal.at[spot], tile_sem.at[which, spot]
+                source.at[:, :, :, pl.ds(index * tile, tile)],
+                goal.at[index % 2],
+                tile_sem.at[which, index % 2],
             )
             for which, (source, goal) in enumerate(((normed_ref, normed), (grads_ref, grads)))
         ]
 
     def stored(index):
-        there = outer_ref.at[pl.ds(pl.multiple_of(index * tile, tile), tile)]
-        spot = lax.rem(index, 2)
-        return pltpu.make_async_copy(stage.at[spot], there, stage_sem.at[spot])
-
-    def outer_tiles(first, last):
-        def one(index, carry):
-            spot = lax.rem(index, 2)
-
-            @pl.when(index >= 2)
-            def _():
-                stored(index - 2).wait()
-
-            for copy in fetch(index):
-                copy.wait()
-            stage[spot, :, :inner] = outer_sum(
-                normed[spot].reshape(total_rows, tile), gates[...].reshape(total_rows, inner)
-            ).astype(stage.dtype)
-            stage[spot, :, inner:] = outer_sum(
-                grads[spot].reshape(total_rows, tile),
-                hidden[...].reshape(total_rows, hidden.shape[3]),
-            ).astype(stage.dtype)
-            stored(index).start()
-
-            @pl.when(index + 2 < tiles)
-            def _():
-                for copy in fetch(index + 2):
-                    copy.start()
-
-            return carry
-
-        lax.fori_loop(first, last, one, 0)
+        return pltpu.make_async_copy(
+            stage.at[index % 2],
+            outer_ref.at[pl.ds(index * tile, tile)],
+            stage_sem.at[index % 2],
+        )
+
+    def outer_tile(index):
+        spot = index % 2
+        if index >= 2:
+            stored(index - 2).wait()
+        for copy in fetch(index):
+            copy.wait()
+        stage[spot, :, :inner] = outer_sum(
+            normed[spot].reshape(total_rows, tile), gates[...].reshape(total_rows, inner)
+        ).astype(stage.dtype)
+        stage[spot, :, inner:] = outer_sum(
+            grads[spot].reshape(total_rows, tile),
+            hidden[...].reshape(total_rows, hidden.shape[3]),
+        ).astype(stage.dtype)
+        stored(index).start()
+        if index + 2 < tiles:
+            for copy in fetch(index + 2):
+                copy.start()
 
     for index in range(2):
         for copy in fetch(index):
             copy.start()
-    greet_cross(group, planes)
+    greet([(flip(1), depth), (flip(2), depth), (flip(4), depth)])
     loads[0].wait()
     loads[1].wait()
-    piece = kept.shape[2]
 
     def layer_rows(index, clip, span, result):
-        result = (values_ref[clip, span] + result).astype(kept.dtype)
-        start = index % (rows // sub) * sub
-        for part in range(sub // piece):
-            kept[clip, start // piece + part] = result[part * piece : part * piece + piece]
-
-    first = reduce_steps(
+        layer_ref[clip, span] = (values_ref[clip, span] + result).astype(layer_ref.dtype)
+
+    steps = reduce_steps(
         clips,
         rows,
         sub,
         terms_of(
-            clips, rows, lambda number: hidden[order[number]], down, (0, down.shape[1]), first_refs[0]
+            clips, rows, lambda number: hidden[order[number]], down, (0, down.shape[1]), reduce_refs[0]
         ),
         layer_rows,
-        *first_refs,
-    )
-
-    def gate_rows(number):
-        for copy in gate_loads[number]:
-            copy.wait()
-        return gates[:, order[number]]
-
-    second = reduce_steps(
-        clips,
-        rows,
-        sub,
-        terms_of(clips, rows, gate_rows, gate_mat, (0, inner), second_refs[0]),
-        final_back(values_ref, gain_ref, base_ref, sum_ref, stats_ref),
-        *second_refs,
-    )
-    next(first)
+        *reduce_refs,
+    )
+    next(steps)
     loads[2].wait()
-    next(second)
-    next(first)
-    outer_tiles(0, 2)
-    next(first)
-    going = outward_steps(group, planes, kept, own_ref, mid, *sems)
-    next(going)
-    next(second)
-    outer_tiles(2, tiles)
-    next(going)
-    next(second)
-    next(going)
+    outer_tile(0)
+    next(steps)
+    for index in range(1, tiles):
+        outer_tile(index)
+    next(steps)
     for index in range(max(tiles - 2, 0), tiles):
         stored(index).wait()
-    next(first)
-    next(second)
-
-
-def ff_back(gates, gate_mat, hidden, down, normed, grads, base, values, gain, planes, collective_id, sub=64):
-    clips, rows, wide = base.shape
-    group = 8
-    piece = rows // planes
+    next(steps)
+
+
+def ff_outer(gates, hidden, down, normed, grads, values, collective_id, sub=64):
+    clips, rows, wide = values.shape
     low = jnp.bfloat16
     inner, columns = gates.shape[1], gates.shape[1] + hidden.shape[1]
-    tile = 256
+    tile = 512
     inside = pl.BlockSpec(memory_space=pltpu.VMEM)
-    moved = jax.ShapeDtypeStruct((group, piece, wide), low)
-    *results, _ = pl.pallas_call(
-        functools.partial(ff_back_body, group, planes, clips, rows, sub),
+    return pl.pallas_call(
+        functools.partial(ff_outer_body, clips, rows, sub),
         out_shape=[
-            jax.ShapeDtypeStruct((clips, rows, wide), jnp.float32),
-            jax.ShapeDtypeStruct((2, wide), jnp.float32),
+            jax.ShapeDtypeStruct((clips, rows, wide), low),
             jax.ShapeDtypeStruct((wide, columns), low),
-            moved,
-            moved,
         ],
-        in_specs=[any_spec()] * 6 + [inside] * 3,
-        out_specs=[inside] * 2 + [any_spec()] * 3,
+        in_specs=[any_spec()] * 5 + [inside],
+        out_specs=[inside, any_spec()],
         scratch_shapes=[
             pltpu.VMEM((clips, 8, rows, inner), low),
-            pltpu.VMEM(gate_mat.shape, low),
             pltpu.VMEM((8, clips, rows, hidden.shape[1]), low),
             pltpu.VMEM(down.shape, low),
             pltpu.VMEM((2, clips, 8, rows, tile), low),
             pltpu.VMEM((2, 8, clips, rows, tile), low),
             pltpu.VMEM((2, tile, columns), low),
-            pltpu.VMEM((clips, planes, piece, wide), low),
             DMA((3,)),
-            DMA((8, clips)),
             DMA((2, 2)),
             DMA((2,)),
         ]
-        + reduce_scratch(clips, rows, sub, wide) * 2
-        + outward_scratch(group, planes),
+        + reduce_scratch(clips, rows, sub, wide),
         compiler_params=communicating(collective_id),
     )(
         gates.reshape(clips, 8, rows, inner),
-        gate_mat,
         hidden.reshape(8, clips, rows, hidden.shape[1]),
         down,
         normed.reshape(clips, 8, rows, wide),
         grads.reshape(8, clips, rows, wide),
-        base,
         values,
-        gain,
-    )
-    return results
+    )
 
 
 def rotary_lanes(places):
@@ -1989,12 +2228,11 @@
     lse_ref,
     gate_up_ref,
     down_ref,
-    kept_ref,
-    mid,
+    mid_ref,
     raw_ref,
     *sems,
 ):
-    group, planes = gate_up_ref.shape[0], kept_ref.shape[1]
+    group = gate_up_ref.shape[0]
     hidden = down_ref.shape[2]
     step, last = pl.program_id(0), pl.num_programs(0) - 1
 
@@ -2005,25 +2243,19 @@
 
     start_swap, end_swap = swap_beside(
         [
+            (lambda other: own_ref.at[other], lambda other: mid_ref.at[other]),
             (columns(0), lambda other: gate_up_ref.at[other, :, pl.ds(0, hidden)]),
             (columns(1), lambda other: gate_up_ref.at[other, :, pl.ds(hidden, hidden)]),
             (columns(2), lambda other: down_ref.at[other]),
         ],
-        *sems[:3],
-    )
-    start_rows, pass_rows, end_rows = inward_beside(
-        group, planes, own_ref, kept_ref, mid, *sems[3:]
-    )
+        *sems,
+    )
+    place, depth, flip = plane_places()
 
     @pl.when(step == 0)
     def _():
-        greet_cross(group, planes)
-        start_rows()
+        greet([(flip(mask), depth) for mask in range(1, group)])
         start_swap()
-
-    @pl.when(step == last)
-    def _():
-        pass_rows()
 
     def project(index, carry):
         place = pl.ds(pl.multiple_of(index * tile, tile), tile)
@@ -2071,22 +2303,18 @@
 
         lax.fori_loop(0, rows // tile, one, 0)
 
-    @pl.when(step == last)
-    def _():
-        end_swap()
-        end_rows()
+    pl.when(step == last)(end_swap)
 
 
 def flash_forward(normed, matrix, stamps, bias, rotary, heads, ff_low, rows_of_clip, collective_id):
     clips, rows = bias.shape
     wide = heads * HDIM
     group, piece, features = rows_of_clip.shape
-    planes = group // clips
     owned, columns = ff_low.shape
     hidden = columns // (3 * group)
     like = lambda *shape: jax.ShapeDtypeStruct(shape, rows_of_clip.dtype)
     blocked = lambda lanes: pl.BlockSpec((rows, lanes), lambda clip: (clip, 0))
-    *results, _ = pl.pallas_call(
+    return pl.pallas_call(
         functools.partial(flash_forward_body, heads, rows // 4),
         grid=(clips,),
         out_shape=[
@@ -2095,7 +2323,6 @@
             jax.ShapeDtypeStruct((clips * rows, 128), jnp.float32),
             like(group, owned, 2 * hidden),
             like(group, owned, hidden),
-            like(clips, planes, piece, features),
             like(group, piece, features),
         ],
         in_specs=[
@@ -2107,31 +2334,33 @@
             any_spec(),
             any_spec(),
         ],
-        out_specs=[blocked(3 * wide), blocked(wide), blocked(128)] + [any_spec()] * 4,
-        scratch_shapes=[pltpu.VMEM((rows, 3 * wide), jnp.float32)]
-        + swap_beside_scratch(3)
-        + inward_scratch(group, planes),
+        out_specs=[blocked(3 * wide), blocked(wide), blocked(128)] + [any_spec()] * 3,
+        scratch_shapes=[pltpu.VMEM((rows, 3 * wide), jnp.float32)] + swap_beside_scratch(4),
         compiler_params=communicating(collective_id),
     )(normed, matrix, stamps[:, None], bias[:, None], rotary, ff_low, rows_of_clip)
-    return results
 
 
 def flash_backward_body(
     heads,
     tile,
     turned_ref,
+    mixed_ref,
     grad_ref,
     lse_ref,
     stamp_ref,
     bias_ref,
     rotary_ref,
     cut_ref,
+    normed_ref,
+    stamp_normed_ref,
     out_ref,
     stamp_out_ref,
     mine_ref,
+    outer_ref,
     query_grad,
     key_grad,
     value_grad,
+    outer_total,
     *sems,
 ):
     place, depth, flip = plane_places()
@@ -2149,18 +2378,35 @@
     scale = HDIM**-0.5
     low = turned_ref.dtype
     f32 = jnp.float32
-    lse_rows = lse_ref[...].T
     first_row = lax.broadcasted_iota(jnp.int32, (8, tile), 0) == 0
+    ones = lambda count, width: jnp.ones((count, width), low)
+    blank = lambda count, width: jnp.zeros((count, width), low)
+    bias = bias_ref[0].astype(low)
+
+    def widened(count, *parts):
+        have = sum(part.shape[1] for part in parts)
+        return jnp.concatenate(list(parts) + [blank(count, 128 - have)], axis=1)
+
+    def negative_parts(column):
+        parts, rest = [], -column
+        for _ in range(3):
+            parts.append(rest.astype(low))
+            rest = rest - parts[-1].astype(f32)
+        return parts
+
     for head in range(heads):
         lanes = slice(head * HDIM, head * HDIM + HDIM)
         later = slice(wide + head * HDIM, wide + head * HDIM + HDIM)
         keys = turned_ref[:, later]
         values = turned_ref[:, 2 * wide + head * HDIM : 2 * wide + head * HDIM + HDIM]
         keys_across = keys.astype(f32).T.astype(low)
+        wide_keys = widened(rows, keys, bias, ones(rows, 3))
+        wide_values = widened(rows, values, ones(rows, 3))
         stamp_key = jnp.broadcast_to(stamp_ref[0, :, lanes], (8, HDIM))
         stamp_value = jnp.broadcast_to(stamp_ref[0, :, later], (8, HDIM))
+        wide_stamp_key = widened(8, stamp_key, blank(8, 1), ones(8, 3))
+        wide_stamp_value = widened(8, stamp_value, ones(8, 3))
         stamp_column = stamp_ref[0, :, lanes].astype(f32).T
-        bias = bias_ref[0]
         key_total = jnp.zeros((rows, HDIM), f32)
         value_total = jnp.zeros((rows, HDIM), f32)
         stamp_key_total = jnp.zeros((8, HDIM), f32)
@@ -2169,24 +2415,23 @@
             place = slice(step * tile, step * tile + tile)
             query = turned_ref[place, lanes] * jnp.asarray(scale, low)
             grad = grad_ref[place, lanes]
-            lse = lse_rows[head : head + 1, place]
-            prob = jnp.exp(times_transposed(keys, query) + bias - lse)
-            stamp_prob = jnp.exp(times_transposed(stamp_key, query) - lse)
-            grad_prob = times_transposed(values, grad)
-            stamp_grad_prob = times_transposed(stamp_value, grad)
-            delta = jnp.sum(prob * grad_prob, axis=0, keepdims=True)
-            delta = delta + (stamp_prob * stamp_grad_prob)[:1]
-            scores = (prob * (grad_prob - delta)).astype(low)
-            stamp_scores = (stamp_prob * (stamp_grad_prob - delta)).astype(low)
-            stamp_scores = jnp.where(first_row, stamp_scores.astype(f32), 0.0)
+            delta = jnp.sum(
+                grad.astype(f32) * mixed_ref[place, lanes].astype(f32), axis=1, keepdims=True
+            )
+            lse = lse_ref[place, head : head + 1]
+            wide_query = widened(tile, query, ones(tile, 1), *negative_parts(lse))
+            wide_grad = widened(tile, grad, *negative_parts(delta))
+            prob = jnp.exp(times_transposed(wide_keys, wide_query))
+            scores = (prob * times_transposed(wide_values, wide_grad)).astype(low)
+            stamp_prob = jnp.exp(times_transposed(wide_stamp_key, wide_query))
+            stamp_scores = stamp_prob * times_transposed(wide_stamp_value, wide_grad)
+            stamp_scores = jnp.where(first_row, stamp_scores, 0.0).astype(low)
             value_total += jnp.dot(prob.astype(low), grad, preferred_element_type=f32)
             key_total += jnp.dot(scores, query, preferred_element_type=f32)
             across = jnp.dot(keys_across, scores, preferred_element_type=f32)
-            across = across + stamp_column * stamp_scores[:1]
+            across = across + stamp_column * stamp_scores[:1].astype(f32)
             query_grad[place, lanes] = across.T * scale
-            stamp_key_total += jnp.dot(
-                stamp_scores.astype(low), query, preferred_element_type=f32
-            )
+            stamp_key_total += jnp.dot(stamp_scores, query, preferred_element_type=f32)
             stamp_value_total += jnp.dot(
                 jnp.where(first_row, stamp_prob, 0.0).astype(low), grad, preferred_element_type=f32
             )
@@ -2199,39 +2444,81 @@
         lanes = slice(pair * 128, pair * 128 + 128)
         out_ref[:, lanes] = turn_heads(both[:, lanes], rotary_ref[0], -rotary_ref[1]).astype(low)
     out_ref[:, 2 * wide :] = value_grad[...].astype(low)
-    pl.when(pl.program_id(0) == pl.num_programs(0) - 1)(end_swap)
-
-
-def flash_backward(turned, grad, lse, stamps, bias, rotary, heads, cut, collective_id):
+    count = outer_total.shape[1]
+    tile = 512
+    for start in range(0, normed_ref.shape[1], tile):
+        span = slice(start, start + tile)
+        product = outer_sum(normed_ref[:, span], out_ref[...])
+        stamp_part = stamp_normed_ref[0, span] * stamp_out_ref[0]
+        product = product + jnp.concatenate(
+            [jnp.zeros((tile, count - 2 * wide), f32), stamp_part], axis=1
+        )
+
+        @pl.when(pl.program_id(0) == 0)
+        def _():
+            outer_total[span] = product
+
+        @pl.when(pl.program_id(0) > 0)
+        def _():
+            outer_total[span] += product
+
+    @pl.when(pl.program_id(0) == pl.num_programs(0) - 1)
+    def _():
+        outer_ref[...] = outer_total[...].astype(outer_ref.dtype)
+        end_swap()
+
+
+def flash_backward(
+    turned, mixed, grad, lse, stamps, bias, rotary, heads, cut, normed, stamp_normed, collective_id
+):
     clips, rows = bias.shape
     wide = heads * HDIM
     blocked = lambda lanes: pl.BlockSpec((rows, lanes), lambda clip: (clip, 0))
-    grads, stamp_grads, mine = pl.pallas_call(
+    features = normed.shape[1]
+    grads, stamp_grads, mine, outer = pl.pallas_call(
         functools.partial(flash_backward_body, heads, rows // 4),
         grid=(clips,),
         out_shape=[
             jax.ShapeDtypeStruct((clips * rows, 3 * wide), jnp.bfloat16),
             jax.ShapeDtypeStruct((clips, 1, 2 * wide), jnp.float32),
             jax.ShapeDtypeStruct(cut.shape, cut.dtype),
+            jax.ShapeDtypeStruct((features, 3 * wide), jnp.bfloat16),
         ],
         in_specs=[
             blocked(3 * wide),
+            blocked(wide),
             blocked(wide),
             blocked(128),
             pl.BlockSpec((1, 1, 2 * wide), lambda clip: (clip, 0, 0)),
             pl.BlockSpec((1, rows, 1), lambda clip: (clip, 0, 0)),
             pl.BlockSpec((2, rows, 128), lambda clip: (0, 0, 0)),
             any_spec(),
+            blocked(features),
+            pl.BlockSpec((1, features, 1), lambda clip: (clip, 0, 0)),
         ],
         out_specs=[
             blocked(3 * wide),
             pl.BlockSpec((1, 1, 2 * wide), lambda clip: (clip, 0, 0)),
             any_spec(),
+            pl.BlockSpec((features, 3 * wide), lambda clip: (0, 0)),
         ],
-        scratch_shapes=[pltpu.VMEM((rows, wide), jnp.float32)] * 3 + swap_beside_scratch(1),
+        scratch_shapes=[pltpu.VMEM((rows, wide), jnp.float32)] * 3
+        + [pltpu.VMEM((features, 3 * wide), jnp.float32)]
+        + swap_beside_scratch(1),
         compiler_params=communicating(collective_id),
-    )(turned, grad, lse, stamps[:, None], bias[:, :, None], rotary, cut)
-    return grads, stamp_grads[:, 0], mine
+    )(
+        turned,
+        mixed,
+        grad,
+        lse,
+        stamps[:, None],
+        bias[:, :, None],
+        rotary,
+        cut,
+        normed,
+        stamp_normed.astype(jnp.float32)[:, :, None],
+    )
+    return grads, stamp_grads[:, 0], mine, outer
 
 
 def adam_body(factor_ref, weight_ref, first_ref, second_ref, grad_ref, *outs):
@@ -2270,15 +2557,11 @@
             weight_out[...], first_out[...], second_out[...] = results
 
 
-def adam_blocks(factor, weight, first, second, owned, width):
+def adam_blocks(factor, weight, first, second, owned, places):
     rows, columns = weight.shape
     group = owned[0].shape[0]
-    blocks = columns // (group * width)
-    places = [
-        (which, start, start + width)
-        for which, pieces in enumerate(owned)
-        for start in range(0, pieces.shape[2], width)
-    ][:blocks]
+    blocks = len(places)
+    width = columns // (group * blocks)
     piece = pl.BlockSpec((rows, group * width), lambda block: (0, block))
     whole = [pl.BlockSpec(pieces.shape, lambda block: (0, 0, 0)) for pieces in owned]
     return pl.pallas_call(
@@ -2367,17 +2650,17 @@
         ],
         axis=0,
     )
-    stream, gain_rows, packs, qkv_mine, rest_mine = enter(
+    stream, gain_rows, packs, qkv_mine, rest_mine, ff_low = enter(
         to_plane_order(frames[0]).reshape(group, piece, wide),
         norm_block,
         pack,
         attn_cut[:, :, : 3 * head_wide],
         jnp.concatenate([attn_cut[:, :, 3 * head_wide :], cross_cut], axis=2),
+        ff_weight,
         planes,
         1,
     )
     stream = stream.reshape(clips, own_rows, wide).astype(jnp.float32)
-    ff_low = ff_weight.astype(jnp.bfloat16)
 
     def over_planes(block):
         return lax.all_gather(block.reshape(group * owned, -1), "seq", axis=0, tiled=True)
@@ -2420,7 +2703,7 @@
     stamp_pair = stamp_pair.astype(jnp.bfloat16)
     rotary = rotary_lanes(true_place)
     key_bias = jnp.where(key_keep, 0.0, masked_score)
-    rotated, self_low, self_lse, gate_up_mine, down_mine, grad_out_low = flash_forward(
+    rotated, self_low, self_lse, gate_up_mine, down_mine, grad_out_mid = flash_forward(
         group_one,
         w_qkv,
         stamp_pair,
@@ -2431,52 +2714,47 @@
         masked.reshape(group, piece, wide),
         2,
     )
-    grad_out_low = grad_out_low.reshape(clips, own_rows, wide)
-    grad_out = grad_out_low.astype(jnp.float32)
     w_gate_up = over_planes(gate_up_mine)
     w_down = over_planes(down_mine)
     cond_pair = jnp.dot(cond_flat, w_cond, preferred_element_type=jnp.float32)
     cond_pair = cond_pair.astype(jnp.bfloat16).reshape(clips, cond_count, 2 * head_wide)
     cond_bias = jnp.where(cond_keep, 0.0, masked_score)[:, None]
-    (resid_one,) = dot_reduce(self_low, w_rest, clips, 6, stream, of_self_out)
-    group_two, cross_query, cross_out = gather_dot(
-        resid_one,
+    resid_one, group_two, cross_query, cross_out, grad_out_low = reduce_gather(
+        self_low,
         w_rest,
-        None,
-        7,
-        gain_rows[2:4],
-        span=of_cross_query,
+        clips,
+        6,
+        stream,
+        w_rest,
+        span=of_self_out,
+        gains=gain_rows[2:4],
+        second_span=of_cross_query,
         pair=cond_pair,
         bias=cond_bias,
-    )
+        passing=grad_out_mid,
+    )
+    grad_out_low = grad_out_low.reshape(clips, own_rows, wide)
     (resid_two,) = dot_reduce(cross_out, w_rest, clips, 8, resid_one, of_cross_out)
     group_three, gate_up = gather_dot(resid_two, w_gate_up, jnp.float32, 9, gain_rows[4:6])
     gate_up, grad_out_low = lax.optimization_barrier((gate_up, grad_out_low))
     group_grad_out, grad_gate_up, hidden = gather_dot(
         grad_out_low, w_down, None, 10, gate_up=gate_up
     )
+
     def over_rows(block):
         return lax.psum_scatter(
             block.astype(jnp.bfloat16), "seq", scatter_dimension=0, tiled=True
         ).reshape(group, owned, -1)
 
-    grad_two, stats_three, ff_piece, layer_out = ff_back(
-        grad_gate_up,
-        w_gate_up,
-        hidden,
-        w_down,
-        group_three,
-        group_grad_out,
-        grad_out_low,
-        resid_two,
-        gain_rows[4:5],
-        planes,
-        13,
-    )
-    layer_out = to_whole_order(layer_out.reshape(frame_rows, wide)).astype(jnp.bfloat16)
-    layer_out = layer_out.reshape(frames.shape)
+    layer_rows, ff_piece = ff_outer(
+        grad_gate_up, hidden, w_down, group_three, group_grad_out, resid_two, 12
+    )
+    ff_piece, grad_gate_up = lax.optimization_barrier((ff_piece, grad_gate_up))
     ff_rows = over_rows(ff_piece)
-    group_cross_branch, grad_cross_query, cond_grad = gather_dot(
+    grad_two, stats_three = dot_reduce(
+        grad_gate_up, w_gate_up, clips, 13, grad_out_low, back=(resid_two, gain_rows[4:5])
+    )
+    _, grad_cross_query, cond_grad, cross_piece = gather_dot(
         grad_two,
         w_rest,
         None,
@@ -2485,47 +2763,45 @@
         pair=cond_pair,
         bias=cond_bias,
         query=cross_query,
-    )
-    grad_one, stats_two = dot_reduce(
+        outer=(group_two, cross_out),
+    )
+    cond_grad = cond_grad.reshape(clips * cond_count, 2 * head_wide)
+    cond_piece = split_outer(cond_flat, cond_grad)
+    cond_piece = cond_piece.reshape(group, planes, cond_owned, 2 * head_wide)
+    cond_piece = jnp.swapaxes(cond_piece, 0, 1).reshape(wide, head_wide).astype(jnp.bfloat16)
+    grad_one, stats_two, _, grad_self_mixed, rest_piece, layer_out, cross_rows = reduce_gather(
         grad_cross_query,
         w_rest,
         clips,
         16,
         grad_two,
-        of_cross_query,
+        w_rest,
+        span=of_cross_query,
         back=(resid_one, gain_rows[2:3]),
-    )
-    group_self_branch, grad_self_mixed = gather_dot(
-        grad_one, w_rest, jnp.bfloat16, 17, span=of_self_out
-    )
-    cond_grad = cond_grad.reshape(clips * cond_count, 2 * head_wide)
-    cross_piece = split_outer(cond_flat, cond_grad)
-    cross_piece = cross_piece.reshape(group, planes, cond_owned, 2 * head_wide)
-    cross_piece = jnp.swapaxes(cross_piece, 0, 1).reshape(wide, head_wide)
-    rest_piece = jnp.concatenate(
-        [
-            outer_sum(group_self_branch, self_low),
-            outer_sum(group_two, grad_cross_query),
-            outer_sum(group_cross_branch, cross_out),
-            cross_piece,
-        ],
-        axis=1,
-    )
-    rest_piece = rest_piece.astype(jnp.bfloat16)
-    grad_self_mixed, rest_piece = lax.optimization_barrier((grad_self_mixed, rest_piece))
+        second_span=of_self_out,
+        outer=(self_low, cond_piece),
+        adding=cross_piece.reshape(planes, group * owned, 2 * head_wide),
+        leaving=layer_rows.reshape(clips, planes, piece, wide),
+    )
+    layer_out = to_whole_order(layer_out.reshape(frame_rows, wide)).astype(jnp.bfloat16)
+    layer_out = layer_out.reshape(frames.shape)
     rest_piece, ff_rows = lax.optimization_barrier((rest_piece, ff_rows))
     rest_rows = over_rows(rest_piece)
-    grad_project, stamp_grad, ff_owned = flash_backward(
-        rotated, grad_self_mixed, self_lse, stamp_pair, key_bias, rotary, heads, ff_rows, 3
+    grad_project, stamp_grad, ff_owned, qkv_piece = flash_backward(
+        rotated,
+        self_low,
+        grad_self_mixed,
+        self_lse,
+        stamp_pair,
+        key_bias,
+        rotary,
+        heads,
+        ff_rows,
+        group_one,
+        stamp_normed,
+        3,
     )
     grad_stamp_normed = split_times_transposed(stamp_grad, w_qkv[:, head_wide:])
-    qkv_piece = outer_sum(group_one, grad_project)
-    stamp_weight_grad = split_outer(stamp_normed, stamp_grad)
-    qkv_piece = jnp.concatenate(
-        [qkv_piece[:, :head_wide], qkv_piece[:, head_wide:] + stamp_weight_grad], axis=1
-    )
-    qkv_piece = qkv_piece.astype(jnp.bfloat16)
-    grad_project, qkv_piece = lax.optimization_barrier((grad_project, qkv_piece))
     qkv_rows = over_rows(qkv_piece)
     grad_project, rest_rows = lax.optimization_barrier((grad_project, rest_rows))
     frames_grad, stats_one = dot_reduce(
@@ -2545,16 +2821,15 @@
     norm_parts = norm_parts.reshape(group * planes, 6, owned)
     norm_parts = jnp.pad(norm_parts, ((0, 0), (0, 2), (0, 128 - owned)))
     ff_squares = jnp.sum(jnp.square(ff_owned.astype(jnp.float32)))
-    frames_grad, qkv_owned, rest_owned, norm_sum, total = leave(
+    frames_grad, owned_pieces, norm_sum, total = leave(
         frames_grad.reshape(clips, planes, piece, wide),
-        qkv_rows,
-        rest_rows,
+        [qkv_rows, cross_rows.reshape(group, owned, -1), rest_rows],
         norm_parts,
         ff_squares.reshape(1, 1),
         20,
     )
     frames_grad = to_whole_order(frames_grad.reshape(frame_rows, wide)).reshape(frames.shape)
-    cross_reduced = rest_owned[:, :, 3 * head_wide :].reshape(group, cond_owned, 2, head_wide)
+    cross_reduced = owned_pieces[2][:, :, head_wide:].reshape(group, cond_owned, 2, head_wide)
     cross_reduced = cross_reduced.transpose(1, 2, 0, 3).reshape(cross_weight.shape)
     cross_reduced = cross_reduced.astype(jnp.float32)
     norm_reduced = norm_sum[:6, :owned]
@@ -2562,7 +2837,15 @@
     factor = jnp.minimum(1.0, clip_limit / grad_norm)
     factor_block = factor.reshape(1, 1)
     attn_new, attn_first_new, attn_second_new = adam_blocks(
-        factor_block, attn_weight, attn_first, attn_second, [qkv_owned, rest_owned], head_wide
+        factor_block,
+        attn_weight,
+        attn_first,
+        attn_second,
+        owned_pieces,
+        [
+            (which, block * head_wide, (block + 1) * head_wide)
+            for which, block in ((0, 0), (0, 1), (0, 2), (2, 0), (1, 0), (1, 1))
+        ],
     )
     cross_new, cross_first_new, cross_second_new = adam_step(
         cross_weight, cross_first, cross_second, cross_reduced * factor, matrix_rate, matrix_decay

time: 741 us -> 710 us (0.958)
  matrix products: 36.5 us -> 18.4 us
  Pallas kernels: 626 us -> 617 us
    pallas_call x2 -> x4, Pallas kernels: 127 us -> 229 us  [the longest x2 152 us: reduce_gather(): pl.pallas_call(functools.partial(reduce_gather_body, clips, rows, sub, sp...]
    pallas_call x6 -> x4, Pallas kernels: 218 us -> 149 us  [gather_dot(): pl.pallas_call(functools.partial(gather_dot_body, clips, rows, sub, gains...]
    pallas_call x4 -> x3, Pallas kernels: 144 us -> 110 us  [dot_reduce(): pl.pallas_call(functools.partial(dot_reduce_body, clips, rows, sub, windo...]
    dot_general x8 -> x2, matrix products: 19 us -> 0.79 us  [outer_sum(): lax.dot_general(left_mat, right_mat, (((0,), (0,)), ((), ())), preferred_...]
    pallas_call x1, Pallas kernels: 52.8 us -> 38.2 us  [flash_forward(): pl.pallas_call(functools.partial(flash_forward_body, heads, rows // 4), g...]
    all_gather x4, waiting for transfers between devices: 0.05 us -> 10.3 us  [over_planes(): lax.all_gather(block.reshape(group * owned, -1), 'seq', axis=0, tiled=True)]
  transfers between devices with their start and end apart: 7 -> 7, of which waited for: 2 -> 1; matrix products, arithmetic and copies ran while one was open for 8% -> 5% of each run, Pallas kernels for 56% -> 64%
where the time goes in v5:
time: 710 us; the launch traced here: 704 us
  Pallas kernels  617 us (87%)
  local copies, waits for them, and re-layouts  22.6 us (3%)
  matrix products  18.4 us (3%)
  between operations  17.7 us (2%)
  other arithmetic  16 us (2%)
  waiting for transfers between devices  11.7 us (2%)
    pallas_call x2, Pallas kernels, reduce_gather(): pl.pallas_call(functools.partial(reduce_gather_body, clips, rows, sub, sp...  152 us
    pallas_call x4, Pallas kernels, gather_dot(): pl.pallas_call(functools.partial(gather_dot_body, clips, rows, sub, gains...  149 us
    pallas_call x3, Pallas kernels, dot_reduce(): pl.pallas_call(functools.partial(dot_reduce_body, clips, rows, sub, windo...  110 us
    pallas_call x1, Pallas kernels, leave(): pl.pallas_call(functools.partial(leave_body, group, planes, len(cuts)), o...  39.4 us
    pallas_call x1, Pallas kernels, ff_outer(): pl.pallas_call(functools.partial(ff_outer_body, clips, rows, sub), out_sh...  38.4 us
    pallas_call x1, Pallas kernels, flash_forward(): pl.pallas_call(functools.partial(flash_forward_body, heads, rows // 4), g...  38.2 us
    pallas_call x1, Pallas kernels, enter(): pl.pallas_call(functools.partial(enter_body, group, planes), out_shape=[l...  36.9 us
    pallas_call x1, Pallas kernels, flash_backward(): pl.pallas_call(functools.partial(flash_backward_body, heads, rows // 4),...  35.8 us
  transfers between devices with their start and end apart: 7, of which 1 were waited for; matrix products, arithmetic and copies ran while one was open for 5% of the time, Pallas kernels for 64%

profile of v5, /device:TPU:9, one launch (start us, length us, event | category | flops | bytes accessed | tf_op | source)
XLA Modules:
  0.0 703.9 jit_solution(14939355318835757817)
XLA Ops:
  14.7 2.7 fusion.11
  19.0 36.9 %shard_map.319 = (bf16[2,4,32,1536]{3,2,1,0:T(8,128)(2,1)}, f32[8,1536]{1,0:T(8,128)}, f32[8,8,1536]{2,1,0:T(8,128)}, bf16[8,48,576]{2,1,0:T(8,128)(2,1)}, bf16[...) custom-call(bf16[8,32,1536]{2,1,0:T(8,128)(2,1)} %bitcast.126, ...), custom_call_target="tpu_custom_call" | custom-call | tf_op jit(solution)/shard_map/pallas_call | solution.py:943
  58.1 4.6 gather_fusion
  65.4 37.6 %shard_map.320 = (bf16[2,8,128,1536]{3,2,1,0:T(8,128)(2,1)}, bf16[8,2,16,768]{3,2,1,0:T(8,128)(2,1)}) custom-call(f32[2,128,1536]{2,1,0:T(8,128)} %bitcast_convert_fusion.own_ref.base_ref.refs_0_, f32[2,1536]{1,0:T(2,128)} %get-tuple-element.164.refs_0_, bf16[4,2,16,768]{3,2,1,0:T(8,128)(2,1)} %select_select_fusion.refs_1_), custom_call_target="tpu_custom_call" | custom-call | tf_op jit(solution)/shard_map/pallas_call | solution.py:1529
  104.8 1.8 fusion.40
  108.2 2.9 fusion.12
  111.2 2.0 fusion.18
  113.8 38.2 %shard_map.321 = (bf16[2048,576]{1,0:T(8,128)(2,1)}, bf16[2048,192]{1,0:T(8,128)(2,1)}, f32[2048,128]{1,0:T(8,128)}, bf16[8,48,1536]{2,1,0:T(8,128)(2,1)}, bf16[...) custom-call(bf16[2048,1536]{1,0:T(8,128)(2,1)} %bitcast.102, ...), custom_call_target="tpu_custom_call" | custom-call | tf_op jit(solution)/shard_map/pallas_call | solution.py:2317
  157.5 67.0 %shard_map.322 = (f32[2,128,1536]{2,1,0:T(8,128)}, bf16[2,8,128,1536]{3,2,1,0:T(8,128)(2,1)}, bf16[2,8,128,192]{3,2,1,0:T(8,128)(2,1)}, bf16[2,8,128,192]{3,2,1,0:T(8,128)(2,1)}, bf16[2,4,32,1536]{3,2,1,0:T(8,128)(2,1)}) custom-call(bf16[2,8,128,192]{3,2,1,0:T(8,128)(2,1)} %bitcast.104, ...), custom_call_target="tpu_custom_call" | custom-call | tf_op jit(solution)/shard_map/pallas_call | solution.py:1986
  224.5 34.2 %shard_map.323.own_ref.values_ref.refs_0_ = f32[2,128,1536]{2,1,0:T(8,128)} custom-call(bf16[2,8,128,192]{3,2,1,0:T(8,128)(2,1)} %get-tuple-element.88.left_ref.refs_5_, bf16[1536,768]{1,0:T(8,128)(2,1)} %all-gather.7.cloned.1.call-done.mat_ref.refs_1_.refs_0_.refs_2_, f32[2,128,1536]{2,1,0:T(8,128)} %get-tuple-element.89.base_ref.refs_0_), custom_call_target="tpu_custom_call" | custom-call | tf_op jit(solution)/shard_map/pallas_call | solution.py:1754
  258.7 36.4 %shard_map.324 = (bf16[2,8,128,1536]{3,2,1,0:T(8,128)(2,1)}, f32[2,8,128,1536]{3,2,1,0:T(8,128)}) custom-call(f32[2,128,1536]{2,1,0:T(8,128)} %shard_map.323.own_ref.values_ref.refs_0_, f32[2,1536]{1,0:T(2,128)} %get-tuple-element.162.refs_0_, bf16[1536,1536]{1,0:T(8,128)(2,1)} %all-gather.9.cloned.1.call-done.refs_1_.mat_ref), custom_call_target="tpu_custom_call" | custom-call | tf_op jit(solution)/shard_map/pallas_call | solution.py:1529
  295.2 10.3 %all-gather.11.cloned.1.call-done.refs_0_.down_ref = bf16[1536,768]{1,0:T(8,128)(2,1)} async-done(((bf16[384,768]{1,0:T(8,128)(2,1)}), bf16[1536,768]{1,0:T(8,128)(2,1)}) %all-gather.11.cloned.1.call-update) | async-done | bytes 2359312 | tf_op jit(solution)/shard_map/all_gather | solution.py:2666
  305.5 35.1 %shard_map.325 = (bf16[8,2,128,1536]{3,2,1,0:T(8,128)(2,1)}, bf16[2,8,128,1536]{3,2,1,0:T(8,128)(2,1)}, bf16[8,2,128,768]{3,2,1,0:T(8,128)(2,1)}) custom-call(bf16[2,128,1536]{2,1,0:T(8,128)(2,1)} %bitcast.110, bf16[1536,768]{1,0:T(8,128)(2,1)} %all-gather.11.cloned.1.call-done.refs_0_.down_ref, f32[2,8,128,1536]{3,2,1,0:T(8,128)} %get-tuple-element.91), custom_call_target="tpu_custom_call" | custom-call | tf_op jit(solution)/shard_map/pallas_call | solution.py:1529
  340.6 38.4 %shard_map.326 = (bf16[2,128,1536]{2,1,0:T(8,128)(2,1)}, bf16[1536,2304]{1,0:T(8,128)(2,1)}) custom-call(bf16[2,8,128,1536]{3,2,1,0:T(8,128)(2,1)} %get-tuple-element.96.gates_ref, bf16[8,2,128,768]{3,2,1,0:T(8,128)(2,1)} %get-tuple-element.97.hidden_ref, bf16[1536,768]{1,0:T(8,128)(2,1)} %all-gather.11.cloned.1.call-done.refs_0_.down_ref, ...), custom_call_target="tpu_custom_call" | custom-call | tf_op jit(solution)/shard_map/pallas_call | solution.py:2125
  379.1 39.4 %shard_map.327 = (f32[2,128,1536]{2,1,0:T(8,128)}, f32[2,1536]{1,0:T(2,128)}) custom-call(bf16[2,8,128,1536]{3,2,1,0:T(8,128)(2,1)} %get-tuple-element.96.gates_ref, bf16[1536,1536]{1,0:T(8,128)(2,1)} %all-gather.9.cloned.1.call-done.refs_1_.mat_ref, bf16[2,128,1536]{2,1,0:T(8,128)(2,1)} %bitcast.111, f32[2,128,1536]{2,1,0:T(8,128)} %shard_map.323.own_ref.values_ref.refs_0_, ...), custom_call_target="tpu_custom_call" | custom-call | tf_op jit(solution)/shard_map/pallas_call | solution.py:1754
  418.5 39.7 %shard_map.328 = (bf16[2,8,128,1536]{3,2,1,0:T(8,128)(2,1)}, bf16[2,8,128,192]{3,2,1,0:T(8,128)(2,1)}, f32[2,128,384]{2,1,0:T(8,128)}, bf16[1536,384]{1,0:T(8,128)(2,1)}) custom-call(f32[2,128,1536]{2,1,0:T(8,128)} %get-tuple-element.102.own_ref.base_ref, bf16[1536,768]{1,0:T(8,128)(2,1)} %all-gather.7.cloned.1.call-done.mat_ref.refs_1_.refs_0_.refs_2_, ...), custom_call_target="tpu_custom_call" | custom-call | tf_op jit(solution)/shard_map/pallas_call | solution.py:1529
  461.6 84.6 %shard_map.329 = (f32[2,128,1536]{2,1,0:T(8,128)}, f32[2,1536]{1,0:T(2,128)}, bf16[2,8,128,1536]{3,2,1,0:T(8,128)(2,1)}, bf16[2,8,128,192]{3,2,1,0:T(8,128)(2,1)...) custom-call(bf16[2,8,128,192]{3,2,1,0:T(8,128)(2,1)} %get-tuple-elem, ...), custom_call_target="tpu_custom_call" | custom-call | tf_op jit(solution)/shard_map/pallas_call | solution.py:1986
  549.2 35.8 %shard_map.330 = (bf16[2048,576]{1,0:T(8,128)(2,1)}, f32[2,1,384]{2,1,0:T(1,128)}, bf16[8,48,2304]{2,1,0:T(8,128)(2,1)}, bf16[1536,576]{1,0:T(8,128)(2,1)}) custom-call(bf16[2048,576]{1,0:T(8,128)(2,1)} %get-tuple-element.110.turned_ref, bf16[2048,192]{1,0:T(8,128)(2,1)} %get-tuple-element.84.mixed_ref, bf16[2048,192]{1,0:T(8,128)(2,1)} %bitcast.123, ...), custom_call_target="tpu_custom_call" | custom-call | tf_op jit(solution)/shard_map/pallas_call | solution.py:2478
  586.1 2.9 fusion.14
  592.2 36.1 %shard_map.331 = (bf16[2,128,1536]{2,1,0:T(8,128)(2,1)}, f32[2,1536]{1,0:T(2,128)}) custom-call(bf16[2,8,128,576]{3,2,1,0:T(8,128)(2,1)} %bitcast.112, bf16[1536,576]{1,0:T(8,128)(2,1)} %all-gather.5.cloned.1.call-done.mat_ref, f32[2,128,1536]{2,1,0:T(8,128)} %get-tuple-element.119.base_ref, f32[2,128,1536]{2,1,0:T(8,128)} %bitcast_convert_fusion.own_ref.base_ref.refs_0_, ...), custom_call_target="tpu_custom_call" | custom-call | tf_op jit(solution)/shard_map/pallas_call | solution.py:1754
  629.9 39.4 %shard_map.332 = (bf16[8,32,1536]{2,1,0:T(8,128)(2,1)}, bf16[8,48,576]{2,1,0:T(8,128)(2,1)}, bf16[8,48,384]{2,1,0:T(8,128)(2,1)}, bf16[8,48,384]{2,1,0:T(8,128)(...) custom-call(bf16[2,4,32,1536]{3,2,1,0:T(8,128)(2,1)} %bitcast.128, ...), custom_call_target="tpu_custom_call" | custom-call | tf_op jit(solution)/shard_map/pallas_call | solution.py:724
  673.0 3.0 fusion.10
  676.0 10.3 %shard_map.334 = (f32[48,18432]{1,0:T(8,128)}, f32[48,18432]{1,0:T(8,128)}, f32[48,18432]{1,0:T(8,128)}) custom-call(f32[1,1]{1,0:T(1,128)} %bitcast.52.factor_ref, f32[48,18432]{1,0:T(8,128)} %weight_ref.3, f32[48,18432]{1,0:T(8,128)} %first_ref.3, f32[48,18432]{1,0:T(8,128)} %second_ref.3, bf16[8,48,2304]{2,1,0:T(8,128)(2,1)} %get-tuple-element.128.grad_ref), custom_call_target="tpu_custom_call" | custom-call | tf_op jit(solution)/shard_map/pallas_call | solution.py:2583
  688.0 7.4 %shard_map.333 = (f32[48,9216]{1,0:T(8,128)}, f32[48,9216]{1,0:T(8,128)}, f32[48,9216]{1,0:T(8,128)}) custom-call(f32[1,1]{1,0:T(1,128)} %bitcast.52.factor_ref, f32[48,9216]{1,0:T(8,128)} %weight_ref.2, f32[48,9216]{1,0:T(8,128)} %first_ref.2, f32[48,9216]{1,0:T(8,128)} %second_ref.2, bf16[8,48,576]{2,1,0:T(8,128)(2,1)} %get-tuple-element.131.refs_0_, ...), custom_call_target="tpu_custom_call" | custom-call | tf_op jit(solution)/shard_map/pallas_call | solution.py:2567
  (141 shorter events, 39.3 us)
Async XLA Ops:
  7.2 7.5 %copy-start = (bf16[1,256,1536]{2,1,0:T(8,128)(2,1)S(1)}, bf16[1,256,1536]{2,1,0:T(8,128)(2,1)}, u32[]{:S(2)}) copy-start(bf16[1,256,1536]{2,1,0:T(8,128)(2,1)} %param.21) | copy-start | bytes 2359300
  7.2 104.0 %all-gather.5.cloned.1.call-start = ((), (), s32[]{:S(2)}) async-start(), calls=%async_computation.3 | async-start | bytes 2457600 | tf_op jit(solution)/shard_map/all_gather | solution.py:2666
  14.7 3.7 copy-start.14
  55.9 7.5 %copy-start.9 = (f32[8,1536]{1,0:T(8,128)S(1)}, f32[8,1536]{1,0:T(8,128)}, u32[]{:S(2)}) copy-start(f32[8,1536]{1,0:T(8,128)} %get-tuple-element.79) | copy-start | bytes 147460
  55.9 8.1 %copy-start.5 = (bf16[2,4,32,1536]{3,2,1,0:T(8,128)(2,1)S(1)}, bf16[2,4,32,1536]{3,2,1,0:T(8,128)(2,1)}, u32[]{:S(2)}) copy-start(bf16[2,4,32,1536]{3,2,1,0:T(8,128)(2,1)} %get-tuple-element.78) | copy-start | bytes 2359300
  56.0 98.5 %all-gather.7.cloned.1.call-start = ((), (), s32[]{:S(2)}) async-start(), calls=%async_computation.4 | async-start | bytes 2949120 | tf_op jit(solution)/shard_map/all_gather | solution.py:2666
  56.7 202.0 %all-gather.9.cloned.1.call-start = ((), (), s32[]{:S(2)}) async-start(), calls=%async_computation.5 | async-start | bytes 5898240 | tf_op jit(solution)/shard_map/all_gather | solution.py:2666
  65.4 41.4 %copy-start.10 = (s32[1024]{0:T(1024)S(1)}, s32[1024]{0:T(1024)}, u32[]{:S(2)}) copy-start(s32[1024]{0:T(1024)} %constant.115) | copy-start | bytes 12292
  65.4 42.7 %copy-start.19 = (bf16[1,256,1536]{2,1,0:T(8,128)(2,1)S(1)}, bf16[1,256,1536]{2,1,0:T(8,128)(2,1)}, u32[]{:S(2)}) copy-start(bf16[1,256,1536]{2,1,0:T(8,128)(2,1)} %param.27) | copy-start | bytes 2359300
  152.0 153.4 %all-gather.11.cloned.1.call-start = ((), (), s32[]{:S(2)}) async-start(), calls=%async_computation.6 | async-start | bytes 2949120 | tf_op jit(solution)/shard_map/all_gather | solution.py:2666
  152.6 393.6 %reduce-scatter.4.cloned.1.call-start = ((), (), s32[]{:S(2)}) async-start(), calls=%async_computation.7 | async-start | bytes 8847360 | tf_op jit(solution)/shard_map/reduce_scatter | solution.py:2745
  379.0 213.2 %reduce-scatter.6.cloned.1.call-start = ((), (), s32[]{:S(2)}) async-start(), calls=%async_computation.8 | async-start | bytes 1474560 | tf_op jit(solution)/shard_map/reduce_scatter | solution.py:2745
  546.3 83.6 %reduce-scatter.8.cloned.1.call-start = ((), (), s32[]{:S(2)}) async-start(), calls=%async_computation.9 | async-start | bytes 2457600 | tf_op jit(solution)/shard_map/reduce_scatter | solution.py:2745
  586.1 2.9 copy-start.2
  586.1 3.0 copy-start.18
  592.2 36.8 %copy-start.12 = (f32[2,1536]{1,0:T(2,128)S(1)}, f32[2,1536]{1,0:T(2,128)}, u32[]{:S(2)}) copy-start(f32[2,1536]{1,0:T(2,128)} %get-tuple-element.127) | copy-start | bytes 36868
  592.2 36.8 %copy-start.13 = (f32[2,1536]{1,0:T(2,128)S(1)}, f32[2,1536]{1,0:T(2,128)}, u32[]{:S(2)}) copy-start(f32[2,1536]{1,0:T(2,128)} %get-tuple-element.126) | copy-start | bytes 36868
  669.3 3.7 copy-start.21
  675.9 10.4 %copy-start.15 = (f32[6,48]{1,0:T(8,128)S(1)}, f32[6,48]{1,0:T(8,128)}, u32[]{:S(2)}) copy-start(f32[6,48]{1,0:T(8,128)} %param.36) | copy-start | bytes 3460
  675.9 10.4 %copy-start.16 = (f32[6,48]{1,0:T(8,128)S(1)}, f32[6,48]{1,0:T(8,128)}, u32[]{:S(2)}) copy-start(f32[6,48]{1,0:T(8,128)} %param.37) | copy-start | bytes 3460
  675.9 10.4 %copy-start.17 = (f32[8,128]{1,0:T(8,128)S(1)}, f32[8,128]{1,0:T(8,128)}, u32[]{:S(2)}) copy-start(f32[8,128]{1,0:T(8,128)} %get-tuple-element.135) | copy-start | bytes 12292
  675.9 11.0 %copy-start.7 = (f32[24,3072]{1,0:T(8,128)S(1)}, f32[24,3072]{1,0:T(8,128)}, u32[]{:S(2)}) copy-start(f32[24,3072]{1,0:T(8,128)} %param.34) | copy-start | bytes 884740
  675.9 11.0 %copy-start.8 = (f32[24,3072]{1,0:T(8,128)S(1)}, f32[24,3072]{1,0:T(8,128)}, u32[]{:S(2)}) copy-start(f32[24,3072]{1,0:T(8,128)} %param.35) | copy-start | bytes 884740
  688.0 7.4 %copy-start.1 = (bf16[1,256,1536]{2,1,0:T(8,128)(2,1)S(1)}, bf16[1,256,1536]{2,1,0:T(8,128)(2,1)}, u32[]{:S(2)}) copy-start(bf16[1,256,1536]{2,1,0:T(8,128)(2,1)} %param.21) | copy-start | bytes 2359300
  (7 other events, 12.8 us)
Sparse Core Ops, SparseCore 0:
  56.1 45.1 all-gather.4
  102.8 49.9 all-gather.6
  154.4 99.6 all-gather.8
  255.6 49.8 all-gather.10
  379.1 159.6 reduce-scatter.3
  546.4 27.2 reduce-scatter.5
  585.2 38.1 reduce-scatter.7

commit v6 on v5

--- a/solution.py
+++ b/solution.py
@@ -649,18 +649,18 @@
     ]
 
 
-def leave_body(group, planes, cuts, kept_ref, *refs):
-    cut_refs, refs = refs[:cuts], refs[cuts:]
-    parts_ref, squares_ref, own_ref, *refs = refs
-    mine_refs, refs = refs[:cuts], refs[cuts:]
-    norm_ref, total_ref, mid, terms, block, blocks, *sems = refs
-    part_send, part_recv, block_send, block_recv = sems[:4]
+def settle_body(group, planes, dones, kept_ref, cut_ref, parts_ref, squares_ref, *refs):
+    done_refs, refs = refs[:dones], refs[dones:]
+    own_ref, mine_ref, norm_ref, total_ref, mid, terms, block, blocks, *sems = refs
+    part_send, part_recv, block_send, block_recv, *sems = sems
     place, depth, flip = plane_places()
     devices = [(flip(mask), lax.rem(depth + step, planes)) for mask, step in everyone(planes)]
     greet(devices)
     here = place * planes + depth
-    rows = outward_steps(group, planes, kept_ref, own_ref, mid, *sems[4:9])
-    next(rows)
+    start_swap, end_swap = swap_beside(
+        [(lambda other: cut_ref.at[other], lambda other: mine_ref.at[other])], *sems[:3]
+    )
+    start_swap()
     copies = []
     for index, (other, plane) in enumerate(devices):
         copy = remote(
@@ -672,31 +672,26 @@
         )
         copy.start()
         copies.append(copy)
+    rows = outward_steps(group, planes, kept_ref, own_ref, mid, *sems[3:])
+    next(rows)
     terms[here] = parts_ref[here]
-    start_swap, end_swap = swap_beside(
-        [
-            (
-                lambda other, cut_ref=cut_ref: cut_ref.at[other],
-                lambda other, mine_ref=mine_ref: mine_ref.at[other],
-            )
-            for cut_ref, mine_ref in zip(cut_refs, mine_refs)
-        ],
-        *sems[9:],
-    )
-    start_swap()
-    next(rows)
+
+    def squares_of(array_ref):
+        values = [array_ref[piece].astype(jnp.float32) for piece in range(array_ref.shape[0])]
+        return jnp.sum(sum(value * value for value in values))
+
+    squares = squares_ref[0, 0]
+    for done_ref in done_refs:
+        squares = squares + squares_of(done_ref)
     for other, plane in devices:
         source = other * planes + plane
         one = terms.at[source]
         remote(one, one, part_send.at[0], part_recv.at[source], (other, plane)).wait_recv()
     norm_sum = jnp.sum(terms[...], axis=0)
     norm_ref[...] = norm_sum
+    squares = squares + jnp.sum(norm_sum * norm_sum)
     end_swap()
-    squares = squares_ref[0, 0] + jnp.sum(norm_sum * norm_sum)
-    for mine_ref in mine_refs:
-        for piece in range(group):
-            values = mine_ref[piece].astype(jnp.float32)
-            squares = squares + jnp.sum(values * values)
+    squares = squares + squares_of(mine_ref)
     block[...] = jnp.full(block.shape, squares)
     blocks[here] = block[...]
     for index, (other, plane) in enumerate(devices):
@@ -706,6 +701,7 @@
         copy.start()
         copies.append(copy)
     next(rows)
+    next(rows)
     for other, plane in devices:
         source = other * planes + plane
         one = blocks.at[source]
@@ -715,23 +711,24 @@
         copy.wait_send()
 
 
-def leave(kept_rows, cuts, norm_parts, squares, collective_id):
+def settle(kept_rows, cut, done, norm_parts, squares, collective_id):
     per, planes, rows, wide = kept_rows.shape
     group = per * planes
-    count = group * planes
+    count = norm_parts.shape[0]
     inside = pl.BlockSpec(memory_space=pltpu.VMEM)
     like = lambda shape, array: jax.ShapeDtypeStruct(shape, array.dtype)
-    own, *results, norm_sum, total, _ = pl.pallas_call(
-        functools.partial(leave_body, group, planes, len(cuts)),
-        out_shape=[like((group, rows, wide), kept_rows)]
-        + [like(cut.shape, cut) for cut in cuts]
-        + [
+    *results, _ = pl.pallas_call(
+        functools.partial(settle_body, group, planes, len(done)),
+        out_shape=[
+            like((group, rows, wide), kept_rows),
+            like(cut.shape, cut),
             like(norm_parts.shape[1:], norm_parts),
             like((8, 128), norm_parts),
             like((group, rows, wide), kept_rows),
         ],
-        in_specs=[any_spec()] * (1 + len(cuts)) + [inside, pl.BlockSpec(memory_space=pltpu.SMEM)],
-        out_specs=[any_spec()] + [inside] * (len(cuts) + 2) + [any_spec()],
+        in_specs=[any_spec(), any_spec(), inside, pl.BlockSpec(memory_space=pltpu.SMEM)]
+        + [inside] * len(done),
+        out_specs=[any_spec()] + [inside] * 3 + [any_spec()],
         scratch_shapes=[
             pltpu.VMEM(norm_parts.shape, jnp.float32),
             pltpu.VMEM((8, 128), jnp.float32),
@@ -741,25 +738,43 @@
             DMA((count,)),
             DMA((count,)),
         ]
-        + outward_scratch(group, planes)
-        + swap_beside_scratch(len(cuts)),
+        + swap_beside_scratch(1)
+        + outward_scratch(group, planes),
         compiler_params=communicating(collective_id),
-    )(kept_rows, *cuts, norm_parts, squares)
-    return own, results, norm_sum, total
+    )(kept_rows, cut, norm_parts, squares, *done)
+    return results
 
 
 def everyone(planes):
     return [(mask, step) for mask in range(8) for step in range(planes) if mask or step]
+
+
+def to_plane_features(values, group, planes):
+    width = values.shape[1] // (group * planes)
+    starts = [
+        (owner * planes + plane) * width for plane in range(planes) for owner in range(group)
+    ]
+    return jnp.concatenate([values[:, start : start + width] for start in starts], axis=1)
+
+
+def to_whole_features(values, group, planes):
+    width = values.shape[1] // (group * planes)
+    starts = [
+        (plane * group + owner) * width for owner in range(group) for plane in range(planes)
+    ]
+    return jnp.concatenate([values[:, start : start + width] for start in starts], axis=1)
 
 
 def enter_body(
     group,
     planes,
-    own_ref,
+    frames_ref,
+    grads_ref,
+    valid_ref,
     norm_ref,
     pack_ref,
-    first_cut_ref,
-    rest_cut_ref,
+    attn_ref,
+    cross_ref,
     ff_ref,
     kept_ref,
     gains_ref,
@@ -767,39 +782,51 @@
     first_mine_ref,
     rest_mine_ref,
     ff_low_ref,
+    grads_mid_ref,
     mid,
     norms_ref,
+    pieces,
+    grad_pieces,
+    attn_full,
+    cross_full,
+    first_cut,
+    rest_cut,
     ff_full,
     ff_low,
-    ff_sem,
-    *sems,
+    load_sem,
+    near_send,
+    near_recv,
+    far_send,
+    far_recv,
+    local_sem,
+    norm_send,
+    norm_recv,
+    swap_send,
+    swap_recv,
+    stay_sem,
 ):
-    (
-        near_send,
-        near_recv,
-        far_send,
-        far_recv,
-        local_sem,
-        norm_send,
-        norm_recv,
-        pack_send,
-        pack_recv,
-        cut_send,
-        cut_recv,
-        stay_sem,
-    ) = sems
     place, depth, flip = plane_places()
     per = group // planes
+    low = pieces.dtype
+    f32 = jnp.float32
     others = everyone(planes)
-    ff_load = pltpu.make_async_copy(ff_ref, ff_full, ff_sem.at[0])
-    ff_load.start()
+    loads = [
+        pltpu.make_async_copy(source, goal, load_sem.at[which])
+        for which, (source, goal) in enumerate(
+            ((attn_ref, attn_full), (cross_ref, cross_full), (ff_ref, ff_full))
+        )
+    ]
+    for copy in loads:
+        copy.start()
+    own = to_plane_features(frames_ref[...].astype(f32), group, planes).astype(low)
+    pieces[...] = own.reshape(pieces.shape)
     greet([(flip(mask), lax.rem(depth + step, planes)) for mask, step in others])
     here = place * planes + depth
     first = []
     for mask in (6, 7, 2, 3, 4, 5, 1):
         other = flip(mask)
         copy = remote(
-            own_ref.at[other],
+            pieces.at[other],
             mid.at[place],
             near_send.at[mask],
             near_recv.at[mask],
@@ -818,55 +845,49 @@
         )
         copy.start()
         small.append(copy)
-    for mask in range(1, group):
-        copy = remote(
-            pack_ref,
-            packs_ref.at[place],
-            pack_send.at[mask],
-            pack_recv.at[mask],
-            (flip(mask), depth),
-        )
-        copy.start()
-        small.append(copy)
-    stays = [
-        pltpu.make_async_copy(norm_ref, norms_ref.at[here], stay_sem.at[0]),
-        pltpu.make_async_copy(pack_ref, packs_ref.at[place], stay_sem.at[1]),
-        pltpu.make_async_copy(
-            first_cut_ref.at[place], first_mine_ref.at[place], stay_sem.at[2]
-        ),
-        pltpu.make_async_copy(rest_cut_ref.at[place], rest_mine_ref.at[place], stay_sem.at[3]),
-    ]
-    for stay in stays:
-        stay.start()
-    cuts = []
-    for which, (cut_ref, mine_ref) in enumerate(
-        ((first_cut_ref, first_mine_ref), (rest_cut_ref, rest_mine_ref))
-    ):
+    swaps = []
+
+    def swap(which, source, goal):
         for mask in (6, 7, 2, 3, 4, 5, 1):
             other = flip(mask)
             copy = remote(
-                cut_ref.at[other],
-                mine_ref.at[place],
-                cut_send.at[which, mask],
-                cut_recv.at[which, mask],
+                source(other),
+                goal.at[place],
+                swap_send.at[which, mask],
+                swap_recv.at[which, mask],
                 (other, depth),
             )
             copy.start()
-            cuts.append(copy)
-    ff_load.wait()
-    tile = ff_full.shape[1] // 24
-
-    def round_tile(index, carry):
-        lanes = pl.ds(pl.multiple_of(index * tile, 128), tile)
-        ff_low[:, lanes] = ff_full[:, lanes].astype(ff_low.dtype)
-        return carry
-
+            swaps.append(copy)
+        stay = pltpu.make_async_copy(source(place), goal.at[place], stay_sem.at[which])
+        stay.start()
+        stays.append(stay)
+
+    stays = []
+    swap(0, lambda other: pack_ref, packs_ref)
+    norms_ref[here] = norm_ref[...]
+    loads[0].wait()
+    loads[1].wait()
+    wide = attn_full.shape[1] // 6
+    piece = wide // group
+    for device in range(group):
+        for block in range(6):
+            cut_ref = (first_cut, rest_cut)[block // 3]
+            start = block * wide + device * piece
+            cut_ref[device, :, block % 3 * piece : (block % 3 + 1) * piece] = attn_full[
+                :, start : start + piece
+            ].astype(low)
+        keys = cross_full[:, device * piece : (device + 1) * piece]
+        values = cross_full[:, wide + device * piece : wide + (device + 1) * piece]
+        rest_cut[device, :, 3 * piece :] = jnp.concatenate([keys, values], axis=0).astype(low)
+    swap(1, lambda other: first_cut.at[other], first_mine_ref)
+    swap(2, lambda other: rest_cut.at[other], rest_mine_ref)
     second = []
     arrivals = dict(first)
     for mask in (0, 1, 2, 3, 4, 5, 6, 7):
         source = flip(mask)
         goal, slot = lax.div(source, per), lax.rem(source, per)
-        block = own_ref.at[place]
+        block = pieces.at[place]
         if mask:
             arrivals[mask].wait_recv()
             block = mid.at[source]
@@ -881,9 +902,40 @@
         pl.when(goal != depth)(away.start)
         pl.when(goal == depth)(stay.start)
         second.append((goal, away, stay))
+    grads = to_plane_features(grads_ref[...].astype(f32) * valid_ref[...], group, planes)
+    grad_pieces[...] = grads.astype(low).reshape(grad_pieces.shape)
+    grads_store = pltpu.make_async_copy(grad_pieces, grads_mid_ref, stay_sem.at[3])
+    grads_store.start()
+    loads[2].wait()
+    tile = ff_full.shape[1] // 24
+
+    def round_tile(index, carry):
+        lanes = pl.ds(pl.multiple_of(index * tile, 128), tile)
+        ff_low[:, lanes] = ff_full[:, lanes].astype(low)
+        return carry
+
     lax.fori_loop(0, 24, round_tile, 0)
-    ff_store = pltpu.make_async_copy(ff_low, ff_low_ref, ff_sem.at[1])
+    ff_store = pltpu.make_async_copy(ff_low, ff_low_ref, load_sem.at[3])
     ff_store.start()
+    for mask, step in others:
+        source = flip(mask) * planes + lax.rem(depth + step, planes)
+        block = norms_ref.at[source]
+        remote(
+            block,
+            block,
+            norm_send.at[0],
+            norm_recv.at[source],
+            (flip(mask), lax.rem(depth + step, planes)),
+        ).wait_recv()
+    width = gains_ref.shape[1] // (group * planes)
+    gains_ref[...] = jnp.concatenate(
+        [
+            norms_ref[owner * planes + plane, :, :width]
+            for plane in range(planes)
+            for owner in range(group)
+        ],
+        axis=1,
+    )
     for slot in range(per):
         for origin in range(planes):
             block = kept_ref.at[slot, origin]
@@ -897,67 +949,56 @@
                 ).wait_recv
             )
     ff_store.wait()
-    for mask, step in others:
-        source = flip(mask) * planes + lax.rem(depth + step, planes)
-        block = norms_ref.at[source]
-        remote(
-            block,
-            block,
-            norm_send.at[0],
-            norm_recv.at[source],
-            (flip(mask), lax.rem(depth + step, planes)),
-        ).wait_recv()
-    for copy in small:
-        copy.wait_send()
-    stays[0].wait()
-    width = gains_ref.shape[1] // (group * planes)
-    gains_ref[...] = jnp.concatenate(
-        [
-            norms_ref[owner * planes + plane, :, :width]
-            for plane in range(planes)
-            for owner in range(group)
-        ],
-        axis=1,
-    )
-    for mask in range(1, group):
-        block = packs_ref.at[flip(mask)]
-        remote(
-            block, block, pack_send.at[0], pack_recv.at[mask], (flip(mask), depth)
-        ).wait_recv()
-    for copy in cuts:
+    grads_store.wait()
+    for copy in swaps:
         copy.wait()
+    for stay in stays:
+        stay.wait()
     for goal, away, stay in second:
         pl.when(goal != depth)(away.wait_send)
         pl.when(goal == depth)(stay.wait)
     for mask, copy in first:
         copy.wait_send()
-    for stay in stays[1:]:
-        stay.wait()
-
-
-def enter(rows_of_clip, norm_block, pack, first_cut, rest_cut, ff_weight, planes, collective_id):
-    group, rows, wide = rows_of_clip.shape
+    for copy in small:
+        copy.wait_send()
+
+
+def enter(frames, grads, valid, norm_block, pack, attn, cross, ff, planes, collective_id):
+    rows, wide = frames.shape
+    group = 8
     count = group * planes
-    like = lambda shape, array: jax.ShapeDtypeStruct(shape, array.dtype)
+    piece = rows // group
+    owned = attn.shape[0]
+    third = attn.shape[1] // (2 * group)
+    rest = third + cross.shape[0] * cross.shape[1] // (owned * group)
+    low, f32 = jnp.bfloat16, jnp.float32
     inside = pl.BlockSpec(memory_space=pltpu.VMEM)
+    like = jax.ShapeDtypeStruct
     *results, _ = pl.pallas_call(
         functools.partial(enter_body, group, planes),
         out_shape=[
-            like((group // planes, planes, rows, wide), rows_of_clip),
-            like((norm_block.shape[0], wide), norm_block),
-            like((group,) + pack.shape, pack),
-            like(first_cut.shape, first_cut),
-            like(rest_cut.shape, rest_cut),
-            like(ff_weight.shape, rest_cut),
-            like((group, rows, wide), rows_of_clip),
+            like((group // planes, planes, piece, wide), low),
+            like((norm_block.shape[0], wide), f32),
+            like((group,) + pack.shape, f32),
+            like((group, owned, third), low),
+            like((group, owned, rest), low),
+            like(ff.shape, low),
+            like((group, piece, wide), low),
+            like((group, piece, wide), low),
         ],
-        in_specs=[any_spec(), inside] + [any_spec()] * 4,
-        out_specs=[any_spec(), inside] + [any_spec()] * 5,
+        in_specs=[inside] * 4 + [any_spec()] * 4,
+        out_specs=[any_spec(), inside] + [any_spec()] * 6,
         scratch_shapes=[
-            pltpu.VMEM((count,) + norm_block.shape, norm_block.dtype),
-            pltpu.VMEM(ff_weight.shape, ff_weight.dtype),
-            pltpu.VMEM(ff_weight.shape, rest_cut.dtype),
-            DMA((2,)),
+            pltpu.VMEM((count,) + norm_block.shape, f32),
+            pltpu.VMEM((group, piece, wide), low),
+            pltpu.VMEM((group, piece, wide), low),
+            pltpu.VMEM(attn.shape, f32),
+            pltpu.VMEM(cross.shape, f32),
+            pltpu.VMEM((group, owned, third), low),
+            pltpu.VMEM((group, owned, rest), low),
+            pltpu.VMEM(ff.shape, f32),
+            pltpu.VMEM(ff.shape, low),
+            DMA((4,)),
             DMA((group,)),
             DMA((group,)),
             DMA((group,)),
@@ -965,14 +1006,12 @@
             DMA((group,)),
             DMA((count,)),
             DMA((count,)),
-            DMA((group,)),
-            DMA((group,)),
-            DMA((2, group)),
-            DMA((2, group)),
+            DMA((4, group)),
+            DMA((4, group)),
             DMA((4,)),
         ],
         compiler_params=communicating(collective_id),
-    )(rows_of_clip, norm_block, pack, first_cut, rest_cut, ff_weight)
+    )(frames, grads, valid, norm_block, pack, attn, cross, ff)
     return results
 
 
@@ -1670,7 +1709,7 @@
     return result, stats
 
 
-def final_back(values_ref, gain_ref, base_ref, sum_ref, stats_ref):
+def final_back(values_ref, gain_ref, base_ref, sum_ref, stats_ref, order=None):
     def final(index, clip, span, result):
         if values_ref is not None:
             result, stats = norm_back(values_ref[clip, span], gain_ref[...], result)
@@ -1678,6 +1717,8 @@
                 row = row + stats_ref[which : which + 1] if index else row
                 stats_ref[which : which + 1] = row
         result = base_ref[clip, span].astype(jnp.float32) + result
+        if order:
+            result = to_whole_features(result, *order)
         sum_ref[clip, span] = result.astype(sum_ref.dtype)
         return result
 
@@ -1696,13 +1737,16 @@
     return multiply
 
 
-def dot_reduce_body(clips, rows, sub, window, span, back, left_ref, mat_ref, base_ref, *refs):
+def dot_reduce_body(clips, rows, sub, window, span, back, order, swapped, left_ref, mat_ref, base_ref, *refs):
     refs = list(refs)
     take = lambda count: [refs.pop(0) for _ in range(count)]
     values_ref, gain_ref = take(2) if back else (None, None)
+    cut_ref = take(1)[0] if swapped else None
     sum_ref = take(1)[0]
     stats_ref = take(1)[0] if back else None
+    mine_ref = take(1)[0] if swapped else None
     left, mat, mat_sem, left_sem = take(4)
+    swap_sems = take(3) if swapped else None
     terms = refs[0]
     place, depth, flip = plane_places()
     load = pltpu.make_async_copy(mat_ref.at[:, pl.ds(*window)], mat, mat_sem)
@@ -1717,7 +1761,14 @@
         ]
         for copy in loads[number]:
             copy.start()
-    greet([(flip(1), depth), (flip(2), depth), (flip(4), depth)])
+    if swapped:
+        start_swap, end_swap = swap_beside(
+            [(lambda other: cut_ref.at[other], lambda other: mine_ref.at[other])], *swap_sems
+        )
+        greet([(flip(mask), depth) for mask in range(1, 8)])
+        start_swap()
+    else:
+        greet([(flip(1), depth), (flip(2), depth), (flip(4), depth)])
     load.wait()
 
     def blocks(number):
@@ -1730,14 +1781,28 @@
         rows,
         sub,
         terms_of(clips, rows, blocks, mat, span, terms),
-        final_back(values_ref, gain_ref, base_ref, sum_ref, stats_ref),
+        final_back(values_ref, gain_ref, base_ref, sum_ref, stats_ref, order),
         *refs,
     )
     for _ in steps:
         pass
-
-
-def dot_reduce(left, matrix, clips, collective_id, base, span=None, back=None, kind=jnp.float32, sub=64):
+    if swapped:
+        end_swap()
+
+
+def dot_reduce(
+    left,
+    matrix,
+    clips,
+    collective_id,
+    base,
+    span=None,
+    back=None,
+    kind=jnp.float32,
+    order=None,
+    cut=None,
+    sub=64,
+):
     wide = matrix.shape[0]
     rows, inner = left.shape[0] // (8 * clips), left.shape[1]
     low = jnp.bfloat16
@@ -1751,8 +1816,25 @@
         in_specs += [inside] * 2
         outs.append(jax.ShapeDtypeStruct((2, wide), jnp.float32))
         out_specs.append(inside)
+    swap_sems = []
+    if cut is not None:
+        args.append(cut)
+        in_specs.append(any_spec())
+        outs.append(jax.ShapeDtypeStruct(cut.shape, cut.dtype))
+        out_specs.append(any_spec())
+        swap_sems = swap_beside_scratch(1)
     return pl.pallas_call(
-        functools.partial(dot_reduce_body, clips, rows, sub, window, span, back is not None),
+        functools.partial(
+            dot_reduce_body,
+            clips,
+            rows,
+            sub,
+            window,
+            span,
+            back is not None,
+            order,
+            cut is not None,
+        ),
         out_shape=outs,
         in_specs=in_specs,
         out_specs=out_specs,
@@ -1762,6 +1844,7 @@
             DMA(()),
             DMA((8, clips)),
         ]
+        + swap_sems
         + reduce_scratch(clips, rows, sub, wide),
         compiler_params=communicating(collective_id),
     )(*args)
@@ -2012,6 +2095,7 @@
 
 
 def ff_outer_body(
+    order_of,
     clips,
     rows,
     sub,
@@ -2092,7 +2176,8 @@
     loads[1].wait()
 
     def layer_rows(index, clip, span, result):
-        layer_ref[clip, span] = (values_ref[clip, span] + result).astype(layer_ref.dtype)
+        result = to_whole_features(values_ref[clip, span] + result, *order_of)
+        layer_ref[clip, span] = result.astype(layer_ref.dtype)
 
     steps = reduce_steps(
         clips,
@@ -2116,14 +2201,14 @@
     next(steps)
 
 
-def ff_outer(gates, hidden, down, normed, grads, values, collective_id, sub=64):
+def ff_outer(gates, hidden, down, normed, grads, values, planes, collective_id, sub=64):
     clips, rows, wide = values.shape
     low = jnp.bfloat16
     inner, columns = gates.shape[1], gates.shape[1] + hidden.shape[1]
     tile = 512
     inside = pl.BlockSpec(memory_space=pltpu.VMEM)
     return pl.pallas_call(
-        functools.partial(ff_outer_body, clips, rows, sub),
+        functools.partial(ff_outer_body, (8, planes), clips, rows, sub),
         out_shape=[
             jax.ShapeDtypeStruct((clips, rows, wide), low),
             jax.ShapeDtypeStruct((wide, columns), low),
@@ -2351,11 +2436,13 @@
     bias_ref,
     rotary_ref,
     cut_ref,
+    cross_cut_ref,
     normed_ref,
     stamp_normed_ref,
     out_ref,
     stamp_out_ref,
     mine_ref,
+    cross_mine_ref,
     outer_ref,
     query_grad,
     key_grad,
@@ -2365,7 +2452,11 @@
 ):
     place, depth, flip = plane_places()
     start_swap, end_swap = swap_beside(
-        [(lambda other: cut_ref.at[other], lambda other: mine_ref.at[other])], *sems
+        [
+            (lambda other: cut_ref.at[other], lambda other: mine_ref.at[other]),
+            (lambda other: cross_cut_ref.at[other], lambda other: cross_mine_ref.at[other]),
+        ],
+        *sems,
     )
 
     @pl.when(pl.program_id(0) == 0)
@@ -2469,19 +2560,32 @@
 
 
 def flash_backward(
-    turned, mixed, grad, lse, stamps, bias, rotary, heads, cut, normed, stamp_normed, collective_id
+    turned,
+    mixed,
+    grad,
+    lse,
+    stamps,
+    bias,
+    rotary,
+    heads,
+    cut,
+    cross_cut,
+    normed,
+    stamp_normed,
+    collective_id,
 ):
-    clips, rows = bias.shape
+    clips, rows, _ = bias.shape
     wide = heads * HDIM
     blocked = lambda lanes: pl.BlockSpec((rows, lanes), lambda clip: (clip, 0))
     features = normed.shape[1]
-    grads, stamp_grads, mine, outer = pl.pallas_call(
+    grads, stamp_grads, mine, cross_mine, outer = pl.pallas_call(
         functools.partial(flash_backward_body, heads, rows // 4),
         grid=(clips,),
         out_shape=[
             jax.ShapeDtypeStruct((clips * rows, 3 * wide), jnp.bfloat16),
             jax.ShapeDtypeStruct((clips, 1, 2 * wide), jnp.float32),
             jax.ShapeDtypeStruct(cut.shape, cut.dtype),
+            jax.ShapeDtypeStruct(cross_cut.shape, cross_cut.dtype),
             jax.ShapeDtypeStruct((features, 3 * wide), jnp.bfloat16),
         ],
         in_specs=[
@@ -2493,6 +2597,7 @@
             pl.BlockSpec((1, rows, 1), lambda clip: (clip, 0, 0)),
             pl.BlockSpec((2, rows, 128), lambda clip: (0, 0, 0)),
             any_spec(),
+            any_spec(),
             blocked(features),
             pl.BlockSpec((1, features, 1), lambda clip: (clip, 0, 0)),
         ],
@@ -2500,11 +2605,12 @@
             blocked(3 * wide),
             pl.BlockSpec((1, 1, 2 * wide), lambda clip: (clip, 0, 0)),
             any_spec(),
+            any_spec(),
             pl.BlockSpec((features, 3 * wide), lambda clip: (0, 0)),
         ],
         scratch_shapes=[pltpu.VMEM((rows, wide), jnp.float32)] * 3
         + [pltpu.VMEM((features, 3 * wide), jnp.float32)]
-        + swap_beside_scratch(1),
+        + swap_beside_scratch(2),
         compiler_params=communicating(collective_id),
     )(
         turned,
@@ -2512,82 +2618,85 @@
         grad,
         lse,
         stamps[:, None],
-        bias[:, :, None],
+        bias,
         rotary,
         cut,
+        cross_cut,
         normed,
-        stamp_normed.astype(jnp.float32)[:, :, None],
-    )
-    return grads, stamp_grads[:, 0], mine, outer
-
-
-def adam_body(factor_ref, weight_ref, first_ref, second_ref, grad_ref, *outs):
-    gradient = jnp.concatenate(
-        [grad_ref[part] for part in range(grad_ref.shape[0])], axis=1
-    ).astype(jnp.float32)
-    results = adam_step(
-        weight_ref[...],
-        first_ref[...],
-        second_ref[...],
-        gradient * factor_ref[0, 0],
-        matrix_rate,
-        matrix_decay,
-    )
-    for out, result in zip(outs, results):
-        out[...] = result
-
-
-def adam_blocks_body(places, factor_ref, weight_ref, first_ref, second_ref, *refs):
-    *owned_refs, weight_out, first_out, second_out = refs
+        stamp_normed,
+    )
+    return grads, stamp_grads[:, 0], mine, cross_mine, outer
+
+
+def adam_body(ff_steps, places, *refs):
+    refs = list(refs)
+    take = lambda count: [refs.pop(0) for _ in range(count)]
+    total_ref = take(1)[0]
+    ff_refs, ff_grad_ref = take(3), take(1)[0]
+    attn_refs = take(3)
+    attn_grads = take(1 + max(which for which, _, _ in places))
+    ff_outs, attn_outs = take(3), take(3)
+    step = pl.program_id(0)
+    factor = jnp.minimum(1.0, clip_limit / jnp.sqrt(total_ref[0:1, 0:1]))
+
+    def update(olds, gradient, outs):
+        results = adam_step(
+            *[old[...] for old in olds],
+            gradient.astype(jnp.float32) * factor,
+            matrix_rate,
+            matrix_decay,
+        )
+        for out, result in zip(outs, results):
+            out[...] = result
+
+    @pl.when(step < ff_steps)
+    def _():
+        gradient = jnp.concatenate(
+            [ff_grad_ref[part] for part in range(ff_grad_ref.shape[0])], axis=1
+        )
+        update(ff_refs, gradient, ff_outs)
+
     for block, (which, start, stop) in enumerate(places):
 
-        @pl.when(pl.program_id(0) == block)
-        def _(owned_ref=owned_refs[which], start=start, stop=stop):
+        @pl.when(step == ff_steps + block)
+        def _(owned_ref=attn_grads[which], start=start, stop=stop):
             gradient = jnp.concatenate(
                 [owned_ref[part, :, start:stop] for part in range(owned_ref.shape[0])], axis=1
-            ).astype(jnp.float32)
-            results = adam_step(
-                weight_ref[...],
-                first_ref[...],
-                second_ref[...],
-                gradient * factor_ref[0, 0],
-                matrix_rate,
-                matrix_decay,
             )
-            weight_out[...], first_out[...], second_out[...] = results
-
-
-def adam_blocks(factor, weight, first, second, owned, places):
-    rows, columns = weight.shape
-    group = owned[0].shape[0]
-    blocks = len(places)
-    width = columns // (group * blocks)
-    piece = pl.BlockSpec((rows, group * width), lambda block: (0, block))
-    whole = [pl.BlockSpec(pieces.shape, lambda block: (0, 0, 0)) for pieces in owned]
-    return pl.pallas_call(
-        functools.partial(adam_blocks_body, places),
-        grid=(blocks,),
-        out_shape=[jax.ShapeDtypeStruct(weight.shape, jnp.float32)] * 3,
-        in_specs=[pl.BlockSpec(memory_space=pltpu.SMEM), piece, piece, piece] + whole,
-        out_specs=[piece] * 3,
+            update(attn_refs, gradient, attn_outs)
+
+
+def adam(total, ff, ff_grad, attn, attn_grads, places):
+    rows, columns = ff[0].shape
+    group, _, held = ff_grad.shape
+    parts = group // 2
+    width = columns // (3 * group)
+    ff_steps = 3 * group // parts
+    steps = ff_steps + len(places)
+    ff_step = lambda step: jnp.minimum(step, ff_steps - 1)
+    ff_piece = pl.BlockSpec((rows, parts * width), lambda step: (0, ff_step(step)))
+    ff_grads = pl.BlockSpec(
+        (parts, rows, width), lambda step: (lax.rem(ff_step(step), 2), 0, lax.div(ff_step(step), 2))
+    )
+    attn_piece = pl.BlockSpec(
+        (rows, attn[0].shape[1] // len(places)), lambda step: (0, jnp.maximum(step - ff_steps, 0))
+    )
+    whole = [pl.BlockSpec(grad.shape, lambda step: (0, 0, 0)) for grad in attn_grads]
+    f32 = jnp.float32
+    results = pl.pallas_call(
+        functools.partial(adam_body, ff_steps, places),
+        grid=(steps,),
+        out_shape=[jax.ShapeDtypeStruct(ff[0].shape, f32)] * 3
+        + [jax.ShapeDtypeStruct(attn[0].shape, f32)] * 3,
+        in_specs=[pl.BlockSpec((8, 128), lambda step: (0, 0))]
+        + [ff_piece] * 3
+        + [ff_grads]
+        + [attn_piece] * 3
+        + whole,
+        out_specs=[ff_piece] * 3 + [attn_piece] * 3,
         compiler_params=pltpu.CompilerParams(vmem_limit_bytes=VMEM_LIMIT),
-    )(factor, weight, first, second, *owned)
-
-
-def adam_matrix(factor, weight, first, second, owned, width, parts):
-    rows, columns = weight.shape
-    group = owned.shape[0]
-    steps = group // parts
-    piece = pl.BlockSpec((rows, parts * width), lambda block, step: (0, block * steps + step))
-    grads = pl.BlockSpec((parts, rows, width), lambda block, step: (step, 0, block))
-    return pl.pallas_call(
-        adam_body,
-        grid=(columns // (group * width), steps),
-        out_shape=[jax.ShapeDtypeStruct(weight.shape, jnp.float32)] * 3,
-        in_specs=[pl.BlockSpec(memory_space=pltpu.SMEM), piece, piece, piece, grads],
-        out_specs=[piece] * 3,
-        compiler_params=pltpu.CompilerParams(vmem_limit_bytes=VMEM_LIMIT),
-    )(factor, weight, first, second, owned)
+    )(total, *ff, ff_grad, *attn, *attn_grads)
+    return results[:3], results[3:]
 
 
 def plane_device(
@@ -2625,19 +2734,6 @@
     cond_count, cond_wide = cond_ids.shape[1], cond_table.shape[1]
     cond_owned = cross_weight.shape[0]
 
-    order = jnp.arange(wide).reshape(group, planes, owned).swapaxes(0, 1).reshape(wide)
-    order_mat = (jnp.arange(wide)[:, None] == order[None, :]).astype(jnp.bfloat16)
-
-    def to_plane_order(values):
-        return jnp.dot(values, order_mat, preferred_element_type=jnp.float32).astype(jnp.bfloat16)
-
-    def to_whole_order(values):
-        return times_transposed(values, order_mat)
-
-    attn_low = attn_weight.astype(jnp.bfloat16).reshape(owned, 6, group, head_wide)
-    attn_cut = attn_low.transpose(2, 0, 1, 3).reshape(group, owned, 6 * head_wide)
-    cross_low = cross_weight.astype(jnp.bfloat16).reshape(cond_owned, 2, group, head_wide)
-    cross_cut = cross_low.transpose(2, 0, 1, 3).reshape(group, owned, -1)
     norm_block = norm_param.astype(jnp.bfloat16).astype(jnp.float32)
     norm_block = jnp.pad(norm_block, ((0, 2), (0, 128 - owned)))
     pack = jnp.concatenate(
@@ -2650,12 +2746,16 @@
         ],
         axis=0,
     )
-    stream, gain_rows, packs, qkv_mine, rest_mine, ff_low = enter(
-        to_plane_order(frames[0]).reshape(group, piece, wide),
+    positions = depth * frame_rows + jnp.arange(frame_rows)
+    valid = (positions < lengths).astype(jnp.float32)[:, None]
+    stream, gain_rows, packs, qkv_mine, rest_mine, ff_low, grad_pieces = enter(
+        frames[0],
+        cotangent[0],
+        valid,
         norm_block,
         pack,
-        attn_cut[:, :, : 3 * head_wide],
-        jnp.concatenate([attn_cut[:, :, 3 * head_wide :], cross_cut], axis=2),
+        attn_weight,
+        cross_weight,
         ff_weight,
         planes,
         1,
@@ -2670,10 +2770,11 @@
     of_self_out = (0, head_wide)
     of_cross_query = (head_wide, 2 * head_wide)
     of_cross_out = (2 * head_wide, 3 * head_wide)
-    w_cond = w_rest[:, 3 * head_wide :].reshape(planes, group, cond_owned, -1)
-    w_cond = jnp.swapaxes(w_cond, 0, 1).reshape(cond_wide, 2 * head_wide)
+    w_cond = w_rest[:, 3 * head_wide :].reshape(planes, group, 2, cond_owned, head_wide)
+    w_cond = w_cond.transpose(1, 0, 3, 2, 4).reshape(cond_wide, 2 * head_wide)
     plane_packs = lax.dynamic_slice_in_dim(packs, depth * clips, clips, axis=0)
-    stamps = to_plane_order(plane_packs[:, 0].astype(jnp.bfloat16)).astype(jnp.float32)
+    stamps = plane_packs[:, 0].reshape(clips, group, planes, owned)
+    stamps = stamps.swapaxes(1, 2).reshape(clips, wide)
     cond_keep = plane_packs[:, 2, :cond_count] > 0
     clip_lengths = plane_packs[:, 3, 0].astype(jnp.int32)
     share = cond_count // group
@@ -2685,10 +2786,6 @@
     picked = jnp.take(cond_table, jnp.clip(relative, 0, vocab_rows - 1), axis=0)
     picked = jnp.where(inside[..., None], picked, jnp.zeros((), picked.dtype))
     picked = picked.reshape(planes, clips, share, cond_wide)
-    positions = depth * frame_rows + jnp.arange(frame_rows)
-    frame_valid = (positions[None, :] < lengths[:, None]).astype(cotangent.dtype)
-    masked = to_plane_order((cotangent * frame_valid[..., None])[0])
-
     group_rows = clips * seq_frames
     row_place = np.arange(seq_frames)
     row_owner, row_rest = row_place // own_rows, row_place % own_rows
@@ -2711,7 +2808,7 @@
         rotary,
         heads,
         ff_low,
-        masked.reshape(group, piece, wide),
+        grad_pieces,
         2,
     )
     w_gate_up = over_planes(gate_up_mine)
@@ -2736,7 +2833,11 @@
     grad_out_low = grad_out_low.reshape(clips, own_rows, wide)
     (resid_two,) = dot_reduce(cross_out, w_rest, clips, 8, resid_one, of_cross_out)
     group_three, gate_up = gather_dot(resid_two, w_gate_up, jnp.float32, 9, gain_rows[4:6])
-    gate_up, grad_out_low = lax.optimization_barrier((gate_up, grad_out_low))
+    stamp_column = stamp_normed.astype(jnp.float32)[:, :, None]
+    bias_column = key_bias[:, :, None]
+    gate_up, grad_out_low, stamp_column, bias_column = lax.optimization_barrier(
+        (gate_up, grad_out_low, stamp_column, bias_column)
+    )
     group_grad_out, grad_gate_up, hidden = gather_dot(
         grad_out_low, w_down, None, 10, gate_up=gate_up
     )
@@ -2747,7 +2848,7 @@
         ).reshape(group, owned, -1)
 
     layer_rows, ff_piece = ff_outer(
-        grad_gate_up, hidden, w_down, group_three, group_grad_out, resid_two, 12
+        grad_gate_up, hidden, w_down, group_three, group_grad_out, resid_two, planes, 12
     )
     ff_piece, grad_gate_up = lax.optimization_barrier((ff_piece, grad_gate_up))
     ff_rows = over_rows(ff_piece)
@@ -2767,8 +2868,9 @@
     )
     cond_grad = cond_grad.reshape(clips * cond_count, 2 * head_wide)
     cond_piece = split_outer(cond_flat, cond_grad)
-    cond_piece = cond_piece.reshape(group, planes, cond_owned, 2 * head_wide)
-    cond_piece = jnp.swapaxes(cond_piece, 0, 1).reshape(wide, head_wide).astype(jnp.bfloat16)
+    cond_piece = cond_piece.reshape(group, planes, cond_owned, 2, head_wide)
+    cond_piece = cond_piece.transpose(1, 0, 3, 2, 4).reshape(wide, head_wide)
+    cond_piece = cond_piece.astype(jnp.bfloat16)
     grad_one, stats_two, _, grad_self_mixed, rest_piece, layer_out, cross_rows = reduce_gather(
         grad_cross_query,
         w_rest,
@@ -2783,28 +2885,27 @@
         adding=cross_piece.reshape(planes, group * owned, 2 * head_wide),
         leaving=layer_rows.reshape(clips, planes, piece, wide),
     )
-    layer_out = to_whole_order(layer_out.reshape(frame_rows, wide)).astype(jnp.bfloat16)
-    layer_out = layer_out.reshape(frames.shape)
     rest_piece, ff_rows = lax.optimization_barrier((rest_piece, ff_rows))
     rest_rows = over_rows(rest_piece)
-    grad_project, stamp_grad, ff_owned, qkv_piece = flash_backward(
+    grad_project, stamp_grad, ff_owned, cross_owned, qkv_piece = flash_backward(
         rotated,
         self_low,
         grad_self_mixed,
         self_lse,
         stamp_pair,
-        key_bias,
+        bias_column,
         rotary,
         heads,
         ff_rows,
+        cross_rows.reshape(group, owned, -1),
         group_one,
-        stamp_normed,
+        stamp_column,
         3,
     )
     grad_stamp_normed = split_times_transposed(stamp_grad, w_qkv[:, head_wide:])
     qkv_rows = over_rows(qkv_piece)
     grad_project, rest_rows = lax.optimization_barrier((grad_project, rest_rows))
-    frames_grad, stats_one = dot_reduce(
+    frames_grad, stats_one, rest_owned = dot_reduce(
         grad_project,
         w_qkv,
         clips,
@@ -2812,6 +2913,8 @@
         grad_one,
         back=(stream, gain_rows[0:1]),
         kind=jnp.bfloat16,
+        order=(group, planes),
+        cut=rest_rows,
     )
     _, norm_stamp_back = jax.vjp(layer_norm, stamps, gain_rows[0], gain_rows[1])
     _, grad_gain_stamp, grad_bias_stamp = norm_stamp_back(grad_stamp_normed)
@@ -2821,40 +2924,40 @@
     norm_parts = norm_parts.reshape(group * planes, 6, owned)
     norm_parts = jnp.pad(norm_parts, ((0, 0), (0, 2), (0, 128 - owned)))
     ff_squares = jnp.sum(jnp.square(ff_owned.astype(jnp.float32)))
-    frames_grad, owned_pieces, norm_sum, total = leave(
+    frames_grad, qkv_owned, norm_sum, total = settle(
         frames_grad.reshape(clips, planes, piece, wide),
-        [qkv_rows, cross_rows.reshape(group, owned, -1), rest_rows],
+        qkv_rows,
+        [cross_owned, rest_owned],
         norm_parts,
         ff_squares.reshape(1, 1),
         20,
     )
-    frames_grad = to_whole_order(frames_grad.reshape(frame_rows, wide)).reshape(frames.shape)
-    cross_reduced = owned_pieces[2][:, :, head_wide:].reshape(group, cond_owned, 2, head_wide)
-    cross_reduced = cross_reduced.transpose(1, 2, 0, 3).reshape(cross_weight.shape)
+    cross_reduced = rest_owned[:, :, head_wide:].reshape(group, 2, cond_owned, head_wide)
+    cross_reduced = cross_reduced.transpose(2, 1, 0, 3).reshape(cross_weight.shape)
     cross_reduced = cross_reduced.astype(jnp.float32)
     norm_reduced = norm_sum[:6, :owned]
     grad_norm = jnp.sqrt(total[0, 0])
     factor = jnp.minimum(1.0, clip_limit / grad_norm)
-    factor_block = factor.reshape(1, 1)
-    attn_new, attn_first_new, attn_second_new = adam_blocks(
-        factor_block,
-        attn_weight,
-        attn_first,
-        attn_second,
-        owned_pieces,
+    ff_results, attn_results = adam(
+        total,
+        (ff_weight, ff_first, ff_second),
+        ff_owned,
+        (attn_weight, attn_first, attn_second),
+        [qkv_owned, cross_owned, rest_owned],
         [
             (which, block * head_wide, (block + 1) * head_wide)
             for which, block in ((0, 0), (0, 1), (0, 2), (2, 0), (1, 0), (1, 1))
         ],
     )
+    ff_new, ff_first_new, ff_second_new = ff_results
+    attn_new, attn_first_new, attn_second_new = attn_results
+    frames_grad = frames_grad.reshape(frames.shape).astype(jnp.float32)
+    layer_out = layer_out.reshape(frames.shape)
     cross_new, cross_first_new, cross_second_new = adam_step(
         cross_weight, cross_first, cross_second, cross_reduced * factor, matrix_rate, matrix_decay
     )
     norm_new, norm_first_new, norm_second_new = adam_step(
         norm_param, norm_first, norm_second, norm_reduced * factor, gain_rate, 0.0
-    )
-    ff_new, ff_first_new, ff_second_new = adam_matrix(
-        factor_block, ff_weight, ff_first, ff_second, ff_owned, ff_wide, group // 2
     )
     return (
         layer_out,

time: 710 us -> 704 us (level)
  matrix products: 18.4 us -> 4.92 us
    dot_general x3 -> x0, matrix products: 7.42 us -> none  [to_plane_order(): jnp.dot(values, order_mat, preferred_element_type=jnp.float32)]
    pallas_call x4 -> x3, Pallas kernels: 95.5 us -> 96.9 us  [the longest x1 40.2 us: settle(): pl.pallas_call(functools.partial(settle_body, group, planes, len(done)),...]
  transfers between devices with their start and end apart: 7 -> 7, of which waited for: 1 -> 1; matrix products, arithmetic and copies ran while one was open for 5% -> 4% of each run, Pallas kernels for 64% -> 65%
where the time goes in v6:
time: 704 us; the launch traced here: 694 us
  Pallas kernels  622 us (88%)
  other arithmetic  19.2 us (3%)
  local copies, waits for them, and re-layouts  18.6 us (3%)
  between operations  17.4 us (2%)
  waiting for transfers between devices  11.5 us (2%)
    pallas_call x2, Pallas kernels, reduce_gather(): pl.pallas_call(functools.partial(reduce_gather_body, clips, rows, sub, sp...  153 us
    pallas_call x4, Pallas kernels, gather_dot(): pl.pallas_call(functools.partial(gather_dot_body, clips, rows, sub, gains...  149 us
    pallas_call x3, Pallas kernels, dot_reduce(): pl.pallas_call(functools.partial(dot_reduce_body, clips, rows, sub, windo...  110 us
    pallas_call x1, Pallas kernels, settle(): pl.pallas_call(functools.partial(settle_body, group, planes, len(done)),...  40.2 us
    pallas_call x1, Pallas kernels, flash_forward(): pl.pallas_call(functools.partial(flash_forward_body, heads, rows // 4), g...  38.5 us
    pallas_call x1, Pallas kernels, ff_outer(): pl.pallas_call(functools.partial(ff_outer_body, (8, planes), clips, rows,...  38.4 us
    pallas_call x1, Pallas kernels, enter(): pl.pallas_call(functools.partial(enter_body, group, planes), out_shape=[l...  38.4 us
    pallas_call x1, Pallas kernels, flash_backward(): pl.pallas_call(functools.partial(flash_backward_body, heads, rows // 4),...  36.1 us
  transfers between devices with their start and end apart: 7, of which 1 were waited for; matrix products, arithmetic and copies ran while one was open for 4% of the time, Pallas kernels for 65%

profile of v6, /device:TPU:9, one launch (start us, length us, event | category | flops | bytes accessed | tf_op | source)
XLA Modules:
  0.0 694.4 jit_solution(13717785097588224753)
XLA Ops:
  12.5 38.4 %shard_map.319 = (bf16[2,4,32,1536]{3,2,1,0:T(8,128)(2,1)}, f32[8,1536]{1,0:T(8,128)}, f32[8,8,1536]{2,1,0:T(8,128)}, bf16[8,48,576]{2,1,0:T(8,128)(2,1)}, bf16[...) custom-call(bf16[256,1536]{1,0:T(8,128)(2,1)} %bitcast.105, ...), custom_call_target="tpu_custom_call" | custom-call | tf_op jit(solution)/shard_map/pallas_call | solution.py:977
  54.1 4.6 gather_fusion
  60.1 1.4 bitcast_convert_fusion.1.own_ref.base_ref.refs_0_
  61.4 36.9 %shard_map.320 = (bf16[2,8,128,1536]{3,2,1,0:T(8,128)(2,1)}, bf16[8,2,16,768]{3,2,1,0:T(8,128)(2,1)}) custom-call(f32[2,128,1536]{2,1,0:T(8,128)} %bitcast_convert_fusion.1.own_ref.base_ref.refs_0_, f32[2,1536]{1,0:T(2,128)} %get-tuple-element.168.refs_0_, bf16[4,2,16,768]{3,2,1,0:T(8,128)(2,1)} %select_select_fusion.refs_1_), custom_call_target="tpu_custom_call" | custom-call | tf_op jit(solution)/shard_map/pallas_call | solution.py:1568
  100.7 1.9 fusion.1
  103.2 38.5 %shard_map.321 = (bf16[2048,576]{1,0:T(8,128)(2,1)}, bf16[2048,192]{1,0:T(8,128)(2,1)}, f32[2048,128]{1,0:T(8,128)}, bf16[8,48,1536]{2,1,0:T(8,128)(2,1)}, bf16[...) custom-call(bf16[2048,1536]{1,0:T(8,128)(2,1)} %bitcast.85, bf16[1536,576]{1,0:T(8,128)(2,1)} %all-gather.5.cloned.1.call-done.mat_ref, ...), custom_call_target="tpu_custom_call" | custom-call | tf_op jit(solution)/shard_map/pallas_call | solution.py:2402
  146.1 1.6 fusion.6.stamp_normed_ref
  147.7 1.5 slice.69
  151.4 68.2 %shard_map.322 = (f32[2,128,1536]{2,1,0:T(8,128)}, bf16[2,8,128,1536]{3,2,1,0:T(8,128)(2,1)}, bf16[2,8,128,192]{3,2,1,0:T(8,128)(2,1)}, bf16[2,8,128,192]{3,2,1,0:T(8,128)(2,1)}, bf16[2,4,32,1536]{3,2,1,0:T(8,128)(2,1)}) custom-call(bf16[2,8,128,192]{3,2,1,0:T(8,128)(2,1)} %bitcast.87, ...), custom_call_target="tpu_custom_call" | custom-call | tf_op jit(solution)/shard_map/pallas_call | solution.py:2069
  219.6 34.5 %shard_map.323.own_ref.values_ref.refs_0_ = f32[2,128,1536]{2,1,0:T(8,128)} custom-call(bf16[2,8,128,192]{3,2,1,0:T(8,128)(2,1)} %get-tuple-element.92.left_ref.refs_5_, bf16[1536,768]{1,0:T(8,128)(2,1)} %all-gather.7.cloned.1.call-done.mat_ref.refs_1_.refs_0_.refs_2_, f32[2,128,1536]{2,1,0:T(8,128)} %get-tuple-element.93.base_ref.refs_0_), custom_call_target="tpu_custom_call" | custom-call | tf_op jit(solution)/shard_map/pallas_call | solution.py:1826
  254.1 36.5 %shard_map.324 = (bf16[2,8,128,1536]{3,2,1,0:T(8,128)(2,1)}, f32[2,8,128,1536]{3,2,1,0:T(8,128)}) custom-call(f32[2,128,1536]{2,1,0:T(8,128)} %shard_map.323.own_ref.values_ref.refs_0_, f32[2,1536]{1,0:T(2,128)} %get-tuple-element.166.refs_0_, bf16[1536,1536]{1,0:T(8,128)(2,1)} %all-gather.9.cloned.1.call-done.refs_1_.mat_ref), custom_call_target="tpu_custom_call" | custom-call | tf_op jit(solution)/shard_map/pallas_call | solution.py:1568
  290.6 10.1 %all-gather.11.cloned.1.call-done.refs_0_.down_ref = bf16[1536,768]{1,0:T(8,128)(2,1)} async-done(((bf16[384,768]{1,0:T(8,128)(2,1)}), bf16[1536,768]{1,0:T(8,128)(2,1)}) %all-gather.11.cloned.1.call-update) | async-done | bytes 2359312 | tf_op jit(solution)/shard_map/all_gather | solution.py:2766
  300.7 35.1 %shard_map.325 = (bf16[8,2,128,1536]{3,2,1,0:T(8,128)(2,1)}, bf16[2,8,128,1536]{3,2,1,0:T(8,128)(2,1)}, bf16[8,2,128,768]{3,2,1,0:T(8,128)(2,1)}) custom-call(bf16[2,128,1536]{2,1,0:T(8,128)(2,1)} %bitcast.95, bf16[1536,768]{1,0:T(8,128)(2,1)} %all-gather.11.cloned.1.call-done.refs_0_.down_ref, f32[2,8,128,1536]{3,2,1,0:T(8,128)} %get-tuple-element.95), custom_call_target="tpu_custom_call" | custom-call | tf_op jit(solution)/shard_map/pallas_call | solution.py:1568
  335.8 38.4 %shard_map.326 = (bf16[2,128,1536]{2,1,0:T(8,128)(2,1)}, bf16[1536,2304]{1,0:T(8,128)(2,1)}) custom-call(bf16[2,8,128,1536]{3,2,1,0:T(8,128)(2,1)} %get-tuple-element.100.gates_ref, bf16[8,2,128,768]{3,2,1,0:T(8,128)(2,1)} %get-tuple-element.101.hidden_ref, bf16[1536,768]{1,0:T(8,128)(2,1)} %all-gather.11.cloned.1.call-done.refs_0_.down_ref, ...), custom_call_target="tpu_custom_call" | custom-call | tf_op jit(solution)/shard_map/pallas_call | solution.py:2210
  374.3 38.9 %shard_map.327 = (f32[2,128,1536]{2,1,0:T(8,128)}, f32[2,1536]{1,0:T(2,128)}) custom-call(bf16[2,8,128,1536]{3,2,1,0:T(8,128)(2,1)} %get-tuple-element.100.gates_ref, bf16[1536,1536]{1,0:T(8,128)(2,1)} %all-gather.9.cloned.1.call-done.refs_1_.mat_ref, bf16[2,128,1536]{2,1,0:T(8,128)(2,1)} %bitcast.96, f32[2,128,1536]{2,1,0:T(8,128)} %shard_map.323.own_ref.values_ref.refs_0_, ...), custom_call_target="tpu_custom_call" | custom-call | tf_op jit(solution)/shard_map/pallas_call | solution.py:1826
  413.1 40.4 %shard_map.328 = (bf16[2,8,128,1536]{3,2,1,0:T(8,128)(2,1)}, bf16[2,8,128,192]{3,2,1,0:T(8,128)(2,1)}, f32[2,128,384]{2,1,0:T(8,128)}, bf16[1536,384]{1,0:T(8,128)(2,1)}) custom-call(f32[2,128,1536]{2,1,0:T(8,128)} %get-tuple-element.106.own_ref.base_ref, bf16[1536,768]{1,0:T(8,128)(2,1)} %all-gather.7.cloned.1.call-done.mat_ref.refs_1_.refs_0_.refs_2_, ...), custom_call_target="tpu_custom_call" | custom-call | tf_op jit(solution)/shard_map/pallas_call | solution.py:1568
  457.0 84.8 %shard_map.329 = (f32[2,128,1536]{2,1,0:T(8,128)}, f32[2,1536]{1,0:T(2,128)}, bf16[2,8,128,1536]{3,2,1,0:T(8,128)(2,1)}, bf16[2,8,128,192]{3,2,1,0:T(8,128)(2,1)...) custom-call(bf16[2,8,128,192]{3,2,1,0:T(8,128)(2,1)} %get-tuple-elem, ...), custom_call_target="tpu_custom_call" | custom-call | tf_op jit(solution)/shard_map/pallas_call | solution.py:2069
  541.9 36.1 %shard_map.330 = (bf16[2048,576]{1,0:T(8,128)(2,1)}, f32[2,1,384]{2,1,0:T(1,128)}, bf16[8,48,2304]{2,1,0:T(8,128)(2,1)}, bf16[8,48,384]{2,1,0:T(8,128)(2,1)}, bf16[1536,576]{1,0:T(8,128)(2,1)}) custom-call(bf16[2048,576]{1,0:T(8,128)(2,1)} %get-tuple-element.114.turned_ref, bf16[2048,192]{1,0:T(8,128)(2,1)} %get-tuple-element.88.mixed_ref, ...), custom_call_target="tpu_custom_call" | custom-call | tf_op jit(solution)/shard_map/pallas_call | solution.py:2581
  578.1 1.5 copy-done
  580.8 1.5 multiply_reduce_fusion
  582.3 36.9 %shard_map.331 = (bf16[2,128,1536]{2,1,0:T(8,128)(2,1)}, f32[2,1536]{1,0:T(2,128)}, bf16[8,48,384]{2,1,0:T(8,128)(2,1)}) custom-call(bf16[2,8,128,576]{3,2,1,0:T(8,128)(2,1)} %bitcast.97, bf16[1536,576]{1,0:T(8,128)(2,1)} %all-gather.5.cloned.1.call-done.mat_ref, f32[2,128,1536]{2,1,0:T(8,128)} %get-tuple-element.126.base_ref, ...), custom_call_target="tpu_custom_call" | custom-call | tf_op jit(solution)/shard_map/pallas_call | solution.py:1826
  620.9 40.2 %shard_map.332 = (bf16[8,32,1536]{2,1,0:T(8,128)(2,1)}, bf16[8,48,576]{2,1,0:T(8,128)(2,1)}, f32[8,128]{1,0:T(8,128)}, f32[8,128]{1,0:T(8,128)}, bf16[8,32,1536]{2,1,0:T(8,128)(2,1)}) custom-call(bf16[2,4,32,1536]{3,2,1,0:T(8,128)(2,1)} %bitcast.110, bf16[8,48,576]{2,1,0:T(8,128)(2,1)} %bitcast.118, f32[32,8,128]{2,1,0:T(8,128)} %pad.21.parts_ref, ...), custom_call_target="tpu_custom_call" | custom-call | tf_op jit(solution)/shard_map/pallas_call | solution.py:720
  663.7 1.5 bitcast_convert_fusion
  666.9 18.4 %shard_map.333 = (f32[48,18432]{1,0:T(8,128)}, f32[48,18432]{1,0:T(8,128)}, f32[48,18432]{1,0:T(8,128)}, f32[48,9216]{1,0:T(8,128)}, f32[48,9216]{1,0:T(8,128)}, /*index=5*/f32[48,9216]{1,0:T(8,128)}) custom-call(f32[8,128]{1,0:T(8,128)} %get-tuple-element.138.refs_0_, f32[48,18432]{1,0:T(8,128)} %refs_1_.1, f32[48,18432]{1,0:T(8,128)} %refs_2_.1, ...), custom_call_target="tpu_custom_call" | custom-call | tf_op jit(solution)/shard_map/pallas_call | solution.py:2686
  (117 shorter events, 29.4 us)
Async XLA Ops:
  7.2 93.5 %all-gather.5.cloned.1.call-start = ((), (), s32[]{:S(2)}) async-start(), calls=%async_computation.3 | async-start | bytes 2457600 | tf_op jit(solution)/shard_map/all_gather | solution.py:2766
  50.9 8.5 %copy-start.10 = (f32[8,1536]{1,0:T(8,128)S(1)}, f32[8,1536]{1,0:T(8,128)}, u32[]{:S(2)}) copy-start(f32[8,1536]{1,0:T(8,128)} %get-tuple-element.82) | copy-start | bytes 147460
  50.9 9.1 %copy-start.5 = (bf16[2,4,32,1536]{3,2,1,0:T(8,128)(2,1)S(1)}, bf16[2,4,32,1536]{3,2,1,0:T(8,128)(2,1)}, u32[]{:S(2)}) copy-start(bf16[2,4,32,1536]{3,2,1,0:T(8,128)(2,1)} %get-tuple-element.81) | copy-start | bytes 2359300
  51.0 96.8 %all-gather.7.cloned.1.call-start = ((), (), s32[]{:S(2)}) async-start(), calls=%async_computation.4 | async-start | bytes 2949120 | tf_op jit(solution)/shard_map/all_gather | solution.py:2766
  51.7 202.4 %all-gather.9.cloned.1.call-start = ((), (), s32[]{:S(2)}) async-start(), calls=%async_computation.5 | async-start | bytes 5898240 | tf_op jit(solution)/shard_map/all_gather | solution.py:2766
  60.1 39.3 %copy-start.11 = (s32[1024]{0:T(1024)S(1)}, s32[1024]{0:T(1024)}, u32[]{:S(2)}) copy-start(s32[1024]{0:T(1024)} %constant.111) | copy-start | bytes 12292
  141.7 1.9 copy-start.7
  141.7 159.0 %all-gather.11.cloned.1.call-start = ((), (), s32[]{:S(2)}) async-start(), calls=%async_computation.6 | async-start | bytes 2949120 | tf_op jit(solution)/shard_map/all_gather | solution.py:2766
  142.3 399.6 %reduce-scatter.4.cloned.1.call-start = ((), (), s32[]{:S(2)}) async-start(), calls=%async_computation.7 | async-start | bytes 8847360 | tf_op jit(solution)/shard_map/reduce_scatter | solution.py:2846
  374.2 208.0 %reduce-scatter.6.cloned.1.call-start = ((), (), s32[]{:S(2)}) async-start(), calls=%async_computation.8 | async-start | bytes 1474560 | tf_op jit(solution)/shard_map/reduce_scatter | solution.py:2846
  541.9 79.0 %reduce-scatter.8.cloned.1.call-start = ((), (), s32[]{:S(2)}) async-start(), calls=%async_computation.9 | async-start | bytes 2457600 | tf_op jit(solution)/shard_map/reduce_scatter | solution.py:2846
  578.1 2.7 copy-start.1
  582.3 37.7 %copy-start.13 = (f32[2,1536]{1,0:T(2,128)S(1)}, f32[2,1536]{1,0:T(2,128)}, u32[]{:S(2)}) copy-start(f32[2,1536]{1,0:T(2,128)} %get-tuple-element.133) | copy-start | bytes 36868
  582.3 37.7 %copy-start.14 = (f32[2,1536]{1,0:T(2,128)S(1)}, f32[2,1536]{1,0:T(2,128)}, u32[]{:S(2)}) copy-start(f32[2,1536]{1,0:T(2,128)} %get-tuple-element.132) | copy-start | bytes 36868
  619.2 43.9 %copy-start.2 = (bf16[8,48,384]{2,1,0:T(8,128)(2,1)S(1)}, bf16[8,48,384]{2,1,0:T(8,128)(2,1)}, u32[]{:S(2)}) copy-start(bf16[8,48,384]{2,1,0:T(8,128)(2,1)} %get-tuple-element.136.refs_1_.refs_10_) | copy-start | bytes 884740
  661.1 2.6 copy-start.6
  663.2 2.0 copy-start.12
  663.3 2.0 copy-start.15
  663.3 2.0 copy-start.16
  663.3 2.0 copy-start.17
  663.3 2.6 copy-start.3
  663.3 2.6 copy-start.8
  663.3 2.6 copy-start.9
  666.9 18.4 %copy-start.4 = (bf16[8,32,1536]{2,1,0:T(8,128)(2,1)S(1)}, bf16[8,32,1536]{2,1,0:T(8,128)(2,1)}, u32[]{:S(2)}) copy-start(bf16[8,32,1536]{2,1,0:T(8,128)(2,1)} %get-tuple-element.113) | copy-start | bytes 2359300
  (2 other events, 3.1 us)
Sparse Core Ops, SparseCore 0:
  51.1 44.9 all-gather.4
  97.7 49.9 all-gather.6
  149.2 100.3 all-gather.8
  251.0 49.6 all-gather.10
  374.3 160.6 reduce-scatter.3
  542.0 27.2 reduce-scatter.5
  578.2 38.3 reduce-scatter.7

commit v7 on v6

--- a/solution.py
+++ b/solution.py
@@ -2628,6 +2628,15 @@
     return grads, stamp_grads[:, 0], mine, cross_mine, outer
 
 
+def matrix_step(weight, first, second, gradient):
+    first_new = beta_first * first + (1.0 - beta_first) * gradient
+    second_new = beta_second * second + (1.0 - beta_second) * (gradient * gradient)
+    over_first = matrix_rate / (1.0 - beta_first**UPDATE_STEP)
+    over_second = 1.0 / (1.0 - beta_second**UPDATE_STEP)
+    change = first_new * over_first / (jnp.sqrt(second_new * over_second) + adam_eps)
+    return (weight * (1.0 - matrix_rate * matrix_decay) - change, first_new, second_new)
+
+
 def adam_body(ff_steps, places, *refs):
     refs = list(refs)
     take = lambda count: [refs.pop(0) for _ in range(count)]
@@ -2640,11 +2649,8 @@
     factor = jnp.minimum(1.0, clip_limit / jnp.sqrt(total_ref[0:1, 0:1]))
 
     def update(olds, gradient, outs):
-        results = adam_step(
-            *[old[...] for old in olds],
-            gradient.astype(jnp.float32) * factor,
-            matrix_rate,
-            matrix_decay,
+        results = matrix_step(
+            *[old[...] for old in olds], gradient.astype(jnp.float32) * factor
         )
         for out, result in zip(outs, results):
             out[...] = result

time: 704 us -> 704 us (level)
  no operation moved by 1% of the time
where the time goes in v7:
time: 704 us; the launch traced here: 695 us
  Pallas kernels  622 us (88%)
  other arithmetic  19.2 us (3%)
  local copies, waits for them, and re-layouts  18.6 us (3%)
  between operations  17.4 us (2%)
  waiting for transfers between devices  11.5 us (2%)
    pallas_call x2, Pallas kernels, reduce_gather(): pl.pallas_call(functools.partial(reduce_gather_body, clips, rows, sub, sp...  153 us
    pallas_call x4, Pallas kernels, gather_dot(): pl.pallas_call(functools.partial(gather_dot_body, clips, rows, sub, gains...  149 us
    pallas_call x3, Pallas kernels, dot_reduce(): pl.pallas_call(functools.partial(dot_reduce_body, clips, rows, sub, windo...  110 us
    pallas_call x1, Pallas kernels, settle(): pl.pallas_call(functools.partial(settle_body, group, planes, len(done)),...  40.2 us
    pallas_call x1, Pallas kernels, flash_forward(): pl.pallas_call(functools.partial(flash_forward_body, heads, rows // 4), g...  38.5 us
    pallas_call x1, Pallas kernels, ff_outer(): pl.pallas_call(functools.partial(ff_outer_body, (8, planes), clips, rows,...  38.4 us
    pallas_call x1, Pallas kernels, enter(): pl.pallas_call(functools.partial(enter_body, group, planes), out_shape=[l...  38.4 us
    pallas_call x1, Pallas kernels, flash_backward(): pl.pallas_call(functools.partial(flash_backward_body, heads, rows // 4),...  36.1 us
  transfers between devices with their start and end apart: 7, of which 1 were waited for; matrix products, arithmetic and copies ran while one was open for 4% of the time, Pallas kernels for 65%

profile of v7, /device:TPU:9, one launch (start us, length us, event | category | flops | bytes accessed | tf_op | source)
XLA Modules:
  0.0 694.5 jit_solution(7777812371254149902)
XLA Ops:
  12.5 38.4 %shard_map.319 = (bf16[2,4,32,1536]{3,2,1,0:T(8,128)(2,1)}, f32[8,1536]{1,0:T(8,128)}, f32[8,8,1536]{2,1,0:T(8,128)}, bf16[8,48,576]{2,1,0:T(8,128)(2,1)}, bf16[...) custom-call(bf16[256,1536]{1,0:T(8,128)(2,1)} %bitcast.105, ...), custom_call_target="tpu_custom_call" | custom-call | tf_op jit(solution)/shard_map/pallas_call | solution.py:977
  54.1 4.6 gather_fusion
  60.1 1.4 bitcast_convert_fusion.1.own_ref.base_ref.refs_0_
  61.4 36.9 %shard_map.320 = (bf16[2,8,128,1536]{3,2,1,0:T(8,128)(2,1)}, bf16[8,2,16,768]{3,2,1,0:T(8,128)(2,1)}) custom-call(f32[2,128,1536]{2,1,0:T(8,128)} %bitcast_convert_fusion.1.own_ref.base_ref.refs_0_, f32[2,1536]{1,0:T(2,128)} %get-tuple-element.168.refs_0_, bf16[4,2,16,768]{3,2,1,0:T(8,128)(2,1)} %select_select_fusion.refs_1_), custom_call_target="tpu_custom_call" | custom-call | tf_op jit(solution)/shard_map/pallas_call | solution.py:1568
  100.7 1.9 fusion.1
  103.2 38.5 %shard_map.321 = (bf16[2048,576]{1,0:T(8,128)(2,1)}, bf16[2048,192]{1,0:T(8,128)(2,1)}, f32[2048,128]{1,0:T(8,128)}, bf16[8,48,1536]{2,1,0:T(8,128)(2,1)}, bf16[...) custom-call(bf16[2048,1536]{1,0:T(8,128)(2,1)} %bitcast.85, bf16[1536,576]{1,0:T(8,128)(2,1)} %all-gather.5.cloned.1.call-done.mat_ref, ...), custom_call_target="tpu_custom_call" | custom-call | tf_op jit(solution)/shard_map/pallas_call | solution.py:2402
  146.1 1.6 fusion.6.stamp_normed_ref
  147.7 1.5 slice.69
  151.4 68.2 %shard_map.322 = (f32[2,128,1536]{2,1,0:T(8,128)}, bf16[2,8,128,1536]{3,2,1,0:T(8,128)(2,1)}, bf16[2,8,128,192]{3,2,1,0:T(8,128)(2,1)}, bf16[2,8,128,192]{3,2,1,0:T(8,128)(2,1)}, bf16[2,4,32,1536]{3,2,1,0:T(8,128)(2,1)}) custom-call(bf16[2,8,128,192]{3,2,1,0:T(8,128)(2,1)} %bitcast.87, ...), custom_call_target="tpu_custom_call" | custom-call | tf_op jit(solution)/shard_map/pallas_call | solution.py:2069
  219.6 34.5 %shard_map.323.own_ref.values_ref.refs_0_ = f32[2,128,1536]{2,1,0:T(8,128)} custom-call(bf16[2,8,128,192]{3,2,1,0:T(8,128)(2,1)} %get-tuple-element.92.left_ref.refs_5_, bf16[1536,768]{1,0:T(8,128)(2,1)} %all-gather.7.cloned.1.call-done.mat_ref.refs_1_.refs_0_.refs_2_, f32[2,128,1536]{2,1,0:T(8,128)} %get-tuple-element.93.base_ref.refs_0_), custom_call_target="tpu_custom_call" | custom-call | tf_op jit(solution)/shard_map/pallas_call | solution.py:1826
  254.1 36.5 %shard_map.324 = (bf16[2,8,128,1536]{3,2,1,0:T(8,128)(2,1)}, f32[2,8,128,1536]{3,2,1,0:T(8,128)}) custom-call(f32[2,128,1536]{2,1,0:T(8,128)} %shard_map.323.own_ref.values_ref.refs_0_, f32[2,1536]{1,0:T(2,128)} %get-tuple-element.166.refs_0_, bf16[1536,1536]{1,0:T(8,128)(2,1)} %all-gather.9.cloned.1.call-done.refs_1_.mat_ref), custom_call_target="tpu_custom_call" | custom-call | tf_op jit(solution)/shard_map/pallas_call | solution.py:1568
  290.6 10.1 %all-gather.11.cloned.1.call-done.refs_0_.down_ref = bf16[1536,768]{1,0:T(8,128)(2,1)} async-done(((bf16[384,768]{1,0:T(8,128)(2,1)}), bf16[1536,768]{1,0:T(8,128)(2,1)}) %all-gather.11.cloned.1.call-update) | async-done | bytes 2359312 | tf_op jit(solution)/shard_map/all_gather | solution.py:2772
  300.7 35.1 %shard_map.325 = (bf16[8,2,128,1536]{3,2,1,0:T(8,128)(2,1)}, bf16[2,8,128,1536]{3,2,1,0:T(8,128)(2,1)}, bf16[8,2,128,768]{3,2,1,0:T(8,128)(2,1)}) custom-call(bf16[2,128,1536]{2,1,0:T(8,128)(2,1)} %bitcast.95, bf16[1536,768]{1,0:T(8,128)(2,1)} %all-gather.11.cloned.1.call-done.refs_0_.down_ref, f32[2,8,128,1536]{3,2,1,0:T(8,128)} %get-tuple-element.95), custom_call_target="tpu_custom_call" | custom-call | tf_op jit(solution)/shard_map/pallas_call | solution.py:1568
  335.8 38.4 %shard_map.326 = (bf16[2,128,1536]{2,1,0:T(8,128)(2,1)}, bf16[1536,2304]{1,0:T(8,128)(2,1)}) custom-call(bf16[2,8,128,1536]{3,2,1,0:T(8,128)(2,1)} %get-tuple-element.100.gates_ref, bf16[8,2,128,768]{3,2,1,0:T(8,128)(2,1)} %get-tuple-element.101.hidden_ref, bf16[1536,768]{1,0:T(8,128)(2,1)} %all-gather.11.cloned.1.call-done.refs_0_.down_ref, ...), custom_call_target="tpu_custom_call" | custom-call | tf_op jit(solution)/shard_map/pallas_call | solution.py:2210
  374.3 38.9 %shard_map.327 = (f32[2,128,1536]{2,1,0:T(8,128)}, f32[2,1536]{1,0:T(2,128)}) custom-call(bf16[2,8,128,1536]{3,2,1,0:T(8,128)(2,1)} %get-tuple-element.100.gates_ref, bf16[1536,1536]{1,0:T(8,128)(2,1)} %all-gather.9.cloned.1.call-done.refs_1_.mat_ref, bf16[2,128,1536]{2,1,0:T(8,128)(2,1)} %bitcast.96, f32[2,128,1536]{2,1,0:T(8,128)} %shard_map.323.own_ref.values_ref.refs_0_, ...), custom_call_target="tpu_custom_call" | custom-call | tf_op jit(solution)/shard_map/pallas_call | solution.py:1826
  413.1 40.4 %shard_map.328 = (bf16[2,8,128,1536]{3,2,1,0:T(8,128)(2,1)}, bf16[2,8,128,192]{3,2,1,0:T(8,128)(2,1)}, f32[2,128,384]{2,1,0:T(8,128)}, bf16[1536,384]{1,0:T(8,128)(2,1)}) custom-call(f32[2,128,1536]{2,1,0:T(8,128)} %get-tuple-element.106.own_ref.base_ref, bf16[1536,768]{1,0:T(8,128)(2,1)} %all-gather.7.cloned.1.call-done.mat_ref.refs_1_.refs_0_.refs_2_, ...), custom_call_target="tpu_custom_call" | custom-call | tf_op jit(solution)/shard_map/pallas_call | solution.py:1568
  457.0 84.8 %shard_map.329 = (f32[2,128,1536]{2,1,0:T(8,128)}, f32[2,1536]{1,0:T(2,128)}, bf16[2,8,128,1536]{3,2,1,0:T(8,128)(2,1)}, bf16[2,8,128,192]{3,2,1,0:T(8,128)(2,1)...) custom-call(bf16[2,8,128,192]{3,2,1,0:T(8,128)(2,1)} %get-tuple-elem, ...), custom_call_target="tpu_custom_call" | custom-call | tf_op jit(solution)/shard_map/pallas_call | solution.py:2069
  541.9 36.1 %shard_map.330 = (bf16[2048,576]{1,0:T(8,128)(2,1)}, f32[2,1,384]{2,1,0:T(1,128)}, bf16[8,48,2304]{2,1,0:T(8,128)(2,1)}, bf16[8,48,384]{2,1,0:T(8,128)(2,1)}, bf16[1536,576]{1,0:T(8,128)(2,1)}) custom-call(bf16[2048,576]{1,0:T(8,128)(2,1)} %get-tuple-element.114.turned_ref, bf16[2048,192]{1,0:T(8,128)(2,1)} %get-tuple-element.88.mixed_ref, ...), custom_call_target="tpu_custom_call" | custom-call | tf_op jit(solution)/shard_map/pallas_call | solution.py:2581
  578.1 1.5 copy-done
  580.8 1.5 multiply_reduce_fusion
  582.3 36.9 %shard_map.331 = (bf16[2,128,1536]{2,1,0:T(8,128)(2,1)}, f32[2,1536]{1,0:T(2,128)}, bf16[8,48,384]{2,1,0:T(8,128)(2,1)}) custom-call(bf16[2,8,128,576]{3,2,1,0:T(8,128)(2,1)} %bitcast.97, bf16[1536,576]{1,0:T(8,128)(2,1)} %all-gather.5.cloned.1.call-done.mat_ref, f32[2,128,1536]{2,1,0:T(8,128)} %get-tuple-element.126.base_ref, ...), custom_call_target="tpu_custom_call" | custom-call | tf_op jit(solution)/shard_map/pallas_call | solution.py:1826
  620.9 40.2 %shard_map.332 = (bf16[8,32,1536]{2,1,0:T(8,128)(2,1)}, bf16[8,48,576]{2,1,0:T(8,128)(2,1)}, f32[8,128]{1,0:T(8,128)}, f32[8,128]{1,0:T(8,128)}, bf16[8,32,1536]{2,1,0:T(8,128)(2,1)}) custom-call(bf16[2,4,32,1536]{3,2,1,0:T(8,128)(2,1)} %bitcast.110, bf16[8,48,576]{2,1,0:T(8,128)(2,1)} %bitcast.118, f32[32,8,128]{2,1,0:T(8,128)} %pad.21.parts_ref, ...), custom_call_target="tpu_custom_call" | custom-call | tf_op jit(solution)/shard_map/pallas_call | solution.py:720
  663.7 1.5 bitcast_convert_fusion
  666.9 18.5 %shard_map.333 = (f32[48,18432]{1,0:T(8,128)}, f32[48,18432]{1,0:T(8,128)}, f32[48,18432]{1,0:T(8,128)}, f32[48,9216]{1,0:T(8,128)}, f32[48,9216]{1,0:T(8,128)}, /*index=5*/f32[48,9216]{1,0:T(8,128)}) custom-call(f32[8,128]{1,0:T(8,128)} %get-tuple-element.138.refs_0_, f32[48,18432]{1,0:T(8,128)} %refs_1_.1, f32[48,18432]{1,0:T(8,128)} %refs_2_.1, ...), custom_call_target="tpu_custom_call" | custom-call | tf_op jit(solution)/shard_map/pallas_call | solution.py:2692
  (117 shorter events, 29.4 us)
Async XLA Ops:
  7.2 93.5 %all-gather.5.cloned.1.call-start = ((), (), s32[]{:S(2)}) async-start(), calls=%async_computation.3 | async-start | bytes 2457600 | tf_op jit(solution)/shard_map/all_gather | solution.py:2772
  50.9 8.5 %copy-start.10 = (f32[8,1536]{1,0:T(8,128)S(1)}, f32[8,1536]{1,0:T(8,128)}, u32[]{:S(2)}) copy-start(f32[8,1536]{1,0:T(8,128)} %get-tuple-element.82) | copy-start | bytes 147460
  50.9 9.1 %copy-start.5 = (bf16[2,4,32,1536]{3,2,1,0:T(8,128)(2,1)S(1)}, bf16[2,4,32,1536]{3,2,1,0:T(8,128)(2,1)}, u32[]{:S(2)}) copy-start(bf16[2,4,32,1536]{3,2,1,0:T(8,128)(2,1)} %get-tuple-element.81) | copy-start | bytes 2359300
  51.0 96.8 %all-gather.7.cloned.1.call-start = ((), (), s32[]{:S(2)}) async-start(), calls=%async_computation.4 | async-start | bytes 2949120 | tf_op jit(solution)/shard_map/all_gather | solution.py:2772
  51.7 202.4 %all-gather.9.cloned.1.call-start = ((), (), s32[]{:S(2)}) async-start(), calls=%async_computation.5 | async-start | bytes 5898240 | tf_op jit(solution)/shard_map/all_gather | solution.py:2772
  60.1 39.3 %copy-start.11 = (s32[1024]{0:T(1024)S(1)}, s32[1024]{0:T(1024)}, u32[]{:S(2)}) copy-start(s32[1024]{0:T(1024)} %constant.111) | copy-start | bytes 12292
  141.7 1.9 copy-start.7
  141.7 159.0 %all-gather.11.cloned.1.call-start = ((), (), s32[]{:S(2)}) async-start(), calls=%async_computation.6 | async-start | bytes 2949120 | tf_op jit(solution)/shard_map/all_gather | solution.py:2772
  142.3 399.6 %reduce-scatter.4.cloned.1.call-start = ((), (), s32[]{:S(2)}) async-start(), calls=%async_computation.7 | async-start | bytes 8847360 | tf_op jit(solution)/shard_map/reduce_scatter | solution.py:2852
  374.2 208.0 %reduce-scatter.6.cloned.1.call-start = ((), (), s32[]{:S(2)}) async-start(), calls=%async_computation.8 | async-start | bytes 1474560 | tf_op jit(solution)/shard_map/reduce_scatter | solution.py:2852
  541.9 79.0 %reduce-scatter.8.cloned.1.call-start = ((), (), s32[]{:S(2)}) async-start(), calls=%async_computation.9 | async-start | bytes 2457600 | tf_op jit(solution)/shard_map/reduce_scatter | solution.py:2852
  578.1 2.7 copy-start.1
  582.3 37.7 %copy-start.13 = (f32[2,1536]{1,0:T(2,128)S(1)}, f32[2,1536]{1,0:T(2,128)}, u32[]{:S(2)}) copy-start(f32[2,1536]{1,0:T(2,128)} %get-tuple-element.133) | copy-start | bytes 36868
  582.3 37.7 %copy-start.14 = (f32[2,1536]{1,0:T(2,128)S(1)}, f32[2,1536]{1,0:T(2,128)}, u32[]{:S(2)}) copy-start(f32[2,1536]{1,0:T(2,128)} %get-tuple-element.132) | copy-start | bytes 36868
  619.2 43.9 %copy-start.2 = (bf16[8,48,384]{2,1,0:T(8,128)(2,1)S(1)}, bf16[8,48,384]{2,1,0:T(8,128)(2,1)}, u32[]{:S(2)}) copy-start(bf16[8,48,384]{2,1,0:T(8,128)(2,1)} %get-tuple-element.136.refs_1_.refs_10_) | copy-start | bytes 884740
  661.1 2.6 copy-start.6
  663.2 2.0 copy-start.12
  663.3 2.0 copy-start.15
  663.3 2.0 copy-start.16
  663.3 2.0 copy-start.17
  663.3 2.6 copy-start.3
  663.3 2.6 copy-start.8
  663.3 2.6 copy-start.9
  666.9 18.6 %copy-start.4 = (bf16[8,32,1536]{2,1,0:T(8,128)(2,1)S(1)}, bf16[8,32,1536]{2,1,0:T(8,128)(2,1)}, u32[]{:S(2)}) copy-start(bf16[8,32,1536]{2,1,0:T(8,128)(2,1)} %get-tuple-element.113) | copy-start | bytes 2359300
  (2 other events, 3.1 us)
Sparse Core Ops, SparseCore 0:
  51.1 44.9 all-gather.4
  97.7 49.9 all-gather.6
  149.2 100.3 all-gather.8
  251.0 49.6 all-gather.10
  374.3 160.6 reduce-scatter.3
  542.0 27.2 reduce-scatter.5
  578.2 38.3 reduce-scatter.7

commit v8 on v6

--- a/solution.py
+++ b/solution.py
@@ -584,13 +584,20 @@
     )
 
 
+def by_distance(planes, depth):
+    low = [jnp.where(which >= depth, which + 1, which) for which in range(planes - 1)]
+    return [
+        jnp.where(depth < planes // 2, up, down) for up, down in zip(low, reversed(low))
+    ]
+
+
 def outward_steps(group, planes, kept_ref, own_ref, mid, *sems):
     far_send, far_recv, near_send, near_recv, local_sem = sems
     place, depth, flip = plane_places()
     per = group // planes
     first = []
-    for step in range(1, planes):
-        origin = lax.rem(depth + step, planes)
+    others = by_distance(planes, depth)
+    for step, origin in reversed(list(enumerate(others))):
         for slot in range(per):
             clip = per * depth + slot
             copy = remote(
@@ -617,8 +624,7 @@
     for slot in range(per):
         hand_over(kept_ref.at[slot, depth], per * depth + slot)
     yield
-    for step in range(1, planes):
-        source = lax.rem(depth + step, planes)
+    for source in others:
         for slot in range(per):
             clip = per * source + slot
             block = mid.at[clip]
@@ -2447,7 +2453,8 @@
     query_grad,
     key_grad,
     value_grad,
-    outer_total,
+    all_grads,
+    stamp_grads,
     *sems,
 ):
     place, depth, flip = plane_places()
@@ -2535,27 +2542,25 @@
         lanes = slice(pair * 128, pair * 128 + 128)
         out_ref[:, lanes] = turn_heads(both[:, lanes], rotary_ref[0], -rotary_ref[1]).astype(low)
     out_ref[:, 2 * wide :] = value_grad[...].astype(low)
-    count = outer_total.shape[1]
+    count = all_grads.shape[1]
     tile = 512
-    for start in range(0, normed_ref.shape[1], tile):
-        span = slice(start, start + tile)
-        product = outer_sum(normed_ref[:, span], out_ref[...])
-        stamp_part = stamp_normed_ref[0, span] * stamp_out_ref[0]
-        product = product + jnp.concatenate(
-            [jnp.zeros((tile, count - 2 * wide), f32), stamp_part], axis=1
-        )
-
-        @pl.when(pl.program_id(0) == 0)
-        def _():
-            outer_total[span] = product
-
-        @pl.when(pl.program_id(0) > 0)
-        def _():
-            outer_total[span] += product
-
-    @pl.when(pl.program_id(0) == pl.num_programs(0) - 1)
+    step = pl.program_id(0)
+    all_grads[pl.ds(pl.multiple_of(step * rows, rows), rows)] = out_ref[...]
+    stamp_grads[step] = stamp_out_ref[0]
+
+    @pl.when(step == pl.num_programs(0) - 1)
     def _():
-        outer_ref[...] = outer_total[...].astype(outer_ref.dtype)
+        for start in range(0, normed_ref.shape[1], tile):
+            span = slice(start, start + tile)
+            product = outer_sum(normed_ref[:, span], all_grads[...])
+            stamp_part = sum(
+                stamp_normed_ref[clip, span] * stamp_grads[clip]
+                for clip in range(stamp_grads.shape[0])
+            )
+            outer_ref[span, : count - 2 * wide] = product[:, : count - 2 * wide].astype(low)
+            outer_ref[span, count - 2 * wide :] = (
+                product[:, count - 2 * wide :] + stamp_part
+            ).astype(low)
         end_swap()
 
 
@@ -2598,8 +2603,8 @@
             pl.BlockSpec((2, rows, 128), lambda clip: (0, 0, 0)),
             any_spec(),
             any_spec(),
-            blocked(features),
-            pl.BlockSpec((1, features, 1), lambda clip: (clip, 0, 0)),
+            pl.BlockSpec(normed.shape, lambda clip: (0, 0)),
+            pl.BlockSpec((clips, features, 1), lambda clip: (0, 0, 0)),
         ],
         out_specs=[
             blocked(3 * wide),
@@ -2609,7 +2614,10 @@
             pl.BlockSpec((features, 3 * wide), lambda clip: (0, 0)),
         ],
         scratch_shapes=[pltpu.VMEM((rows, wide), jnp.float32)] * 3
-        + [pltpu.VMEM((features, 3 * wide), jnp.float32)]
+        + [
+            pltpu.VMEM((clips * rows, 3 * wide), jnp.bfloat16),
+            pltpu.VMEM((clips, 1, 2 * wide), jnp.float32),
+        ]
         + swap_beside_scratch(2),
         compiler_params=communicating(collective_id),
     )(

time: 704 us -> 703 us (level)
  no operation moved by 1% of the time
where the time goes in v8:
time: 703 us; the launch traced here: 690 us
  Pallas kernels  618 us (88%)
  other arithmetic  19.1 us (3%)
  local copies, waits for them, and re-layouts  18.6 us (3%)
  between operations  17.5 us (2%)
  waiting for transfers between devices  11.5 us (2%)
    pallas_call x2, Pallas kernels, reduce_gather(): pl.pallas_call(functools.partial(reduce_gather_body, clips, rows, sub, sp...  153 us
    pallas_call x4, Pallas kernels, gather_dot(): pl.pallas_call(functools.partial(gather_dot_body, clips, rows, sub, gains...  149 us
    pallas_call x3, Pallas kernels, dot_reduce(): pl.pallas_call(functools.partial(dot_reduce_body, clips, rows, sub, windo...  110 us
    pallas_call x1, Pallas kernels, flash_forward(): pl.pallas_call(functools.partial(flash_forward_body, heads, rows // 4), g...  38.5 us
    pallas_call x1, Pallas kernels, ff_outer(): pl.pallas_call(functools.partial(ff_outer_body, (8, planes), clips, rows,...  38.4 us
    pallas_call x1, Pallas kernels, enter(): pl.pallas_call(functools.partial(enter_body, group, planes), out_shape=[l...  38.4 us
    pallas_call x1, Pallas kernels, settle(): pl.pallas_call(functools.partial(settle_body, group, planes, len(done)),...  36 us
    pallas_call x1, Pallas kernels, flash_backward(): pl.pallas_call(functools.partial(flash_backward_body, heads, rows // 4),...  35.8 us
  transfers between devices with their start and end apart: 7, of which 1 were waited for; matrix products, arithmetic and copies ran while one was open for 4% of the time, Pallas kernels for 65%

profile of v8, /device:TPU:9, one launch (start us, length us, event | category | flops | bytes accessed | tf_op | source)
XLA Modules:
  0.0 689.9 jit_solution(462897567160586995)
XLA Ops:
  11.2 1.4 concatenate.6.pack_ref
  12.5 38.4 %shard_map.319 = (bf16[2,4,32,1536]{3,2,1,0:T(8,128)(2,1)}, f32[8,1536]{1,0:T(8,128)}, f32[8,8,1536]{2,1,0:T(8,128)}, bf16[8,48,576]{2,1,0:T(8,128)(2,1)}, bf16[...) custom-call(bf16[256,1536]{1,0:T(8,128)(2,1)} %bitcast.105, ...), custom_call_target="tpu_custom_call" | custom-call | tf_op jit(solution)/shard_map/pallas_call | solution.py:983
  54.1 4.6 gather_fusion
  60.1 1.4 bitcast_convert_fusion.1.own_ref.base_ref.refs_0_
  61.4 36.9 %shard_map.320 = (bf16[2,8,128,1536]{3,2,1,0:T(8,128)(2,1)}, bf16[8,2,16,768]{3,2,1,0:T(8,128)(2,1)}) custom-call(f32[2,128,1536]{2,1,0:T(8,128)} %bitcast_convert_fusion.1.own_ref.base_ref.refs_0_, f32[2,1536]{1,0:T(2,128)} %get-tuple-element.168.refs_0_, bf16[4,2,16,768]{3,2,1,0:T(8,128)(2,1)} %select_select_fusion.refs_1_), custom_call_target="tpu_custom_call" | custom-call | tf_op jit(solution)/shard_map/pallas_call | solution.py:1574
  100.7 1.9 fusion.1
  103.2 38.5 %shard_map.321 = (bf16[2048,576]{1,0:T(8,128)(2,1)}, bf16[2048,192]{1,0:T(8,128)(2,1)}, f32[2048,128]{1,0:T(8,128)}, bf16[8,48,1536]{2,1,0:T(8,128)(2,1)}, bf16[...) custom-call(bf16[2048,1536]{1,0:T(8,128)(2,1)} %bitcast.85, bf16[1536,576]{1,0:T(8,128)(2,1)} %all-gather.5.cloned.1.call-done.mat_ref, ...), custom_call_target="tpu_custom_call" | custom-call | tf_op jit(solution)/shard_map/pallas_call | solution.py:2408
  146.1 1.6 fusion.6.stamp_normed_ref
  147.7 1.5 slice.69
  151.4 68.2 %shard_map.322 = (f32[2,128,1536]{2,1,0:T(8,128)}, bf16[2,8,128,1536]{3,2,1,0:T(8,128)(2,1)}, bf16[2,8,128,192]{3,2,1,0:T(8,128)(2,1)}, bf16[2,8,128,192]{3,2,1,0:T(8,128)(2,1)}, bf16[2,4,32,1536]{3,2,1,0:T(8,128)(2,1)}) custom-call(bf16[2,8,128,192]{3,2,1,0:T(8,128)(2,1)} %bitcast.87, ...), custom_call_target="tpu_custom_call" | custom-call | tf_op jit(solution)/shard_map/pallas_call | solution.py:2075
  219.6 34.5 %shard_map.323.own_ref.values_ref.refs_0_ = f32[2,128,1536]{2,1,0:T(8,128)} custom-call(bf16[2,8,128,192]{3,2,1,0:T(8,128)(2,1)} %get-tuple-element.92.left_ref.refs_5_, bf16[1536,768]{1,0:T(8,128)(2,1)} %all-gather.7.cloned.1.call-done.mat_ref.refs_1_.refs_0_.refs_2_, f32[2,128,1536]{2,1,0:T(8,128)} %get-tuple-element.93.base_ref.refs_0_), custom_call_target="tpu_custom_call" | custom-call | tf_op jit(solution)/shard_map/pallas_call | solution.py:1832
  254.1 36.5 %shard_map.324 = (bf16[2,8,128,1536]{3,2,1,0:T(8,128)(2,1)}, f32[2,8,128,1536]{3,2,1,0:T(8,128)}) custom-call(f32[2,128,1536]{2,1,0:T(8,128)} %shard_map.323.own_ref.values_ref.refs_0_, f32[2,1536]{1,0:T(2,128)} %get-tuple-element.166.refs_0_, bf16[1536,1536]{1,0:T(8,128)(2,1)} %all-gather.9.cloned.1.call-done.refs_1_.mat_ref), custom_call_target="tpu_custom_call" | custom-call | tf_op jit(solution)/shard_map/pallas_call | solution.py:1574
  290.6 10.1 %all-gather.11.cloned.1.call-done.refs_0_.down_ref = bf16[1536,768]{1,0:T(8,128)(2,1)} async-done(((bf16[384,768]{1,0:T(8,128)(2,1)}), bf16[1536,768]{1,0:T(8,128)(2,1)}) %all-gather.11.cloned.1.call-update) | async-done | bytes 2359312 | tf_op jit(solution)/shard_map/all_gather | solution.py:2774
  300.7 35.1 %shard_map.325 = (bf16[8,2,128,1536]{3,2,1,0:T(8,128)(2,1)}, bf16[2,8,128,1536]{3,2,1,0:T(8,128)(2,1)}, bf16[8,2,128,768]{3,2,1,0:T(8,128)(2,1)}) custom-call(bf16[2,128,1536]{2,1,0:T(8,128)(2,1)} %bitcast.95, bf16[1536,768]{1,0:T(8,128)(2,1)} %all-gather.11.cloned.1.call-done.refs_0_.down_ref, f32[2,8,128,1536]{3,2,1,0:T(8,128)} %get-tuple-element.95), custom_call_target="tpu_custom_call" | custom-call | tf_op jit(solution)/shard_map/pallas_call | solution.py:1574
  335.8 38.4 %shard_map.326 = (bf16[2,128,1536]{2,1,0:T(8,128)(2,1)}, bf16[1536,2304]{1,0:T(8,128)(2,1)}) custom-call(bf16[2,8,128,1536]{3,2,1,0:T(8,128)(2,1)} %get-tuple-element.100.gates_ref, bf16[8,2,128,768]{3,2,1,0:T(8,128)(2,1)} %get-tuple-element.101.hidden_ref, bf16[1536,768]{1,0:T(8,128)(2,1)} %all-gather.11.cloned.1.call-done.refs_0_.down_ref, ...), custom_call_target="tpu_custom_call" | custom-call | tf_op jit(solution)/shard_map/pallas_call | solution.py:2216
  374.3 38.9 %shard_map.327 = (f32[2,128,1536]{2,1,0:T(8,128)}, f32[2,1536]{1,0:T(2,128)}) custom-call(bf16[2,8,128,1536]{3,2,1,0:T(8,128)(2,1)} %get-tuple-element.100.gates_ref, bf16[1536,1536]{1,0:T(8,128)(2,1)} %all-gather.9.cloned.1.call-done.refs_1_.mat_ref, bf16[2,128,1536]{2,1,0:T(8,128)(2,1)} %bitcast.96, f32[2,128,1536]{2,1,0:T(8,128)} %shard_map.323.own_ref.values_ref.refs_0_, ...), custom_call_target="tpu_custom_call" | custom-call | tf_op jit(solution)/shard_map/pallas_call | solution.py:1832
  413.1 40.4 %shard_map.328 = (bf16[2,8,128,1536]{3,2,1,0:T(8,128)(2,1)}, bf16[2,8,128,192]{3,2,1,0:T(8,128)(2,1)}, f32[2,128,384]{2,1,0:T(8,128)}, bf16[1536,384]{1,0:T(8,128)(2,1)}) custom-call(f32[2,128,1536]{2,1,0:T(8,128)} %get-tuple-element.106.own_ref.base_ref, bf16[1536,768]{1,0:T(8,128)(2,1)} %all-gather.7.cloned.1.call-done.mat_ref.refs_1_.refs_0_.refs_2_, ...), custom_call_target="tpu_custom_call" | custom-call | tf_op jit(solution)/shard_map/pallas_call | solution.py:1574
  457.0 84.8 %shard_map.329 = (f32[2,128,1536]{2,1,0:T(8,128)}, f32[2,1536]{1,0:T(2,128)}, bf16[2,8,128,1536]{3,2,1,0:T(8,128)(2,1)}, bf16[2,8,128,192]{3,2,1,0:T(8,128)(2,1)...) custom-call(bf16[2,8,128,192]{3,2,1,0:T(8,128)(2,1)} %get-tuple-elem, ...), custom_call_target="tpu_custom_call" | custom-call | tf_op jit(solution)/shard_map/pallas_call | solution.py:2075
  541.9 35.8 %shard_map.330 = (bf16[2048,576]{1,0:T(8,128)(2,1)}, f32[2,1,384]{2,1,0:T(1,128)}, bf16[8,48,2304]{2,1,0:T(8,128)(2,1)}, bf16[8,48,384]{2,1,0:T(8,128)(2,1)}, bf16[1536,576]{1,0:T(8,128)(2,1)}) custom-call(bf16[2048,576]{1,0:T(8,128)(2,1)} %get-tuple-element.114.turned_ref, bf16[2048,192]{1,0:T(8,128)(2,1)} %get-tuple-element.88.mixed_ref, ...), custom_call_target="tpu_custom_call" | custom-call | tf_op jit(solution)/shard_map/pallas_call | solution.py:2586
  577.8 1.5 copy-done
  580.5 1.5 multiply_reduce_fusion
  582.0 36.9 %shard_map.331 = (bf16[2,128,1536]{2,1,0:T(8,128)(2,1)}, f32[2,1536]{1,0:T(2,128)}, bf16[8,48,384]{2,1,0:T(8,128)(2,1)}) custom-call(bf16[2,8,128,576]{3,2,1,0:T(8,128)(2,1)} %bitcast.97, bf16[1536,576]{1,0:T(8,128)(2,1)} %all-gather.5.cloned.1.call-done.mat_ref, f32[2,128,1536]{2,1,0:T(8,128)} %get-tuple-element.126.base_ref, ...), custom_call_target="tpu_custom_call" | custom-call | tf_op jit(solution)/shard_map/pallas_call | solution.py:1832
  620.6 36.0 %shard_map.332 = (bf16[8,32,1536]{2,1,0:T(8,128)(2,1)}, bf16[8,48,576]{2,1,0:T(8,128)(2,1)}, f32[8,128]{1,0:T(8,128)}, f32[8,128]{1,0:T(8,128)}, bf16[8,32,1536]{2,1,0:T(8,128)(2,1)}) custom-call(bf16[2,4,32,1536]{3,2,1,0:T(8,128)(2,1)} %bitcast.110, bf16[8,48,576]{2,1,0:T(8,128)(2,1)} %bitcast.118, f32[32,8,128]{2,1,0:T(8,128)} %pad.21.parts_ref, ...), custom_call_target="tpu_custom_call" | custom-call | tf_op jit(solution)/shard_map/pallas_call | solution.py:726
  662.4 18.4 %shard_map.333 = (f32[48,18432]{1,0:T(8,128)}, f32[48,18432]{1,0:T(8,128)}, f32[48,18432]{1,0:T(8,128)}, f32[48,9216]{1,0:T(8,128)}, f32[48,9216]{1,0:T(8,128)}, /*index=5*/f32[48,9216]{1,0:T(8,128)}) custom-call(f32[8,128]{1,0:T(8,128)} %get-tuple-element.138.refs_0_, f32[48,18432]{1,0:T(8,128)} %refs_1_.1, f32[48,18432]{1,0:T(8,128)} %refs_2_.1, ...), custom_call_target="tpu_custom_call" | custom-call | tf_op jit(solution)/shard_map/pallas_call | solution.py:2694
  (117 shorter events, 29.3 us)
Async XLA Ops:
  7.2 93.5 %all-gather.5.cloned.1.call-start = ((), (), s32[]{:S(2)}) async-start(), calls=%async_computation.3 | async-start | bytes 2457600 | tf_op jit(solution)/shard_map/all_gather | solution.py:2774
  50.9 8.5 %copy-start.10 = (f32[8,1536]{1,0:T(8,128)S(1)}, f32[8,1536]{1,0:T(8,128)}, u32[]{:S(2)}) copy-start(f32[8,1536]{1,0:T(8,128)} %get-tuple-element.82) | copy-start | bytes 147460
  50.9 9.1 %copy-start.5 = (bf16[2,4,32,1536]{3,2,1,0:T(8,128)(2,1)S(1)}, bf16[2,4,32,1536]{3,2,1,0:T(8,128)(2,1)}, u32[]{:S(2)}) copy-start(bf16[2,4,32,1536]{3,2,1,0:T(8,128)(2,1)} %get-tuple-element.81) | copy-start | bytes 2359300
  51.0 96.8 %all-gather.7.cloned.1.call-start = ((), (), s32[]{:S(2)}) async-start(), calls=%async_computation.4 | async-start | bytes 2949120 | tf_op jit(solution)/shard_map/all_gather | solution.py:2774
  51.7 202.4 %all-gather.9.cloned.1.call-start = ((), (), s32[]{:S(2)}) async-start(), calls=%async_computation.5 | async-start | bytes 5898240 | tf_op jit(solution)/shard_map/all_gather | solution.py:2774
  60.1 39.3 %copy-start.11 = (s32[1024]{0:T(1024)S(1)}, s32[1024]{0:T(1024)}, u32[]{:S(2)}) copy-start(s32[1024]{0:T(1024)} %constant.111) | copy-start | bytes 12292
  141.7 1.9 copy-start.7
  141.7 159.0 %all-gather.11.cloned.1.call-start = ((), (), s32[]{:S(2)}) async-start(), calls=%async_computation.6 | async-start | bytes 2949120 | tf_op jit(solution)/shard_map/all_gather | solution.py:2774
  142.3 399.6 %reduce-scatter.4.cloned.1.call-start = ((), (), s32[]{:S(2)}) async-start(), calls=%async_computation.7 | async-start | bytes 8847360 | tf_op jit(solution)/shard_map/reduce_scatter | solution.py:2854
  374.2 207.7 %reduce-scatter.6.cloned.1.call-start = ((), (), s32[]{:S(2)}) async-start(), calls=%async_computation.8 | async-start | bytes 1474560 | tf_op jit(solution)/shard_map/reduce_scatter | solution.py:2854
  541.9 78.7 %reduce-scatter.8.cloned.1.call-start = ((), (), s32[]{:S(2)}) async-start(), calls=%async_computation.9 | async-start | bytes 2457600 | tf_op jit(solution)/shard_map/reduce_scatter | solution.py:2854
  577.8 2.7 copy-start.1
  582.0 37.7 %copy-start.13 = (f32[2,1536]{1,0:T(2,128)S(1)}, f32[2,1536]{1,0:T(2,128)}, u32[]{:S(2)}) copy-start(f32[2,1536]{1,0:T(2,128)} %get-tuple-element.133) | copy-start | bytes 36868
  582.0 37.7 %copy-start.14 = (f32[2,1536]{1,0:T(2,128)S(1)}, f32[2,1536]{1,0:T(2,128)}, u32[]{:S(2)}) copy-start(f32[2,1536]{1,0:T(2,128)} %get-tuple-element.132) | copy-start | bytes 36868
  618.9 39.7 %copy-start.2 = (bf16[8,48,384]{2,1,0:T(8,128)(2,1)S(1)}, bf16[8,48,384]{2,1,0:T(8,128)(2,1)}, u32[]{:S(2)}) copy-start(bf16[8,48,384]{2,1,0:T(8,128)(2,1)} %get-tuple-element.136.refs_1_.refs_10_) | copy-start | bytes 884740
  656.6 2.6 copy-start.6
  658.7 2.0 copy-start.12
  658.7 2.0 copy-start.15
  658.8 2.0 copy-start.16
  658.8 2.0 copy-start.17
  658.8 2.6 copy-start.3
  658.8 2.6 copy-start.8
  658.8 2.6 copy-start.9
  662.4 18.4 %copy-start.4 = (bf16[8,32,1536]{2,1,0:T(8,128)(2,1)S(1)}, bf16[8,32,1536]{2,1,0:T(8,128)(2,1)}, u32[]{:S(2)}) copy-start(bf16[8,32,1536]{2,1,0:T(8,128)(2,1)} %get-tuple-element.113) | copy-start | bytes 2359300
  (2 other events, 3.1 us)
Sparse Core Ops, SparseCore 0:
  51.1 44.9 all-gather.4
  97.7 49.9 all-gather.6
  149.2 100.3 all-gather.8
  251.0 49.6 all-gather.10
  374.3 160.6 reduce-scatter.3
  542.0 27.2 reduce-scatter.5
  577.9 38.3 reduce-scatter.7
